TPU v7x, 256 devices: a whole 4x4x8 slice. The times are simulated.
256 devices in a mesh: seq: 256 (over y, z, x, core).
Axes of the slice: x: 4, y: 4, z: 8, core: 2. Of those that a mesh axis runs over, the one named last changes fastest.
Arguments:
- inputs: bfloat16 [131072, 3072], P('seq'), may hold values from -6 to 6
- query_proj: bfloat16 [131072, 192], P('seq'), may hold values from -6 to 6
- key_proj: bfloat16 [131072, 192], P('seq'), may hold values from -6 to 6
- value_proj: bfloat16 [131072, 192], P('seq'), may hold values from -6 to 6
- grad_out: bfloat16 [131072, 192], P('seq'), may hold values from -6 to 6
Outputs:
- query_weight_grad: float32 [3072, 192], P('seq')
- key_weight_grad: float32 [3072, 192], P('seq')
- value_weight_grad: float32 [3072, 192], P('seq')
All inputs are finite; a program needn't handle non-finite values.
Results may differ from a plain program's by a relative error of at most 0.0041.
Values sent between devices are 32-bit elements; how exact they have to be, the bound alone decides.
No kernel may reach another device: no remote copies, remote signals or barrier semaphores. Data moves between devices by JAX's collectives and lax.ppermute only.
A program may use at most 192 MiB of HBM per device.

v0:
```python
import math

import jax
import jax.numpy as jnp
from jax import lax
from jax.sharding import PartitionSpec as P

HEAD = 96


def entering(value, axis, join, neutral, backward):
    count, mine = (lax.axis_size(axis), lax.axis_index(axis))
    pieces = lax.all_gather(value, axis)
    if backward:
        pieces = pieces[::-1]
        mine = count - 1 - mine
    so_far = jnp.full_like(value, 0) + jnp.asarray(neutral, value.dtype)

    def hop(position, so_far):
        longer = join(so_far, pieces[position])
        return jnp.where(position < mine, longer, so_far)

    return lax.fori_loop(0, count - 1, hop, so_far)


def add_pair(earlier, later):
    return earlier + later


def causal_mask(length):
    position = jnp.arange(length)
    return (position[:, None] <= position[None, :])[None]


def query_grads(queries, keys_in, values_in, grad_rows, before, factor):
    length = queries.shape[0]
    value_grad = jnp.einsum(
        "sha,tha->hst", values_in, grad_rows, preferred_element_type=jnp.float32
    )
    value_grad = jnp.where(causal_mask(length), value_grad, 0.0).astype(jnp.bfloat16)
    before_b = before.astype(jnp.bfloat16)
    result = jnp.einsum("hst,sha->tha", value_grad, keys_in, preferred_element_type=jnp.float32)
    result = result + jnp.einsum(
        "thb,hab->tha", grad_rows, before_b, preferred_element_type=jnp.float32
    )
    return ((factor * result).astype(jnp.bfloat16).reshape(length, -1), value_grad)


def key_value_grads(queries, keys_in, values_in, grad_rows, value_grad, later_sum, factor):
    length = queries.shape[0]
    key_query = jnp.einsum("sha,tha->hst", keys_in, queries, preferred_element_type=jnp.float32)
    key_query = jnp.where(causal_mask(length), key_query, 0.0).astype(jnp.bfloat16)
    later_b = later_sum.astype(jnp.bfloat16)
    key_grad = jnp.einsum("hst,tha->sha", value_grad, queries, preferred_element_type=jnp.float32)
    key_grad = key_grad + jnp.einsum(
        "shb,hab->sha", values_in, later_b, preferred_element_type=jnp.float32
    )
    val_grad = jnp.einsum("hst,thb->shb", key_query, grad_rows, preferred_element_type=jnp.float32)
    val_grad = val_grad + jnp.einsum(
        "sha,hab->shb", keys_in, later_b, preferred_element_type=jnp.float32
    )
    return (
        (factor * key_grad).astype(jnp.bfloat16).reshape(length, -1),
        (factor * val_grad).astype(jnp.bfloat16).reshape(length, -1),
    )


def weight_term(inputs, grads):
    return lax.dot_general(
        inputs, grads, (((0,), (0,)), ((), ())), preferred_element_type=jnp.float32
    )


def per_device(inputs, query_proj, key_proj, value_proj, grad_out):
    length = query_proj.shape[0]
    width = query_proj.shape[1]
    head_count = width // HEAD
    devices = lax.axis_size("seq")
    factor = 1.0 / (math.sqrt(HEAD) * length * devices)
    queries = query_proj.reshape(length, head_count, HEAD)
    keys_in = key_proj.reshape(length, head_count, HEAD)
    values_in = value_proj.reshape(length, head_count, HEAD)
    grad_rows = grad_out.reshape(length, head_count, HEAD)
    key_state = jnp.einsum("tha,thb->hab", keys_in, values_in, preferred_element_type=jnp.float32)
    query_state = jnp.einsum("tha,thb->hab", queries, grad_rows, preferred_element_type=jnp.float32)
    zero_state = jnp.zeros_like(key_state)
    before = entering(key_state, "seq", add_pair, zero_state, False)
    later_sum = entering(query_state, "seq", add_pair, zero_state, True)
    query_grad, value_grad = query_grads(queries, keys_in, values_in, grad_rows, before, factor)
    key_grad, val_grad = key_value_grads(
        queries, keys_in, values_in, grad_rows, value_grad, later_sum, factor
    )
    stacked = jnp.concatenate([query_grad, key_grad, val_grad], axis=1)
    summed = lax.psum_scatter(weight_term(inputs, stacked), "seq", scatter_dimension=0, tiled=True)
    return (summed[:, :width], summed[:, width : 2 * width], summed[:, 2 * width :])


def solution(mesh):
    return jax.shard_map(
        per_device,
        mesh=mesh,
        in_specs=(P("seq", None), P("seq", None), P("seq", None), P("seq", None), P("seq", None)),
        out_specs=(P("seq", None), P("seq", None), P("seq", None)),
        check_vma=False,
    )
```

profile of v0, /device:TPU:1, one launch (start us, length us, event | category | flops | bytes accessed | tf_op | source)
XLA Modules:
  0.0 951.5 jit_solution(11638550297806552601)
XLA Ops:
  7.2 2.0 fusion.25
  9.4 1.9 fusion.24
  12.1 1.7 select_convert_fusion.1
  13.8 1.0 copy-done.1
  14.8 1.2 convolution_bitcast_fusion.4
  16.0 138.0 %all-gather.7.cloned.1.call-done = f32[512,96,96]{2,1,0:T(8,128)} async-done(((f32[2,96,96]{2,1,0:T(8,128)}), f32[512,96,96]{2,1,0:T(8,128)}) %all-gather.7.cloned.1.call-update) | async-done | bytes 18874384 | tf_op jit(solution)/shard_map/all_gather | solution.py:13
  154.0 18.6 %rev.3 = f32[256,2,96,96]{3,2,1,0:T(8,128)} reverse(f32[256,2,96,96]{3,2,1,0:T(8,128)} %bitcast.68), dimensions={0} | reverse | bytes 37748736 | tf_op jit(solution)/shard_map/rev | solution.py:15
  172.6 242.8 %while.29 = (s32[]{:T(128)}, f32[2,96,96]{2,1,0:T(8,128)S(1)}, s32[]{:T(128)}, f32[256,2,96,96]{3,2,1,0:T(8,128)}, s32[]{:T(128)}, /*index=5*/s32[]{:T(128)}) while((s32[]{:T(128)}, f32[2,96,96]{2,1,0:T(8,128)S(1)}, s32[]{:T(128)}, f32[256,2,96,96]{3,2,1,0:T(8,128)}, s32[]{:T(128)}, /*index=5*/s32[]{:T(128)}) %tuple.67), condition=%wide.region_3.4_spmd.clone, body=%wide.region_2.3_spmd.clone.sunk | while | flops 55300 | bytes 221277 | solution.py:23
  177.3 0.9 add_select_fusion.5
  179.2 0.9 add_select_fusion.5
  209.6 0.9 add_select_fusion.5
  210.6 0.9 add_select_fusion.5
  216.3 0.9 add_select_fusion.5
  225.8 0.9 add_select_fusion.5
  226.8 0.9 add_select_fusion.5
  242.0 0.9 add_select_fusion.5
  242.9 1.0 add_select_fusion.5
  248.7 0.9 add_select_fusion.5
  249.7 0.9 add_select_fusion.5
  252.5 0.9 add_select_fusion.5
  255.4 0.9 add_select_fusion.5
  257.3 0.9 add_select_fusion.5
  258.2 0.9 add_select_fusion.5
  260.2 0.9 add_select_fusion.5
  263.0 1.0 add_select_fusion.5
  264.0 0.9 add_select_fusion.5
  265.0 0.9 add_select_fusion.5
  265.9 1.0 add_select_fusion.5
  266.9 1.0 add_select_fusion.5
  268.9 0.9 add_select_fusion.5
  269.8 0.9 add_select_fusion.5
  272.7 0.9 add_select_fusion.5
  274.6 0.9 add_select_fusion.5
  275.6 0.9 add_select_fusion.5
  278.4 0.9 add_select_fusion.5
  281.3 0.9 add_select_fusion.5
  285.1 1.0 add_select_fusion.5
  287.0 1.0 add_select_fusion.5
  289.9 0.9 add_select_fusion.5
  415.4 1.0 convolution_bitcast_fusion.2
  416.4 2.7 fusion.8
  419.1 242.5 %while.28 = (s32[]{:T(128)}, f32[2,96,96]{2,1,0:T(8,128)S(1)}, s32[]{:T(128)}, f32[256,2,96,96]{3,2,1,0:T(8,128)}, s32[]{:T(128)}, /*index=5*/s32[]{:T(128)}) while((s32[]{:T(128)}, f32[2,96,96]{2,1,0:T(8,128)S(1)}, s32[]{:T(128)}, f32[256,2,96,96]{3,2,1,0:T(8,128)}, s32[]{:T(128)}, /*index=5*/s32[]{:T(128)}) %tuple.79), condition=%wide.region_1.2_spmd.clone, body=%wide.region_0.1_spmd.clone.sunk | while | flops 55300 | bytes 221277 | solution.py:23
  661.7 1.2 convolution_bitcast_fusion.5
  662.8 1.5 fusion.9
  664.3 1.3 fusion.10
  665.7 5.0 convolution_bitcast_fusion
  670.7 271.0 %all-reduce.3.cloned.1.call-done = f32[3072,576]{0,1:T(8,128)} async-done(((f32[3072,576]{0,1:T(8,128)}), f32[3072,576]{0,1:T(8,128)}) %all-reduce.3.cloned.1.call-update) | async-done | bytes 7077904
  941.7 1.3 fusion.23
  (501 shorter events, 447.0 us)
Async XLA Ops:
  7.2 658.5 %copy-start = (bf16[512,3072]{1,0:T(8,128)(2,1)S(1)}, bf16[512,3072]{1,0:T(8,128)(2,1)}, u32[]{:S(2)}) copy-start(bf16[512,3072]{1,0:T(8,128)(2,1)} %param.9) | copy-start | bytes 9437188
  7.2 7.6 copy-start.3
  7.2 146.8 %all-gather.7.cloned.1.call-start = ((), (), s32[]{:S(2)}) async-start(), calls=%async_computation.1 | async-start | bytes 25264128 | tf_op jit(solution)/shard_map/all_gather | solution.py:13
  9.3 409.8 %all-gather.5.cloned.1.call-start = ((), (), s32[]{:S(2)}) async-start(), calls=%async_computation | async-start | bytes 25264128 | tf_op jit(solution)/shard_map/all_gather | solution.py:13
  11.2 930.4 %all-reduce.3.cloned.1.call-start = ((), (), s32[]{:S(2)}) async-start(), calls=%async_computation.2 | async-start | bytes 14155776
  13.8 1.1 copy-start.1
  154.0 261.4 %copy-start.2 = (bf16[512,192]{0,1:T(8,128)(2,1)S(1)}, bf16[512,192]{0,1:T(8,128)(2,1)}, u32[]{:S(2)}) copy-start(bf16[512,192]{0,1:T(8,128)(2,1)} %param.11) | copy-start | bytes 589828
  661.6 4.0 copy-start.4
Sparse Core Ops, SparseCore 0:
  11.9 142.0 all-gather.6
  157.8 134.8 all-gather.4
  670.8 270.8 all-reduce.2
where the time goes:
time: 968 us; the launch traced here: 952 us
  other arithmetic  474 us (49%)
  waiting for transfers between devices  409 us (42%)
  local copies, waits for them, and re-layouts  23 us (2%)
  matrix products  19.5 us (2%)
  between operations  13.9 us (1%)
  loops' own time  12.2 us (1%)
    select_n x510, other arithmetic, hop(): return jnp.where(position < mine, longer, so_far)  473 us
    unnamed x4, waiting for transfers between devices  271 us
    all_gather x2, waiting for transfers between devices, entering(): pieces = lax.all_gather(value, axis)  138 us
  transfers between devices with their start and end apart: 3, of which 2 were waited for; matrix products, arithmetic and copies ran while one was open for 28% of the time, Pallas kernels for 0%

commit v1 on v0

v1 whole, which is shorter than its diff:
```python
import functools
import math

import jax
import jax.numpy as jnp
from jax import lax
from jax.experimental import pallas as pl
from jax.experimental.pallas import tpu as pltpu
from jax.sharding import PartitionSpec as P

HEAD = 96
NY, NZ, NX, NC = 4, 8, 4, 2
SEQ = "seq"
F32 = jnp.float32
BF16 = jnp.bfloat16


def coords(i):
    c, i = i % NC, i // NC
    x, i = i % NX, i // NX
    return i // NZ, i % NZ, x, c


def index(y, z, x, c):
    return ((y * NZ + z) * NX + x) * NC + c


def permute(value, move):
    count = NY * NZ * NX * NC
    return lax.ppermute(value, SEQ, [(i, index(*move(*coords(i)))) for i in range(count)])


def swap_cores(value):
    return permute(value, lambda y, z, x, c: (y, z, x, 1 - c))


def along_x(d):
    return lambda y, z, x, c: (y, z, (x + d * (1 - 2 * c)) % NX, c)


def along_y(d):
    return lambda y, z, x, c: ((y + d * (1 - 2 * c)) % NY, z, x, c)


def along_z_low(d):
    return lambda y, z, x, c: (y, z // 4 * 4 + (z % 4 + d * (1 - 2 * c)) % 4, x, c)


def along_z_high(d):
    return lambda y, z, x, c: (y, (z + 4 * d) % NZ, x, c)


def first_axis(d):
    return lambda y, z, x, c: (y, z, (x + d) % NX, c) if c == 0 else ((y + d) % NY, z, x, c)


def second_axis(d):
    return lambda y, z, x, c: ((y + d) % NY, z, x, c) if c == 0 else (y, z, (x + d) % NX, c)


def z_axis(d):
    return lambda y, z, x, c: (y, (z + d) % NZ, x, c)


def rows_dot(a, b):
    return lax.dot_general(a, b, (((0,), (0,)), ((), ())), preferred_element_type=F32)


def lanes_dot(a, b):
    return lax.dot_general(a, b, (((1,), (1,)), ((), ())), preferred_element_type=F32)


def head(ref, h):
    return ref[:, h * HEAD : (h + 1) * HEAD]


def states_kernel(core, q, k, v, g, keep, send):
    first = core[0] == 0
    for h in range(2):
        rows = slice(h * HEAD, (h + 1) * HEAD)
        key_state = rows_dot(head(k, h), head(v, h))
        query_state = rows_dot(head(q, h), head(g, h))
        keep[rows, :] = jnp.where(first, key_state, query_state)
        send[rows, :] = jnp.where(first, query_state, key_state)


def local_kernel(q, k, v, g, out):
    length = q.shape[0]
    s = lax.broadcasted_iota(jnp.int32, (length, length), 0)
    t = lax.broadcasted_iota(jnp.int32, (length, length), 1)
    causal = s <= t
    width = 2 * HEAD
    for h in range(2):
        qh, kh, vh, gh = head(q, h), head(k, h), head(v, h), head(g, h)
        vg = jnp.where(causal, lanes_dot(vh, gh), 0.0).astype(BF16)
        kq = jnp.where(causal, lanes_dot(kh, qh), 0.0).astype(BF16)
        at = h * HEAD
        out[:, at : at + HEAD] = rows_dot(vg, kh)
        out[:, width + at : width + at + HEAD] = jnp.dot(vg, qh, preferred_element_type=F32)
        out[:, 2 * width + at : 2 * width + at + HEAD] = jnp.dot(kq, gh, preferred_element_type=F32)


def weight_kernel(factor, core, x, loc, k, v, g, own, other, keep, send, d, block):
    y = pl.program_id(0)
    c = core[0]

    @pl.when(y == 0)
    def _():
        width = 2 * HEAD
        first = c == 0
        before = jnp.where(first, own[...], other[...]).astype(BF16)
        later = jnp.where(first, other[...], own[...]).astype(BF16)
        for h in range(2):
            rows = slice(h * HEAD, (h + 1) * HEAD)
            parts = (
                lanes_dot(head(g, h), before[rows, :]),
                lanes_dot(head(v, h), later[rows, :]),
                jnp.dot(head(k, h), later[rows, :], preferred_element_type=F32),
            )
            for n, part in enumerate(parts):
                at = n * width + h * HEAD
                d[:, at : at + HEAD] = (factor * (loc[:, at : at + HEAD] + part)).astype(BF16)

    block[...] = rows_dot(x[...], d[...])
    for half in range(2):
        ref_for = {0: keep, 1: send}
        for role in range(2):
            ref = ref_for[role]

            @pl.when(c == (half if role == 0 else 1 - half))
            def _(ref=ref, half=half):
                for xi in range(NX):
                    for z in range(NZ):
                        at = ((z * NX + xi) * NC + half) * 12
                        value = block[at : at + 12, :]
                        if half == 0:
                            ref[xi, y, z * 12 : z * 12 + 12, :] = value
                        else:
                            ref[y, xi, z * 12 : z * 12 + 12, :] = value


VMEM = pl.BlockSpec(memory_space=pltpu.VMEM)
SMEM = pl.BlockSpec(memory_space=pltpu.SMEM)


def cost(flops, moved):
    return pl.CostEstimate(flops=flops, bytes_accessed=moved, transcendentals=0)


def states(core, q, k, v, g):
    shape = jax.ShapeDtypeStruct((2 * HEAD, HEAD), F32)
    return pl.pallas_call(
        states_kernel,
        out_shape=(shape, shape),
        in_specs=[SMEM] + [VMEM] * 4,
        out_specs=(VMEM, VMEM),
        cost_estimate=cost(4 * 512 * 192 * 192, 10**6),
    )(core, q, k, v, g)


def local(q, k, v, g):
    return pl.pallas_call(
        local_kernel,
        out_shape=jax.ShapeDtypeStruct((q.shape[0], 6 * HEAD), F32),
        in_specs=[VMEM] * 4,
        out_specs=VMEM,
        cost_estimate=cost(20 * 512 * 512 * 96, 2 * 10**6),
        compiler_params=pltpu.CompilerParams(vmem_limit_bytes=24 * 2**20),
    )(q, k, v, g)


def weight_terms(core, x, loc, k, v, g, own, other, factor):
    length, features = x.shape
    rows = features // NY
    whole = lambda a: pl.BlockSpec(a.shape, lambda y: (0,) * a.ndim)
    shape = jax.ShapeDtypeStruct((NX, NY, NZ * 12, 6 * HEAD), F32)
    out = pl.BlockSpec(shape.shape, lambda y: (0, 0, 0, 0))
    return pl.pallas_call(
        functools.partial(weight_kernel, factor),
        grid=(NY,),
        out_shape=(shape, shape),
        in_specs=[SMEM, pl.BlockSpec((length, rows), lambda y: (0, y))]
        + [whole(a) for a in (loc, k, v, g, own, other)],
        out_specs=(out, out),
        scratch_shapes=[pltpu.VMEM((length, 6 * HEAD), BF16), pltpu.VMEM((rows, 6 * HEAD), F32)],
        cost_estimate=cost(2 * 512 * 3072 * 576, 12 * 10**6),
        compiler_params=pltpu.CompilerParams(vmem_limit_bytes=48 * 2**20),
    )(core, x, loc, k, v, g, own, other)


def gather_before(total, move, count, rank):
    before = jnp.zeros_like(total)
    whole = total
    for d in range(1, count):
        came = permute(total, move(d))
        before = before + jnp.where(rank >= d, came, 0.0)
        whole = whole + came
    return before, whole


def entering(core, me, keep, send):
    y, z, x, c = me
    chip = keep + swap_cores(send)
    flip = lambda p, n: jnp.where(c == 0, p, n - 1 - p)
    before, total = gather_before(chip, along_x, NX, flip(x, NX))
    more, total = gather_before(total, along_z_low, 4, flip(z % 4, 4))
    before = before + more
    more, total = gather_before(total, along_z_high, 2, flip(z // 4, 2))
    before = before + more
    more, _ = gather_before(total, along_y, NY, flip(y, NY))
    before = before + more
    return before, swap_cores(before + keep)


def pick(array, i):
    return lax.dynamic_index_in_dim(array, i, 0, keepdims=False)


def scatter_sum(me, keep, send):
    y, z, x, c = me
    mine = jnp.where(c == 0, x, y)
    partner = jnp.where(c == 0, y, x)
    far = (2, 1, 3, 0)
    total = None
    for d in far:
        part = pick(keep, (mine + d) % 4) + swap_cores(pick(send, (partner + d) % 4))
        if d:
            part = permute(part, first_axis(d))
        total = part if total is None else total + part
    value, total = total, None
    for d in far:
        part = pick(value, (partner + d) % 4)
        if d:
            part = permute(part, second_axis(d))
        total = part if total is None else total + part
    value = total.reshape(NZ, 12, total.shape[-1])
    total = pick(value, z)
    for d in (4, 3, 5, 2, 6, 1, 7):
        total = total + permute(pick(value, (z + d) % NZ), z_axis(d))
    return total


def per_device(inputs, query_proj, key_proj, value_proj, grad_out):
    length, width = query_proj.shape
    factor = 1.0 / (math.sqrt(HEAD) * length * lax.axis_size(SEQ))
    me = coords(lax.axis_index(SEQ))
    core = me[3].astype(jnp.int32).reshape(1)
    keep, send = states(core, query_proj, key_proj, value_proj, grad_out)
    loc = local(query_proj, key_proj, value_proj, grad_out)
    own, other = entering(core, me, keep, send)
    keep, send = weight_terms(
        core, inputs, loc, key_proj, value_proj, grad_out, own, other, factor
    )
    summed = scatter_sum(me, keep, send)
    return (summed[:, :width], summed[:, width : 2 * width], summed[:, 2 * width :])


def solution(mesh):
    return jax.shard_map(
        per_device,
        mesh=mesh,
        in_specs=(P(SEQ, None),) * 5,
        out_specs=(P(SEQ, None),) * 3,
        check_vma=False,
    )
```

time: 968 us -> 145 us (0.15)
  the two profiles are of different devices: /device:TPU:1 before, /device:TPU:32 now
where the time goes in v1:
time: 145 us; the launch traced here: 144 us
  waiting for transfers between devices  64.1 us (44%)
  starting transfers between devices  45.1 us (31%)
  local copies, waits for them, and re-layouts  13.7 us (9%)
  Pallas kernels  12.3 us (8%)
  other arithmetic  8.34 us (6%)
    ppermute x29, waiting for transfers between devices, permute(): lax.ppermute(value, SEQ, [(i, index(*move(*coords(i)))) for i in range(co...  64.1 us
    ppermute x29, starting transfers between devices, permute(): lax.ppermute(value, SEQ, [(i, index(*move(*coords(i)))) for i in range(co...  45.1 us
    unnamed x14, local copies, waits for them, and re-layouts  9.09 us
    pallas_call x1, Pallas kernels, weight_terms(): pl.pallas_call(functools.partial(weight_kernel, factor), grid=(NY,), out_...  7.93 us
    add x1, other arithmetic, scatter_sum(): pick(keep, (mine + d) % 4) + swap_cores(pick(send, (partner + d) % 4))  4.02 us
    squeeze x3, local copies, waits for them, and re-layouts, pick(): return lax.dynamic_index_in_dim(array, i, 0, keepdims=False)  3.86 us
  transfers between devices with their start and end apart: 29, of which 20 were waited for; matrix products, arithmetic and copies ran while one was open for 3% of the time, Pallas kernels for 1%

profile of v1, /device:TPU:32, one launch (start us, length us, event | category | flops | bytes accessed | tf_op | source)
XLA Modules:
  0.0 144.4 jit_solution(6987495163210310688)
XLA Ops:
  0.6 1.8 %copy.19.q = bf16[512,192]{1,0:T(8,128)(2,1)} copy(bf16[512,192]{0,1:T(8,128)(2,1)} %param.6) | data formatting | bytes 393216 | tf_op args[1]
  2.4 1.8 %copy.20.k = bf16[512,192]{1,0:T(8,128)(2,1)} copy(bf16[512,192]{0,1:T(8,128)(2,1)} %param.7) | data formatting | bytes 393216 | tf_op args[2]
  4.2 1.8 %copy.21.v = bf16[512,192]{1,0:T(8,128)(2,1)} copy(bf16[512,192]{0,1:T(8,128)(2,1)} %param.8) | data formatting | bytes 393216 | tf_op args[3]
  6.0 1.8 %copy.22.g = bf16[512,192]{1,0:T(8,128)(2,1)} copy(bf16[512,192]{0,1:T(8,128)(2,1)} %param.9) | data formatting | bytes 393216 | tf_op args[4]
  7.8 2.6 %shard_map.77 = (f32[192,96]{1,0:T(8,128)}, f32[192,96]{1,0:T(8,128)}) custom-call(s32[1]{0:T(128)} %bitcast.core, bf16[512,192]{1,0:T(8,128)(2,1)} %copy.19.q, bf16[512,192]{1,0:T(8,128)(2,1)} %copy.20.k, bf16[512,192]{1,0:T(8,128)(2,1)} %copy.21.v, bf16[512,192]{1,0:T(8,128)(2,1)} %copy.22.g), custom_call_target="tpu_custom_call" | custom-call | flops 75497472 | bytes 1000000 | tf_op jit(solution)/shard_map/pallas_call | solution.py:152
  10.4 1.5 %collective-permute-done = f32[192,96]{1,0:T(8,128)S(1)} collective-permute-done((f32[192,96]{1,0:T(8,128)}, f32[192,96]{1,0:T(8,128)S(1)}, u32[]{:S(2)}, u32[]{:S(2)}) %collective-permute-start) | collective-permute-done | bytes 73760 | tf_op jit(solution)/shard_map/ppermute | solution.py:30
  11.9 0.9 add.270
  12.8 2.8 %collective-permute-start.3 = (f32[192,96]{1,0:T(8,128)S(1)}, f32[192,96]{1,0:T(8,128)S(1)}, u32[]{:S(2)}, u32[]{:S(2)}) collective-permute-start(f32[192,96]{1,0:T(8,128)S(1)} %add.270), channel_id=1, source_target_pairs={{0,6},{1,3},{2,0},{3,5},{4,2},{5,7},{6,4},{7,1},{8,14},{9,11},{10,... | collective-permute-start | bytes 221192 | tf_op jit(solution)/shard_map/ppermute | solution.py:30
  16.4 0.9 collective-permute-start.1
  17.3 2.8 %collective-permute-done.3 = f32[192,96]{1,0:T(8,128)S(1)} collective-permute-done((f32[192,96]{1,0:T(8,128)S(1)}, f32[192,96]{1,0:T(8,128)S(1)}, u32[]{:S(2)}, u32[]{:S(2)}) %collective-permute-start.3) | collective-permute-done | bytes 73760 | tf_op jit(solution)/shard_map/ppermute | solution.py:30
  20.1 1.7 %collective-permute-done.2 = f32[192,96]{1,0:T(8,128)S(1)} collective-permute-done((f32[192,96]{1,0:T(8,128)S(1)}, f32[192,96]{1,0:T(8,128)S(1)}, u32[]{:S(2)}, u32[]{:S(2)}) %collective-permute-start.2) | collective-permute-done | bytes 73760 | tf_op jit(solution)/shard_map/ppermute | solution.py:30
  21.8 1.0 collective-permute-done.1
  23.0 3.3 %collective-permute-start.5 = (f32[192,96]{1,0:T(8,128)S(1)}, f32[192,96]{1,0:T(8,128)S(1)}, u32[]{:S(2)}, u32[]{:S(2)}) collective-permute-start(f32[192,96]{1,0:T(8,128)S(1)} %add_add_fusion.2), channel_id=1, source_target_pairs={{0,16},{1,17},{2,18},{3,19},{4,20},{5,21},{6,22},{7,23},{8,24},{9,... | collective-permute-start | bytes 221192 | tf_op jit(solution)/shard_map/ppermute | solution.py:30
  26.3 2.8 %collective-permute-start.4 = (f32[192,96]{1,0:T(8,128)S(1)}, f32[192,96]{1,0:T(8,128)S(1)}, u32[]{:S(2)}, u32[]{:S(2)}) collective-permute-start(f32[192,96]{1,0:T(8,128)S(1)} %add_add_fusion.2), channel_id=1, source_target_pairs={{0,8},{1,25},{2,10},{3,27},{4,12},{5,29},{6,14},{7,31},{8,16},{9,1... | collective-permute-start | bytes 221192 | tf_op jit(solution)/shard_map/ppermute | solution.py:30
  29.1 0.9 collective-permute-done.6
  30.1 1.2 collective-permute-done.5
  31.3 1.1 collective-permute-done.4
  32.4 6.4 %collective-permute-start.7 = (f32[192,96]{1,0:T(8,128)S(1)}, f32[192,96]{1,0:T(8,128)S(1)}, u32[]{:S(2)}, u32[]{:S(2)}) collective-permute-start(f32[192,96]{1,0:T(8,128)S(1)} %add_add_fusion.1), channel_id=1, source_target_pairs={{0,32},{1,33},{2,34},{3,35},{4,36},{5,37},{6,38},{7,39},{8,40},{9,... | collective-permute-start | bytes 221192 | tf_op jit(solution)/shard_map/ppermute | solution.py:30
  38.8 5.4 %collective-permute-done.7 = f32[192,96]{1,0:T(8,128)S(1)} collective-permute-done((f32[192,96]{1,0:T(8,128)S(1)}, f32[192,96]{1,0:T(8,128)S(1)}, u32[]{:S(2)}, u32[]{:S(2)}) %collective-permute-start.7) | collective-permute-done | bytes 73760 | tf_op jit(solution)/shard_map/ppermute | solution.py:30
  44.2 2.9 %collective-permute-start.10 = (f32[192,96]{1,0:T(8,128)S(1)}, f32[192,96]{1,0:T(8,128)S(1)}, u32[]{:S(2)}, u32[]{:S(2)}) collective-permute-start(f32[192,96]{1,0:T(8,128)S(1)} %add.285), channel_id=1, source_target_pairs={{0,192},{1,65},{2,194},{3,67},{4,196},{5,69},{6,198},{7,71},{8,200... | collective-permute-start | bytes 221192 | tf_op jit(solution)/shard_map/ppermute | solution.py:30
  47.8 1.0 collective-permute-start.8
  48.8 2.8 %collective-permute-done.10 = f32[192,96]{1,0:T(8,128)S(1)} collective-permute-done((f32[192,96]{1,0:T(8,128)S(1)}, f32[192,96]{1,0:T(8,128)S(1)}, u32[]{:S(2)}, u32[]{:S(2)}) %collective-permute-start.10) | collective-permute-done | bytes 73760 | tf_op jit(solution)/shard_map/ppermute | solution.py:30
  51.6 1.8 %collective-permute-done.9 = f32[192,96]{1,0:T(8,128)S(1)} collective-permute-done((f32[192,96]{1,0:T(8,128)S(1)}, f32[192,96]{1,0:T(8,128)S(1)}, u32[]{:S(2)}, u32[]{:S(2)}) %collective-permute-start.9) | collective-permute-done | bytes 73760 | tf_op jit(solution)/shard_map/ppermute | solution.py:30
  53.4 1.0 collective-permute-done.8
  54.4 1.0 fusion.7
  55.7 1.8 %shard_map.76.loc = f32[512,576]{1,0:T(8,128)S(1)} custom-call(bf16[512,192]{1,0:T(8,128)(2,1)S(1)} %copy-done.3, bf16[512,192]{1,0:T(8,128)(2,1)S(1)} %copy-done, bf16[512,192]{1,0:T(8,128)(2,1)S(1)} %copy-done.1, bf16[512,192]{1,0:T(8,128)(2,1)S(1)} %copy-done.2), custom_call_target="tpu_custom_call" | custom-call | flops 503316480 | bytes 2000000 | tf_op jit(solution)/shard_map/pallas_call | solution.py:162
  57.6 1.9 %copy-done.4 = bf16[512,3072]{1,0:T(8,128)(2,1)S(1)} copy-done((bf16[512,3072]{1,0:T(8,128)(2,1)S(1)}, bf16[512,3072]{1,0:T(8,128)(2,1)}, u32[]{:S(2)}) %copy-start.4) | copy-done | bytes 3145752
  59.5 7.9 %shard_map.78 = (f32[4,4,96,576]{3,2,1,0:T(8,128)}, f32[4,4,96,576]{3,2,1,0:T(8,128)}) custom-call(s32[1]{0:T(128)} %bitcast.core, bf16[512,3072]{1,0:T(8,128)(2,1)S(1)} %copy-done.4, f32[512,576]{1,0:T(8,128)S(1)} %shard_map.76.loc, bf16[512,192]{1,0:T(8,128)(2,1)S(1)} %copy-done, bf16[512,192]{1,0:T(8,128)(2,1)S(1)} %copy-done.1, ...), custom_call_target="tpu_custom_call" | custom-call | flops 1811939328 | bytes 12000000 | tf_op jit(solution)/shard_map/pallas_call | solution.py:178
  67.4 3.8 %dynamic-slice_bitcast_fusion.2 = (f32[4,96,576]{2,1,0:T(8,128)}, f32[4,96,576]{2,1,0:T(8,128)S(1)}, f32[4,96,576]{2,1,0:T(8,128)}, f32[4,96,576]{2,1,0:T(8,128)S(1)}) fusion(f32[4,4,96,576]{3,2,1,0:T(8,128)} %get-tuple-element.10, s32[]{:T(128)S(6)} %select_n.276, s32[]{:T(128)S(6)} %select_n.284, s32[]{:T(128)S(6)} %select_n.280, s32[]{:T(128)S(6)} %select_n.272), kind=kLoop, calls=%fused_computation.7 | loop fusion | bytes 7077904 | tf_op jit(solution)/shard_map/jit(dynamic_index_in_dim)/squeeze | solution.py:216
  72.2 3.2 %collective-permute-done.14 = f32[4,96,576]{2,1,0:T(8,128)S(1)} collective-permute-done((f32[4,96,576]{2,1,0:T(8,128)}, f32[4,96,576]{2,1,0:T(8,128)S(1)}, u32[]{:S(2)}, u32[]{:S(2)}) %collective-permute-start.14) | collective-permute-done | bytes 884768 | tf_op jit(solution)/shard_map/ppermute | solution.py:30
  75.3 1.5 %collective-permute-done.16 = f32[4,96,576]{2,1,0:T(8,128)} collective-permute-done((f32[4,96,576]{2,1,0:T(8,128)}, f32[4,96,576]{2,1,0:T(8,128)}, u32[]{:S(2)}, u32[]{:S(2)}) %collective-permute-start.16) | collective-permute-done | bytes 884768 | tf_op jit(solution)/shard_map/ppermute | solution.py:30
  76.9 4.0 %bitcast_add_fusion.2 = (f32[4,96,576]{2,1,0:T(8,128)S(1)}, f32[4,96,576]{2,1,0:T(8,128)}, f32[4,96,576]{2,1,0:T(8,128)}) fusion(f32[4,96,576]{2,1,0:T(8,128)S(1)} %collective-permute-done.14, f32[4,4,96,576]{3,2,1,0:T(8,128)} %get-tuple-element.9, s32[]{:T(128)S(6)} %select_n.274, f32[4,96,576]{2,1,0:T(8,128)} %collective-permute-done.16, s32[]{:T(128)S(6)} %select_n.278, ...), kind=kLoop, calls=%fused_computation.3 | loop fusion | flops 663552 | bytes 7962636 | tf_op jit(solution)/shard_map/add | solution.py:226
  80.9 2.8 %collective-permute-start.17 = (f32[4,96,576]{2,1,0:T(8,128)}, f32[4,96,576]{2,1,0:T(8,128)S(1)}, u32[]{:S(2)}, u32[]{:S(2)}) collective-permute-start(f32[4,96,576]{2,1,0:T(8,128)} %get-tuple-element.14), channel_id=1, source_target_pairs={{0,6},{1,193},{2,0},{3,195},{4,2},{5,197},{6,4},{7,199},{8,14},{9,... | collective-permute-start | bytes 2654216 | tf_op jit(solution)/shard_map/ppermute | solution.py:30
  83.7 0.9 collective-permute-start.15
  84.6 21.6 %collective-permute-done.17 = f32[4,96,576]{2,1,0:T(8,128)S(1)} collective-permute-done((f32[4,96,576]{2,1,0:T(8,128)}, f32[4,96,576]{2,1,0:T(8,128)S(1)}, u32[]{:S(2)}, u32[]{:S(2)}) %collective-permute-start.17) | collective-permute-done | bytes 884768 | tf_op jit(solution)/shard_map/ppermute | solution.py:30
  106.2 3.5 %collective-permute-done.15 = f32[4,96,576]{2,1,0:T(8,128)} collective-permute-done((f32[4,96,576]{2,1,0:T(8,128)S(1)}, f32[4,96,576]{2,1,0:T(8,128)}, u32[]{:S(2)}, u32[]{:S(2)}) %collective-permute-start.15) | collective-permute-done | bytes 884768 | tf_op jit(solution)/shard_map/ppermute | solution.py:30
  109.7 2.3 %fusion = f32[4,96,576]{2,1,0:T(8,128)S(1)} fusion(f32[4,96,576]{2,1,0:T(8,128)} %collective-permute-done.18, f32[4,4,96,576]{3,2,1,0:T(8,128)} %get-tuple-element.9, s32[]{:T(128)S(6)} %select_n.282, f32[4,96,576]{2,1,0:T(8,128)S(1)} %collective-permute-done.17, f32[4,96,576]{2,1,0:T(8,128)} %collective-permute-done.13, f32[4,96,576]{2,1,0:T(8,128)} %collective-permute-done.15), kind=kLoop, calls=%fused_computation.1 | loop fusion | flops 884736 | bytes 5308420 | tf_op jit(solution)/shard_map/add | solution.py:229
  112.1 1.6 %collective-permute-start.21 = (f32[96,576]{1,0:T(8,128)S(1)}, f32[96,576]{1,0:T(8,128)S(1)}, u32[]{:S(2)}, u32[]{:S(2)}) collective-permute-start(f32[96,576]{1,0:T(8,128)S(1)} %get-tuple-element.21), channel_id=1, source_target_pairs={{0,192},{1,7},{2,194},{3,1},{4,196},{5,3},{6,198},{7,5},{8,200},{9... | collective-permute-start | bytes 663560 | tf_op jit(solution)/shard_map/ppermute | solution.py:30
  115.1 3.2 %collective-permute-done.21 = f32[96,576]{1,0:T(8,128)S(1)} collective-permute-done((f32[96,576]{1,0:T(8,128)S(1)}, f32[96,576]{1,0:T(8,128)S(1)}, u32[]{:S(2)}, u32[]{:S(2)}) %collective-permute-start.21) | collective-permute-done | bytes 221216 | tf_op jit(solution)/shard_map/ppermute | solution.py:30
  118.3 3.1 %collective-permute-done.19 = f32[96,576]{1,0:T(8,128)S(1)} collective-permute-done((f32[96,576]{1,0:T(8,128)S(1)}, f32[96,576]{1,0:T(8,128)S(1)}, u32[]{:S(2)}, u32[]{:S(2)}) %collective-permute-start.19) | collective-permute-done | bytes 221216 | tf_op jit(solution)/shard_map/ppermute | solution.py:30
  121.5 2.5 %collective-permute-done.20 = f32[96,576]{1,0:T(8,128)S(1)} collective-permute-done((f32[96,576]{1,0:T(8,128)S(1)}, f32[96,576]{1,0:T(8,128)S(1)}, u32[]{:S(2)}, u32[]{:S(2)}) %collective-permute-start.20) | collective-permute-done | bytes 221216 | tf_op jit(solution)/shard_map/ppermute | solution.py:30
  124.2 2.0 %collective-permute-start.27 = (f32[12,576]{1,0:T(8,128)S(1)}, f32[12,576]{1,0:T(8,128)S(1)}, u32[]{:S(2)}, u32[]{:S(2)}) collective-permute-start(f32[12,576]{1,0:T(8,128)S(1)} %get-tuple-element.25), channel_id=1, source_target_pairs={{0,8},{1,9},{2,10},{3,11},{4,12},{5,13},{6,14},{7,15},{8,16},{9,17... | collective-permute-start | bytes 82952 | tf_op jit(solution)/shard_map/ppermute | solution.py:30
  126.2 4.5 %collective-permute-start.26 = (f32[12,576]{1,0:T(8,128)S(1)}, f32[12,576]{1,0:T(8,128)S(1)}, u32[]{:S(2)}, u32[]{:S(2)}) collective-permute-start(f32[12,576]{1,0:T(8,128)S(1)} %get-tuple-element.26), channel_id=1, source_target_pairs={{0,48},{1,49},{2,50},{3,51},{4,52},{5,53},{6,54},{7,55},{8,56},{9,... | collective-permute-start | bytes 82952 | tf_op jit(solution)/shard_map/ppermute | solution.py:30
  130.7 3.4 %collective-permute-start.24 = (f32[12,576]{1,0:T(8,128)S(1)}, f32[12,576]{1,0:T(8,128)S(1)}, u32[]{:S(2)}, u32[]{:S(2)}) collective-permute-start(f32[12,576]{1,0:T(8,128)S(1)} %get-tuple-element.28), channel_id=1, source_target_pairs={{0,40},{1,41},{2,42},{3,43},{4,44},{5,45},{6,46},{7,47},{8,48},{9,... | collective-permute-start | bytes 82952 | tf_op jit(solution)/shard_map/ppermute | solution.py:30
  134.1 1.6 %collective-permute-start.23 = (f32[12,576]{1,0:T(8,128)S(1)}, f32[12,576]{1,0:T(8,128)S(1)}, u32[]{:S(2)}, u32[]{:S(2)}) collective-permute-start(f32[12,576]{1,0:T(8,128)S(1)} %get-tuple-element.29), channel_id=1, source_target_pairs={{0,24},{1,25},{2,26},{3,27},{4,28},{5,29},{6,30},{7,31},{8,32},{9,... | collective-permute-start | bytes 82952 | tf_op jit(solution)/shard_map/ppermute | solution.py:30
  135.7 3.7 %collective-permute-start.22 = (f32[12,576]{1,0:T(8,128)S(1)}, f32[12,576]{1,0:T(8,128)S(1)}, u32[]{:S(2)}, u32[]{:S(2)}) collective-permute-start(f32[12,576]{1,0:T(8,128)S(1)} %get-tuple-element.23), channel_id=1, source_target_pairs={{0,32},{1,33},{2,34},{3,35},{4,36},{5,37},{6,38},{7,39},{8,40},{9,... | collective-permute-start | bytes 82952 | tf_op jit(solution)/shard_map/ppermute | solution.py:30
  139.4 2.2 %collective-permute-done.23 = f32[12,576]{1,0:T(8,128)S(1)} collective-permute-done((f32[12,576]{1,0:T(8,128)S(1)}, f32[12,576]{1,0:T(8,128)S(1)}, u32[]{:S(2)}, u32[]{:S(2)}) %collective-permute-start.23) | collective-permute-done | bytes 27680 | tf_op jit(solution)/shard_map/ppermute | solution.py:30
  141.6 2.0 %collective-permute-done.22 = f32[12,576]{1,0:T(8,128)S(1)} collective-permute-done((f32[12,576]{1,0:T(8,128)S(1)}, f32[12,576]{1,0:T(8,128)S(1)}, u32[]{:S(2)}, u32[]{:S(2)}) %collective-permute-start.22) | collective-permute-done | bytes 27680 | tf_op jit(solution)/shard_map/ppermute | solution.py:30
  (41 shorter events, 5.5 us)
Async XLA Ops:
  2.4 53.3 %copy-start.3 = (bf16[512,192]{1,0:T(8,128)(2,1)S(1)}, bf16[512,192]{1,0:T(8,128)(2,1)}, u32[]{:S(2)}) copy-start(bf16[512,192]{1,0:T(8,128)(2,1)} %copy.19.q) | copy-start | bytes 589828
  4.2 51.5 %copy-start = (bf16[512,192]{1,0:T(8,128)(2,1)S(1)}, bf16[512,192]{1,0:T(8,128)(2,1)}, u32[]{:S(2)}) copy-start(bf16[512,192]{1,0:T(8,128)(2,1)} %copy.20.k) | copy-start | bytes 589828
  6.0 49.7 %copy-start.1 = (bf16[512,192]{1,0:T(8,128)(2,1)S(1)}, bf16[512,192]{1,0:T(8,128)(2,1)}, u32[]{:S(2)}) copy-start(bf16[512,192]{1,0:T(8,128)(2,1)} %copy.21.v) | copy-start | bytes 589828
  7.8 47.9 %copy-start.2 = (bf16[512,192]{1,0:T(8,128)(2,1)S(1)}, bf16[512,192]{1,0:T(8,128)(2,1)}, u32[]{:S(2)}) copy-start(bf16[512,192]{1,0:T(8,128)(2,1)} %copy.22.g) | copy-start | bytes 589828
  10.4 1.5 %collective-permute-start = (f32[192,96]{1,0:T(8,128)}, f32[192,96]{1,0:T(8,128)S(1)}, u32[]{:S(2)}, u32[]{:S(2)}) collective-permute-start(f32[192,96]{1,0:T(8,128)} %get-tuple-element.8), channel_id=1, source_target_pairs={{0,1},{1,0},{2,3},{3,2},{4,5},{5,4},{6,7},{7,6},{8,9},{9,8},{10,11... | collective-permute-start | bytes 221192 | tf_op jit(solution)/shard_map/ppermute | solution.py:30
  12.8 7.3 %collective-permute-start.3 = (f32[192,96]{1,0:T(8,128)S(1)}, f32[192,96]{1,0:T(8,128)S(1)}, u32[]{:S(2)}, u32[]{:S(2)}) collective-permute-start(f32[192,96]{1,0:T(8,128)S(1)} %add.270), channel_id=1, source_target_pairs={{0,6},{1,3},{2,0},{3,5},{4,2},{5,7},{6,4},{7,1},{8,14},{9,11},{10,... | collective-permute-start | bytes 221192 | tf_op jit(solution)/shard_map/ppermute | solution.py:30
  15.6 6.2 %collective-permute-start.2 = (f32[192,96]{1,0:T(8,128)S(1)}, f32[192,96]{1,0:T(8,128)S(1)}, u32[]{:S(2)}, u32[]{:S(2)}) collective-permute-start(f32[192,96]{1,0:T(8,128)S(1)} %add.270), channel_id=1, source_target_pairs={{0,4},{1,5},{2,6},{3,7},{4,0},{5,1},{6,2},{7,3},{8,12},{9,13},{10,... | collective-permute-start | bytes 221192 | tf_op jit(solution)/shard_map/ppermute | solution.py:30
  16.4 6.4 %collective-permute-start.1 = (f32[192,96]{1,0:T(8,128)S(1)}, f32[192,96]{1,0:T(8,128)S(1)}, u32[]{:S(2)}, u32[]{:S(2)}) collective-permute-start(f32[192,96]{1,0:T(8,128)S(1)} %add.270), channel_id=1, source_target_pairs={{0,2},{1,7},{2,4},{3,1},{4,6},{5,3},{6,0},{7,5},{8,10},{9,15},{10,... | collective-permute-start | bytes 221192 | tf_op jit(solution)/shard_map/ppermute | solution.py:30
  22.8 7.2 %collective-permute-start.6 = (f32[192,96]{1,0:T(8,128)S(1)}, f32[192,96]{1,0:T(8,128)S(1)}, u32[]{:S(2)}, u32[]{:S(2)}) collective-permute-start(f32[192,96]{1,0:T(8,128)S(1)} %add_add_fusion.2), channel_id=1, source_target_pairs={{0,24},{1,9},{2,26},{3,11},{4,28},{5,13},{6,30},{7,15},{8,0},{9,17... | collective-permute-start | bytes 221192 | tf_op jit(solution)/shard_map/ppermute | solution.py:30
  23.0 8.3 %collective-permute-start.5 = (f32[192,96]{1,0:T(8,128)S(1)}, f32[192,96]{1,0:T(8,128)S(1)}, u32[]{:S(2)}, u32[]{:S(2)}) collective-permute-start(f32[192,96]{1,0:T(8,128)S(1)} %add_add_fusion.2), channel_id=1, source_target_pairs={{0,16},{1,17},{2,18},{3,19},{4,20},{5,21},{6,22},{7,23},{8,24},{9,... | collective-permute-start | bytes 221192 | tf_op jit(solution)/shard_map/ppermute | solution.py:30
  26.3 6.0 %collective-permute-start.4 = (f32[192,96]{1,0:T(8,128)S(1)}, f32[192,96]{1,0:T(8,128)S(1)}, u32[]{:S(2)}, u32[]{:S(2)}) collective-permute-start(f32[192,96]{1,0:T(8,128)S(1)} %add_add_fusion.2), channel_id=1, source_target_pairs={{0,8},{1,25},{2,10},{3,27},{4,12},{5,29},{6,14},{7,31},{8,16},{9,1... | collective-permute-start | bytes 221192 | tf_op jit(solution)/shard_map/ppermute | solution.py:30
  32.4 11.9 %collective-permute-start.7 = (f32[192,96]{1,0:T(8,128)S(1)}, f32[192,96]{1,0:T(8,128)S(1)}, u32[]{:S(2)}, u32[]{:S(2)}) collective-permute-start(f32[192,96]{1,0:T(8,128)S(1)} %add_add_fusion.1), channel_id=1, source_target_pairs={{0,32},{1,33},{2,34},{3,35},{4,36},{5,37},{6,38},{7,39},{8,40},{9,... | collective-permute-start | bytes 221192 | tf_op jit(solution)/shard_map/ppermute | solution.py:30
  44.2 7.4 %collective-permute-start.10 = (f32[192,96]{1,0:T(8,128)S(1)}, f32[192,96]{1,0:T(8,128)S(1)}, u32[]{:S(2)}, u32[]{:S(2)}) collective-permute-start(f32[192,96]{1,0:T(8,128)S(1)} %add.285), channel_id=1, source_target_pairs={{0,192},{1,65},{2,194},{3,67},{4,196},{5,69},{6,198},{7,71},{8,200... | collective-permute-start | bytes 221192 | tf_op jit(solution)/shard_map/ppermute | solution.py:30
  47.2 6.2 %collective-permute-start.9 = (f32[192,96]{1,0:T(8,128)S(1)}, f32[192,96]{1,0:T(8,128)S(1)}, u32[]{:S(2)}, u32[]{:S(2)}) collective-permute-start(f32[192,96]{1,0:T(8,128)S(1)} %add.285), channel_id=1, source_target_pairs={{0,128},{1,129},{2,130},{3,131},{4,132},{5,133},{6,134},{7,135},{8... | collective-permute-start | bytes 221192 | tf_op jit(solution)/shard_map/ppermute | solution.py:30
  47.8 6.5 %collective-permute-start.8 = (f32[192,96]{1,0:T(8,128)S(1)}, f32[192,96]{1,0:T(8,128)S(1)}, u32[]{:S(2)}, u32[]{:S(2)}) collective-permute-start(f32[192,96]{1,0:T(8,128)S(1)} %add.285), channel_id=1, source_target_pairs={{0,64},{1,193},{2,66},{3,195},{4,68},{5,197},{6,70},{7,199},{8,72}... | collective-permute-start | bytes 221192 | tf_op jit(solution)/shard_map/ppermute | solution.py:30
  55.3 2.2 %collective-permute-start.11 = (f32[192,96]{1,0:T(8,128)S(1)}, f32[192,96]{1,0:T(8,128)S(1)}, u32[]{:S(2)}, u32[]{:S(2)}) collective-permute-start(f32[192,96]{1,0:T(8,128)S(1)} %get-tuple-element.11), channel_id=1, source_target_pairs={{0,1},{1,0},{2,3},{3,2},{4,5},{5,4},{6,7},{7,6},{8,9},{9,8},{10,11... | collective-permute-start | bytes 221192 | tf_op jit(solution)/shard_map/ppermute | solution.py:30
  57.6 1.9 %copy-start.4 = (bf16[512,3072]{1,0:T(8,128)(2,1)S(1)}, bf16[512,3072]{1,0:T(8,128)(2,1)}, u32[]{:S(2)}) copy-start(bf16[512,3072]{1,0:T(8,128)(2,1)} %x.1) | copy-start | bytes 9437188
  71.2 4.2 %collective-permute-start.14 = (f32[4,96,576]{2,1,0:T(8,128)}, f32[4,96,576]{2,1,0:T(8,128)S(1)}, u32[]{:S(2)}, u32[]{:S(2)}) collective-permute-start(f32[4,96,576]{2,1,0:T(8,128)} %get-tuple-element.16), channel_id=1, source_target_pairs={{0,1},{1,0},{2,3},{3,2},{4,5},{5,4},{6,7},{7,6},{8,9},{9,8},{10,11... | collective-permute-start | bytes 2654216 | tf_op jit(solution)/shard_map/ppermute | solution.py:30
  71.7 5.2 %collective-permute-start.16 = (f32[4,96,576]{2,1,0:T(8,128)}, f32[4,96,576]{2,1,0:T(8,128)}, u32[]{:S(2)}, u32[]{:S(2)}) collective-permute-start(f32[4,96,576]{2,1,0:T(8,128)} %get-tuple-element.18), channel_id=1, source_target_pairs={{0,1},{1,0},{2,3},{3,2},{4,5},{5,4},{6,7},{7,6},{8,9},{9,8},{10,11... | collective-permute-start | bytes 2654216 | tf_op jit(solution)/shard_map/ppermute | solution.py:30
  71.7 5.2 %collective-permute-start.12 = (f32[4,96,576]{2,1,0:T(8,128)S(1)}, f32[4,96,576]{2,1,0:T(8,128)}, u32[]{:S(2)}, u32[]{:S(2)}) collective-permute-start(f32[4,96,576]{2,1,0:T(8,128)S(1)} %get-tuple-element.19), channel_id=1, source_target_pairs={{0,1},{1,0},{2,3},{3,2},{4,5},{5,4},{6,7},{7,6},{8,9},{9,8},{10,11... | collective-permute-start | bytes 2654216 | tf_op jit(solution)/shard_map/ppermute | solution.py:30
  72.2 12.4 %collective-permute-start.18 = (f32[4,96,576]{2,1,0:T(8,128)S(1)}, f32[4,96,576]{2,1,0:T(8,128)}, u32[]{:S(2)}, u32[]{:S(2)}) collective-permute-start(f32[4,96,576]{2,1,0:T(8,128)S(1)} %get-tuple-element.17), channel_id=1, source_target_pairs={{0,1},{1,0},{2,3},{3,2},{4,5},{5,4},{6,7},{7,6},{8,9},{9,8},{10,11... | collective-permute-start | bytes 2654216 | tf_op jit(solution)/shard_map/ppermute | solution.py:30
  80.9 25.3 %collective-permute-start.17 = (f32[4,96,576]{2,1,0:T(8,128)}, f32[4,96,576]{2,1,0:T(8,128)S(1)}, u32[]{:S(2)}, u32[]{:S(2)}) collective-permute-start(f32[4,96,576]{2,1,0:T(8,128)} %get-tuple-element.14), channel_id=1, source_target_pairs={{0,6},{1,193},{2,0},{3,195},{4,2},{5,197},{6,4},{7,199},{8,14},{9,... | collective-permute-start | bytes 2654216 | tf_op jit(solution)/shard_map/ppermute | solution.py:30
  83.7 22.5 %collective-permute-start.13 = (f32[4,96,576]{2,1,0:T(8,128)}, f32[4,96,576]{2,1,0:T(8,128)}, u32[]{:S(2)}, u32[]{:S(2)}) collective-permute-start(f32[4,96,576]{2,1,0:T(8,128)} %get-tuple-element.15), channel_id=1, source_target_pairs={{0,4},{1,129},{2,6},{3,131},{4,0},{5,133},{6,2},{7,135},{8,12},{9,... | collective-permute-start | bytes 2654216 | tf_op jit(solution)/shard_map/ppermute | solution.py:30
  83.7 25.9 %collective-permute-start.15 = (f32[4,96,576]{2,1,0:T(8,128)S(1)}, f32[4,96,576]{2,1,0:T(8,128)}, u32[]{:S(2)}, u32[]{:S(2)}) collective-permute-start(f32[4,96,576]{2,1,0:T(8,128)S(1)} %get-tuple-element.13), channel_id=1, source_target_pairs={{0,2},{1,65},{2,4},{3,67},{4,6},{5,69},{6,0},{7,71},{8,10},{9,73},... | collective-permute-start | bytes 2654216 | tf_op jit(solution)/shard_map/ppermute | solution.py:30
  112.1 6.3 %collective-permute-start.21 = (f32[96,576]{1,0:T(8,128)S(1)}, f32[96,576]{1,0:T(8,128)S(1)}, u32[]{:S(2)}, u32[]{:S(2)}) collective-permute-start(f32[96,576]{1,0:T(8,128)S(1)} %get-tuple-element.21), channel_id=1, source_target_pairs={{0,192},{1,7},{2,194},{3,1},{4,196},{5,3},{6,198},{7,5},{8,200},{9... | collective-permute-start | bytes 663560 | tf_op jit(solution)/shard_map/ppermute | solution.py:30
  113.7 7.8 %collective-permute-start.19 = (f32[96,576]{1,0:T(8,128)S(1)}, f32[96,576]{1,0:T(8,128)S(1)}, u32[]{:S(2)}, u32[]{:S(2)}) collective-permute-start(f32[96,576]{1,0:T(8,128)S(1)} %get-tuple-element.22), channel_id=1, source_target_pairs={{0,128},{1,5},{2,130},{3,7},{4,132},{5,1},{6,134},{7,3},{8,136},{9... | collective-permute-start | bytes 663560 | tf_op jit(solution)/shard_map/ppermute | solution.py:30
  114.3 9.7 %collective-permute-start.20 = (f32[96,576]{1,0:T(8,128)S(1)}, f32[96,576]{1,0:T(8,128)S(1)}, u32[]{:S(2)}, u32[]{:S(2)}) collective-permute-start(f32[96,576]{1,0:T(8,128)S(1)} %get-tuple-element.20), channel_id=1, source_target_pairs={{0,64},{1,3},{2,66},{3,5},{4,68},{5,7},{6,70},{7,1},{8,72},{9,11},... | collective-permute-start | bytes 663560 | tf_op jit(solution)/shard_map/ppermute | solution.py:30
  124.1 10.0 %collective-permute-start.28 = (f32[12,576]{1,0:T(8,128)S(1)}, f32[12,576]{1,0:T(8,128)S(1)}, u32[]{:S(2)}, u32[]{:S(2)}) collective-permute-start(f32[12,576]{1,0:T(8,128)S(1)} %get-tuple-element.24), channel_id=1, source_target_pairs={{0,56},{1,57},{2,58},{3,59},{4,60},{5,61},{6,62},{7,63},{8,0},{9,1... | collective-permute-start | bytes 82952 | tf_op jit(solution)/shard_map/ppermute | solution.py:30
  124.2 11.5 %collective-permute-start.27 = (f32[12,576]{1,0:T(8,128)S(1)}, f32[12,576]{1,0:T(8,128)S(1)}, u32[]{:S(2)}, u32[]{:S(2)}) collective-permute-start(f32[12,576]{1,0:T(8,128)S(1)} %get-tuple-element.25), channel_id=1, source_target_pairs={{0,8},{1,9},{2,10},{3,11},{4,12},{5,13},{6,14},{7,15},{8,16},{9,17... | collective-permute-start | bytes 82952 | tf_op jit(solution)/shard_map/ppermute | solution.py:30
  126.2 13.2 %collective-permute-start.26 = (f32[12,576]{1,0:T(8,128)S(1)}, f32[12,576]{1,0:T(8,128)S(1)}, u32[]{:S(2)}, u32[]{:S(2)}) collective-permute-start(f32[12,576]{1,0:T(8,128)S(1)} %get-tuple-element.26), channel_id=1, source_target_pairs={{0,48},{1,49},{2,50},{3,51},{4,52},{5,53},{6,54},{7,55},{8,56},{9,... | collective-permute-start | bytes 82952 | tf_op jit(solution)/shard_map/ppermute | solution.py:30
  130.7 8.7 %collective-permute-start.25 = (f32[12,576]{1,0:T(8,128)S(1)}, f32[12,576]{1,0:T(8,128)S(1)}, u32[]{:S(2)}, u32[]{:S(2)}) collective-permute-start(f32[12,576]{1,0:T(8,128)S(1)} %get-tuple-element.27), channel_id=1, source_target_pairs={{0,16},{1,17},{2,18},{3,19},{4,20},{5,21},{6,22},{7,23},{8,24},{9,... | collective-permute-start | bytes 82952 | tf_op jit(solution)/shard_map/ppermute | solution.py:30
  130.7 8.7 %collective-permute-start.24 = (f32[12,576]{1,0:T(8,128)S(1)}, f32[12,576]{1,0:T(8,128)S(1)}, u32[]{:S(2)}, u32[]{:S(2)}) collective-permute-start(f32[12,576]{1,0:T(8,128)S(1)} %get-tuple-element.28), channel_id=1, source_target_pairs={{0,40},{1,41},{2,42},{3,43},{4,44},{5,45},{6,46},{7,47},{8,48},{9,... | collective-permute-start | bytes 82952 | tf_op jit(solution)/shard_map/ppermute | solution.py:30
  134.1 7.5 %collective-permute-start.23 = (f32[12,576]{1,0:T(8,128)S(1)}, f32[12,576]{1,0:T(8,128)S(1)}, u32[]{:S(2)}, u32[]{:S(2)}) collective-permute-start(f32[12,576]{1,0:T(8,128)S(1)} %get-tuple-element.29), channel_id=1, source_target_pairs={{0,24},{1,25},{2,26},{3,27},{4,28},{5,29},{6,30},{7,31},{8,32},{9,... | collective-permute-start | bytes 82952 | tf_op jit(solution)/shard_map/ppermute | solution.py:30
  135.7 7.9 %collective-permute-start.22 = (f32[12,576]{1,0:T(8,128)S(1)}, f32[12,576]{1,0:T(8,128)S(1)}, u32[]{:S(2)}, u32[]{:S(2)}) collective-permute-start(f32[12,576]{1,0:T(8,128)S(1)} %get-tuple-element.23), channel_id=1, source_target_pairs={{0,32},{1,33},{2,34},{3,35},{4,36},{5,37},{6,38},{7,39},{8,40},{9,... | collective-permute-start | bytes 82952 | tf_op jit(solution)/shard_map/ppermute | solution.py:30

commit v2 on v0

v2 whole, which is shorter than its diff:
```python
import functools
import math

import jax
import jax.numpy as jnp
from jax import lax
from jax.experimental import pallas as pl
from jax.experimental.pallas import tpu as pltpu
from jax.sharding import PartitionSpec as P

HEAD = 96
WIDTH = 2 * HEAD
NY, NZ, NX, NC = 4, 8, 4, 2
SEQ = "seq"
F32 = jnp.float32
BF16 = jnp.bfloat16


def coords(i):
    return i >> 6, (i >> 3) & 7, (i >> 1) & 3, i & 1


def index(y, z, x, c):
    return ((y * NZ + z) * NX + x) * NC + c


def permute(value, move):
    pairs = []
    for i in range(NY * NZ * NX * NC):
        to = move(*coords(i))
        if to is not None:
            pairs.append((i, index(*to)))
    return lax.ppermute(value, SEQ, pairs)


def swap_cores(value):
    return permute(value, lambda y, z, x, c: (y, z, x, 1 - c))


def x_partner(m):
    return lambda y, z, x, c: (y, z, x ^ m, c)


def y_partner(m):
    return lambda y, z, x, c: (y ^ m, z, x, c)


def z_partner(m):
    return lambda y, z, x, c: (y, z ^ m, x, c)


def first_partner(m):
    return lambda y, z, x, c: (y, z, x ^ m, c) if c == 0 else (y ^ m, z, x, c)


def second_partner(m):
    return lambda y, z, x, c: (y ^ m, z, x, c) if c == 0 else (y, z, x ^ m, c)


def last_near(y, z, x, c):
    return (y, z, x, 1 - c) if z >> 2 == c else (y, z ^ 6, x, c)


def last_far(y, z, x, c):
    return None if z >> 2 == c else (y, z ^ 6, x, 1 - c)


def rows_dot(a, b):
    return lax.dot_general(a, b, (((0,), (0,)), ((), ())), preferred_element_type=F32)


def lanes_dot(a, b):
    return lax.dot_general(a, b, (((1,), (1,)), ((), ())), preferred_element_type=F32)


def dot(a, b):
    return jnp.dot(a, b, preferred_element_type=F32)


def head(array, h):
    return array[h * HEAD : (h + 1) * HEAD]


def states_kernel(place, q, k, v, g, keep, send):
    first = place[0] == 0
    for h in range(2):
        rows = slice(h * HEAD, (h + 1) * HEAD)
        key_state = lanes_dot(k[rows, :], v[rows, :])
        query_state = lanes_dot(q[rows, :], g[rows, :])
        keep[rows, :] = jnp.where(first, key_state, query_state)
        send[rows, :] = jnp.where(first, query_state, key_state)


def widen_kernel(q, k, v, g, out):
    for n, ref in enumerate((q, k, v, g)):
        out[n] = ref[...].astype(F32)


def widen_inputs_kernel(place, x, out):
    out[...] = x[...].astype(F32)


def local_kernel(place, q, k, v, g, other, local, outer):
    first = place[0] == 0
    mine = [ref[...] for ref in (q, k, v, g)]
    theirs = [other[n].astype(BF16) for n in range(4)]
    early = [jnp.where(first, a, b) for a, b in zip(mine, theirs)]
    late = [jnp.where(first, b, a) for a, b in zip(mine, theirs)]
    length = q.shape[1]
    s = lax.broadcasted_iota(jnp.int32, (length, length), 0)
    t = lax.broadcasted_iota(jnp.int32, (length, length), 1)
    causal = s <= t
    for core, (qt, kt, vt, gt) in enumerate((early, late)):
        outer[core, :, :] = jnp.zeros(outer.shape[1:], BF16)
        for n, a in enumerate((gt, vt, kt)):
            outer[core, n * 256 : n * 256 + WIDTH, :] = a
        for h in range(2):
            qh, kh, vh, gh = (head(a, h) for a in (qt, kt, vt, gt))
            vg = jnp.where(causal, rows_dot(vh, gh), 0.0).astype(BF16)
            kq = jnp.where(causal, rows_dot(kh, qh), 0.0).astype(BF16)
            dq = dot(kh, vg)
            dk = lanes_dot(qh, vg)
            dv = lanes_dot(gh, kq)
            if core == 0:
                state = lanes_dot(head(late[0], h), head(late[3], h)).astype(BF16)
                dk = dk + dot(state, vh)
                dv = dv + rows_dot(state, kh)
            else:
                state = lanes_dot(head(early[1], h), head(early[2], h)).astype(BF16)
                dq = dq + dot(state, gh)
            for n, a in enumerate((dq, dk, dv)):
                at = n * WIDTH + h * HEAD
                local[core, at : at + HEAD, :] = a.astype(BF16)


def terms_kernel(place, x, wide, local, outer, sums, high, low):
    c = place[0]
    theirs = wide[...].astype(BF16)
    mine = x[...]

    def over_tokens(d):
        contract = (((0,), (1,)), ((), ()))
        one = lax.dot_general(mine, d[c], contract, preferred_element_type=F32)
        return one + lax.dot_general(theirs, d[1 - c], contract, preferred_element_type=F32)

    shape = (1, 4, 96, -1)
    sums[...] = over_tokens(local).reshape(shape)
    outside = over_tokens(outer)
    top = outside.astype(BF16)
    high[...] = top.reshape(shape)
    low[...] = (outside - top.astype(F32)).astype(BF16).reshape(shape)


def join_kernel(factor, part, place, own, other, sums, high, low, keep, send):
    c, pa, pb, pz = (place[i] for i in range(4))
    first = c == 0
    row = lax.broadcasted_iota(jnp.int32, (WIDTH, WIDTH), 0) // HEAD
    col = lax.broadcasted_iota(jnp.int32, (WIDTH, WIDTH), 1) // HEAD

    def by_head(state):
        return jnp.where(row == col, jnp.concatenate([state, state], axis=1), 0.0).astype(BF16)

    before = by_head(jnp.where(first, own[...], other[...]))
    later = by_head(jnp.where(first, other[...], own[...]))

    def slot(p):
        order = (0, 1, 3, 2) if part == 0 else (0, 2, 3, 1)
        out = jnp.int32(0)
        for n in range(1, 4):
            out = jnp.where(p == n, order[n], out)
        return out

    for k in range(2):
        zi = pz ^ (k + 2 * part)

        for y in range(NY):
            pieces = []
            for n, (state, multiply) in enumerate(((before, lanes_dot), (later, lanes_dot), (later, dot))):
                lanes = slice(n * 256, n * 256 + WIDTH)
                total = sums[y, zi, :, n * WIDTH : (n + 1) * WIDTH]
                for ref in (high, low):
                    total = total + multiply(ref[y, zi, :, lanes], state)
                pieces.append(factor * total)
            value = jnp.concatenate(pieces, axis=1)
            for x in range(NX):
                sa = slot(jnp.where(first, x, y) ^ pa)
                sb = slot(jnp.where(first, y, x) ^ pb)
                rows = value[x * 24 : x * 24 + 24, :]

                @pl.when(sa < 2)
                def _(sa=sa, sb=sb, k=k, rows=rows):
                    keep[sa, sb, k] = rows

                @pl.when(sa >= 2)
                def _(sa=sa, sb=sb, k=k, rows=rows):
                    send[sa - 2, sb, k] = rows


VMEM = pl.BlockSpec(memory_space=pltpu.VMEM)
SMEM = pl.BlockSpec(memory_space=pltpu.SMEM)


def cost(flops, moved):
    return pl.CostEstimate(flops=flops, bytes_accessed=moved, transcendentals=0)


def limit(mib):
    return pltpu.CompilerParams(vmem_limit_bytes=mib * 2**20)


def states(place, q, k, v, g):
    shape = jax.ShapeDtypeStruct((WIDTH, HEAD), F32)
    return pl.pallas_call(
        states_kernel,
        name="states",
        out_shape=(shape, shape),
        in_specs=[SMEM] + [VMEM] * 4,
        out_specs=(VMEM, VMEM),
        cost_estimate=cost(4 * 512 * 192 * 192, 10**6),
    )(place, q, k, v, g)


def widen(q, k, v, g):
    return pl.pallas_call(
        widen_kernel,
        name="widen",
        out_shape=jax.ShapeDtypeStruct((4,) + q.shape, F32),
        in_specs=[VMEM] * 4,
        out_specs=VMEM,
        cost_estimate=cost(10**6, 24 * 10**5),
    )(q, k, v, g)


def widen_inputs(place, x):
    length, features = x.shape
    block = (length, features // 8)
    return pl.pallas_call(
        widen_inputs_kernel,
        name="widen_inputs",
        out_shape=jax.ShapeDtypeStruct((length, features // 2), F32),
        grid_spec=pltpu.PrefetchScalarGridSpec(
            num_scalar_prefetch=1,
            grid=(4,),
            in_specs=[pl.BlockSpec(block, lambda y, place: (0, 2 * y + 1 - place[0]))],
            out_specs=pl.BlockSpec(block, lambda y, place: (0, y)),
        ),
        cost_estimate=cost(10**6, 5 * 10**6),
    )(place, x)


def local_terms(place, q, k, v, g, other):
    length = q.shape[1]
    return pl.pallas_call(
        local_kernel,
        name="local_terms",
        out_shape=(
            jax.ShapeDtypeStruct((2, 3 * WIDTH, length), BF16),
            jax.ShapeDtypeStruct((2, 3 * 256, length), BF16),
        ),
        in_specs=[SMEM] + [VMEM] * 5,
        out_specs=(VMEM, VMEM),
        cost_estimate=cost(40 * 512 * 512 * 96, 5 * 10**6),
        compiler_params=limit(32),
    )(place, q, k, v, g, other)


def terms(place, x, wide, local, outer):
    length, features = x.shape
    block = (length, features // 8)
    whole = lambda a: pl.BlockSpec(a.shape, lambda y, place: (0,) * a.ndim)
    out = lambda lanes: pl.BlockSpec((1, 4, 96, lanes), lambda y, place: (y, 0, 0, 0))
    return pl.pallas_call(
        terms_kernel,
        name="terms",
        out_shape=(
            jax.ShapeDtypeStruct((4, 4, 96, 3 * WIDTH), F32),
            jax.ShapeDtypeStruct((4, 4, 96, 3 * 256), BF16),
            jax.ShapeDtypeStruct((4, 4, 96, 3 * 256), BF16),
        ),
        grid_spec=pltpu.PrefetchScalarGridSpec(
            num_scalar_prefetch=1,
            grid=(4,),
            in_specs=[
                pl.BlockSpec(block, lambda y, place: (0, 2 * y + place[0])),
                pl.BlockSpec(block, lambda y, place: (0, y)),
                whole(local),
                whole(outer),
            ],
            out_specs=(out(3 * WIDTH), out(3 * 256), out(3 * 256)),
        ),
        cost_estimate=cost(4 * 512 * 3072 * 576, 12 * 10**6),
        compiler_params=limit(32),
    )(place, x, wide, local, outer)


def join(part, factor, place, own, other, sums, high, low):
    shape = jax.ShapeDtypeStruct((2, 4, 2, 24, 3 * WIDTH), F32)
    return pl.pallas_call(
        functools.partial(join_kernel, factor, part),
        name=f"join{part}",
        out_shape=(shape, shape),
        in_specs=[SMEM] + [VMEM] * 5,
        out_specs=(VMEM, VMEM),
        cost_estimate=cost(12 * 768 * 192 * 192, 10**7),
        compiler_params=limit(32),
    )(place, own, other, sums, high, low)


def before_chip(me, total):
    y, z, x, c = me
    before = jnp.zeros_like(total)
    steps = (
        (x_partner(1), x & 1),
        (x_partner(3), x >> 1),
        (z_partner(1), z & 1),
        (z_partner(2), (z >> 1) & 1),
        (z_partner(6), z >> 2),
        (y_partner(1), y & 1),
        (y_partner(3), y >> 1),
    )
    for move, bit in steps:
        came = permute(total, move)
        before = before + jnp.where(bit != c, came, 0.0)
        total = total + came
    return before


def halve(keep, send, move_one, move_two):
    came = permute(send, move_one)
    return keep[0] + came[0] + permute(keep[1] + came[1], move_two)


def scatter_sum(me, parts):
    y, z, x, c = me
    ends = []
    for (keep, send), (one, two) in zip(parts, ((3, 1), (1, 3))):
        value = halve(keep, send, first_partner(one), first_partner(two))
        ends.append(halve(value[:2], value[2:], second_partner(one), second_partner(two)))
    value = ends[0] + permute(ends[1], z_partner(2))
    value = value[0] + permute(value[1], z_partner(1))
    block = lambda i: jnp.where(i == 0, value[:12], value[12:])
    same = z >> 2 == c
    total = jnp.where(same, block(c), 0.0)
    total = total + permute(block(jnp.where(same, 1 - c, c)), last_near)
    return total + permute(block(1 - c), last_far)


def per_device(inputs, query_proj, key_proj, value_proj, grad_out):
    length, width = query_proj.shape
    factor = 1.0 / (math.sqrt(HEAD) * length * lax.axis_size(SEQ))
    me = coords(lax.axis_index(SEQ))
    y, z, x, c = me
    block = (z & 3) ^ jnp.where(z >> 2 == c, 0, 2)
    place = jnp.stack([c, jnp.where(c == 0, x, y), jnp.where(c == 0, y, x), block]).astype(jnp.int32)
    features_first = [a.T for a in (query_proj, key_proj, value_proj, grad_out)]
    keep, send = states(place, *features_first)
    before = before_chip(me, keep + swap_cores(send))
    other = swap_cores(widen(*features_first))
    wide = swap_cores(widen_inputs(place, inputs))
    local, outer = local_terms(place, *features_first, other)
    pieces = terms(place, inputs, wide, local, outer)
    across = swap_cores(before)
    parts = [join(part, factor, place, before, across, *pieces) for part in range(2)]
    summed = scatter_sum(me, parts)
    return (summed[:, :width], summed[:, width : 2 * width], summed[:, 2 * width :])


def solution(mesh):
    return jax.shard_map(
        per_device,
        mesh=mesh,
        in_specs=(P(SEQ, None),) * 5,
        out_specs=(P(SEQ, None),) * 3,
        check_vma=False,
    )
```

time: 968 us -> 137 us (0.14); the launches traced: 952 us -> 137 us
  other arithmetic: 474 us -> 3.91 us
  waiting for transfers between devices: 409 us -> 53.4 us
  starting transfers between devices: 0.12 us -> 46.5 us
  Pallas kernels: 0 us -> 29.3 us
  local copies, waits for them, and re-layouts: 23 us -> 2.62 us
  matrix products: 19.5 us -> 0 us
  between operations: 13.9 us -> 0.91 us
  loops' own time: 12.2 us -> 0 us
    select_n x510 -> x1, other arithmetic: 473 us -> 0.01 us  [scatter_sum(): block = lambda i: jnp.where(i == 0, value[:12], value[12:])]
    unnamed x4 -> x0, waiting for transfers between devices: 271 us -> none
    all_gather x2 -> x0, waiting for transfers between devices: 138 us -> none  [entering(): pieces = lax.all_gather(value, axis)]
    ppermute x0 -> x23, waiting for transfers between devices: none -> 53.4 us  [permute(): return lax.ppermute(value, SEQ, pairs)]
    ppermute x0 -> x23, starting transfers between devices: none -> 46.5 us  [permute(): return lax.ppermute(value, SEQ, pairs)]
    pallas_call x0 -> x7, Pallas kernels: none -> 29.3 us  [the longest x2 7.71 us: join(): pl.pallas_call(functools.partial(join_kernel, factor, part), name=f'join{...]
    dot_general x10 -> x0, matrix products: 19.5 us -> none  [the longest x1 4.97 us: weight_term(): lax.dot_general(inputs, grads, (((0,), (0,)), ((), ())), preferred_elemen...]
    rev x1 -> x0, local copies, waits for them, and re-layouts: 18.6 us -> none  [entering(): pieces = pieces[::-1]]
  transfers between devices with their start and end apart: 3 -> 23, of which waited for: 2 -> 17; matrix products, arithmetic and copies ran while one was open for 28% -> 2% of each run, Pallas kernels for 0% -> 15%
where the time goes in v2:
time: 137 us
  waiting for transfers between devices  53.4 us (39%)
  starting transfers between devices  46.5 us (34%)
  Pallas kernels  29.3 us (21%)
  other arithmetic  3.91 us (3%)
  local copies, waits for them, and re-layouts  2.62 us (2%)
    ppermute x23, waiting for transfers between devices, permute(): return lax.ppermute(value, SEQ, pairs)  53.4 us
    ppermute x23, starting transfers between devices, permute(): return lax.ppermute(value, SEQ, pairs)  46.5 us
    pallas_call x2, Pallas kernels, join(): pl.pallas_call(functools.partial(join_kernel, factor, part), name=f'join{...  7.71 us
    pallas_call x1, Pallas kernels, terms(): pl.pallas_call(terms_kernel, name='terms', out_shape=(jax.ShapeDtypeStruc...  7.62 us
    pallas_call x1, Pallas kernels, widen_inputs(): pl.pallas_call(widen_inputs_kernel, name='widen_inputs', out_shape=jax.Sh...  4.73 us
    pallas_call x1, Pallas kernels, local_terms(): pl.pallas_call(local_kernel, name='local_terms', out_shape=(jax.ShapeDtyp...  4.52 us
  transfers between devices with their start and end apart: 23, of which 17 were waited for; matrix products, arithmetic and copies ran while one was open for 2% of the time, Pallas kernels for 15%

profile of v2, /device:TPU:1, one launch (start us, length us, event | category | flops | bytes accessed | tf_op | source)
XLA Modules:
  0.0 136.7 jit_solution(16867158148336711119)
XLA Ops:
  0.7 0.7 pad_add_fusion.place
  1.3 4.7 %widen_inputs.1 = f32[512,1536]{1,0:T(8,128)} custom-call(s32[4]{0:T(128)} %pad_add_fusion.place, bf16[512,3072]{1,0:T(8,128)(2,1)} %x.3), custom_call_target="tpu_custom_call" | custom-call | flops 1000000 | bytes 5000000 | tf_op jit(solution)/shard_map/widen_inputs/pallas_call | solution.py:237
  6.1 3.2 %collective-permute-start.9 = (f32[512,1536]{1,0:T(8,128)}, f32[512,1536]{1,0:T(8,128)}, u32[]{:S(2)}, u32[]{:S(2)}) collective-permute-start(f32[512,1536]{1,0:T(8,128)} %widen_inputs.1), channel_id=1, source_target_pairs={{0,1},{1,0},{2,3},{3,2},{4,5},{5,4},{6,7},{7,6},{8,9},{9,8},{10,11... | collective-permute-start | bytes 9437192 | tf_op jit(solution)/shard_map/ppermute | solution.py:33
  9.3 2.5 %widen.1 = f32[4,192,512]{2,1,0:T(8,128)} custom-call(bf16[192,512]{1,0:T(8,128)(2,1)} %bitcast.40, bf16[192,512]{1,0:T(8,128)(2,1)} %bitcast.43, bf16[192,512]{1,0:T(8,128)(2,1)} %bitcast.46, bf16[192,512]{1,0:T(8,128)(2,1)} %bitcast.49), custom_call_target="tpu_custom_call" | custom-call | flops 1000000 | bytes 2400000 | tf_op jit(solution)/shard_map/widen/pallas_call | solution.py:224
  11.9 2.2 %states.1 = (f32[192,96]{1,0:T(8,128)}, f32[192,96]{1,0:T(8,128)}) custom-call(s32[4]{0:T(128)} %pad_add_fusion.place, bf16[192,512]{1,0:T(8,128)(2,1)} %bitcast.41, bf16[192,512]{1,0:T(8,128)(2,1)} %bitcast.44, bf16[192,512]{1,0:T(8,128)(2,1)} %bitcast.47, bf16[192,512]{1,0:T(8,128)(2,1)} %bitcast.50), custom_call_target="tpu_custom_call" | custom-call | flops 75497472 | bytes 1000000 | tf_op jit(solution)/shard_map/states/pallas_call | solution.py:213
  14.6 2.6 %collective-permute-done = f32[192,96]{1,0:T(8,128)S(1)} collective-permute-done((f32[192,96]{1,0:T(8,128)}, f32[192,96]{1,0:T(8,128)S(1)}, u32[]{:S(2)}, u32[]{:S(2)}) %collective-permute-start) | collective-permute-done | bytes 73760 | tf_op jit(solution)/shard_map/ppermute | solution.py:33
  17.2 0.9 add.111
  18.2 4.0 %collective-permute-done.1 = f32[192,96]{1,0:T(8,128)S(1)} collective-permute-done((f32[192,96]{1,0:T(8,128)S(1)}, f32[192,96]{1,0:T(8,128)S(1)}, u32[]{:S(2)}, u32[]{:S(2)}) %collective-permute-start.1) | collective-permute-done | bytes 73760 | tf_op jit(solution)/shard_map/ppermute | solution.py:33
  22.2 0.8 collective-permute-start.2
  23.0 3.9 %collective-permute-done.2 = f32[192,96]{1,0:T(8,128)S(1)} collective-permute-done((f32[192,96]{1,0:T(8,128)S(1)}, f32[192,96]{1,0:T(8,128)S(1)}, u32[]{:S(2)}, u32[]{:S(2)}) %collective-permute-start.2) | collective-permute-done | bytes 73760 | tf_op jit(solution)/shard_map/ppermute | solution.py:33
  27.1 3.5 %collective-permute-done.3 = f32[192,96]{1,0:T(8,128)S(1)} collective-permute-done((f32[192,96]{1,0:T(8,128)S(1)}, f32[192,96]{1,0:T(8,128)S(1)}, u32[]{:S(2)}, u32[]{:S(2)}) %collective-permute-start.3) | collective-permute-done | bytes 73760 | tf_op jit(solution)/shard_map/ppermute | solution.py:33
  30.6 1.5 %collective-permute-start.4 = (f32[192,96]{1,0:T(8,128)S(1)}, f32[192,96]{1,0:T(8,128)S(1)}, u32[]{:S(2)}, u32[]{:S(2)}) collective-permute-start(f32[192,96]{1,0:T(8,128)S(1)} %add.116), channel_id=1, source_target_pairs={{0,16},{1,17},{2,18},{3,19},{4,20},{5,21},{6,22},{7,23},{8,24},{9,... | collective-permute-start | bytes 221192 | tf_op jit(solution)/shard_map/ppermute | solution.py:33
  32.1 4.0 %collective-permute-done.4 = f32[192,96]{1,0:T(8,128)S(1)} collective-permute-done((f32[192,96]{1,0:T(8,128)S(1)}, f32[192,96]{1,0:T(8,128)S(1)}, u32[]{:S(2)}, u32[]{:S(2)}) %collective-permute-start.4) | collective-permute-done | bytes 73760 | tf_op jit(solution)/shard_map/ppermute | solution.py:33
  36.1 3.4 %collective-permute-start.5 = (f32[192,96]{1,0:T(8,128)S(1)}, f32[192,96]{1,0:T(8,128)S(1)}, u32[]{:S(2)}, u32[]{:S(2)}) collective-permute-start(f32[192,96]{1,0:T(8,128)S(1)} %add.118), channel_id=1, source_target_pairs={{0,48},{1,49},{2,50},{3,51},{4,52},{5,53},{6,54},{7,55},{8,56},{9,... | collective-permute-start | bytes 221192 | tf_op jit(solution)/shard_map/ppermute | solution.py:33
  39.5 2.8 %collective-permute-done.5 = f32[192,96]{1,0:T(8,128)S(1)} collective-permute-done((f32[192,96]{1,0:T(8,128)S(1)}, f32[192,96]{1,0:T(8,128)S(1)}, u32[]{:S(2)}, u32[]{:S(2)}) %collective-permute-start.5) | collective-permute-done | bytes 73760 | tf_op jit(solution)/shard_map/ppermute | solution.py:33
  42.3 0.7 collective-permute-start.6
  43.0 3.2 %collective-permute-done.6 = f32[192,96]{1,0:T(8,128)S(1)} collective-permute-done((f32[192,96]{1,0:T(8,128)S(1)}, f32[192,96]{1,0:T(8,128)S(1)}, u32[]{:S(2)}, u32[]{:S(2)}) %collective-permute-start.6) | collective-permute-done | bytes 73760 | tf_op jit(solution)/shard_map/ppermute | solution.py:33
  46.2 0.7 add.122
  46.9 1.8 %collective-permute-start.7 = (f32[192,96]{1,0:T(8,128)}, f32[192,96]{1,0:T(8,128)}, u32[]{:S(2)}, u32[]{:S(2)}) collective-permute-start(f32[192,96]{1,0:T(8,128)} %add.122), channel_id=1, source_target_pairs={{0,192},{1,193},{2,194},{3,195},{4,196},{5,197},{6,198},{7,199},{8... | collective-permute-start | bytes 221192 | tf_op jit(solution)/shard_map/ppermute | solution.py:33
  48.7 3.3 %collective-permute-done.7 = f32[192,96]{1,0:T(8,128)} collective-permute-done((f32[192,96]{1,0:T(8,128)}, f32[192,96]{1,0:T(8,128)}, u32[]{:S(2)}, u32[]{:S(2)}) %collective-permute-start.7) | collective-permute-done | bytes 73760 | tf_op jit(solution)/shard_map/ppermute | solution.py:33
  52.0 1.2 select_add_fusion.own
  53.2 6.2 %collective-permute-start.8 = (f32[192,96]{1,0:T(8,128)S(1)}, f32[192,96]{1,0:T(8,128)S(1)}, u32[]{:S(2)}, u32[]{:S(2)}) collective-permute-start(f32[192,96]{1,0:T(8,128)S(1)} %select_add_fusion.own), channel_id=1, source_target_pairs={{0,1},{1,0},{2,3},{3,2},{4,5},{5,4},{6,7},{7,6},{8,9},{9,8},{10,11... | collective-permute-start | bytes 221192 | tf_op jit(solution)/shard_map/ppermute | solution.py:33
  59.5 0.9 copy-done.3
  60.4 0.9 copy-done.4
  61.3 4.5 %local_terms.1 = (bf16[2,576,512]{2,1,0:T(8,128)(2,1)S(1)}, bf16[2,768,512]{2,1,0:T(8,128)(2,1)S(1)}) custom-call(s32[4]{0:T(128)S(1)} %copy-done.5, bf16[192,512]{1,0:T(8,128)(2,1)S(1)} %bitcast.42, bf16[192,512]{1,0:T(8,128)(2,1)S(1)} %bitcast.45, bf16[192,512]{1,0:T(8,128)(2,1)S(1)} %bitcast.48, bf16[192,512]{1,0:T(8,128)(2,1)S(1)} %bitcast.51, ...), custom_call_target="tpu_custom_call" | custom-call | flops 1006632960 | bytes 5000000 | tf_op jit(solution)/shard_map/local_terms/pallas_call | solution.py:253
  65.9 7.6 %terms.1 = (f32[4,4,96,576]{3,2,1,0:T(8,128)S(1)}, bf16[4,4,96,768]{3,2,1,0:T(8,128)(2,1)S(1)}, bf16[4,4,96,768]{3,2,1,0:T(8,128)(2,1)S(1)}) custom-call(s32[4]{0:T(128)S(1)} %copy-done.5, bf16[512,3072]{1,0:T(8,128)(2,1)S(1)} %copy-done, f32[512,1536]{1,0:T(8,128)} %collective-permute-done.9.wide, bf16[2,576,512]{2,1,0:T(8,128)(2,1)S(1)} %get-tuple-element.16.local, ...), custom_call_target="tpu_custom_call" | custom-call | flops 3623878656 | bytes 12000000 | tf_op jit(solution)/shard_map/terms/pallas_call | solution.py:272
  73.5 3.9 %join1.1 = (f32[2,4,2,24,576]{4,3,2,1,0:T(8,128)S(1)}, f32[2,4,2,24,576]{4,3,2,1,0:T(8,128)S(1)}) custom-call(s32[4]{0:T(128)S(1)} %copy-done.5, f32[192,96]{1,0:T(8,128)S(1)} %select_add_fusion.own, f32[192,96]{1,0:T(8,128)S(1)} %collective-permute-done.8.other, f32[4,4,96,576]{3,2,1,0:T(8,128)S(1)} %get-tuple-element.18.sums, ...), custom_call_target="tpu_custom_call" | custom-call | flops 339738624 | bytes 10000000 | tf_op jit(solution)/shard_map/join1/pallas_call | solution.py:298
  77.4 0.5 collective-permute-start.15
  78.0 3.8 %join0.1 = (f32[2,4,2,24,576]{4,3,2,1,0:T(8,128)S(1)}, f32[2,4,2,24,576]{4,3,2,1,0:T(8,128)S(1)}) custom-call(s32[4]{0:T(128)S(1)} %copy-done.5, f32[192,96]{1,0:T(8,128)S(1)} %select_add_fusion.own, f32[192,96]{1,0:T(8,128)S(1)} %collective-permute-done.8.other, f32[4,4,96,576]{3,2,1,0:T(8,128)S(1)} %get-tuple-element.18.sums, ...), custom_call_target="tpu_custom_call" | custom-call | flops 339738624 | bytes 10000000 | tf_op jit(solution)/shard_map/join0/pallas_call | solution.py:298
  81.8 2.8 %collective-permute-start.11 = (f32[2,4,2,24,576]{4,3,2,1,0:T(8,128)S(1)}, f32[2,4,2,24,576]{4,3,2,1,0:T(8,128)S(1)}, u32[]{:S(2)}, u32[]{:S(2)}) collective-permute-start(f32[2,4,2,24,576]{4,3,2,1,0:T(8,128)S(1)} %get-tuple-element.22), channel_id=1, source_target_pairs={{0,6},{1,193},{2,4},{3,195},{4,2},{5,197},{6,0},{7,199},{8,14},{9,... | collective-permute-start | bytes 2654216 | tf_op jit(solution)/shard_map/ppermute | solution.py:33
  84.5 6.2 %collective-permute-done.15 = f32[2,4,2,24,576]{4,3,2,1,0:T(8,128)S(1)} collective-permute-done((f32[2,4,2,24,576]{4,3,2,1,0:T(8,128)S(1)}, f32[2,4,2,24,576]{4,3,2,1,0:T(8,128)S(1)}, u32[]{:S(2)}, u32[]{:S(2)}) %collective-permute-start.15) | collective-permute-done | bytes 884768 | tf_op jit(solution)/shard_map/ppermute | solution.py:33
  90.8 3.2 %collective-permute-start.16 = (f32[4,2,24,576]{3,2,1,0:T(8,128)S(1)}, f32[4,2,24,576]{3,2,1,0:T(8,128)S(1)}, u32[]{:S(2)}, u32[]{:S(2)}) collective-permute-start(f32[4,2,24,576]{3,2,1,0:T(8,128)S(1)} %fusion), channel_id=1, source_target_pairs={{0,6},{1,193},{2,4},{3,195},{4,2},{5,197},{6,0},{7,199},{8,14},{9,... | collective-permute-start | bytes 1327112 | tf_op jit(solution)/shard_map/ppermute | solution.py:33
  94.1 2.3 %collective-permute-done.11 = f32[2,4,2,24,576]{4,3,2,1,0:T(8,128)S(1)} collective-permute-done((f32[2,4,2,24,576]{4,3,2,1,0:T(8,128)S(1)}, f32[2,4,2,24,576]{4,3,2,1,0:T(8,128)S(1)}, u32[]{:S(2)}, u32[]{:S(2)}) %collective-permute-start.11) | collective-permute-done | bytes 884768 | tf_op jit(solution)/shard_map/ppermute | solution.py:33
  96.4 0.9 collective-permute-start.12
  97.3 4.3 %collective-permute-done.16 = f32[4,2,24,576]{3,2,1,0:T(8,128)S(1)} collective-permute-done((f32[4,2,24,576]{3,2,1,0:T(8,128)S(1)}, f32[4,2,24,576]{3,2,1,0:T(8,128)S(1)}, u32[]{:S(2)}, u32[]{:S(2)}) %collective-permute-start.16) | collective-permute-done | bytes 442400 | tf_op jit(solution)/shard_map/ppermute | solution.py:33
  101.8 2.6 %collective-permute-done.12 = f32[4,2,24,576]{3,2,1,0:T(8,128)S(1)} collective-permute-done((f32[4,2,24,576]{3,2,1,0:T(8,128)S(1)}, f32[4,2,24,576]{3,2,1,0:T(8,128)S(1)}, u32[]{:S(2)}, u32[]{:S(2)}) %collective-permute-start.12) | collective-permute-done | bytes 442400 | tf_op jit(solution)/shard_map/ppermute | solution.py:33
  104.6 2.7 %collective-permute-start.13 = (f32[2,2,24,576]{3,2,1,0:T(8,128)S(1)}, f32[2,2,24,576]{3,2,1,0:T(8,128)S(1)}, u32[]{:S(2)}, u32[]{:S(2)}) collective-permute-start(f32[2,2,24,576]{3,2,1,0:T(8,128)S(1)} %slice.113), channel_id=1, source_target_pairs={{0,192},{1,7},{2,194},{3,5},{4,196},{5,3},{6,198},{7,1},{8,200},{9... | collective-permute-start | bytes 663560 | tf_op jit(solution)/shard_map/ppermute | solution.py:33
  107.2 1.4 %collective-permute-done.17 = f32[2,2,24,576]{3,2,1,0:T(8,128)S(1)} collective-permute-done((f32[2,2,24,576]{3,2,1,0:T(8,128)S(1)}, f32[2,2,24,576]{3,2,1,0:T(8,128)S(1)}, u32[]{:S(2)}, u32[]{:S(2)}) %collective-permute-start.17) | collective-permute-done | bytes 221216 | tf_op jit(solution)/shard_map/ppermute | solution.py:33
  108.6 2.4 %collective-permute-start.18 = (f32[2,24,576]{2,1,0:T(8,128)S(1)}, f32[2,24,576]{2,1,0:T(8,128)S(1)}, u32[]{:S(2)}, u32[]{:S(2)}) collective-permute-start(f32[2,24,576]{2,1,0:T(8,128)S(1)} %fusion.6), channel_id=1, source_target_pairs={{0,192},{1,7},{2,194},{3,5},{4,196},{5,3},{6,198},{7,1},{8,200},{9... | collective-permute-start | bytes 331784 | tf_op jit(solution)/shard_map/ppermute | solution.py:33
  111.1 2.8 %collective-permute-done.18 = f32[2,24,576]{2,1,0:T(8,128)S(1)} collective-permute-done((f32[2,24,576]{2,1,0:T(8,128)S(1)}, f32[2,24,576]{2,1,0:T(8,128)S(1)}, u32[]{:S(2)}, u32[]{:S(2)}) %collective-permute-start.18) | collective-permute-done | bytes 110624 | tf_op jit(solution)/shard_map/ppermute | solution.py:33
  114.0 3.3 %collective-permute-start.19 = (f32[2,24,576]{2,1,0:T(8,128)S(1)}, f32[2,24,576]{2,1,0:T(8,128)S(1)}, u32[]{:S(2)}, u32[]{:S(2)}) collective-permute-start(f32[2,24,576]{2,1,0:T(8,128)S(1)} %fusion.8), channel_id=1, source_target_pairs={{0,16},{1,17},{2,18},{3,19},{4,20},{5,21},{6,22},{7,23},{8,24},{9,... | collective-permute-start | bytes 331784 | tf_op jit(solution)/shard_map/ppermute | solution.py:33
  117.2 2.3 %collective-permute-done.19 = f32[2,24,576]{2,1,0:T(8,128)S(1)} collective-permute-done((f32[2,24,576]{2,1,0:T(8,128)S(1)}, f32[2,24,576]{2,1,0:T(8,128)S(1)}, u32[]{:S(2)}, u32[]{:S(2)}) %collective-permute-start.19) | collective-permute-done | bytes 110624 | tf_op jit(solution)/shard_map/ppermute | solution.py:33
  119.5 1.7 %collective-permute-start.20 = (f32[24,576]{1,0:T(8,128)S(1)}, f32[24,576]{1,0:T(8,128)S(1)}, u32[]{:S(2)}, u32[]{:S(2)}) collective-permute-start(f32[24,576]{1,0:T(8,128)S(1)} %slice_bitcast_fusion), channel_id=1, source_target_pairs={{0,8},{1,9},{2,10},{3,11},{4,12},{5,13},{6,14},{7,15},{8,0},{9,1},... | collective-permute-start | bytes 165896 | tf_op jit(solution)/shard_map/ppermute | solution.py:33
  121.2 2.6 %collective-permute-done.20 = f32[24,576]{1,0:T(8,128)S(1)} collective-permute-done((f32[24,576]{1,0:T(8,128)S(1)}, f32[24,576]{1,0:T(8,128)S(1)}, u32[]{:S(2)}, u32[]{:S(2)}) %collective-permute-start.20) | collective-permute-done | bytes 55328 | tf_op jit(solution)/shard_map/ppermute | solution.py:33
  123.8 3.9 %collective-permute-start.21 = (f32[12,576]{1,0:T(8,128)S(1)}, f32[12,576]{1,0:T(8,128)S(1)}, u32[]{:S(2)}, u32[]{:S(2)}) collective-permute-start(f32[12,576]{1,0:T(8,128)S(1)} %get-tuple-element.25), channel_id=1, source_target_pairs={{0,1},{1,49},{2,3},{3,51},{4,5},{5,53},{6,7},{7,55},{8,9},{9,57},{... | collective-permute-start | bytes 82952 | tf_op jit(solution)/shard_map/ppermute | solution.py:33
  127.7 6.6 %collective-permute-start.22 = (f32[12,576]{1,0:T(8,128)S(1)}, f32[12,576]{1,0:T(8,128)S(1)}, u32[]{:S(2)}, u32[]{:S(2)}) collective-permute-start(f32[12,576]{1,0:T(8,128)S(1)} %get-tuple-element.26), channel_id=1, source_target_pairs={{1,48},{3,50},{5,52},{7,54},{9,56},{11,58},{13,60},{15,62},{17,32}... | collective-permute-start | bytes 82952 | tf_op jit(solution)/shard_map/ppermute | solution.py:33
  134.3 1.7 %collective-permute-done.22 = f32[12,576]{1,0:T(8,128)S(1)} collective-permute-done((f32[12,576]{1,0:T(8,128)S(1)}, f32[12,576]{1,0:T(8,128)S(1)}, u32[]{:S(2)}, u32[]{:S(2)}) %collective-permute-start.22) | collective-permute-done | bytes 27680 | tf_op jit(solution)/shard_map/ppermute | solution.py:33
  136.0 0.7 fusion.14
  (53 shorter events, 1.4 us)
Async XLA Ops:
  6.1 59.8 %collective-permute-start.9 = (f32[512,1536]{1,0:T(8,128)}, f32[512,1536]{1,0:T(8,128)}, u32[]{:S(2)}, u32[]{:S(2)}) collective-permute-start(f32[512,1536]{1,0:T(8,128)} %widen_inputs.1), channel_id=1, source_target_pairs={{0,1},{1,0},{2,3},{3,2},{4,5},{5,4},{6,7},{7,6},{8,9},{9,8},{10,11... | collective-permute-start | bytes 9437192 | tf_op jit(solution)/shard_map/ppermute | solution.py:33
  11.8 47.6 %copy-start.1 = (bf16[512,192]{0,1:T(8,128)(2,1)S(1)}, bf16[512,192]{0,1:T(8,128)(2,1)}, u32[]{:S(2)}) copy-start(bf16[512,192]{0,1:T(8,128)(2,1)} %param.6) | copy-start | bytes 589828
  11.8 47.6 %copy-start.2 = (bf16[512,192]{0,1:T(8,128)(2,1)S(1)}, bf16[512,192]{0,1:T(8,128)(2,1)}, u32[]{:S(2)}) copy-start(bf16[512,192]{0,1:T(8,128)(2,1)} %param.7) | copy-start | bytes 589828
  11.8 47.6 %copy-start.5 = (s32[4]{0:T(128)S(1)}, s32[4]{0:T(128)}, u32[]{:S(2)}) copy-start(s32[4]{0:T(128)} %pad_add_fusion.place) | copy-start | bytes 52
  11.8 47.6 %collective-permute-start.10 = (f32[4,192,512]{2,1,0:T(8,128)}, f32[4,192,512]{2,1,0:T(8,128)}, u32[]{:S(2)}, u32[]{:S(2)}) collective-permute-start(f32[4,192,512]{2,1,0:T(8,128)} %widen.1), channel_id=1, source_target_pairs={{0,1},{1,0},{2,3},{3,2},{4,5},{5,4},{6,7},{7,6},{8,9},{9,8},{10,11... | collective-permute-start | bytes 4718600 | tf_op jit(solution)/shard_map/ppermute | solution.py:33
  14.1 3.0 %collective-permute-start = (f32[192,96]{1,0:T(8,128)}, f32[192,96]{1,0:T(8,128)S(1)}, u32[]{:S(2)}, u32[]{:S(2)}) collective-permute-start(f32[192,96]{1,0:T(8,128)} %get-tuple-element.15), channel_id=1, source_target_pairs={{0,1},{1,0},{2,3},{3,2},{4,5},{5,4},{6,7},{7,6},{8,9},{9,8},{10,11... | collective-permute-start | bytes 221192 | tf_op jit(solution)/shard_map/ppermute | solution.py:33
  18.1 4.1 %collective-permute-start.1 = (f32[192,96]{1,0:T(8,128)S(1)}, f32[192,96]{1,0:T(8,128)S(1)}, u32[]{:S(2)}, u32[]{:S(2)}) collective-permute-start(f32[192,96]{1,0:T(8,128)S(1)} %add.111), channel_id=1, source_target_pairs={{0,2},{1,3},{2,0},{3,1},{4,6},{5,7},{6,4},{7,5},{8,10},{9,11},{10,... | collective-permute-start | bytes 221192 | tf_op jit(solution)/shard_map/ppermute | solution.py:33
  22.2 24.7 %copy-start.6 = (f32[192,96]{1,0:T(8,128)}, f32[192,96]{1,0:T(8,128)S(1)}, u32[]{:S(2)}) copy-start(f32[192,96]{1,0:T(8,128)S(1)} %collective-permute-done.1) | copy-start | bytes 221188
  22.2 4.8 %collective-permute-start.2 = (f32[192,96]{1,0:T(8,128)S(1)}, f32[192,96]{1,0:T(8,128)S(1)}, u32[]{:S(2)}, u32[]{:S(2)}) collective-permute-start(f32[192,96]{1,0:T(8,128)S(1)} %add.112), channel_id=1, source_target_pairs={{0,6},{1,7},{2,4},{3,5},{4,2},{5,3},{6,0},{7,1},{8,14},{9,15},{10,... | collective-permute-start | bytes 221192 | tf_op jit(solution)/shard_map/ppermute | solution.py:33
  27.0 19.9 %copy-start.7 = (f32[192,96]{1,0:T(8,128)}, f32[192,96]{1,0:T(8,128)S(1)}, u32[]{:S(2)}) copy-start(f32[192,96]{1,0:T(8,128)S(1)} %collective-permute-done.2) | copy-start | bytes 221188
  27.0 3.6 %collective-permute-start.3 = (f32[192,96]{1,0:T(8,128)S(1)}, f32[192,96]{1,0:T(8,128)S(1)}, u32[]{:S(2)}, u32[]{:S(2)}) collective-permute-start(f32[192,96]{1,0:T(8,128)S(1)} %add.114), channel_id=1, source_target_pairs={{0,8},{1,9},{2,10},{3,11},{4,12},{5,13},{6,14},{7,15},{8,0},{9,1},... | collective-permute-start | bytes 221192 | tf_op jit(solution)/shard_map/ppermute | solution.py:33
  30.5 16.3 %copy-start.8 = (f32[192,96]{1,0:T(8,128)}, f32[192,96]{1,0:T(8,128)S(1)}, u32[]{:S(2)}) copy-start(f32[192,96]{1,0:T(8,128)S(1)} %collective-permute-done.3) | copy-start | bytes 221188
  30.6 5.5 %collective-permute-start.4 = (f32[192,96]{1,0:T(8,128)S(1)}, f32[192,96]{1,0:T(8,128)S(1)}, u32[]{:S(2)}, u32[]{:S(2)}) collective-permute-start(f32[192,96]{1,0:T(8,128)S(1)} %add.116), channel_id=1, source_target_pairs={{0,16},{1,17},{2,18},{3,19},{4,20},{5,21},{6,22},{7,23},{8,24},{9,... | collective-permute-start | bytes 221192 | tf_op jit(solution)/shard_map/ppermute | solution.py:33
  36.1 10.8 %copy-start.9 = (f32[192,96]{1,0:T(8,128)}, f32[192,96]{1,0:T(8,128)S(1)}, u32[]{:S(2)}) copy-start(f32[192,96]{1,0:T(8,128)S(1)} %collective-permute-done.4) | copy-start | bytes 221188
  36.1 6.2 %collective-permute-start.5 = (f32[192,96]{1,0:T(8,128)S(1)}, f32[192,96]{1,0:T(8,128)S(1)}, u32[]{:S(2)}, u32[]{:S(2)}) collective-permute-start(f32[192,96]{1,0:T(8,128)S(1)} %add.118), channel_id=1, source_target_pairs={{0,48},{1,49},{2,50},{3,51},{4,52},{5,53},{6,54},{7,55},{8,56},{9,... | collective-permute-start | bytes 221192 | tf_op jit(solution)/shard_map/ppermute | solution.py:33
  42.3 4.6 %copy-start.10 = (f32[192,96]{1,0:T(8,128)}, f32[192,96]{1,0:T(8,128)S(1)}, u32[]{:S(2)}) copy-start(f32[192,96]{1,0:T(8,128)S(1)} %collective-permute-done.5) | copy-start | bytes 221188
  42.3 23.5 %copy-start = (bf16[512,3072]{1,0:T(8,128)(2,1)S(1)}, bf16[512,3072]{1,0:T(8,128)(2,1)}, u32[]{:S(2)}) copy-start(bf16[512,3072]{1,0:T(8,128)(2,1)} %x.3) | copy-start | bytes 9437188
  42.3 3.8 %collective-permute-start.6 = (f32[192,96]{1,0:T(8,128)S(1)}, f32[192,96]{1,0:T(8,128)S(1)}, u32[]{:S(2)}, u32[]{:S(2)}) collective-permute-start(f32[192,96]{1,0:T(8,128)S(1)} %add.120), channel_id=1, source_target_pairs={{0,64},{1,65},{2,66},{3,67},{4,68},{5,69},{6,70},{7,71},{8,72},{9,... | collective-permute-start | bytes 221192 | tf_op jit(solution)/shard_map/ppermute | solution.py:33
  46.2 0.7 copy-start.11
  46.9 5.1 %collective-permute-start.7 = (f32[192,96]{1,0:T(8,128)}, f32[192,96]{1,0:T(8,128)}, u32[]{:S(2)}, u32[]{:S(2)}) collective-permute-start(f32[192,96]{1,0:T(8,128)} %add.122), channel_id=1, source_target_pairs={{0,192},{1,193},{2,194},{3,195},{4,196},{5,197},{6,198},{7,199},{8... | collective-permute-start | bytes 221192 | tf_op jit(solution)/shard_map/ppermute | solution.py:33
  53.2 20.3 %collective-permute-start.8 = (f32[192,96]{1,0:T(8,128)S(1)}, f32[192,96]{1,0:T(8,128)S(1)}, u32[]{:S(2)}, u32[]{:S(2)}) collective-permute-start(f32[192,96]{1,0:T(8,128)S(1)} %select_add_fusion.own), channel_id=1, source_target_pairs={{0,1},{1,0},{2,3},{3,2},{4,5},{5,4},{6,7},{7,6},{8,9},{9,8},{10,11... | collective-permute-start | bytes 221192 | tf_op jit(solution)/shard_map/ppermute | solution.py:33
  59.5 0.9 copy-start.3
  60.4 0.9 copy-start.4
  77.4 13.3 %collective-permute-start.15 = (f32[2,4,2,24,576]{4,3,2,1,0:T(8,128)S(1)}, f32[2,4,2,24,576]{4,3,2,1,0:T(8,128)S(1)}, u32[]{:S(2)}, u32[]{:S(2)}) collective-permute-start(f32[2,4,2,24,576]{4,3,2,1,0:T(8,128)S(1)} %get-tuple-element.24), channel_id=1, source_target_pairs={{0,2},{1,65},{2,0},{3,67},{4,6},{5,69},{6,4},{7,71},{8,10},{9,73},... | collective-permute-start | bytes 2654216 | tf_op jit(solution)/shard_map/ppermute | solution.py:33
  81.8 14.6 %collective-permute-start.11 = (f32[2,4,2,24,576]{4,3,2,1,0:T(8,128)S(1)}, f32[2,4,2,24,576]{4,3,2,1,0:T(8,128)S(1)}, u32[]{:S(2)}, u32[]{:S(2)}) collective-permute-start(f32[2,4,2,24,576]{4,3,2,1,0:T(8,128)S(1)} %get-tuple-element.22), channel_id=1, source_target_pairs={{0,6},{1,193},{2,4},{3,195},{4,2},{5,197},{6,0},{7,199},{8,14},{9,... | collective-permute-start | bytes 2654216 | tf_op jit(solution)/shard_map/ppermute | solution.py:33
  90.8 10.8 %collective-permute-start.16 = (f32[4,2,24,576]{3,2,1,0:T(8,128)S(1)}, f32[4,2,24,576]{3,2,1,0:T(8,128)S(1)}, u32[]{:S(2)}, u32[]{:S(2)}) collective-permute-start(f32[4,2,24,576]{3,2,1,0:T(8,128)S(1)} %fusion), channel_id=1, source_target_pairs={{0,6},{1,193},{2,4},{3,195},{4,2},{5,197},{6,0},{7,199},{8,14},{9,... | collective-permute-start | bytes 1327112 | tf_op jit(solution)/shard_map/ppermute | solution.py:33
  96.4 8.1 %collective-permute-start.12 = (f32[4,2,24,576]{3,2,1,0:T(8,128)S(1)}, f32[4,2,24,576]{3,2,1,0:T(8,128)S(1)}, u32[]{:S(2)}, u32[]{:S(2)}) collective-permute-start(f32[4,2,24,576]{3,2,1,0:T(8,128)S(1)} %fusion.3), channel_id=1, source_target_pairs={{0,2},{1,65},{2,0},{3,67},{4,6},{5,69},{6,4},{7,71},{8,10},{9,73},... | collective-permute-start | bytes 1327112 | tf_op jit(solution)/shard_map/ppermute | solution.py:33
  101.7 6.9 %collective-permute-start.17 = (f32[2,2,24,576]{3,2,1,0:T(8,128)S(1)}, f32[2,2,24,576]{3,2,1,0:T(8,128)S(1)}, u32[]{:S(2)}, u32[]{:S(2)}) collective-permute-start(f32[2,2,24,576]{3,2,1,0:T(8,128)S(1)} %slice.120), channel_id=1, source_target_pairs={{0,64},{1,3},{2,66},{3,1},{4,68},{5,7},{6,70},{7,5},{8,72},{9,11},... | collective-permute-start | bytes 663560 | tf_op jit(solution)/shard_map/ppermute | solution.py:33
  104.6 6.4 %collective-permute-start.13 = (f32[2,2,24,576]{3,2,1,0:T(8,128)S(1)}, f32[2,2,24,576]{3,2,1,0:T(8,128)S(1)}, u32[]{:S(2)}, u32[]{:S(2)}) collective-permute-start(f32[2,2,24,576]{3,2,1,0:T(8,128)S(1)} %slice.113), channel_id=1, source_target_pairs={{0,192},{1,7},{2,194},{3,5},{4,196},{5,3},{6,198},{7,1},{8,200},{9... | collective-permute-start | bytes 663560 | tf_op jit(solution)/shard_map/ppermute | solution.py:33
  108.6 5.3 %collective-permute-start.18 = (f32[2,24,576]{2,1,0:T(8,128)S(1)}, f32[2,24,576]{2,1,0:T(8,128)S(1)}, u32[]{:S(2)}, u32[]{:S(2)}) collective-permute-start(f32[2,24,576]{2,1,0:T(8,128)S(1)} %fusion.6), channel_id=1, source_target_pairs={{0,192},{1,7},{2,194},{3,5},{4,196},{5,3},{6,198},{7,1},{8,200},{9... | collective-permute-start | bytes 331784 | tf_op jit(solution)/shard_map/ppermute | solution.py:33
  111.0 6.2 %collective-permute-start.14 = (f32[2,24,576]{2,1,0:T(8,128)S(1)}, f32[2,24,576]{2,1,0:T(8,128)S(1)}, u32[]{:S(2)}, u32[]{:S(2)}) collective-permute-start(f32[2,24,576]{2,1,0:T(8,128)S(1)} %fusion.9), channel_id=1, source_target_pairs={{0,64},{1,3},{2,66},{3,1},{4,68},{5,7},{6,70},{7,5},{8,72},{9,11},... | collective-permute-start | bytes 331784 | tf_op jit(solution)/shard_map/ppermute | solution.py:33
  114.0 5.5 %collective-permute-start.19 = (f32[2,24,576]{2,1,0:T(8,128)S(1)}, f32[2,24,576]{2,1,0:T(8,128)S(1)}, u32[]{:S(2)}, u32[]{:S(2)}) collective-permute-start(f32[2,24,576]{2,1,0:T(8,128)S(1)} %fusion.8), channel_id=1, source_target_pairs={{0,16},{1,17},{2,18},{3,19},{4,20},{5,21},{6,22},{7,23},{8,24},{9,... | collective-permute-start | bytes 331784 | tf_op jit(solution)/shard_map/ppermute | solution.py:33
  119.5 4.2 %collective-permute-start.20 = (f32[24,576]{1,0:T(8,128)S(1)}, f32[24,576]{1,0:T(8,128)S(1)}, u32[]{:S(2)}, u32[]{:S(2)}) collective-permute-start(f32[24,576]{1,0:T(8,128)S(1)} %slice_bitcast_fusion), channel_id=1, source_target_pairs={{0,8},{1,9},{2,10},{3,11},{4,12},{5,13},{6,14},{7,15},{8,0},{9,1},... | collective-permute-start | bytes 165896 | tf_op jit(solution)/shard_map/ppermute | solution.py:33
  123.8 10.5 %collective-permute-start.21 = (f32[12,576]{1,0:T(8,128)S(1)}, f32[12,576]{1,0:T(8,128)S(1)}, u32[]{:S(2)}, u32[]{:S(2)}) collective-permute-start(f32[12,576]{1,0:T(8,128)S(1)} %get-tuple-element.25), channel_id=1, source_target_pairs={{0,1},{1,49},{2,3},{3,51},{4,5},{5,53},{6,7},{7,55},{8,9},{9,57},{... | collective-permute-start | bytes 82952 | tf_op jit(solution)/shard_map/ppermute | solution.py:33
  127.7 8.3 %collective-permute-start.22 = (f32[12,576]{1,0:T(8,128)S(1)}, f32[12,576]{1,0:T(8,128)S(1)}, u32[]{:S(2)}, u32[]{:S(2)}) collective-permute-start(f32[12,576]{1,0:T(8,128)S(1)} %get-tuple-element.26), channel_id=1, source_target_pairs={{1,48},{3,50},{5,52},{7,54},{9,56},{11,58},{13,60},{15,62},{17,32}... | collective-permute-start | bytes 82952 | tf_op jit(solution)/shard_map/ppermute | solution.py:33

commit v3 on v2

--- a/solution.py
+++ b/solution.py
@@ -81,14 +81,34 @@
     return array[h * HEAD : (h + 1) * HEAD]
 
 
-def states_kernel(place, q, k, v, g, keep, send):
+PACKED = (144, 128)
+
+
+def pack(pair, ref):
+    ref[0:96, 0:96] = pair[0]
+    ref[0:96, 96:128] = pair[1][:, 0:32]
+    ref[96:144, 0:64] = pair[1][0:48, 32:96]
+    ref[96:144, 64:128] = pair[1][48:96, 32:96]
+
+
+def unpack(array):
+    rest = jnp.concatenate([array[96:144, 0:64], array[96:144, 64:128]], axis=0)
+    return array[0:96, 0:96], jnp.concatenate([array[0:96, 96:128], rest], axis=1)
+
+
+def states_kernel(place, *refs):
+    sources, (keep, send), held, arrived = refs[:4], refs[4:6], refs[6:10], refs[10]
+    copies = [pltpu.make_async_copy(a, b, arrived.at[n]) for n, (a, b) in enumerate(zip(sources, held))]
+    for copy in copies:
+        copy.start()
+    for copy in copies:
+        copy.wait()
+    q, k, v, g = held
     first = place[0] == 0
-    for h in range(2):
-        rows = slice(h * HEAD, (h + 1) * HEAD)
-        key_state = lanes_dot(k[rows, :], v[rows, :])
-        query_state = lanes_dot(q[rows, :], g[rows, :])
-        keep[rows, :] = jnp.where(first, key_state, query_state)
-        send[rows, :] = jnp.where(first, query_state, key_state)
+    key_state = [lanes_dot(head(k[...], h), head(v[...], h)) for h in range(2)]
+    query_state = [lanes_dot(head(q[...], h), head(g[...], h)) for h in range(2)]
+    pack([jnp.where(first, a, b) for a, b in zip(key_state, query_state)], keep)
+    pack([jnp.where(first, b, a) for a, b in zip(key_state, query_state)], send)
 
 
 def widen_kernel(q, k, v, g, out):
@@ -133,32 +153,34 @@
                 local[core, at : at + HEAD, :] = a.astype(BF16)
 
 
-def terms_kernel(place, x, wide, local, outer, sums, high, low):
+def over_tokens(place, x, wide, d):
     c = place[0]
+    contract = (((0,), (1,)), ((), ()))
+    one = lax.dot_general(x[...], d[c], contract, preferred_element_type=F32)
     theirs = wide[...].astype(BF16)
-    mine = x[...]
-
-    def over_tokens(d):
-        contract = (((0,), (1,)), ((), ()))
-        one = lax.dot_general(mine, d[c], contract, preferred_element_type=F32)
-        return one + lax.dot_general(theirs, d[1 - c], contract, preferred_element_type=F32)
-
-    shape = (1, 4, 96, -1)
-    sums[...] = over_tokens(local).reshape(shape)
-    outside = over_tokens(outer)
+    return one + lax.dot_general(theirs, d[1 - c], contract, preferred_element_type=F32)
+
+
+def inner_terms_kernel(place, x, wide, local, sums):
+    sums[...] = over_tokens(place, x, wide, local).reshape(sums.shape)
+
+
+def outer_terms_kernel(place, x, wide, outer, high, low):
+    outside = over_tokens(place, x, wide, outer)
     top = outside.astype(BF16)
-    high[...] = top.reshape(shape)
-    low[...] = (outside - top.astype(F32)).astype(BF16).reshape(shape)
+    high[...] = top.reshape(high.shape)
+    low[...] = (outside - top.astype(F32)).astype(BF16).reshape(low.shape)
 
 
 def join_kernel(factor, part, place, own, other, sums, high, low, keep, send):
-    c, pa, pb, pz = (place[i] for i in range(4))
+    c, pa, pb = (place[i] for i in range(3))
     first = c == 0
-    row = lax.broadcasted_iota(jnp.int32, (WIDTH, WIDTH), 0) // HEAD
-    col = lax.broadcasted_iota(jnp.int32, (WIDTH, WIDTH), 1) // HEAD
 
     def by_head(state):
-        return jnp.where(row == col, jnp.concatenate([state, state], axis=1), 0.0).astype(BF16)
+        one, two = unpack(state)
+        none = jnp.zeros_like(one)
+        rows = [jnp.concatenate(pair, axis=1) for pair in ((one, none), (none, two))]
+        return jnp.concatenate(rows, axis=0).astype(BF16)
 
     before = by_head(jnp.where(first, own[...], other[...]))
     later = by_head(jnp.where(first, other[...], own[...]))
@@ -170,30 +192,28 @@
             out = jnp.where(p == n, order[n], out)
         return out
 
-    for k in range(2):
-        zi = pz ^ (k + 2 * part)
-
-        for y in range(NY):
-            pieces = []
-            for n, (state, multiply) in enumerate(((before, lanes_dot), (later, lanes_dot), (later, dot))):
-                lanes = slice(n * 256, n * 256 + WIDTH)
-                total = sums[y, zi, :, n * WIDTH : (n + 1) * WIDTH]
-                for ref in (high, low):
-                    total = total + multiply(ref[y, zi, :, lanes], state)
-                pieces.append(factor * total)
-            value = jnp.concatenate(pieces, axis=1)
-            for x in range(NX):
-                sa = slot(jnp.where(first, x, y) ^ pa)
-                sb = slot(jnp.where(first, y, x) ^ pb)
-                rows = value[x * 24 : x * 24 + 24, :]
-
-                @pl.when(sa < 2)
-                def _(sa=sa, sb=sb, k=k, rows=rows):
-                    keep[sa, sb, k] = rows
-
-                @pl.when(sa >= 2)
-                def _(sa=sa, sb=sb, k=k, rows=rows):
-                    send[sa - 2, sb, k] = rows
+    pieces = []
+    for n, (state, multiply) in enumerate(((before, lanes_dot), (later, lanes_dot), (later, dot))):
+        total = sums[:, 0, :, n * WIDTH : (n + 1) * WIDTH].reshape(4 * 96, WIDTH)
+        for ref in (high, low):
+            term = ref[:, 0, :, n * 256 : n * 256 + WIDTH].reshape(4 * 96, WIDTH)
+            total = total + multiply(term, state)
+        pieces.append(factor * total)
+    value = jnp.concatenate(pieces, axis=1)
+    for y in range(NY):
+        for x in range(NX):
+            sa = slot(jnp.where(first, x, y) ^ pa)
+            sb = slot(jnp.where(first, y, x) ^ pb)
+            at = y * 96 + x * 24
+            rows = value[at : at + 24, :]
+
+            @pl.when(sa < 2)
+            def _(sa=sa, sb=sb, rows=rows):
+                keep[sa, sb, 0] = rows
+
+            @pl.when(sa >= 2)
+            def _(sa=sa, sb=sb, rows=rows):
+                send[sa - 2, sb, 0] = rows
 
 
 VMEM = pl.BlockSpec(memory_space=pltpu.VMEM)
@@ -209,13 +229,14 @@
 
 
 def states(place, q, k, v, g):
-    shape = jax.ShapeDtypeStruct((WIDTH, HEAD), F32)
+    shape = jax.ShapeDtypeStruct(PACKED, F32)
     return pl.pallas_call(
         states_kernel,
         name="states",
         out_shape=(shape, shape),
-        in_specs=[SMEM] + [VMEM] * 4,
+        in_specs=[SMEM] + [pl.BlockSpec(memory_space=pltpu.HBM)] * 4,
         out_specs=(VMEM, VMEM),
+        scratch_shapes=[pltpu.VMEM(q.shape, BF16)] * 4 + [pltpu.SemaphoreType.DMA((4,))],
         cost_estimate=cost(4 * 512 * 192 * 192, 10**6),
     )(place, q, k, v, g)
 
@@ -264,49 +285,57 @@
     )(place, q, k, v, g, other)
 
 
-def terms(place, x, wide, local, outer):
+def terms(kernel, place, x, wide, d, types):
     length, features = x.shape
+    lanes = d.shape[1]
     block = (length, features // 8)
-    whole = lambda a: pl.BlockSpec(a.shape, lambda y, place: (0,) * a.ndim)
-    out = lambda lanes: pl.BlockSpec((1, 4, 96, lanes), lambda y, place: (y, 0, 0, 0))
-    return pl.pallas_call(
-        terms_kernel,
-        name="terms",
-        out_shape=(
-            jax.ShapeDtypeStruct((4, 4, 96, 3 * WIDTH), F32),
-            jax.ShapeDtypeStruct((4, 4, 96, 3 * 256), BF16),
-            jax.ShapeDtypeStruct((4, 4, 96, 3 * 256), BF16),
-        ),
+    out = pl.BlockSpec((1, 4, 96, lanes), lambda y, place: (y, 0, 0, 0))
+    return pl.pallas_call(
+        kernel,
+        name=kernel.__name__,
+        out_shape=tuple(jax.ShapeDtypeStruct((4, 4, 96, lanes), t) for t in types),
         grid_spec=pltpu.PrefetchScalarGridSpec(
             num_scalar_prefetch=1,
             grid=(4,),
             in_specs=[
                 pl.BlockSpec(block, lambda y, place: (0, 2 * y + place[0])),
                 pl.BlockSpec(block, lambda y, place: (0, y)),
-                whole(local),
-                whole(outer),
+                pl.BlockSpec(d.shape, lambda y, place: (0, 0, 0)),
             ],
-            out_specs=(out(3 * WIDTH), out(3 * 256), out(3 * 256)),
+            out_specs=(out,) * len(types),
         ),
-        cost_estimate=cost(4 * 512 * 3072 * 576, 12 * 10**6),
-        compiler_params=limit(32),
-    )(place, x, wide, local, outer)
+        cost_estimate=cost(2 * 512 * 3072 * 576, 8 * 10**6),
+        compiler_params=limit(24),
+    )(place, x, wide, d)
 
 
 def join(part, factor, place, own, other, sums, high, low):
     shape = jax.ShapeDtypeStruct((2, 4, 2, 24, 3 * WIDTH), F32)
+    state = pl.BlockSpec(PACKED, lambda k, place: (0, 0))
+    block = lambda lanes: pl.BlockSpec(
+        (4, 1, 96, lanes), lambda k, place: (0, place[3] ^ (k + 2 * part), 0, 0)
+    )
+    out = pl.BlockSpec((2, 4, 1, 24, 3 * WIDTH), lambda k, place: (0, 0, k, 0, 0))
     return pl.pallas_call(
         functools.partial(join_kernel, factor, part),
         name=f"join{part}",
         out_shape=(shape, shape),
-        in_specs=[SMEM] + [VMEM] * 5,
-        out_specs=(VMEM, VMEM),
-        cost_estimate=cost(12 * 768 * 192 * 192, 10**7),
-        compiler_params=limit(32),
+        grid_spec=pltpu.PrefetchScalarGridSpec(
+            num_scalar_prefetch=1,
+            grid=(2,),
+            in_specs=[state, state, block(3 * WIDTH), block(3 * 256), block(3 * 256)],
+            out_specs=(out, out),
+        ),
+        cost_estimate=cost(12 * 768 * 192 * 192, 8 * 10**6),
+        compiler_params=limit(24),
     )(place, own, other, sums, high, low)
 
 
-def before_chip(me, total):
+def tie(*values):
+    return lax.optimization_barrier(values)
+
+
+def before_chip(me, total, works):
     y, z, x, c = me
     before = jnp.zeros_like(total)
     steps = (
@@ -318,8 +347,10 @@
         (y_partner(1), y & 1),
         (y_partner(3), y >> 1),
     )
-    for move, bit in steps:
+    for n, (move, bit) in enumerate(steps):
         came = permute(total, move)
+        if n < len(works):
+            came, total = works[n](came, total)
         before = before + jnp.where(bit != c, came, 0.0)
         total = total + came
     return before
@@ -354,13 +385,40 @@
     place = jnp.stack([c, jnp.where(c == 0, x, y), jnp.where(c == 0, y, x), block]).astype(jnp.int32)
     features_first = [a.T for a in (query_proj, key_proj, value_proj, grad_out)]
     keep, send = states(place, *features_first)
-    before = before_chip(me, keep + swap_cores(send))
-    other = swap_cores(widen(*features_first))
-    wide = swap_cores(widen_inputs(place, inputs))
-    local, outer = local_terms(place, *features_first, other)
-    pieces = terms(place, inputs, wide, local, outer)
+    send, *late = tie(send, *features_first)
+    came = swap_cores(send)
+    plain = widen(*late)
+    came, plain = tie(came, plain)
+    other = swap_cores(plain)
+    made = {}
+
+    def inputs_work(came, total):
+        total, x = tie(total, inputs)
+        came, wide = tie(came, widen_inputs(place, x))
+        made["wide"] = swap_cores(wide)
+        return came, total
+
+    def local_work(came, total):
+        total, theirs = tie(total, other)
+        came, *made["local"] = tie(came, *local_terms(place, *late, theirs))
+        return came, total
+
+    def outer_work(came, total):
+        total, d = tie(total, made["local"][1])
+        kernel = outer_terms_kernel
+        came, *made["outer"] = tie(came, *terms(kernel, place, inputs, made["wide"], d, (BF16, BF16)))
+        return came, total
+
+    def inner_work(came, total):
+        total, d = tie(total, made["local"][0])
+        came, made["inner"] = tie(came, *terms(inner_terms_kernel, place, inputs, made["wide"], d, (F32,)))
+        return came, total
+
+    before = before_chip(me, keep + came, (inputs_work, local_work, outer_work, inner_work))
     across = swap_cores(before)
-    parts = [join(part, factor, place, before, across, *pieces) for part in range(2)]
+    parts = [
+        join(part, factor, place, before, across, made["inner"], *made["outer"]) for part in range(2)
+    ]
     summed = scatter_sum(me, parts)
     return (summed[:, :width], summed[:, width : 2 * width], summed[:, 2 * width :])
 

time: 137 us -> 128 us (0.934)
  waiting for transfers between devices: 53.4 us -> 43.2 us
  local copies, waits for them, and re-layouts: 2.62 us -> 6.41 us
  other arithmetic: 3.91 us -> 1.09 us
    ppermute x23, waiting for transfers between devices: 53.4 us -> 43.2 us  [permute(): return lax.ppermute(value, SEQ, pairs)]
    unnamed x24, local copies, waits for them, and re-layouts: 1.89 us -> 5.68 us
    pallas_call x1 -> x2, Pallas kernels: 7.62 us -> 8.53 us  [terms(): pl.pallas_call(kernel, name=kernel.__name__, out_shape=tuple((jax.ShapeDt...]
  transfers between devices with their start and end apart: 23 -> 23, of which waited for: 17 -> 14; matrix products, arithmetic and copies ran while one was open for 2% -> 0% of each run, Pallas kernels for 15% -> 18%
where the time goes in v3:
time: 128 us; the launch traced here: 127 us
  starting transfers between devices  46.6 us (36%)
  waiting for transfers between devices  43.2 us (34%)
  Pallas kernels  29.1 us (23%)
  local copies, waits for them, and re-layouts  6.41 us (5%)
    ppermute x23, starting transfers between devices, permute(): return lax.ppermute(value, SEQ, pairs)  46.6 us
    ppermute x23, waiting for transfers between devices, permute(): return lax.ppermute(value, SEQ, pairs)  43.2 us
    pallas_call x2, Pallas kernels, terms(): pl.pallas_call(kernel, name=kernel.__name__, out_shape=tuple((jax.ShapeDt...  8.53 us
    pallas_call x2, Pallas kernels, join(): pl.pallas_call(functools.partial(join_kernel, factor, part), name=f'join{...  6.68 us
    unnamed x24, local copies, waits for them, and re-layouts  5.68 us
    pallas_call x1, Pallas kernels, widen_inputs(): pl.pallas_call(widen_inputs_kernel, name='widen_inputs', out_shape=jax.Sh...  4.86 us
    pallas_call x1, Pallas kernels, local_terms(): pl.pallas_call(local_kernel, name='local_terms', out_shape=(jax.ShapeDtyp...  3.67 us
    pallas_call x1, Pallas kernels, states(): pl.pallas_call(states_kernel, name='states', out_shape=(shape, shape), in...  2.9 us
  transfers between devices with their start and end apart: 23, of which 14 were waited for; matrix products, arithmetic and copies ran while one was open for 0% of the time, Pallas kernels for 18%

profile of v3, /device:TPU:1, one launch (start us, length us, event | category | flops | bytes accessed | tf_op | source)
XLA Modules:
  0.0 127.4 jit_solution(4643188607780889191)
XLA Ops:
  0.7 0.6 pad_add_fusion.place
  1.2 2.9 %states.1 = (f32[144,128]{1,0:T(8,128)}, f32[144,128]{1,0:T(8,128)}) custom-call(s32[4]{0:T(128)} %pad_add_fusion.place, bf16[192,512]{1,0:T(8,128)(2,1)} %bitcast.40, bf16[192,512]{1,0:T(8,128)(2,1)} %bitcast.43, bf16[192,512]{1,0:T(8,128)(2,1)} %bitcast.46, bf16[192,512]{1,0:T(8,128)(2,1)} %bitcast.49), custom_call_target="tpu_custom_call" | custom-call | flops 75497472 | bytes 1000000 | tf_op jit(solution)/shard_map/states/pallas_call | solution.py:233
  4.2 3.3 %collective-permute-start = (f32[144,128]{1,0:T(8,128)}, f32[144,128]{1,0:T(8,128)S(1)}, u32[]{:S(2)}, u32[]{:S(2)}) collective-permute-start(f32[144,128]{1,0:T(8,128)} %get-tuple-element.40), channel_id=1, source_target_pairs={{0,1},{1,0},{2,3},{3,2},{4,5},{5,4},{6,7},{7,6},{8,9},{9,8},{10,11... | collective-permute-start | bytes 221192 | tf_op jit(solution)/shard_map/ppermute | solution.py:33
  7.5 2.5 %widen.1 = f32[4,192,512]{2,1,0:T(8,128)} custom-call(bf16[192,512]{1,0:T(8,128)(2,1)} %bitcast.41, bf16[192,512]{1,0:T(8,128)(2,1)} %bitcast.44, bf16[192,512]{1,0:T(8,128)(2,1)} %bitcast.47, bf16[192,512]{1,0:T(8,128)(2,1)} %bitcast.50), custom_call_target="tpu_custom_call" | custom-call | flops 1000000 | bytes 2400000 | tf_op jit(solution)/shard_map/widen/pallas_call | solution.py:245
  10.0 0.1 collective-permute-start.1
  10.1 4.9 %widen_inputs.1 = f32[512,1536]{1,0:T(8,128)} custom-call(s32[4]{0:T(128)} %pad_add_fusion.place, bf16[512,3072]{1,0:T(8,128)(2,1)} %x.4), custom_call_target="tpu_custom_call" | custom-call | flops 1000000 | bytes 5000000 | tf_op jit(solution)/shard_map/widen_inputs/pallas_call | solution.py:258
  15.0 0.5 collective-permute-start.3
  15.5 1.4 %collective-permute-start.2 = (f32[144,128]{1,0:T(8,128)S(1)}, f32[144,128]{1,0:T(8,128)S(1)}, u32[]{:S(2)}, u32[]{:S(2)}) collective-permute-start(f32[144,128]{1,0:T(8,128)S(1)} %add.112), channel_id=1, source_target_pairs={{0,6},{1,7},{2,4},{3,5},{4,2},{5,3},{6,0},{7,1},{8,14},{9,15},{10,... | collective-permute-start | bytes 221192 | tf_op jit(solution)/shard_map/ppermute | solution.py:33
  16.9 5.7 %collective-permute-done.3.other = f32[4,192,512]{2,1,0:T(8,128)S(1)} collective-permute-done((f32[4,192,512]{2,1,0:T(8,128)S(1)}, f32[4,192,512]{2,1,0:T(8,128)S(1)}, u32[]{:S(2)}, u32[]{:S(2)}) %collective-permute-start.3) | collective-permute-done | bytes 1572896 | tf_op jit(solution)/shard_map/ppermute | solution.py:33
  22.6 3.7 %local_terms.1 = (bf16[2,576,512]{2,1,0:T(8,128)(2,1)S(1)}, bf16[2,768,512]{2,1,0:T(8,128)(2,1)S(1)}) custom-call(s32[4]{0:T(128)S(1)} %copy-done.9, bf16[192,512]{1,0:T(8,128)(2,1)S(1)} %bitcast.42, bf16[192,512]{1,0:T(8,128)(2,1)S(1)} %bitcast.45, bf16[192,512]{1,0:T(8,128)(2,1)S(1)} %bitcast.48, bf16[192,512]{1,0:T(8,128)(2,1)S(1)} %bitcast.51, ...), custom_call_target="tpu_custom_call" | custom-call | flops 1006632960 | bytes 5000000 | tf_op jit(solution)/shard_map/local_terms/pallas_call | solution.py:274
  26.3 1.4 %collective-permute-start.4 = (f32[144,128]{1,0:T(8,128)S(1)}, f32[144,128]{1,0:T(8,128)S(1)}, u32[]{:S(2)}, u32[]{:S(2)}) collective-permute-start(f32[144,128]{1,0:T(8,128)S(1)} %add.114), channel_id=1, source_target_pairs={{0,8},{1,9},{2,10},{3,11},{4,12},{5,13},{6,14},{7,15},{8,0},{9,1},... | collective-permute-start | bytes 221192 | tf_op jit(solution)/shard_map/ppermute | solution.py:33
  27.7 4.3 %outer_terms_kernel.1 = (bf16[4,4,96,768]{3,2,1,0:T(8,128)(2,1)S(1)}, bf16[4,4,96,768]{3,2,1,0:T(8,128)(2,1)S(1)}) custom-call(s32[4]{0:T(128)S(1)} %copy-done.9, bf16[512,3072]{1,0:T(8,128)(2,1)S(1)} %copy-done.2, f32[512,1536]{1,0:T(8,128)S(1)} %collective-permute-done.5.wide, bf16[2,768,512]{2,1,0:T(8,128)(2,1)S(1)} %get-tuple-element.57.outer), custom_call_target="tpu_custom_call" | custom-call | flops 1811939328 | bytes 8000000 | tf_op jit(solution)/shard_map/outer_terms_kernel/pallas_call | solution.py:293
  32.0 3.1 %collective-permute-start.6 = (f32[144,128]{1,0:T(8,128)S(1)}, f32[144,128]{1,0:T(8,128)S(1)}, u32[]{:S(2)}, u32[]{:S(2)}) collective-permute-start(f32[144,128]{1,0:T(8,128)S(1)} %add.116), channel_id=1, source_target_pairs={{0,16},{1,17},{2,18},{3,19},{4,20},{5,21},{6,22},{7,23},{8,24},{9,... | collective-permute-start | bytes 221192 | tf_op jit(solution)/shard_map/ppermute | solution.py:33
  35.1 4.2 %inner_terms_kernel.1.sums = f32[4,4,96,576]{3,2,1,0:T(8,128)S(1)} custom-call(s32[4]{0:T(128)S(1)} %copy-done.9, bf16[512,3072]{1,0:T(8,128)(2,1)S(1)} %copy-done.2, f32[512,1536]{1,0:T(8,128)S(1)} %collective-permute-done.5.wide, bf16[2,576,512]{2,1,0:T(8,128)(2,1)S(1)} %get-tuple-element.63.local), custom_call_target="tpu_custom_call" | custom-call | flops 1811939328 | bytes 8000000 | tf_op jit(solution)/shard_map/inner_terms_kernel/pallas_call | solution.py:293
  39.4 1.9 %copy-done = f32[4,4,96,576]{3,2,1,0:T(8,128)} copy-done((f32[4,4,96,576]{3,2,1,0:T(8,128)}, f32[4,4,96,576]{3,2,1,0:T(8,128)S(1)}, u32[]{:S(2)}) %copy-start) | copy-done | bytes 3538968
  41.3 3.4 %collective-permute-start.7 = (f32[144,128]{1,0:T(8,128)S(1)}, f32[144,128]{1,0:T(8,128)S(1)}, u32[]{:S(2)}, u32[]{:S(2)}) collective-permute-start(f32[144,128]{1,0:T(8,128)S(1)} %add.118), channel_id=1, source_target_pairs={{0,48},{1,49},{2,50},{3,51},{4,52},{5,53},{6,54},{7,55},{8,56},{9,... | collective-permute-start | bytes 221192 | tf_op jit(solution)/shard_map/ppermute | solution.py:33
  44.7 2.2 %collective-permute-done.7 = f32[144,128]{1,0:T(8,128)S(1)} collective-permute-done((f32[144,128]{1,0:T(8,128)S(1)}, f32[144,128]{1,0:T(8,128)S(1)}, u32[]{:S(2)}, u32[]{:S(2)}) %collective-permute-start.7) | collective-permute-done | bytes 73760 | tf_op jit(solution)/shard_map/ppermute | solution.py:33
  46.8 1.3 %collective-permute-start.8 = (f32[144,128]{1,0:T(8,128)S(1)}, f32[144,128]{1,0:T(8,128)S(1)}, u32[]{:S(2)}, u32[]{:S(2)}) collective-permute-start(f32[144,128]{1,0:T(8,128)S(1)} %add.120), channel_id=1, source_target_pairs={{0,64},{1,65},{2,66},{3,67},{4,68},{5,69},{6,70},{7,71},{8,72},{9,... | collective-permute-start | bytes 221192 | tf_op jit(solution)/shard_map/ppermute | solution.py:33
  48.2 2.0 %collective-permute-done.8 = f32[144,128]{1,0:T(8,128)S(1)} collective-permute-done((f32[144,128]{1,0:T(8,128)S(1)}, f32[144,128]{1,0:T(8,128)S(1)}, u32[]{:S(2)}, u32[]{:S(2)}) %collective-permute-start.8) | collective-permute-done | bytes 73760 | tf_op jit(solution)/shard_map/ppermute | solution.py:33
  50.1 2.8 %collective-permute-start.9 = (f32[144,128]{1,0:T(8,128)S(1)}, f32[144,128]{1,0:T(8,128)S(1)}, u32[]{:S(2)}, u32[]{:S(2)}) collective-permute-start(f32[144,128]{1,0:T(8,128)S(1)} %add.122), channel_id=1, source_target_pairs={{0,192},{1,193},{2,194},{3,195},{4,196},{5,197},{6,198},{7,199},{8... | collective-permute-start | bytes 221192 | tf_op jit(solution)/shard_map/ppermute | solution.py:33
  52.9 1.7 %collective-permute-done.9 = f32[144,128]{1,0:T(8,128)S(1)} collective-permute-done((f32[144,128]{1,0:T(8,128)S(1)}, f32[144,128]{1,0:T(8,128)S(1)}, u32[]{:S(2)}, u32[]{:S(2)}) %collective-permute-start.9) | collective-permute-done | bytes 73760 | tf_op jit(solution)/shard_map/ppermute | solution.py:33
  54.7 4.5 %collective-permute-start.10 = (f32[144,128]{1,0:T(8,128)S(1)}, f32[144,128]{1,0:T(8,128)S(1)}, u32[]{:S(2)}, u32[]{:S(2)}) collective-permute-start(f32[144,128]{1,0:T(8,128)S(1)} %select_add_fusion.own), channel_id=1, source_target_pairs={{0,1},{1,0},{2,3},{3,2},{4,5},{5,4},{6,7},{7,6},{8,9},{9,8},{10,11... | collective-permute-start | bytes 221192 | tf_op jit(solution)/shard_map/ppermute | solution.py:33
  59.2 0.9 collective-permute-done.10.other
  60.1 2.1 %copy-done.1 = f32[4,4,96,576]{3,2,1,0:T(8,128)S(1)} copy-done((f32[4,4,96,576]{3,2,1,0:T(8,128)S(1)}, f32[4,4,96,576]{3,2,1,0:T(8,128)}, u32[]{:S(2)}) %copy-start.1) | copy-done | bytes 3538968
  62.2 1.7 %copy-done.4 = bf16[4,4,96,768]{3,2,1,0:T(8,128)(2,1)S(1)} copy-done((bf16[4,4,96,768]{3,2,1,0:T(8,128)(2,1)S(1)}, bf16[4,4,96,768]{3,2,1,0:T(8,128)(2,1)}, u32[]{:S(2)}) %copy-start.4) | copy-done | bytes 2359320
  63.9 3.3 %join1.1 = (f32[2,4,2,24,576]{4,3,2,1,0:T(8,128)S(1)}, f32[2,4,2,24,576]{4,3,2,1,0:T(8,128)S(1)}) custom-call(s32[4]{0:T(128)S(1)} %copy-done.9, f32[144,128]{1,0:T(8,128)S(1)} %select_add_fusion.own, f32[144,128]{1,0:T(8,128)S(1)} %collective-permute-done.10.other, f32[4,4,96,576]{3,2,1,0:T(8,128)S(1)} %copy-done.1, ...), custom_call_target="tpu_custom_call" | custom-call | flops 339738624 | bytes 8000000 | tf_op jit(solution)/shard_map/join1/pallas_call | solution.py:319
  67.2 0.2 collective-permute-start.15
  67.4 3.3 %join0.1 = (f32[2,4,2,24,576]{4,3,2,1,0:T(8,128)S(1)}, f32[2,4,2,24,576]{4,3,2,1,0:T(8,128)S(1)}) custom-call(s32[4]{0:T(128)S(1)} %copy-done.9, f32[144,128]{1,0:T(8,128)S(1)} %select_add_fusion.own, f32[144,128]{1,0:T(8,128)S(1)} %collective-permute-done.10.other, f32[4,4,96,576]{3,2,1,0:T(8,128)S(1)} %copy-done.1, ...), custom_call_target="tpu_custom_call" | custom-call | flops 339738624 | bytes 8000000 | tf_op jit(solution)/shard_map/join0/pallas_call | solution.py:319
  70.7 2.7 %collective-permute-start.11 = (f32[2,4,2,24,576]{4,3,2,1,0:T(8,128)S(1)}, f32[2,4,2,24,576]{4,3,2,1,0:T(8,128)S(1)}, u32[]{:S(2)}, u32[]{:S(2)}) collective-permute-start(f32[2,4,2,24,576]{4,3,2,1,0:T(8,128)S(1)} %get-tuple-element.70), channel_id=1, source_target_pairs={{0,6},{1,193},{2,4},{3,195},{4,2},{5,197},{6,0},{7,199},{8,14},{9,... | collective-permute-start | bytes 2654216 | tf_op jit(solution)/shard_map/ppermute | solution.py:33
  73.5 7.1 %collective-permute-done.15 = f32[2,4,2,24,576]{4,3,2,1,0:T(8,128)S(1)} collective-permute-done((f32[2,4,2,24,576]{4,3,2,1,0:T(8,128)S(1)}, f32[2,4,2,24,576]{4,3,2,1,0:T(8,128)S(1)}, u32[]{:S(2)}, u32[]{:S(2)}) %collective-permute-start.15) | collective-permute-done | bytes 884768 | tf_op jit(solution)/shard_map/ppermute | solution.py:33
  80.6 2.8 %collective-permute-start.16 = (f32[4,2,24,576]{3,2,1,0:T(8,128)S(1)}, f32[4,2,24,576]{3,2,1,0:T(8,128)S(1)}, u32[]{:S(2)}, u32[]{:S(2)}) collective-permute-start(f32[4,2,24,576]{3,2,1,0:T(8,128)S(1)} %fusion), channel_id=1, source_target_pairs={{0,6},{1,193},{2,4},{3,195},{4,2},{5,197},{6,0},{7,199},{8,14},{9,... | collective-permute-start | bytes 1327112 | tf_op jit(solution)/shard_map/ppermute | solution.py:33
  83.4 1.9 %collective-permute-done.11 = f32[2,4,2,24,576]{4,3,2,1,0:T(8,128)S(1)} collective-permute-done((f32[2,4,2,24,576]{4,3,2,1,0:T(8,128)S(1)}, f32[2,4,2,24,576]{4,3,2,1,0:T(8,128)S(1)}, u32[]{:S(2)}, u32[]{:S(2)}) %collective-permute-start.11) | collective-permute-done | bytes 884768 | tf_op jit(solution)/shard_map/ppermute | solution.py:33
  85.3 0.9 collective-permute-start.12
  86.3 4.3 %collective-permute-done.16 = f32[4,2,24,576]{3,2,1,0:T(8,128)S(1)} collective-permute-done((f32[4,2,24,576]{3,2,1,0:T(8,128)S(1)}, f32[4,2,24,576]{3,2,1,0:T(8,128)S(1)}, u32[]{:S(2)}, u32[]{:S(2)}) %collective-permute-start.16) | collective-permute-done | bytes 442400 | tf_op jit(solution)/shard_map/ppermute | solution.py:33
  90.6 0.2 collective-permute-start.17
  90.8 2.6 %collective-permute-done.12 = f32[4,2,24,576]{3,2,1,0:T(8,128)S(1)} collective-permute-done((f32[4,2,24,576]{3,2,1,0:T(8,128)S(1)}, f32[4,2,24,576]{3,2,1,0:T(8,128)S(1)}, u32[]{:S(2)}, u32[]{:S(2)}) %collective-permute-start.12) | collective-permute-done | bytes 442400 | tf_op jit(solution)/shard_map/ppermute | solution.py:33
  93.5 1.8 %collective-permute-start.13 = (f32[2,2,24,576]{3,2,1,0:T(8,128)S(1)}, f32[2,2,24,576]{3,2,1,0:T(8,128)S(1)}, u32[]{:S(2)}, u32[]{:S(2)}) collective-permute-start(f32[2,2,24,576]{3,2,1,0:T(8,128)S(1)} %slice.113), channel_id=1, source_target_pairs={{0,192},{1,7},{2,194},{3,5},{4,196},{5,3},{6,198},{7,1},{8,200},{9... | collective-permute-start | bytes 663560 | tf_op jit(solution)/shard_map/ppermute | solution.py:33
  95.3 2.9 %collective-permute-done.17 = f32[2,2,24,576]{3,2,1,0:T(8,128)S(1)} collective-permute-done((f32[2,2,24,576]{3,2,1,0:T(8,128)S(1)}, f32[2,2,24,576]{3,2,1,0:T(8,128)S(1)}, u32[]{:S(2)}, u32[]{:S(2)}) %collective-permute-start.17) | collective-permute-done | bytes 221216 | tf_op jit(solution)/shard_map/ppermute | solution.py:33
  98.3 2.3 %collective-permute-start.18 = (f32[2,24,576]{2,1,0:T(8,128)S(1)}, f32[2,24,576]{2,1,0:T(8,128)S(1)}, u32[]{:S(2)}, u32[]{:S(2)}) collective-permute-start(f32[2,24,576]{2,1,0:T(8,128)S(1)} %fusion.6), channel_id=1, source_target_pairs={{0,192},{1,7},{2,194},{3,5},{4,196},{5,3},{6,198},{7,1},{8,200},{9... | collective-permute-start | bytes 331784 | tf_op jit(solution)/shard_map/ppermute | solution.py:33
  100.8 2.9 %collective-permute-done.18 = f32[2,24,576]{2,1,0:T(8,128)S(1)} collective-permute-done((f32[2,24,576]{2,1,0:T(8,128)S(1)}, f32[2,24,576]{2,1,0:T(8,128)S(1)}, u32[]{:S(2)}, u32[]{:S(2)}) %collective-permute-start.18) | collective-permute-done | bytes 110624 | tf_op jit(solution)/shard_map/ppermute | solution.py:33
  103.6 2.0 %collective-permute-start.19 = (f32[2,24,576]{2,1,0:T(8,128)S(1)}, f32[2,24,576]{2,1,0:T(8,128)S(1)}, u32[]{:S(2)}, u32[]{:S(2)}) collective-permute-start(f32[2,24,576]{2,1,0:T(8,128)S(1)} %fusion.8), channel_id=1, source_target_pairs={{0,16},{1,17},{2,18},{3,19},{4,20},{5,21},{6,22},{7,23},{8,24},{9,... | collective-permute-start | bytes 331784 | tf_op jit(solution)/shard_map/ppermute | solution.py:33
  105.6 4.0 %collective-permute-done.19 = f32[2,24,576]{2,1,0:T(8,128)S(1)} collective-permute-done((f32[2,24,576]{2,1,0:T(8,128)S(1)}, f32[2,24,576]{2,1,0:T(8,128)S(1)}, u32[]{:S(2)}, u32[]{:S(2)}) %collective-permute-start.19) | collective-permute-done | bytes 110624 | tf_op jit(solution)/shard_map/ppermute | solution.py:33
  109.7 0.3 collective-permute-start.20
  110.0 3.5 %collective-permute-done.20 = f32[24,576]{1,0:T(8,128)S(1)} collective-permute-done((f32[24,576]{1,0:T(8,128)S(1)}, f32[24,576]{1,0:T(8,128)S(1)}, u32[]{:S(2)}, u32[]{:S(2)}) %collective-permute-start.20) | collective-permute-done | bytes 55328 | tf_op jit(solution)/shard_map/ppermute | solution.py:33
  113.5 3.2 %collective-permute-start.21 = (f32[12,576]{1,0:T(8,128)S(1)}, f32[12,576]{1,0:T(8,128)S(1)}, u32[]{:S(2)}, u32[]{:S(2)}) collective-permute-start(f32[12,576]{1,0:T(8,128)S(1)} %get-tuple-element.73), channel_id=1, source_target_pairs={{0,1},{1,49},{2,3},{3,51},{4,5},{5,53},{6,7},{7,55},{8,9},{9,57},{... | collective-permute-start | bytes 82952 | tf_op jit(solution)/shard_map/ppermute | solution.py:33
  116.8 8.2 %collective-permute-start.22 = (f32[12,576]{1,0:T(8,128)S(1)}, f32[12,576]{1,0:T(8,128)S(1)}, u32[]{:S(2)}, u32[]{:S(2)}) collective-permute-start(f32[12,576]{1,0:T(8,128)S(1)} %get-tuple-element.74), channel_id=1, source_target_pairs={{1,48},{3,50},{5,52},{7,54},{9,56},{11,58},{13,60},{15,62},{17,32}... | collective-permute-start | bytes 82952 | tf_op jit(solution)/shard_map/ppermute | solution.py:33
  125.0 1.7 %collective-permute-done.22 = f32[12,576]{1,0:T(8,128)S(1)} collective-permute-done((f32[12,576]{1,0:T(8,128)S(1)}, f32[12,576]{1,0:T(8,128)S(1)}, u32[]{:S(2)}, u32[]{:S(2)}) %collective-permute-start.22) | collective-permute-done | bytes 27680 | tf_op jit(solution)/shard_map/ppermute | solution.py:33
  126.7 0.7 fusion.14
  (54 shorter events, 0.7 us)
Async XLA Ops:
  4.2 5.8 %copy-start.11 = (f32[144,128]{1,0:T(8,128)S(1)}, f32[144,128]{1,0:T(8,128)}, u32[]{:S(2)}) copy-start(f32[144,128]{1,0:T(8,128)} %get-tuple-element.38) | copy-start | bytes 221188
  4.2 5.8 %collective-permute-start = (f32[144,128]{1,0:T(8,128)}, f32[144,128]{1,0:T(8,128)S(1)}, u32[]{:S(2)}, u32[]{:S(2)}) collective-permute-start(f32[144,128]{1,0:T(8,128)} %get-tuple-element.40), channel_id=1, source_target_pairs={{0,1},{1,0},{2,3},{3,2},{4,5},{5,4},{6,7},{7,6},{8,9},{9,8},{10,11... | collective-permute-start | bytes 221192 | tf_op jit(solution)/shard_map/ppermute | solution.py:33
  10.0 5.1 %copy-start.10 = (f32[4,192,512]{2,1,0:T(8,128)S(1)}, f32[4,192,512]{2,1,0:T(8,128)}, u32[]{:S(2)}) copy-start(f32[4,192,512]{2,1,0:T(8,128)} %widen.1) | copy-start | bytes 4718596
  10.0 12.6 %copy-start.5 = (bf16[512,192]{0,1:T(8,128)(2,1)S(1)}, bf16[512,192]{0,1:T(8,128)(2,1)}, u32[]{:S(2)}) copy-start(bf16[512,192]{0,1:T(8,128)(2,1)} %param.6) | copy-start | bytes 589828
  10.0 12.6 %copy-start.6 = (bf16[512,192]{0,1:T(8,128)(2,1)S(1)}, bf16[512,192]{0,1:T(8,128)(2,1)}, u32[]{:S(2)}) copy-start(bf16[512,192]{0,1:T(8,128)(2,1)} %param.7) | copy-start | bytes 589828
  10.0 12.6 %copy-start.7 = (bf16[512,192]{0,1:T(8,128)(2,1)S(1)}, bf16[512,192]{0,1:T(8,128)(2,1)}, u32[]{:S(2)}) copy-start(bf16[512,192]{0,1:T(8,128)(2,1)} %param.8) | copy-start | bytes 589828
  10.0 12.6 %copy-start.8 = (bf16[512,192]{0,1:T(8,128)(2,1)S(1)}, bf16[512,192]{0,1:T(8,128)(2,1)}, u32[]{:S(2)}) copy-start(bf16[512,192]{0,1:T(8,128)(2,1)} %param.9) | copy-start | bytes 589828
  10.0 12.6 %copy-start.9 = (s32[4]{0:T(128)S(1)}, s32[4]{0:T(128)}, u32[]{:S(2)}) copy-start(s32[4]{0:T(128)} %pad_add_fusion.place) | copy-start | bytes 52
  10.0 5.0 %collective-permute-start.1 = (f32[144,128]{1,0:T(8,128)S(1)}, f32[144,128]{1,0:T(8,128)S(1)}, u32[]{:S(2)}, u32[]{:S(2)}) collective-permute-start(f32[144,128]{1,0:T(8,128)S(1)} %add.111), channel_id=1, source_target_pairs={{0,2},{1,3},{2,0},{3,1},{4,6},{5,7},{6,4},{7,5},{8,10},{9,11},{10,... | collective-permute-start | bytes 221192 | tf_op jit(solution)/shard_map/ppermute | solution.py:33
  15.0 12.7 %copy-start.2 = (bf16[512,3072]{1,0:T(8,128)(2,1)S(1)}, bf16[512,3072]{1,0:T(8,128)(2,1)}, u32[]{:S(2)}) copy-start(bf16[512,3072]{1,0:T(8,128)(2,1)} %x.4) | copy-start | bytes 9437188
  15.0 12.7 %collective-permute-start.5 = (f32[512,1536]{1,0:T(8,128)}, f32[512,1536]{1,0:T(8,128)S(1)}, u32[]{:S(2)}, u32[]{:S(2)}) collective-permute-start(f32[512,1536]{1,0:T(8,128)} %widen_inputs.1), channel_id=1, source_target_pairs={{0,1},{1,0},{2,3},{3,2},{4,5},{5,4},{6,7},{7,6},{8,9},{9,8},{10,11... | collective-permute-start | bytes 9437192 | tf_op jit(solution)/shard_map/ppermute | solution.py:33
  15.0 7.5 %collective-permute-start.3 = (f32[4,192,512]{2,1,0:T(8,128)S(1)}, f32[4,192,512]{2,1,0:T(8,128)S(1)}, u32[]{:S(2)}, u32[]{:S(2)}) collective-permute-start(f32[4,192,512]{2,1,0:T(8,128)S(1)} %copy-done.10), channel_id=1, source_target_pairs={{0,1},{1,0},{2,3},{3,2},{4,5},{5,4},{6,7},{7,6},{8,9},{9,8},{10,11... | collective-permute-start | bytes 4718600 | tf_op jit(solution)/shard_map/ppermute | solution.py:33
  15.5 10.7 %collective-permute-start.2 = (f32[144,128]{1,0:T(8,128)S(1)}, f32[144,128]{1,0:T(8,128)S(1)}, u32[]{:S(2)}, u32[]{:S(2)}) collective-permute-start(f32[144,128]{1,0:T(8,128)S(1)} %add.112), channel_id=1, source_target_pairs={{0,6},{1,7},{2,4},{3,5},{4,2},{5,3},{6,0},{7,1},{8,14},{9,15},{10,... | collective-permute-start | bytes 221192 | tf_op jit(solution)/shard_map/ppermute | solution.py:33
  26.3 5.7 %collective-permute-start.4 = (f32[144,128]{1,0:T(8,128)S(1)}, f32[144,128]{1,0:T(8,128)S(1)}, u32[]{:S(2)}, u32[]{:S(2)}) collective-permute-start(f32[144,128]{1,0:T(8,128)S(1)} %add.114), channel_id=1, source_target_pairs={{0,8},{1,9},{2,10},{3,11},{4,12},{5,13},{6,14},{7,15},{8,0},{9,1},... | collective-permute-start | bytes 221192 | tf_op jit(solution)/shard_map/ppermute | solution.py:33
  32.0 7.4 %copy-start.3 = (bf16[4,4,96,768]{3,2,1,0:T(8,128)(2,1)}, bf16[4,4,96,768]{3,2,1,0:T(8,128)(2,1)S(1)}, u32[]{:S(2)}) copy-start(bf16[4,4,96,768]{3,2,1,0:T(8,128)(2,1)S(1)} %get-tuple-element.68.low) | copy-start | bytes 7077892
  32.0 9.2 %collective-permute-start.6 = (f32[144,128]{1,0:T(8,128)S(1)}, f32[144,128]{1,0:T(8,128)S(1)}, u32[]{:S(2)}, u32[]{:S(2)}) collective-permute-start(f32[144,128]{1,0:T(8,128)S(1)} %add.116), channel_id=1, source_target_pairs={{0,16},{1,17},{2,18},{3,19},{4,20},{5,21},{6,22},{7,23},{8,24},{9,... | collective-permute-start | bytes 221192 | tf_op jit(solution)/shard_map/ppermute | solution.py:33
  39.4 1.9 %copy-start = (f32[4,4,96,576]{3,2,1,0:T(8,128)}, f32[4,4,96,576]{3,2,1,0:T(8,128)S(1)}, u32[]{:S(2)}) copy-start(f32[4,4,96,576]{3,2,1,0:T(8,128)S(1)} %inner_terms_kernel.1.sums) | copy-start | bytes 10616836
  41.3 5.6 %collective-permute-start.7 = (f32[144,128]{1,0:T(8,128)S(1)}, f32[144,128]{1,0:T(8,128)S(1)}, u32[]{:S(2)}, u32[]{:S(2)}) collective-permute-start(f32[144,128]{1,0:T(8,128)S(1)} %add.118), channel_id=1, source_target_pairs={{0,48},{1,49},{2,50},{3,51},{4,52},{5,53},{6,54},{7,55},{8,56},{9,... | collective-permute-start | bytes 221192 | tf_op jit(solution)/shard_map/ppermute | solution.py:33
  46.8 3.3 %collective-permute-start.8 = (f32[144,128]{1,0:T(8,128)S(1)}, f32[144,128]{1,0:T(8,128)S(1)}, u32[]{:S(2)}, u32[]{:S(2)}) collective-permute-start(f32[144,128]{1,0:T(8,128)S(1)} %add.120), channel_id=1, source_target_pairs={{0,64},{1,65},{2,66},{3,67},{4,68},{5,69},{6,70},{7,71},{8,72},{9,... | collective-permute-start | bytes 221192 | tf_op jit(solution)/shard_map/ppermute | solution.py:33
  50.1 4.5 %collective-permute-start.9 = (f32[144,128]{1,0:T(8,128)S(1)}, f32[144,128]{1,0:T(8,128)S(1)}, u32[]{:S(2)}, u32[]{:S(2)}) collective-permute-start(f32[144,128]{1,0:T(8,128)S(1)} %add.122), channel_id=1, source_target_pairs={{0,192},{1,193},{2,194},{3,195},{4,196},{5,197},{6,198},{7,199},{8... | collective-permute-start | bytes 221192 | tf_op jit(solution)/shard_map/ppermute | solution.py:33
  54.7 5.4 %collective-permute-start.10 = (f32[144,128]{1,0:T(8,128)S(1)}, f32[144,128]{1,0:T(8,128)S(1)}, u32[]{:S(2)}, u32[]{:S(2)}) collective-permute-start(f32[144,128]{1,0:T(8,128)S(1)} %select_add_fusion.own), channel_id=1, source_target_pairs={{0,1},{1,0},{2,3},{3,2},{4,5},{5,4},{6,7},{7,6},{8,9},{9,8},{10,11... | collective-permute-start | bytes 221192 | tf_op jit(solution)/shard_map/ppermute | solution.py:33
  60.1 2.1 %copy-start.1 = (f32[4,4,96,576]{3,2,1,0:T(8,128)S(1)}, f32[4,4,96,576]{3,2,1,0:T(8,128)}, u32[]{:S(2)}) copy-start(f32[4,4,96,576]{3,2,1,0:T(8,128)} %copy-done) | copy-start | bytes 10616836
  62.2 1.7 %copy-start.4 = (bf16[4,4,96,768]{3,2,1,0:T(8,128)(2,1)S(1)}, bf16[4,4,96,768]{3,2,1,0:T(8,128)(2,1)}, u32[]{:S(2)}) copy-start(bf16[4,4,96,768]{3,2,1,0:T(8,128)(2,1)} %copy-done.3) | copy-start | bytes 7077892
  67.2 13.3 %collective-permute-start.15 = (f32[2,4,2,24,576]{4,3,2,1,0:T(8,128)S(1)}, f32[2,4,2,24,576]{4,3,2,1,0:T(8,128)S(1)}, u32[]{:S(2)}, u32[]{:S(2)}) collective-permute-start(f32[2,4,2,24,576]{4,3,2,1,0:T(8,128)S(1)} %get-tuple-element.72), channel_id=1, source_target_pairs={{0,2},{1,65},{2,0},{3,67},{4,6},{5,69},{6,4},{7,71},{8,10},{9,73},... | collective-permute-start | bytes 2654216 | tf_op jit(solution)/shard_map/ppermute | solution.py:33
  70.7 14.5 %collective-permute-start.11 = (f32[2,4,2,24,576]{4,3,2,1,0:T(8,128)S(1)}, f32[2,4,2,24,576]{4,3,2,1,0:T(8,128)S(1)}, u32[]{:S(2)}, u32[]{:S(2)}) collective-permute-start(f32[2,4,2,24,576]{4,3,2,1,0:T(8,128)S(1)} %get-tuple-element.70), channel_id=1, source_target_pairs={{0,6},{1,193},{2,4},{3,195},{4,2},{5,197},{6,0},{7,199},{8,14},{9,... | collective-permute-start | bytes 2654216 | tf_op jit(solution)/shard_map/ppermute | solution.py:33
  80.6 9.9 %collective-permute-start.16 = (f32[4,2,24,576]{3,2,1,0:T(8,128)S(1)}, f32[4,2,24,576]{3,2,1,0:T(8,128)S(1)}, u32[]{:S(2)}, u32[]{:S(2)}) collective-permute-start(f32[4,2,24,576]{3,2,1,0:T(8,128)S(1)} %fusion), channel_id=1, source_target_pairs={{0,6},{1,193},{2,4},{3,195},{4,2},{5,197},{6,0},{7,199},{8,14},{9,... | collective-permute-start | bytes 1327112 | tf_op jit(solution)/shard_map/ppermute | solution.py:33
  85.3 8.1 %collective-permute-start.12 = (f32[4,2,24,576]{3,2,1,0:T(8,128)S(1)}, f32[4,2,24,576]{3,2,1,0:T(8,128)S(1)}, u32[]{:S(2)}, u32[]{:S(2)}) collective-permute-start(f32[4,2,24,576]{3,2,1,0:T(8,128)S(1)} %fusion.3), channel_id=1, source_target_pairs={{0,2},{1,65},{2,0},{3,67},{4,6},{5,69},{6,4},{7,71},{8,10},{9,73},... | collective-permute-start | bytes 1327112 | tf_op jit(solution)/shard_map/ppermute | solution.py:33
  90.6 7.6 %collective-permute-start.17 = (f32[2,2,24,576]{3,2,1,0:T(8,128)S(1)}, f32[2,2,24,576]{3,2,1,0:T(8,128)S(1)}, u32[]{:S(2)}, u32[]{:S(2)}) collective-permute-start(f32[2,2,24,576]{3,2,1,0:T(8,128)S(1)} %slice.120), channel_id=1, source_target_pairs={{0,64},{1,3},{2,66},{3,1},{4,68},{5,7},{6,70},{7,5},{8,72},{9,11},... | collective-permute-start | bytes 663560 | tf_op jit(solution)/shard_map/ppermute | solution.py:33
  93.5 7.1 %collective-permute-start.13 = (f32[2,2,24,576]{3,2,1,0:T(8,128)S(1)}, f32[2,2,24,576]{3,2,1,0:T(8,128)S(1)}, u32[]{:S(2)}, u32[]{:S(2)}) collective-permute-start(f32[2,2,24,576]{3,2,1,0:T(8,128)S(1)} %slice.113), channel_id=1, source_target_pairs={{0,192},{1,7},{2,194},{3,5},{4,196},{5,3},{6,198},{7,1},{8,200},{9... | collective-permute-start | bytes 663560 | tf_op jit(solution)/shard_map/ppermute | solution.py:33
  98.3 5.3 %collective-permute-start.18 = (f32[2,24,576]{2,1,0:T(8,128)S(1)}, f32[2,24,576]{2,1,0:T(8,128)S(1)}, u32[]{:S(2)}, u32[]{:S(2)}) collective-permute-start(f32[2,24,576]{2,1,0:T(8,128)S(1)} %fusion.6), channel_id=1, source_target_pairs={{0,192},{1,7},{2,194},{3,5},{4,196},{5,3},{6,198},{7,1},{8,200},{9... | collective-permute-start | bytes 331784 | tf_op jit(solution)/shard_map/ppermute | solution.py:33
  100.7 5.0 %collective-permute-start.14 = (f32[2,24,576]{2,1,0:T(8,128)S(1)}, f32[2,24,576]{2,1,0:T(8,128)S(1)}, u32[]{:S(2)}, u32[]{:S(2)}) collective-permute-start(f32[2,24,576]{2,1,0:T(8,128)S(1)} %fusion.9), channel_id=1, source_target_pairs={{0,64},{1,3},{2,66},{3,1},{4,68},{5,7},{6,70},{7,5},{8,72},{9,11},... | collective-permute-start | bytes 331784 | tf_op jit(solution)/shard_map/ppermute | solution.py:33
  103.6 6.0 %collective-permute-start.19 = (f32[2,24,576]{2,1,0:T(8,128)S(1)}, f32[2,24,576]{2,1,0:T(8,128)S(1)}, u32[]{:S(2)}, u32[]{:S(2)}) collective-permute-start(f32[2,24,576]{2,1,0:T(8,128)S(1)} %fusion.8), channel_id=1, source_target_pairs={{0,16},{1,17},{2,18},{3,19},{4,20},{5,21},{6,22},{7,23},{8,24},{9,... | collective-permute-start | bytes 331784 | tf_op jit(solution)/shard_map/ppermute | solution.py:33
  109.7 3.8 %collective-permute-start.20 = (f32[24,576]{1,0:T(8,128)S(1)}, f32[24,576]{1,0:T(8,128)S(1)}, u32[]{:S(2)}, u32[]{:S(2)}) collective-permute-start(f32[24,576]{1,0:T(8,128)S(1)} %slice_bitcast_fusion), channel_id=1, source_target_pairs={{0,8},{1,9},{2,10},{3,11},{4,12},{5,13},{6,14},{7,15},{8,0},{9,1},... | collective-permute-start | bytes 165896 | tf_op jit(solution)/shard_map/ppermute | solution.py:33
  113.5 11.5 %collective-permute-start.21 = (f32[12,576]{1,0:T(8,128)S(1)}, f32[12,576]{1,0:T(8,128)S(1)}, u32[]{:S(2)}, u32[]{:S(2)}) collective-permute-start(f32[12,576]{1,0:T(8,128)S(1)} %get-tuple-element.73), channel_id=1, source_target_pairs={{0,1},{1,49},{2,3},{3,51},{4,5},{5,53},{6,7},{7,55},{8,9},{9,57},{... | collective-permute-start | bytes 82952 | tf_op jit(solution)/shard_map/ppermute | solution.py:33
  116.8 9.9 %collective-permute-start.22 = (f32[12,576]{1,0:T(8,128)S(1)}, f32[12,576]{1,0:T(8,128)S(1)}, u32[]{:S(2)}, u32[]{:S(2)}) collective-permute-start(f32[12,576]{1,0:T(8,128)S(1)} %get-tuple-element.74), channel_id=1, source_target_pairs={{1,48},{3,50},{5,52},{7,54},{9,56},{11,58},{13,60},{15,62},{17,32}... | collective-permute-start | bytes 82952 | tf_op jit(solution)/shard_map/ppermute | solution.py:33

commit v4 on v3

--- a/solution.py
+++ b/solution.py
@@ -96,7 +96,7 @@
     return array[0:96, 0:96], jnp.concatenate([array[0:96, 96:128], rest], axis=1)
 
 
-def states_kernel(place, *refs):
+def states_kernel(*refs):
     sources, (keep, send), held, arrived = refs[:4], refs[4:6], refs[6:10], refs[10]
     copies = [pltpu.make_async_copy(a, b, arrived.at[n]) for n, (a, b) in enumerate(zip(sources, held))]
     for copy in copies:
@@ -104,7 +104,7 @@
     for copy in copies:
         copy.wait()
     q, k, v, g = held
-    first = place[0] == 0
+    first = lax.axis_index(SEQ) & 1 == 0
     key_state = [lanes_dot(head(k[...], h), head(v[...], h)) for h in range(2)]
     query_state = [lanes_dot(head(q[...], h), head(g[...], h)) for h in range(2)]
     pack([jnp.where(first, a, b) for a, b in zip(key_state, query_state)], keep)
@@ -116,8 +116,16 @@
         out[n] = ref[...].astype(F32)
 
 
-def widen_inputs_kernel(place, x, out):
-    out[...] = x[...].astype(F32)
+def widen_inputs_kernel(place, x, out, held, arrived):
+    lanes = held.shape[2]
+    copies = []
+    for y in range(NY):
+        at = pl.multiple_of((2 * y + 1 - place[0]) * lanes, 128)
+        copies.append(pltpu.make_async_copy(x.at[:, pl.ds(at, lanes)], held.at[y], arrived.at[y]))
+        copies[y].start()
+    for y in range(NY):
+        copies[y].wait()
+        out[y] = held[y].astype(F32)
 
 
 def local_kernel(place, q, k, v, g, other, local, outer):
@@ -153,28 +161,40 @@
                 local[core, at : at + HEAD, :] = a.astype(BF16)
 
 
-def over_tokens(place, x, wide, d):
-    c = place[0]
+def terms_kernel(inner, place, x, wide, d, out, held):
+    c, pa, pb, pz = (place[i] for i in range(4))
+    first = c == 0
+    y = pl.program_id(0)
     contract = (((0,), (1,)), ((), ()))
-    one = lax.dot_general(x[...], d[c], contract, preferred_element_type=F32)
-    theirs = wide[...].astype(BF16)
-    return one + lax.dot_general(theirs, d[1 - c], contract, preferred_element_type=F32)
-
-
-def inner_terms_kernel(place, x, wide, local, sums):
-    sums[...] = over_tokens(place, x, wide, local).reshape(sums.shape)
-
-
-def outer_terms_kernel(place, x, wide, outer, high, low):
-    outside = over_tokens(place, x, wide, outer)
-    top = outside.astype(BF16)
-    high[...] = top.reshape(high.shape)
-    low[...] = (outside - top.astype(F32)).astype(BF16).reshape(low.shape)
-
-
-def join_kernel(factor, part, place, own, other, sums, high, low, keep, send):
-    c, pa, pb = (place[i] for i in range(3))
-    first = c == 0
+    total = lax.dot_general(x[...], d[c], contract, preferred_element_type=F32)
+    theirs = wide[0].astype(BF16)
+    total = total + lax.dot_general(theirs, d[1 - c], contract, preferred_element_type=F32)
+    held[...] = total.reshape(held.shape)
+
+    def slot(p, order):
+        at = jnp.int32(0)
+        for n in range(1, 4):
+            at = jnp.where(p == n, order[n], at)
+        return at
+
+    for part in range(2):
+        pair = [pz ^ (2 * part + k) for k in range(2)]
+        for x_to in range(NX):
+            sa = slot(jnp.where(first, x_to, y) ^ pa, ((0, 1, 3, 2), (0, 2, 3, 1))[part])
+            sb = jnp.where(first, y, x_to) ^ pb
+            sides = []
+            for side in range(2):
+                rows = slice(x_to * 24 + side * 12, x_to * 24 + side * 12 + 12)
+                sides.append(jnp.concatenate([held[z, rows, :] for z in pair], axis=0))
+            if inner:
+                out[part, sa, sb] = jnp.concatenate(sides, axis=1)
+            else:
+                out[part, sa, sb, 0] = sides[0]
+                out[part, sa, sb, 1] = sides[1]
+
+
+def join_kernel(factor, part, half, place, own, other, inner, outer, out):
+    first = place[0] == 0
 
     def by_head(state):
         one, two = unpack(state)
@@ -184,40 +204,22 @@
 
     before = by_head(jnp.where(first, own[...], other[...]))
     later = by_head(jnp.where(first, other[...], own[...]))
-
-    def slot(p):
-        order = (0, 1, 3, 2) if part == 0 else (0, 2, 3, 1)
-        out = jnp.int32(0)
-        for n in range(1, 4):
-            out = jnp.where(p == n, order[n], out)
-        return out
-
-    pieces = []
-    for n, (state, multiply) in enumerate(((before, lanes_dot), (later, lanes_dot), (later, dot))):
-        total = sums[:, 0, :, n * WIDTH : (n + 1) * WIDTH].reshape(4 * 96, WIDTH)
-        for ref in (high, low):
-            term = ref[:, 0, :, n * 256 : n * 256 + WIDTH].reshape(4 * 96, WIDTH)
-            total = total + multiply(term, state)
-        pieces.append(factor * total)
-    value = jnp.concatenate(pieces, axis=1)
-    for y in range(NY):
-        for x in range(NX):
-            sa = slot(jnp.where(first, x, y) ^ pa)
-            sb = slot(jnp.where(first, y, x) ^ pb)
-            at = y * 96 + x * 24
-            rows = value[at : at + 24, :]
-
-            @pl.when(sa < 2)
-            def _(sa=sa, sb=sb, rows=rows):
-                keep[sa, sb, 0] = rows
-
-            @pl.when(sa >= 2)
-            def _(sa=sa, sb=sb, rows=rows):
-                send[sa - 2, sb, 0] = rows
+    for sa in range(2):
+        pieces = []
+        for side in range(2):
+            for n, (state, multiply) in enumerate(((before, lanes_dot), (later, lanes_dot), (later, dot))):
+                term = outer[part, 2 * half + sa, :, side, :, n * 256 : n * 256 + WIDTH]
+                term = term.reshape(4 * 24, WIDTH)
+                high = term.astype(BF16)
+                low = (term - high.astype(F32)).astype(BF16)
+                pieces.append(multiply(high, state) + multiply(low, state))
+        total = jnp.concatenate(pieces, axis=1).reshape(4, 24, 6 * WIDTH)
+        out[sa] = factor * (inner[part, 2 * half + sa] + total)
 
 
 VMEM = pl.BlockSpec(memory_space=pltpu.VMEM)
 SMEM = pl.BlockSpec(memory_space=pltpu.SMEM)
+HBM = pl.BlockSpec(memory_space=pltpu.HBM)
 
 
 def cost(flops, moved):
@@ -228,17 +230,17 @@
     return pltpu.CompilerParams(vmem_limit_bytes=mib * 2**20)
 
 
-def states(place, q, k, v, g):
+def states(q, k, v, g):
     shape = jax.ShapeDtypeStruct(PACKED, F32)
     return pl.pallas_call(
         states_kernel,
         name="states",
         out_shape=(shape, shape),
-        in_specs=[SMEM] + [pl.BlockSpec(memory_space=pltpu.HBM)] * 4,
+        in_specs=[HBM] * 4,
         out_specs=(VMEM, VMEM),
         scratch_shapes=[pltpu.VMEM(q.shape, BF16)] * 4 + [pltpu.SemaphoreType.DMA((4,))],
         cost_estimate=cost(4 * 512 * 192 * 192, 10**6),
-    )(place, q, k, v, g)
+    )(q, k, v, g)
 
 
 def widen(q, k, v, g):
@@ -254,18 +256,16 @@
 
 def widen_inputs(place, x):
     length, features = x.shape
-    block = (length, features // 8)
+    shape = (NY, length, features // 8)
     return pl.pallas_call(
         widen_inputs_kernel,
         name="widen_inputs",
-        out_shape=jax.ShapeDtypeStruct((length, features // 2), F32),
-        grid_spec=pltpu.PrefetchScalarGridSpec(
-            num_scalar_prefetch=1,
-            grid=(4,),
-            in_specs=[pl.BlockSpec(block, lambda y, place: (0, 2 * y + 1 - place[0]))],
-            out_specs=pl.BlockSpec(block, lambda y, place: (0, y)),
-        ),
+        out_shape=jax.ShapeDtypeStruct(shape, F32),
+        in_specs=[SMEM, HBM],
+        out_specs=VMEM,
+        scratch_shapes=[pltpu.VMEM(shape, BF16), pltpu.SemaphoreType.DMA((NY,))],
         cost_estimate=cost(10**6, 5 * 10**6),
+        compiler_params=limit(16),
     )(place, x)
 
 
@@ -285,50 +285,41 @@
     )(place, q, k, v, g, other)
 
 
-def terms(kernel, place, x, wide, d, types):
+def terms(inner, place, x, wide, d):
     length, features = x.shape
     lanes = d.shape[1]
     block = (length, features // 8)
-    out = pl.BlockSpec((1, 4, 96, lanes), lambda y, place: (y, 0, 0, 0))
-    return pl.pallas_call(
-        kernel,
-        name=kernel.__name__,
-        out_shape=tuple(jax.ShapeDtypeStruct((4, 4, 96, lanes), t) for t in types),
+    shape = (2, 4, 4, 24, 2 * lanes) if inner else (2, 4, 4, 2, 24, lanes)
+    return pl.pallas_call(
+        functools.partial(terms_kernel, inner),
+        name="inner_terms" if inner else "outer_terms",
+        out_shape=jax.ShapeDtypeStruct(shape, F32),
         grid_spec=pltpu.PrefetchScalarGridSpec(
             num_scalar_prefetch=1,
             grid=(4,),
             in_specs=[
                 pl.BlockSpec(block, lambda y, place: (0, 2 * y + place[0])),
-                pl.BlockSpec(block, lambda y, place: (0, y)),
+                pl.BlockSpec((1,) + block, lambda y, place: (y, 0, 0)),
                 pl.BlockSpec(d.shape, lambda y, place: (0, 0, 0)),
             ],
-            out_specs=(out,) * len(types),
+            out_specs=pl.BlockSpec(shape, lambda y, place: (0,) * len(shape)),
+            scratch_shapes=[pltpu.VMEM((4, 96, lanes), F32)],
         ),
         cost_estimate=cost(2 * 512 * 3072 * 576, 8 * 10**6),
         compiler_params=limit(24),
     )(place, x, wide, d)
 
 
-def join(part, factor, place, own, other, sums, high, low):
-    shape = jax.ShapeDtypeStruct((2, 4, 2, 24, 3 * WIDTH), F32)
-    state = pl.BlockSpec(PACKED, lambda k, place: (0, 0))
-    block = lambda lanes: pl.BlockSpec(
-        (4, 1, 96, lanes), lambda k, place: (0, place[3] ^ (k + 2 * part), 0, 0)
-    )
-    out = pl.BlockSpec((2, 4, 1, 24, 3 * WIDTH), lambda k, place: (0, 0, k, 0, 0))
-    return pl.pallas_call(
-        functools.partial(join_kernel, factor, part),
-        name=f"join{part}",
-        out_shape=(shape, shape),
-        grid_spec=pltpu.PrefetchScalarGridSpec(
-            num_scalar_prefetch=1,
-            grid=(2,),
-            in_specs=[state, state, block(3 * WIDTH), block(3 * 256), block(3 * 256)],
-            out_specs=(out, out),
-        ),
-        cost_estimate=cost(12 * 768 * 192 * 192, 8 * 10**6),
-        compiler_params=limit(24),
-    )(place, own, other, sums, high, low)
+def join(part, half, factor, place, own, other, inner, outer):
+    return pl.pallas_call(
+        functools.partial(join_kernel, factor, part, half),
+        name=f"join{part}{half}",
+        out_shape=jax.ShapeDtypeStruct((2, 4, 24, 6 * WIDTH), F32),
+        in_specs=[SMEM] + [VMEM] * 4,
+        out_specs=VMEM,
+        cost_estimate=cost(12 * 384 * 192 * 192, 4 * 10**6),
+        compiler_params=limit(20),
+    )(place, own, other, inner, outer)
 
 
 def tie(*values):
@@ -349,7 +340,7 @@
     )
     for n, (move, bit) in enumerate(steps):
         came = permute(total, move)
-        if n < len(works):
+        if n < len(works) and works[n]:
             came, total = works[n](came, total)
         before = before + jnp.where(bit != c, came, 0.0)
         total = total + came
@@ -365,11 +356,17 @@
     y, z, x, c = me
     ends = []
     for (keep, send), (one, two) in zip(parts, ((3, 1), (1, 3))):
-        value = halve(keep, send, first_partner(one), first_partner(two))
-        ends.append(halve(value[:2], value[2:], second_partner(one), second_partner(two)))
-    value = ends[0] + permute(ends[1], z_partner(2))
-    value = value[0] + permute(value[1], z_partner(1))
-    block = lambda i: jnp.where(i == 0, value[:12], value[12:])
+        ends.append(halve(keep, send, first_partner(one), first_partner(two)))
+    chunk = lambda r: jnp.stack([end[r] for end in ends])
+    value = chunk(0)
+    for r in (2, 1, 3):
+        value = value + permute(chunk(r), second_partner(r))
+    chunk = lambda r: value[r >> 1, 12 * (r & 1) : 12 * (r & 1) + 12]
+    total = chunk(0)
+    for r in (3, 2, 1):
+        total = total + permute(chunk(r), z_partner(r))
+    left, right = jnp.split(total, 2, axis=1)
+    block = lambda i: jnp.where(i == 0, left, right)
     same = z >> 2 == c
     total = jnp.where(same, block(c), 0.0)
     total = total + permute(block(jnp.where(same, 1 - c, c)), last_near)
@@ -384,7 +381,7 @@
     block = (z & 3) ^ jnp.where(z >> 2 == c, 0, 2)
     place = jnp.stack([c, jnp.where(c == 0, x, y), jnp.where(c == 0, y, x), block]).astype(jnp.int32)
     features_first = [a.T for a in (query_proj, key_proj, value_proj, grad_out)]
-    keep, send = states(place, *features_first)
+    keep, send = states(*features_first)
     send, *late = tie(send, *features_first)
     came = swap_cores(send)
     plain = widen(*late)
@@ -405,20 +402,21 @@
 
     def outer_work(came, total):
         total, d = tie(total, made["local"][1])
-        kernel = outer_terms_kernel
-        came, *made["outer"] = tie(came, *terms(kernel, place, inputs, made["wide"], d, (BF16, BF16)))
+        came, made["outer"] = tie(came, terms(False, place, inputs, made["wide"], d))
         return came, total
 
     def inner_work(came, total):
         total, d = tie(total, made["local"][0])
-        came, made["inner"] = tie(came, *terms(inner_terms_kernel, place, inputs, made["wide"], d, (F32,)))
+        came, made["inner"] = tie(came, terms(True, place, inputs, made["wide"], d))
         return came, total
 
-    before = before_chip(me, keep + came, (inputs_work, local_work, outer_work, inner_work))
+    works = (inputs_work, None, local_work, outer_work, inner_work)
+    before = before_chip(me, keep + came, works)
     across = swap_cores(before)
-    parts = [
-        join(part, factor, place, before, across, made["inner"], *made["outer"]) for part in range(2)
-    ]
+    joined = lambda part, half: join(
+        part, half, factor, place, before, across, made["inner"], made["outer"]
+    )
+    parts = [(joined(part, 0), joined(part, 1)) for part in range(2)]
     summed = scatter_sum(me, parts)
     return (summed[:, :width], summed[:, width : 2 * width], summed[:, 2 * width :])
 

time: 128 us -> 117 us (0.914)
  starting transfers between devices: 46.6 us -> 39.9 us
  Pallas kernels: 29.1 us -> 24.8 us
  other arithmetic: 1.09 us -> 3.43 us
  waiting for transfers between devices: 43.2 us -> 41.4 us
    ppermute x23, starting transfers between devices: 46.6 us -> 39.9 us  [permute(): return lax.ppermute(value, SEQ, pairs)]
    pallas_call x1, Pallas kernels: 4.86 us -> 1.02 us  [widen_inputs(): pl.pallas_call(widen_inputs_kernel, name='widen_inputs', out_shape=jax.Sh...]
    ppermute x23, waiting for transfers between devices: 43.2 us -> 41.4 us  [permute(): return lax.ppermute(value, SEQ, pairs)]
    unnamed x24 -> x30, local copies, waits for them, and re-layouts: 5.68 us -> 5.04 us
    pallas_call x4 -> x6, Pallas kernels: 15.2 us -> 15.2 us  [the longest x2 9.3 us: terms(): pl.pallas_call(functools.partial(terms_kernel, inner), name='inner_terms'...]
  transfers between devices with their start and end apart: 23 -> 23, of which waited for: 14 -> 16; matrix products, arithmetic and copies ran while one was open for 0% -> 0% of each run, Pallas kernels for 18% -> 18%
where the time goes in v4:
time: 117 us; the launch traced here: 116 us
  waiting for transfers between devices  41.4 us (35%)
  starting transfers between devices  39.9 us (34%)
  Pallas kernels  24.8 us (21%)
  local copies, waits for them, and re-layouts  5.8 us (5%)
  other arithmetic  3.43 us (3%)
    ppermute x23, waiting for transfers between devices, permute(): return lax.ppermute(value, SEQ, pairs)  41.4 us
    ppermute x23, starting transfers between devices, permute(): return lax.ppermute(value, SEQ, pairs)  39.9 us
    pallas_call x2, Pallas kernels, terms(): pl.pallas_call(functools.partial(terms_kernel, inner), name='inner_terms'...  9.3 us
    pallas_call x4, Pallas kernels, join(): pl.pallas_call(functools.partial(join_kernel, factor, part, half), name=f...  5.93 us
    unnamed x30, local copies, waits for them, and re-layouts  5.04 us
    pallas_call x1, Pallas kernels, local_terms(): pl.pallas_call(local_kernel, name='local_terms', out_shape=(jax.ShapeDtyp...  3.67 us
    pallas_call x1, Pallas kernels, widen(): pl.pallas_call(widen_kernel, name='widen', out_shape=jax.ShapeDtypeStruct...  2.49 us
    pallas_call x1, Pallas kernels, states(): pl.pallas_call(states_kernel, name='states', out_shape=(shape, shape), in...  2.39 us
  transfers between devices with their start and end apart: 23, of which 16 were waited for; matrix products, arithmetic and copies ran while one was open for 0% of the time, Pallas kernels for 18%

profile of v4, /device:TPU:1, one launch (start us, length us, event | category | flops | bytes accessed | tf_op | source)
XLA Modules:
  0.0 116.3 jit_solution(17384040306079679142)
XLA Ops:
  0.6 2.4 %states.1 = (f32[144,128]{1,0:T(8,128)}, f32[144,128]{1,0:T(8,128)}) custom-call(bf16[192,512]{1,0:T(8,128)(2,1)} %bitcast.34, bf16[192,512]{1,0:T(8,128)(2,1)} %bitcast.37, bf16[192,512]{1,0:T(8,128)(2,1)} %bitcast.40, bf16[192,512]{1,0:T(8,128)(2,1)} %bitcast.43), custom_call_target="tpu_custom_call" | custom-call | flops 75497472 | bytes 1000000 | tf_op jit(solution)/shard_map/states/pallas_call | solution.py:235
  3.0 3.3 %collective-permute-start = (f32[144,128]{1,0:T(8,128)}, f32[144,128]{1,0:T(8,128)S(1)}, u32[]{:S(2)}, u32[]{:S(2)}) collective-permute-start(f32[144,128]{1,0:T(8,128)} %get-tuple-element.33), channel_id=1, source_target_pairs={{0,1},{1,0},{2,3},{3,2},{4,5},{5,4},{6,7},{7,6},{8,9},{9,8},{10,11... | collective-permute-start | bytes 221192 | tf_op jit(solution)/shard_map/ppermute | solution.py:33
  6.4 2.5 %widen.1 = f32[4,192,512]{2,1,0:T(8,128)} custom-call(bf16[192,512]{1,0:T(8,128)(2,1)} %bitcast.35, bf16[192,512]{1,0:T(8,128)(2,1)} %bitcast.38, bf16[192,512]{1,0:T(8,128)(2,1)} %bitcast.41, bf16[192,512]{1,0:T(8,128)(2,1)} %bitcast.44), custom_call_target="tpu_custom_call" | custom-call | flops 1000000 | bytes 2400000 | tf_op jit(solution)/shard_map/widen/pallas_call | solution.py:247
  8.9 0.9 add.93
  10.0 1.0 widen_inputs.1
  11.0 2.7 %collective-permute-done.1 = f32[144,128]{1,0:T(8,128)S(1)} collective-permute-done((f32[144,128]{1,0:T(8,128)S(1)}, f32[144,128]{1,0:T(8,128)S(1)}, u32[]{:S(2)}, u32[]{:S(2)}) %collective-permute-start.1) | collective-permute-done | bytes 73760 | tf_op jit(solution)/shard_map/ppermute | solution.py:33
  13.7 0.8 collective-permute-start.6
  14.6 0.8 collective-permute-start.2
  15.5 3.7 %collective-permute-done.2 = f32[144,128]{1,0:T(8,128)S(1)} collective-permute-done((f32[144,128]{1,0:T(8,128)S(1)}, f32[144,128]{1,0:T(8,128)S(1)}, u32[]{:S(2)}, u32[]{:S(2)}) %collective-permute-start.2) | collective-permute-done | bytes 73760 | tf_op jit(solution)/shard_map/ppermute | solution.py:33
  19.3 0.5 copy-done.10
  19.8 2.3 %collective-permute-done.4.other = f32[4,192,512]{2,1,0:T(8,128)S(1)} collective-permute-done((f32[4,192,512]{2,1,0:T(8,128)S(1)}, f32[4,192,512]{2,1,0:T(8,128)S(1)}, u32[]{:S(2)}, u32[]{:S(2)}) %collective-permute-start.4) | collective-permute-done | bytes 1572896 | tf_op jit(solution)/shard_map/ppermute | solution.py:33
  22.1 3.7 %local_terms.1 = (bf16[2,576,512]{2,1,0:T(8,128)(2,1)S(1)}, bf16[2,768,512]{2,1,0:T(8,128)(2,1)S(1)}) custom-call(s32[4]{0:T(128)S(1)} %pad_add_fusion.place, bf16[192,512]{1,0:T(8,128)(2,1)S(1)} %bitcast.36, bf16[192,512]{1,0:T(8,128)(2,1)S(1)} %bitcast.39, bf16[192,512]{1,0:T(8,128)(2,1)S(1)} %bitcast.42, bf16[192,512]{1,0:T(8,128)(2,1)S(1)} %bitcast.45, ...), custom_call_target="tpu_custom_call" | custom-call | flops 1006632960 | bytes 5000000 | tf_op jit(solution)/shard_map/local_terms/pallas_call | solution.py:274
  25.8 1.3 %collective-permute-start.5 = (f32[144,128]{1,0:T(8,128)S(1)}, f32[144,128]{1,0:T(8,128)S(1)}, u32[]{:S(2)}, u32[]{:S(2)}) collective-permute-start(f32[144,128]{1,0:T(8,128)S(1)} %add.98), channel_id=1, source_target_pairs={{0,16},{1,17},{2,18},{3,19},{4,20},{5,21},{6,22},{7,23},{8,24},{9,... | collective-permute-start | bytes 221192 | tf_op jit(solution)/shard_map/ppermute | solution.py:33
  27.2 4.4 %outer_terms.1.outer = f32[2,4,4,2,24,768]{5,4,3,2,1,0:T(8,128)S(1)} custom-call(s32[4]{0:T(128)S(1)} %pad_add_fusion.place, bf16[512,3072]{1,0:T(8,128)(2,1)S(1)} %copy-done.2, f32[4,512,384]{2,1,0:T(8,128)S(1)} %collective-permute-done.6.wide, bf16[2,768,512]{2,1,0:T(8,128)(2,1)S(1)} %get-tuple-element.50.d), custom_call_target="tpu_custom_call" | custom-call | flops 1811939328 | bytes 8000000 | tf_op jit(solution)/shard_map/outer_terms/pallas_call | solution.py:293
  31.6 2.1 %copy-done = f32[2,4,4,2,24,768]{5,4,3,2,1,0:T(8,128)} copy-done((f32[2,4,4,2,24,768]{5,4,3,2,1,0:T(8,128)}, f32[2,4,4,2,24,768]{5,4,3,2,1,0:T(8,128)S(1)}, u32[]{:S(2)}) %copy-start) | copy-done | bytes 4718616
  33.8 4.3 %collective-permute-start.7 = (f32[144,128]{1,0:T(8,128)S(1)}, f32[144,128]{1,0:T(8,128)S(1)}, u32[]{:S(2)}, u32[]{:S(2)}) collective-permute-start(f32[144,128]{1,0:T(8,128)S(1)} %add.100), channel_id=1, source_target_pairs={{0,48},{1,49},{2,50},{3,51},{4,52},{5,53},{6,54},{7,55},{8,56},{9,... | collective-permute-start | bytes 221192 | tf_op jit(solution)/shard_map/ppermute | solution.py:33
  38.1 4.8 %inner_terms.1.inner = f32[2,4,4,24,1152]{4,3,2,1,0:T(8,128)S(1)} custom-call(s32[4]{0:T(128)S(1)} %pad_add_fusion.place, bf16[512,3072]{1,0:T(8,128)(2,1)S(1)} %copy-done.3, f32[4,512,384]{2,1,0:T(8,128)S(1)} %collective-permute-done.6.wide, bf16[2,576,512]{2,1,0:T(8,128)(2,1)S(1)} %get-tuple-element.54.d), custom_call_target="tpu_custom_call" | custom-call | flops 1811939328 | bytes 8000000 | tf_op jit(solution)/shard_map/inner_terms/pallas_call | solution.py:293
  43.0 1.4 %collective-permute-start.8 = (f32[144,128]{1,0:T(8,128)S(1)}, f32[144,128]{1,0:T(8,128)S(1)}, u32[]{:S(2)}, u32[]{:S(2)}) collective-permute-start(f32[144,128]{1,0:T(8,128)S(1)} %add.102), channel_id=1, source_target_pairs={{0,64},{1,65},{2,66},{3,67},{4,68},{5,69},{6,70},{7,71},{8,72},{9,... | collective-permute-start | bytes 221192 | tf_op jit(solution)/shard_map/ppermute | solution.py:33
  44.4 1.9 %collective-permute-done.8 = f32[144,128]{1,0:T(8,128)S(1)} collective-permute-done((f32[144,128]{1,0:T(8,128)S(1)}, f32[144,128]{1,0:T(8,128)S(1)}, u32[]{:S(2)}, u32[]{:S(2)}) %collective-permute-start.8) | collective-permute-done | bytes 73760 | tf_op jit(solution)/shard_map/ppermute | solution.py:33
  46.3 0.6 add.104
  46.9 2.7 %collective-permute-start.9 = (f32[144,128]{1,0:T(8,128)}, f32[144,128]{1,0:T(8,128)}, u32[]{:S(2)}, u32[]{:S(2)}) collective-permute-start(f32[144,128]{1,0:T(8,128)} %add.104), channel_id=1, source_target_pairs={{0,192},{1,193},{2,194},{3,195},{4,196},{5,197},{6,198},{7,199},{8... | collective-permute-start | bytes 221192 | tf_op jit(solution)/shard_map/ppermute | solution.py:33
  49.7 2.1 %collective-permute-done.9 = f32[144,128]{1,0:T(8,128)} collective-permute-done((f32[144,128]{1,0:T(8,128)}, f32[144,128]{1,0:T(8,128)}, u32[]{:S(2)}, u32[]{:S(2)}) %collective-permute-start.9) | collective-permute-done | bytes 73760 | tf_op jit(solution)/shard_map/ppermute | solution.py:33
  51.7 1.1 select_add_fusion.own
  52.9 2.4 %collective-permute-start.10 = (f32[144,128]{1,0:T(8,128)S(1)}, f32[144,128]{1,0:T(8,128)S(1)}, u32[]{:S(2)}, u32[]{:S(2)}) collective-permute-start(f32[144,128]{1,0:T(8,128)S(1)} %select_add_fusion.own), channel_id=1, source_target_pairs={{0,1},{1,0},{2,3},{3,2},{4,5},{5,4},{6,7},{7,6},{8,9},{9,8},{10,11... | collective-permute-start | bytes 221192 | tf_op jit(solution)/shard_map/ppermute | solution.py:33
  55.2 0.9 collective-permute-done.10.other
  56.1 2.3 %copy-done.1 = f32[2,4,4,2,24,768]{5,4,3,2,1,0:T(8,128)S(1)} copy-done((f32[2,4,4,2,24,768]{5,4,3,2,1,0:T(8,128)S(1)}, f32[2,4,4,2,24,768]{5,4,3,2,1,0:T(8,128)}, u32[]{:S(2)}) %copy-start.1) | copy-done | bytes 4718616
  58.5 1.5 %join01.1 = f32[2,4,24,1152]{3,2,1,0:T(8,128)S(1)} custom-call(s32[4]{0:T(128)S(1)} %pad_add_fusion.place, f32[144,128]{1,0:T(8,128)S(1)} %select_add_fusion.own, f32[144,128]{1,0:T(8,128)S(1)} %collective-permute-done.10.other, f32[2,4,4,24,1152]{4,3,2,1,0:T(8,128)S(1)} %inner_terms.1.inner, f32[2,4,4,2,24,768]{5,4,3,2,1,0:T(8,128)S(1)} %copy-done.1), custom_call_target="tpu_custom_call" | custom-call | flops 169869312 | bytes 4000000 | tf_op jit(solution)/shard_map/join01/pallas_call | solution.py:314
  60.0 3.7 %collective-permute-start.11 = (f32[2,4,24,1152]{3,2,1,0:T(8,128)S(1)}, f32[2,4,24,1152]{3,2,1,0:T(8,128)S(1)}, u32[]{:S(2)}, u32[]{:S(2)}) collective-permute-start(f32[2,4,24,1152]{3,2,1,0:T(8,128)S(1)} %join01.1), channel_id=1, source_target_pairs={{0,6},{1,193},{2,4},{3,195},{4,2},{5,197},{6,0},{7,199},{8,14},{9,... | collective-permute-start | bytes 2654216 | tf_op jit(solution)/shard_map/ppermute | solution.py:33
  63.7 1.5 %join11.1 = f32[2,4,24,1152]{3,2,1,0:T(8,128)S(1)} custom-call(s32[4]{0:T(128)S(1)} %pad_add_fusion.place, f32[144,128]{1,0:T(8,128)S(1)} %select_add_fusion.own, f32[144,128]{1,0:T(8,128)S(1)} %collective-permute-done.10.other, f32[2,4,4,24,1152]{4,3,2,1,0:T(8,128)S(1)} %inner_terms.1.inner, f32[2,4,4,2,24,768]{5,4,3,2,1,0:T(8,128)S(1)} %copy-done.1), custom_call_target="tpu_custom_call" | custom-call | flops 169869312 | bytes 4000000 | tf_op jit(solution)/shard_map/join11/pallas_call | solution.py:314
  65.3 1.5 %join00.1 = f32[2,4,24,1152]{3,2,1,0:T(8,128)S(1)} custom-call(s32[4]{0:T(128)S(1)} %pad_add_fusion.place, f32[144,128]{1,0:T(8,128)S(1)} %select_add_fusion.own, f32[144,128]{1,0:T(8,128)S(1)} %collective-permute-done.10.other, f32[2,4,4,24,1152]{4,3,2,1,0:T(8,128)S(1)} %inner_terms.1.inner, f32[2,4,4,2,24,768]{5,4,3,2,1,0:T(8,128)S(1)} %copy-done.1), custom_call_target="tpu_custom_call" | custom-call | flops 169869312 | bytes 4000000 | tf_op jit(solution)/shard_map/join00/pallas_call | solution.py:314
  66.8 1.5 %join10.1 = f32[2,4,24,1152]{3,2,1,0:T(8,128)S(1)} custom-call(s32[4]{0:T(128)S(1)} %pad_add_fusion.place, f32[144,128]{1,0:T(8,128)S(1)} %select_add_fusion.own, f32[144,128]{1,0:T(8,128)S(1)} %collective-permute-done.10.other, f32[2,4,4,24,1152]{4,3,2,1,0:T(8,128)S(1)} %inner_terms.1.inner, f32[2,4,4,2,24,768]{5,4,3,2,1,0:T(8,128)S(1)} %copy-done.1), custom_call_target="tpu_custom_call" | custom-call | flops 169869312 | bytes 4000000 | tf_op jit(solution)/shard_map/join10/pallas_call | solution.py:314
  68.3 6.2 %collective-permute-done.11 = f32[2,4,24,1152]{3,2,1,0:T(8,128)S(1)} collective-permute-done((f32[2,4,24,1152]{3,2,1,0:T(8,128)S(1)}, f32[2,4,24,1152]{3,2,1,0:T(8,128)S(1)}, u32[]{:S(2)}, u32[]{:S(2)}) %collective-permute-start.11) | collective-permute-done | bytes 884768 | tf_op jit(solution)/shard_map/ppermute | solution.py:33
  74.6 2.9 %collective-permute-done.13 = f32[2,4,24,1152]{3,2,1,0:T(8,128)S(1)} collective-permute-done((f32[2,4,24,1152]{3,2,1,0:T(8,128)S(1)}, f32[2,4,24,1152]{3,2,1,0:T(8,128)S(1)}, u32[]{:S(2)}, u32[]{:S(2)}) %collective-permute-start.13) | collective-permute-done | bytes 884768 | tf_op jit(solution)/shard_map/ppermute | solution.py:33
  77.6 4.6 %collective-permute-done.12 = f32[4,24,1152]{2,1,0:T(8,128)S(1)} collective-permute-done((f32[4,24,1152]{2,1,0:T(8,128)S(1)}, f32[4,24,1152]{2,1,0:T(8,128)S(1)}, u32[]{:S(2)}, u32[]{:S(2)}) %collective-permute-start.12) | collective-permute-done | bytes 442400 | tf_op jit(solution)/shard_map/ppermute | solution.py:33
  82.3 3.9 %collective-permute-done.14 = f32[4,24,1152]{2,1,0:T(8,128)S(1)} collective-permute-done((f32[4,24,1152]{2,1,0:T(8,128)S(1)}, f32[4,24,1152]{2,1,0:T(8,128)S(1)}, u32[]{:S(2)}, u32[]{:S(2)}) %collective-permute-start.14) | collective-permute-done | bytes 442400 | tf_op jit(solution)/shard_map/ppermute | solution.py:33
  86.4 2.3 %collective-permute-start.15 = (f32[2,24,1152]{2,1,0:T(8,128)S(1)}, f32[2,24,1152]{2,1,0:T(8,128)S(1)}, u32[]{:S(2)}, u32[]{:S(2)}) collective-permute-start(f32[2,24,1152]{2,1,0:T(8,128)S(1)} %pad_maximum_fusion), channel_id=1, source_target_pairs={{0,128},{1,5},{2,130},{3,7},{4,132},{5,1},{6,134},{7,3},{8,136},{9... | collective-permute-start | bytes 663560 | tf_op jit(solution)/shard_map/ppermute | solution.py:33
  89.2 0.8 collective-permute-start.17
  90.0 2.8 %collective-permute-done.15 = f32[2,24,1152]{2,1,0:T(8,128)S(1)} collective-permute-done((f32[2,24,1152]{2,1,0:T(8,128)S(1)}, f32[2,24,1152]{2,1,0:T(8,128)S(1)}, u32[]{:S(2)}, u32[]{:S(2)}) %collective-permute-start.15) | collective-permute-done | bytes 221216 | tf_op jit(solution)/shard_map/ppermute | solution.py:33
  92.8 2.2 %collective-permute-done.16 = f32[2,24,1152]{2,1,0:T(8,128)S(1)} collective-permute-done((f32[2,24,1152]{2,1,0:T(8,128)S(1)}, f32[2,24,1152]{2,1,0:T(8,128)S(1)}, u32[]{:S(2)}, u32[]{:S(2)}) %collective-permute-start.16) | collective-permute-done | bytes 221216 | tf_op jit(solution)/shard_map/ppermute | solution.py:33
  95.0 0.5 collective-permute-done.17
  95.6 1.8 %collective-permute-start.18 = (f32[12,1152]{1,0:T(8,128)S(1)}, f32[12,1152]{1,0:T(8,128)S(1)}, u32[]{:S(2)}, u32[]{:S(2)}) collective-permute-start(f32[12,1152]{1,0:T(8,128)S(1)} %get-tuple-element.67), channel_id=1, source_target_pairs={{0,24},{1,25},{2,26},{3,27},{4,28},{5,29},{6,30},{7,31},{8,16},{9,... | collective-permute-start | bytes 165896 | tf_op jit(solution)/shard_map/ppermute | solution.py:33
  97.7 1.6 %collective-permute-start.20 = (f32[12,1152]{1,0:T(8,128)S(1)}, f32[12,1152]{1,0:T(8,128)S(1)}, u32[]{:S(2)}, u32[]{:S(2)}) collective-permute-start(f32[12,1152]{1,0:T(8,128)S(1)} %get-tuple-element.68), channel_id=1, source_target_pairs={{0,8},{1,9},{2,10},{3,11},{4,12},{5,13},{6,14},{7,15},{8,0},{9,1},... | collective-permute-start | bytes 165896 | tf_op jit(solution)/shard_map/ppermute | solution.py:33
  99.3 1.5 %collective-permute-done.18 = f32[12,1152]{1,0:T(8,128)S(1)} collective-permute-done((f32[12,1152]{1,0:T(8,128)S(1)}, f32[12,1152]{1,0:T(8,128)S(1)}, u32[]{:S(2)}, u32[]{:S(2)}) %collective-permute-start.18) | collective-permute-done | bytes 55328 | tf_op jit(solution)/shard_map/ppermute | solution.py:33
  100.8 1.5 %collective-permute-done.19 = f32[12,1152]{1,0:T(8,128)S(1)} collective-permute-done((f32[12,1152]{1,0:T(8,128)S(1)}, f32[12,1152]{1,0:T(8,128)S(1)}, u32[]{:S(2)}, u32[]{:S(2)}) %collective-permute-start.19) | collective-permute-done | bytes 55328 | tf_op jit(solution)/shard_map/ppermute | solution.py:33
  102.4 1.3 %collective-permute-start.21 = (f32[12,576]{1,0:T(8,128)S(1)}, f32[12,576]{1,0:T(8,128)S(1)}, u32[]{:S(2)}, u32[]{:S(2)}) collective-permute-start(f32[12,576]{1,0:T(8,128)S(1)} %get-tuple-element.70), channel_id=1, source_target_pairs={{0,1},{1,49},{2,3},{3,51},{4,5},{5,53},{6,7},{7,55},{8,9},{9,57},{... | collective-permute-start | bytes 82952 | tf_op jit(solution)/shard_map/ppermute | solution.py:33
  103.7 10.1 %collective-permute-start.22 = (f32[12,576]{1,0:T(8,128)S(1)}, f32[12,576]{1,0:T(8,128)S(1)}, u32[]{:S(2)}, u32[]{:S(2)}) collective-permute-start(f32[12,576]{1,0:T(8,128)S(1)} %get-tuple-element.71), channel_id=1, source_target_pairs={{1,48},{3,50},{5,52},{7,54},{9,56},{11,58},{13,60},{15,62},{17,32}... | collective-permute-start | bytes 82952 | tf_op jit(solution)/shard_map/ppermute | solution.py:33
  113.8 1.7 %collective-permute-done.22 = f32[12,576]{1,0:T(8,128)S(1)} collective-permute-done((f32[12,576]{1,0:T(8,128)S(1)}, f32[12,576]{1,0:T(8,128)S(1)}, u32[]{:S(2)}, u32[]{:S(2)}) %collective-permute-start.22) | collective-permute-done | bytes 27680 | tf_op jit(solution)/shard_map/ppermute | solution.py:33
  115.6 0.7 fusion.13
  (62 shorter events, 2.1 us)
Async XLA Ops:
  0.6 9.3 %copy-start.2 = (bf16[512,3072]{1,0:T(8,128)(2,1)S(1)}, bf16[512,3072]{1,0:T(8,128)(2,1)}, u32[]{:S(2)}) copy-start(bf16[512,3072]{1,0:T(8,128)(2,1)} %x.4) | copy-start | bytes 9437188
  3.0 5.8 %collective-permute-start = (f32[144,128]{1,0:T(8,128)}, f32[144,128]{1,0:T(8,128)S(1)}, u32[]{:S(2)}, u32[]{:S(2)}) collective-permute-start(f32[144,128]{1,0:T(8,128)} %get-tuple-element.33), channel_id=1, source_target_pairs={{0,1},{1,0},{2,3},{3,2},{4,5},{5,4},{6,7},{7,6},{8,9},{9,8},{10,11... | collective-permute-start | bytes 221192 | tf_op jit(solution)/shard_map/ppermute | solution.py:33
  9.8 3.9 %collective-permute-start.1 = (f32[144,128]{1,0:T(8,128)S(1)}, f32[144,128]{1,0:T(8,128)S(1)}, u32[]{:S(2)}, u32[]{:S(2)}) collective-permute-start(f32[144,128]{1,0:T(8,128)S(1)} %add.93), channel_id=1, source_target_pairs={{0,2},{1,3},{2,0},{3,1},{4,6},{5,7},{6,4},{7,5},{8,10},{9,11},{10,... | collective-permute-start | bytes 221192 | tf_op jit(solution)/shard_map/ppermute | solution.py:33
  9.9 4.6 %copy-start.8 = (f32[4,192,512]{2,1,0:T(8,128)S(1)}, f32[4,192,512]{2,1,0:T(8,128)}, u32[]{:S(2)}) copy-start(f32[4,192,512]{2,1,0:T(8,128)} %widen.1) | copy-start | bytes 4718596
  10.0 12.1 %copy-start.4 = (bf16[512,192]{0,1:T(8,128)(2,1)S(1)}, bf16[512,192]{0,1:T(8,128)(2,1)}, u32[]{:S(2)}) copy-start(bf16[512,192]{0,1:T(8,128)(2,1)} %param.6) | copy-start | bytes 589828
  10.0 12.1 %copy-start.5 = (bf16[512,192]{0,1:T(8,128)(2,1)S(1)}, bf16[512,192]{0,1:T(8,128)(2,1)}, u32[]{:S(2)}) copy-start(bf16[512,192]{0,1:T(8,128)(2,1)} %param.7) | copy-start | bytes 589828
  10.0 12.1 %copy-start.6 = (bf16[512,192]{0,1:T(8,128)(2,1)S(1)}, bf16[512,192]{0,1:T(8,128)(2,1)}, u32[]{:S(2)}) copy-start(bf16[512,192]{0,1:T(8,128)(2,1)} %param.8) | copy-start | bytes 589828
  10.0 12.1 %copy-start.7 = (bf16[512,192]{0,1:T(8,128)(2,1)S(1)}, bf16[512,192]{0,1:T(8,128)(2,1)}, u32[]{:S(2)}) copy-start(bf16[512,192]{0,1:T(8,128)(2,1)} %param.9) | copy-start | bytes 589828
  13.7 5.6 %copy-start.9 = (f32[144,128]{1,0:T(8,128)}, f32[144,128]{1,0:T(8,128)S(1)}, u32[]{:S(2)}) copy-start(f32[144,128]{1,0:T(8,128)S(1)} %collective-permute-done.1) | copy-start | bytes 221188
  13.7 13.5 %collective-permute-start.6 = (f32[4,512,384]{2,1,0:T(8,128)S(1)}, f32[4,512,384]{2,1,0:T(8,128)S(1)}, u32[]{:S(2)}, u32[]{:S(2)}) collective-permute-start(f32[4,512,384]{2,1,0:T(8,128)S(1)} %widen_inputs.1), channel_id=1, source_target_pairs={{0,1},{1,0},{2,3},{3,2},{4,5},{5,4},{6,7},{7,6},{8,9},{9,8},{10,11... | collective-permute-start | bytes 9437192 | tf_op jit(solution)/shard_map/ppermute | solution.py:33
  14.5 7.5 %collective-permute-start.4 = (f32[4,192,512]{2,1,0:T(8,128)S(1)}, f32[4,192,512]{2,1,0:T(8,128)S(1)}, u32[]{:S(2)}, u32[]{:S(2)}) collective-permute-start(f32[4,192,512]{2,1,0:T(8,128)S(1)} %copy-done.8), channel_id=1, source_target_pairs={{0,1},{1,0},{2,3},{3,2},{4,5},{5,4},{6,7},{7,6},{8,9},{9,8},{10,11... | collective-permute-start | bytes 4718600 | tf_op jit(solution)/shard_map/ppermute | solution.py:33
  14.6 4.5 %collective-permute-start.2 = (f32[144,128]{1,0:T(8,128)S(1)}, f32[144,128]{1,0:T(8,128)S(1)}, u32[]{:S(2)}, u32[]{:S(2)}) collective-permute-start(f32[144,128]{1,0:T(8,128)S(1)} %add.94), channel_id=1, source_target_pairs={{0,6},{1,7},{2,4},{3,5},{4,2},{5,3},{6,0},{7,1},{8,14},{9,15},{10,... | collective-permute-start | bytes 221192 | tf_op jit(solution)/shard_map/ppermute | solution.py:33
  19.1 0.6 copy-start.10
  19.2 6.6 %collective-permute-start.3 = (f32[144,128]{1,0:T(8,128)S(1)}, f32[144,128]{1,0:T(8,128)S(1)}, u32[]{:S(2)}, u32[]{:S(2)}) collective-permute-start(f32[144,128]{1,0:T(8,128)S(1)} %add.96), channel_id=1, source_target_pairs={{0,8},{1,9},{2,10},{3,11},{4,12},{5,13},{6,14},{7,15},{8,0},{9,1},... | collective-permute-start | bytes 221192 | tf_op jit(solution)/shard_map/ppermute | solution.py:33
  25.8 5.8 %copy-start.11 = (f32[144,128]{1,0:T(8,128)}, f32[144,128]{1,0:T(8,128)S(1)}, u32[]{:S(2)}) copy-start(f32[144,128]{1,0:T(8,128)S(1)} %collective-permute-done.3) | copy-start | bytes 221188
  25.8 12.3 %copy-start.3 = (bf16[512,3072]{1,0:T(8,128)(2,1)S(1)}, bf16[512,3072]{1,0:T(8,128)(2,1)}, u32[]{:S(2)}) copy-start(bf16[512,3072]{1,0:T(8,128)(2,1)} %x.4) | copy-start | bytes 9437188
  25.8 8.0 %collective-permute-start.5 = (f32[144,128]{1,0:T(8,128)S(1)}, f32[144,128]{1,0:T(8,128)S(1)}, u32[]{:S(2)}, u32[]{:S(2)}) collective-permute-start(f32[144,128]{1,0:T(8,128)S(1)} %add.98), channel_id=1, source_target_pairs={{0,16},{1,17},{2,18},{3,19},{4,20},{5,21},{6,22},{7,23},{8,24},{9,... | collective-permute-start | bytes 221192 | tf_op jit(solution)/shard_map/ppermute | solution.py:33
  31.6 2.1 %copy-start = (f32[2,4,4,2,24,768]{5,4,3,2,1,0:T(8,128)}, f32[2,4,4,2,24,768]{5,4,3,2,1,0:T(8,128)S(1)}, u32[]{:S(2)}) copy-start(f32[2,4,4,2,24,768]{5,4,3,2,1,0:T(8,128)S(1)} %outer_terms.1.outer) | copy-start | bytes 14155780
  33.8 9.2 %copy-start.12 = (f32[144,128]{1,0:T(8,128)}, f32[144,128]{1,0:T(8,128)S(1)}, u32[]{:S(2)}) copy-start(f32[144,128]{1,0:T(8,128)S(1)} %collective-permute-done.5) | copy-start | bytes 221188
  33.8 9.2 %collective-permute-start.7 = (f32[144,128]{1,0:T(8,128)S(1)}, f32[144,128]{1,0:T(8,128)S(1)}, u32[]{:S(2)}, u32[]{:S(2)}) collective-permute-start(f32[144,128]{1,0:T(8,128)S(1)} %add.100), channel_id=1, source_target_pairs={{0,48},{1,49},{2,50},{3,51},{4,52},{5,53},{6,54},{7,55},{8,56},{9,... | collective-permute-start | bytes 221192 | tf_op jit(solution)/shard_map/ppermute | solution.py:33
  43.0 4.0 %copy-start.13 = (f32[144,128]{1,0:T(8,128)}, f32[144,128]{1,0:T(8,128)S(1)}, u32[]{:S(2)}) copy-start(f32[144,128]{1,0:T(8,128)S(1)} %collective-permute-done.7) | copy-start | bytes 221188
  43.0 3.3 %collective-permute-start.8 = (f32[144,128]{1,0:T(8,128)S(1)}, f32[144,128]{1,0:T(8,128)S(1)}, u32[]{:S(2)}, u32[]{:S(2)}) collective-permute-start(f32[144,128]{1,0:T(8,128)S(1)} %add.102), channel_id=1, source_target_pairs={{0,64},{1,65},{2,66},{3,67},{4,68},{5,69},{6,70},{7,71},{8,72},{9,... | collective-permute-start | bytes 221192 | tf_op jit(solution)/shard_map/ppermute | solution.py:33
  46.3 0.7 copy-start.14
  46.9 4.8 %collective-permute-start.9 = (f32[144,128]{1,0:T(8,128)}, f32[144,128]{1,0:T(8,128)}, u32[]{:S(2)}, u32[]{:S(2)}) collective-permute-start(f32[144,128]{1,0:T(8,128)} %add.104), channel_id=1, source_target_pairs={{0,192},{1,193},{2,194},{3,195},{4,196},{5,197},{6,198},{7,199},{8... | collective-permute-start | bytes 221192 | tf_op jit(solution)/shard_map/ppermute | solution.py:33
  52.9 3.3 %collective-permute-start.10 = (f32[144,128]{1,0:T(8,128)S(1)}, f32[144,128]{1,0:T(8,128)S(1)}, u32[]{:S(2)}, u32[]{:S(2)}) collective-permute-start(f32[144,128]{1,0:T(8,128)S(1)} %select_add_fusion.own), channel_id=1, source_target_pairs={{0,1},{1,0},{2,3},{3,2},{4,5},{5,4},{6,7},{7,6},{8,9},{9,8},{10,11... | collective-permute-start | bytes 221192 | tf_op jit(solution)/shard_map/ppermute | solution.py:33
  56.1 2.3 %copy-start.1 = (f32[2,4,4,2,24,768]{5,4,3,2,1,0:T(8,128)S(1)}, f32[2,4,4,2,24,768]{5,4,3,2,1,0:T(8,128)}, u32[]{:S(2)}) copy-start(f32[2,4,4,2,24,768]{5,4,3,2,1,0:T(8,128)} %copy-done) | copy-start | bytes 14155780
  60.0 14.5 %collective-permute-start.11 = (f32[2,4,24,1152]{3,2,1,0:T(8,128)S(1)}, f32[2,4,24,1152]{3,2,1,0:T(8,128)S(1)}, u32[]{:S(2)}, u32[]{:S(2)}) collective-permute-start(f32[2,4,24,1152]{3,2,1,0:T(8,128)S(1)} %join01.1), channel_id=1, source_target_pairs={{0,6},{1,193},{2,4},{3,195},{4,2},{5,197},{6,0},{7,199},{8,14},{9,... | collective-permute-start | bytes 2654216 | tf_op jit(solution)/shard_map/ppermute | solution.py:33
  65.2 12.3 %collective-permute-start.13 = (f32[2,4,24,1152]{3,2,1,0:T(8,128)S(1)}, f32[2,4,24,1152]{3,2,1,0:T(8,128)S(1)}, u32[]{:S(2)}, u32[]{:S(2)}) collective-permute-start(f32[2,4,24,1152]{3,2,1,0:T(8,128)S(1)} %join11.1), channel_id=1, source_target_pairs={{0,2},{1,65},{2,0},{3,67},{4,6},{5,69},{6,4},{7,71},{8,10},{9,73},... | collective-permute-start | bytes 2654216 | tf_op jit(solution)/shard_map/ppermute | solution.py:33
  74.5 7.7 %collective-permute-start.12 = (f32[4,24,1152]{2,1,0:T(8,128)S(1)}, f32[4,24,1152]{2,1,0:T(8,128)S(1)}, u32[]{:S(2)}, u32[]{:S(2)}) collective-permute-start(f32[4,24,1152]{2,1,0:T(8,128)S(1)} %fusion.3), channel_id=1, source_target_pairs={{0,2},{1,65},{2,0},{3,67},{4,6},{5,69},{6,4},{7,71},{8,10},{9,73},... | collective-permute-start | bytes 1327112 | tf_op jit(solution)/shard_map/ppermute | solution.py:33
  77.5 8.7 %collective-permute-start.14 = (f32[4,24,1152]{2,1,0:T(8,128)S(1)}, f32[4,24,1152]{2,1,0:T(8,128)S(1)}, u32[]{:S(2)}, u32[]{:S(2)}) collective-permute-start(f32[4,24,1152]{2,1,0:T(8,128)S(1)} %fusion), channel_id=1, source_target_pairs={{0,6},{1,193},{2,4},{3,195},{4,2},{5,197},{6,0},{7,199},{8,14},{9,... | collective-permute-start | bytes 1327112 | tf_op jit(solution)/shard_map/ppermute | solution.py:33
  86.4 6.4 %collective-permute-start.15 = (f32[2,24,1152]{2,1,0:T(8,128)S(1)}, f32[2,24,1152]{2,1,0:T(8,128)S(1)}, u32[]{:S(2)}, u32[]{:S(2)}) collective-permute-start(f32[2,24,1152]{2,1,0:T(8,128)S(1)} %pad_maximum_fusion), channel_id=1, source_target_pairs={{0,128},{1,5},{2,130},{3,7},{4,132},{5,1},{6,134},{7,3},{8,136},{9... | collective-permute-start | bytes 663560 | tf_op jit(solution)/shard_map/ppermute | solution.py:33
  88.7 6.3 %collective-permute-start.16 = (f32[2,24,1152]{2,1,0:T(8,128)S(1)}, f32[2,24,1152]{2,1,0:T(8,128)S(1)}, u32[]{:S(2)}, u32[]{:S(2)}) collective-permute-start(f32[2,24,1152]{2,1,0:T(8,128)S(1)} %pad_maximum_fusion.1), channel_id=1, source_target_pairs={{0,64},{1,3},{2,66},{3,1},{4,68},{5,7},{6,70},{7,5},{8,72},{9,11},... | collective-permute-start | bytes 663560 | tf_op jit(solution)/shard_map/ppermute | solution.py:33
  89.2 6.4 %collective-permute-start.17 = (f32[2,24,1152]{2,1,0:T(8,128)S(1)}, f32[2,24,1152]{2,1,0:T(8,128)S(1)}, u32[]{:S(2)}, u32[]{:S(2)}) collective-permute-start(f32[2,24,1152]{2,1,0:T(8,128)S(1)} %pad_maximum_fusion.2), channel_id=1, source_target_pairs={{0,192},{1,7},{2,194},{3,5},{4,196},{5,3},{6,198},{7,1},{8,200},{9... | collective-permute-start | bytes 663560 | tf_op jit(solution)/shard_map/ppermute | solution.py:33
  95.6 5.1 %collective-permute-start.18 = (f32[12,1152]{1,0:T(8,128)S(1)}, f32[12,1152]{1,0:T(8,128)S(1)}, u32[]{:S(2)}, u32[]{:S(2)}) collective-permute-start(f32[12,1152]{1,0:T(8,128)S(1)} %get-tuple-element.67), channel_id=1, source_target_pairs={{0,24},{1,25},{2,26},{3,27},{4,28},{5,29},{6,30},{7,31},{8,16},{9,... | collective-permute-start | bytes 165896 | tf_op jit(solution)/shard_map/ppermute | solution.py:33
  97.4 4.9 %collective-permute-start.19 = (f32[12,1152]{1,0:T(8,128)S(1)}, f32[12,1152]{1,0:T(8,128)S(1)}, u32[]{:S(2)}, u32[]{:S(2)}) collective-permute-start(f32[12,1152]{1,0:T(8,128)S(1)} %get-tuple-element.69), channel_id=1, source_target_pairs={{0,16},{1,17},{2,18},{3,19},{4,20},{5,21},{6,22},{7,23},{8,24},{9,... | collective-permute-start | bytes 165896 | tf_op jit(solution)/shard_map/ppermute | solution.py:33
  97.7 4.6 %collective-permute-start.20 = (f32[12,1152]{1,0:T(8,128)S(1)}, f32[12,1152]{1,0:T(8,128)S(1)}, u32[]{:S(2)}, u32[]{:S(2)}) collective-permute-start(f32[12,1152]{1,0:T(8,128)S(1)} %get-tuple-element.68), channel_id=1, source_target_pairs={{0,8},{1,9},{2,10},{3,11},{4,12},{5,13},{6,14},{7,15},{8,0},{9,1},... | collective-permute-start | bytes 165896 | tf_op jit(solution)/shard_map/ppermute | solution.py:33
  102.4 11.4 %collective-permute-start.21 = (f32[12,576]{1,0:T(8,128)S(1)}, f32[12,576]{1,0:T(8,128)S(1)}, u32[]{:S(2)}, u32[]{:S(2)}) collective-permute-start(f32[12,576]{1,0:T(8,128)S(1)} %get-tuple-element.70), channel_id=1, source_target_pairs={{0,1},{1,49},{2,3},{3,51},{4,5},{5,53},{6,7},{7,55},{8,9},{9,57},{... | collective-permute-start | bytes 82952 | tf_op jit(solution)/shard_map/ppermute | solution.py:33
  103.7 11.8 %collective-permute-start.22 = (f32[12,576]{1,0:T(8,128)S(1)}, f32[12,576]{1,0:T(8,128)S(1)}, u32[]{:S(2)}, u32[]{:S(2)}) collective-permute-start(f32[12,576]{1,0:T(8,128)S(1)} %get-tuple-element.71), channel_id=1, source_target_pairs={{1,48},{3,50},{5,52},{7,54},{9,56},{11,58},{13,60},{15,62},{17,32}... | collective-permute-start | bytes 82952 | tf_op jit(solution)/shard_map/ppermute | solution.py:33

commit v5 on v4

v5 whole, which is shorter than its diff:
```python
import functools
import math

import jax
import jax.numpy as jnp
from jax import lax
from jax.experimental import pallas as pl
from jax.experimental.pallas import tpu as pltpu
from jax.sharding import PartitionSpec as P

HEAD = 96
WIDTH = 2 * HEAD
NY, NZ, NX, NC = 4, 8, 4, 2
SEQ = "seq"
F32 = jnp.float32
BF16 = jnp.bfloat16


def coords(i):
    return i >> 6, (i >> 3) & 7, (i >> 1) & 3, i & 1


def index(y, z, x, c):
    return ((y * NZ + z) * NX + x) * NC + c


def permute(value, move):
    pairs = []
    for i in range(NY * NZ * NX * NC):
        to = move(*coords(i))
        if to is not None:
            pairs.append((i, index(*to)))
    return lax.ppermute(value, SEQ, pairs)


def swap_cores(value):
    return permute(value, lambda y, z, x, c: (y, z, x, 1 - c))


def x_partner(m):
    return lambda y, z, x, c: (y, z, x ^ m, c)


def y_partner(m):
    return lambda y, z, x, c: (y ^ m, z, x, c)


def z_partner(m):
    return lambda y, z, x, c: (y, z ^ m, x, c)


def last_near(y, z, x, c):
    return (y, z, x, 1 - c) if z >> 2 == c else (y, z ^ 6, x, c)


def last_far(y, z, x, c):
    return None if z >> 2 == c else (y, z ^ 6, x, 1 - c)


def rows_dot(a, b):
    return lax.dot_general(a, b, (((0,), (0,)), ((), ())), preferred_element_type=F32)


def lanes_dot(a, b):
    return lax.dot_general(a, b, (((1,), (1,)), ((), ())), preferred_element_type=F32)


def dot(a, b):
    return jnp.dot(a, b, preferred_element_type=F32)


def head(array, h):
    return array[h * HEAD : (h + 1) * HEAD]


PACKED = (144, 128)


def pack(pair, ref):
    ref[0:96, 0:96] = pair[0]
    ref[0:96, 96:128] = pair[1][:, 0:32]
    ref[96:144, 0:64] = pair[1][0:48, 32:96]
    ref[96:144, 64:128] = pair[1][48:96, 32:96]


def unpack(array):
    rest = jnp.concatenate([array[96:144, 0:64], array[96:144, 64:128]], axis=0)
    return array[0:96, 0:96], jnp.concatenate([array[0:96, 96:128], rest], axis=1)


def states_kernel(*refs):
    sources, (keep, send, wide), held, arrived = refs[:4], refs[4:7], refs[7:11], refs[11]
    copies = [pltpu.make_async_copy(a, b, arrived.at[n]) for n, (a, b) in enumerate(zip(sources, held))]
    for copy in copies:
        copy.start()
    for copy in copies:
        copy.wait()
    q, k, v, g = held
    first = lax.axis_index(SEQ) & 1 == 0
    key_state = [lanes_dot(head(k[...], h), head(v[...], h)) for h in range(2)]
    query_state = [lanes_dot(head(q[...], h), head(g[...], h)) for h in range(2)]
    pack([jnp.where(first, a, b) for a, b in zip(key_state, query_state)], keep)
    pack([jnp.where(first, b, a) for a, b in zip(key_state, query_state)], send)
    for n, ref in enumerate(held):
        wide[n] = ref[...].astype(F32)


def halves_kernel(place, x, mine, wide, held, widened, arrived, left):
    lanes = held.shape[3]
    into, out = [], []
    for n, core in enumerate((1 - place[0], place[0])):
        for y in range(NY):
            at = pl.multiple_of((2 * y + core) * lanes, 128)
            to = wide.at[y] if n == 0 else mine.at[y]
            source = widened.at[y] if n == 0 else held.at[1, y]
            into.append(pltpu.make_async_copy(x.at[:, pl.ds(at, lanes)], held.at[n, y], arrived.at[n, y]))
            out.append(pltpu.make_async_copy(source, to, left.at[n, y]))
    for copy in into:
        copy.start()
    for n in range(2 * NY):
        into[n].wait()
        if n < NY:
            widened[n] = held[0, n].astype(F32)
        out[n].start()
    for copy in out:
        copy.wait()


def local_kernel(place, own, other, *outs):
    first = place[0] == 0
    mine, theirs = ([ref[n].astype(BF16) for n in range(4)] for ref in (own, other))
    early = [jnp.where(first, a, b) for a, b in zip(mine, theirs)]
    late = [jnp.where(first, b, a) for a, b in zip(mine, theirs)]
    length = mine[0].shape[1]
    s = lax.broadcasted_iota(jnp.int32, (length, length), 0)
    t = lax.broadcasted_iota(jnp.int32, (length, length), 1)
    causal = s <= t
    for core, (qt, kt, vt, gt) in enumerate((early, late)):
        for out, a in zip(outs, (gt, vt, kt)):
            out[core, WIDTH : 2 * WIDTH, :] = a
        for h in range(2):
            qh, kh, vh, gh = (head(a, h) for a in (qt, kt, vt, gt))
            vg = jnp.where(causal, rows_dot(vh, gh), 0.0).astype(BF16)
            kq = jnp.where(causal, rows_dot(kh, qh), 0.0).astype(BF16)
            dq = dot(kh, vg)
            dk = lanes_dot(qh, vg)
            dv = lanes_dot(gh, kq)
            if core == 0:
                state = lanes_dot(head(late[0], h), head(late[3], h)).astype(BF16)
                dk = dk + dot(state, vh)
                dv = dv + rows_dot(state, kh)
            else:
                state = lanes_dot(head(early[1], h), head(early[2], h)).astype(BF16)
                dq = dq + dot(state, gh)
            for out, a in zip(outs, (dq, dk, dv)):
                out[core, h * HEAD : (h + 1) * HEAD, :] = a.astype(BF16)


def terms_kernel(place, x, wide, d, inner, outer, held):
    c, pz = place[0], place[3]
    contract = (((0,), (1,)), ((), ()))
    for y in range(NY):
        total = lax.dot_general(x[y], d[c], contract, preferred_element_type=F32)
        theirs = wide[y].astype(BF16)
        total = total + lax.dot_general(theirs, d[1 - c], contract, preferred_element_type=F32)
        held[y] = total.reshape(held.shape[1:])
        for part in range(2):
            pair = [pz ^ (2 * part + k) for k in range(2)]
            for x_to in range(NX):
                for side in range(2):
                    rows = slice(x_to * 24 + side * 12, x_to * 24 + side * 12 + 12)
                    value = jnp.concatenate([held[y, z, rows, :] for z in pair], axis=0)
                    inner[part, side, x_to, y] = value[:, :WIDTH]
                    outer[part, side, x_to, y] = value[:, WIDTH:]


COLUMNS = (((0, 0), (0, 1), (1, 0)), ((1, 1), (2, 0), (2, 1)))
ORDERS = ((0, 1, 3, 2), (0, 3, 1, 2))


def join_kernel(factor, half, place, own, other, *refs):
    inner, outer, outs = refs[0:3], refs[3:6], refs[6:]
    first, px, py = place[0] == 0, place[1], place[2]

    def by_head(state):
        one, two = unpack(state)
        none = jnp.zeros_like(one)
        rows = [jnp.concatenate(pair, axis=1) for pair in ((one, none), (none, two))]
        return jnp.concatenate(rows, axis=0).astype(BF16)

    before = by_head(jnp.where(first, own[...], other[...]))
    later = by_head(jnp.where(first, other[...], own[...]))
    steps = ((before, lanes_dot), (later, lanes_dot), (later, dot))
    for part in range(2):
        for axis in range(2):
            out = outs[part * 2 + axis]
            for sa in range(2):
                a = ORDERS[part][2 * half + sa]
                at = [(px ^ a, py ^ b) if axis == 0 else (px ^ b, py ^ a) for b in range(4)]
                pieces = []
                for w, side in COLUMNS[axis]:
                    state, multiply = steps[w]
                    term = jnp.concatenate([outer[w][part, side, i, j] for i, j in at], axis=0)
                    add = jnp.concatenate([inner[w][part, side, i, j] for i, j in at], axis=0)
                    high = term.astype(BF16)
                    low = (term - high.astype(F32)).astype(BF16)
                    pieces.append(factor * (add + multiply(high, state) + multiply(low, state)))
                out[sa] = jnp.concatenate(pieces, axis=1).reshape(out.shape[1:])


VMEM = pl.BlockSpec(memory_space=pltpu.VMEM)
SMEM = pl.BlockSpec(memory_space=pltpu.SMEM)
HBM = pl.BlockSpec(memory_space=pltpu.HBM)
ANY = pl.BlockSpec(memory_space=pl.ANY)


def cost(flops, moved):
    return pl.CostEstimate(flops=flops, bytes_accessed=moved, transcendentals=0)


def limit(mib):
    return pltpu.CompilerParams(vmem_limit_bytes=mib * 2**20)


def states(*features):
    shape = jax.ShapeDtypeStruct(PACKED, F32)
    return pl.pallas_call(
        states_kernel,
        name="states",
        out_shape=(shape, shape, jax.ShapeDtypeStruct((4,) + features[0].shape, F32)),
        in_specs=[HBM] * 4,
        out_specs=(VMEM,) * 3,
        scratch_shapes=[pltpu.VMEM(a.shape, BF16) for a in features] + [pltpu.SemaphoreType.DMA((4,))],
        cost_estimate=cost(4 * 512 * 192 * 192, 10**6),
    )(*features)


def halves(place, x):
    length, features = x.shape
    shape = (NY, length, features // 8)
    return pl.pallas_call(
        halves_kernel,
        name="halves",
        out_shape=(jax.ShapeDtypeStruct(shape, BF16), jax.ShapeDtypeStruct(shape, F32)),
        in_specs=[SMEM, HBM],
        out_specs=(HBM, HBM),
        scratch_shapes=[pltpu.VMEM((2,) + shape, BF16), pltpu.VMEM(shape, F32)]
        + [pltpu.SemaphoreType.DMA((2, NY))] * 2,
        cost_estimate=cost(10**6, 5 * 10**6),
        compiler_params=limit(62),
    )(place, x)


def local_terms(place, mine, theirs):
    shape = jax.ShapeDtypeStruct((2, 2 * WIDTH, mine.shape[2]), BF16)
    return pl.pallas_call(
        local_kernel,
        name="local_terms",
        out_shape=(shape,) * 3,
        in_specs=[SMEM, VMEM, VMEM],
        out_specs=(VMEM,) * 3,
        cost_estimate=cost(40 * 512 * 512 * 96, 5 * 10**6),
        compiler_params=limit(20),
    )(place, mine, theirs)


def terms(place, x, wide, d):
    shape = jax.ShapeDtypeStruct((2, 2, NX, NY, 24, WIDTH), F32)
    return pl.pallas_call(
        terms_kernel,
        name="terms",
        out_shape=(shape, shape),
        in_specs=[SMEM] + [VMEM] * 3,
        out_specs=(VMEM, VMEM),
        scratch_shapes=[pltpu.VMEM((NY, 4, 96, 2 * WIDTH), F32)],
        cost_estimate=cost(2 * 512 * 3072 * 384, 8 * 10**6),
        compiler_params=limit(20),
    )(place, x, wide, d)


def join(half, factor, place, own, other, inner, outer):
    return pl.pallas_call(
        functools.partial(join_kernel, factor, half),
        name=f"join{half}",
        out_shape=(jax.ShapeDtypeStruct((2, 4, 24, 3 * WIDTH), F32),) * 4,
        in_specs=[SMEM] + [VMEM] * 8,
        out_specs=(VMEM,) * 4,
        cost_estimate=cost(24 * 384 * 192 * 192, 8 * 10**6),
        compiler_params=limit(20),
    )(place, own, other, *inner, *outer)


def tie(*values):
    return lax.optimization_barrier(values)


def before_chip(me, total, works):
    y, z, x, c = me
    before = jnp.zeros_like(total)
    steps = (
        (x_partner(1), x & 1),
        (x_partner(3), x >> 1),
        (z_partner(1), z & 1),
        (z_partner(2), (z >> 1) & 1),
        (z_partner(6), z >> 2),
        (y_partner(1), y & 1),
        (y_partner(3), y >> 1),
    )
    for n, (move, bit) in enumerate(steps):
        came = permute(total, move)
        if n in works:
            came, total = works[n](came, total)
        before = before + jnp.where(bit != c, came, 0.0)
        total = total + came
    return before


def scatter_sum(me, keep, send):
    y, z, x, c = me
    partners = (x_partner, y_partner)
    streams = [(part, axis) for part in range(2) for axis in range(2)]
    one = {}
    for n, (part, axis) in enumerate(streams):
        came = permute(send[n], partners[axis]((3, 1)[part]))
        one[n] = (keep[n][0] + came[0], keep[n][1] + came[1])
    ends = {}
    for n, (part, axis) in enumerate(streams):
        ends[part, axis] = one[n][0] + permute(one[n][1], partners[axis]((1, 3)[part]))
    chunk = lambda axis, r: jnp.stack([ends[part, axis][r] for part in range(2)])
    value = [chunk(axis, 0) for axis in range(2)]
    for r in (2, 1, 3):
        for axis in range(2):
            value[axis] = value[axis] + permute(chunk(axis, r), partners[1 - axis](r))
    value = jnp.concatenate(value, axis=2)
    chunk = lambda r: value[r >> 1, 12 * (r & 1) : 12 * (r & 1) + 12]
    total = chunk(0)
    for r in (3, 2, 1):
        total = total + permute(chunk(r), z_partner(r))
    order = COLUMNS[0] + COLUMNS[1]
    column = lambda n: total[:, n * WIDTH : (n + 1) * WIDTH]
    sides = [
        jnp.concatenate([column(order.index((w, side))) for w in range(3)], axis=1) for side in range(2)
    ]
    block = lambda i: jnp.where(i == 0, *sides)
    same = z >> 2 == c
    total = jnp.where(same, block(c), 0.0)
    total = total + permute(block(jnp.where(same, 1 - c, c)), last_near)
    return total + permute(block(1 - c), last_far)


def per_device(inputs, query_proj, key_proj, value_proj, grad_out):
    length, width = query_proj.shape
    factor = 1.0 / (math.sqrt(HEAD) * length * lax.axis_size(SEQ))
    me = coords(lax.axis_index(SEQ))
    y, z, x, c = me
    block = (z & 3) ^ jnp.where(z >> 2 == c, 0, 2)
    place = jnp.stack([c, x, y, block]).astype(jnp.int32)
    mine = [a.T for a in (query_proj, key_proj, value_proj, grad_out)]
    keep, send, wide = states(*mine)
    theirs = swap_cores(wide)
    total = keep + swap_cores(send)
    made = {}

    def halves_work(came, total):
        total, x = tie(total, inputs)
        came, (made["mine"], half) = tie(came, halves(place, x))
        made["wide"] = swap_cores(half)
        return came, total

    def local_work(came, total):
        total, there = tie(total, theirs)
        came, made["local"] = tie(came, local_terms(place, wide, there))
        return came, total

    def terms_work(n):
        def work(came, total):
            total, d = tie(total, made["local"][n])
            came, made[n] = tie(came, terms(place, made["mine"], made["wide"], d))
            return came, total

        return work

    works = {0: halves_work, 3: local_work, 4: terms_work(0), 5: terms_work(1), 6: terms_work(2)}
    before = before_chip(me, total, works)
    across = swap_cores(before)
    inner, outer = zip(*(made[n] for n in range(3)))
    send = join(1, factor, place, before, across, inner, outer)
    keep = join(0, factor, place, before, across, inner, outer)
    summed = scatter_sum(me, keep, send)
    return (summed[:, :width], summed[:, width : 2 * width], summed[:, 2 * width :])


def solution(mesh):
    return jax.shard_map(
        per_device,
        mesh=mesh,
        in_specs=(P(SEQ, None),) * 5,
        out_specs=(P(SEQ, None),) * 3,
        check_vma=False,
    )
```

time: 117 us -> 111 us (0.949)
  waiting for transfers between devices: 41.4 us -> 27.7 us
  starting transfers between devices: 39.9 us -> 53.5 us
  local copies, waits for them, and re-layouts: 5.8 us -> 2.26 us
    ppermute x23 -> x30, waiting for transfers between devices: 41.4 us -> 27.7 us  [permute(): return lax.ppermute(value, SEQ, pairs)]
    ppermute x23 -> x30, starting transfers between devices: 39.9 us -> 53.5 us  [permute(): return lax.ppermute(value, SEQ, pairs)]
    unnamed x30 -> x6, local copies, waits for them, and re-layouts: 5.04 us -> 1.42 us
    pallas_call x10 -> x8, Pallas kernels: 24.8 us -> 23.7 us  [the longest x3 7.91 us: terms(): pl.pallas_call(terms_kernel, name='terms', out_shape=(shape, shape), in_s...]
  transfers between devices with their start and end apart: 23 -> 30, of which waited for: 16 -> 15; matrix products, arithmetic and copies ran while one was open for 0% -> 1% of each run, Pallas kernels for 18% -> 17%
where the time goes in v5:
time: 111 us; the launch traced here: 110 us
  starting transfers between devices  53.5 us (48%)
  waiting for transfers between devices  27.7 us (25%)
  Pallas kernels  23.7 us (21%)
  other arithmetic  2.38 us (2%)
  local copies, waits for them, and re-layouts  2.26 us (2%)
    ppermute x30, starting transfers between devices, permute(): return lax.ppermute(value, SEQ, pairs)  53.5 us
    ppermute x30, waiting for transfers between devices, permute(): return lax.ppermute(value, SEQ, pairs)  27.7 us
    pallas_call x3, Pallas kernels, terms(): pl.pallas_call(terms_kernel, name='terms', out_shape=(shape, shape), in_s...  7.91 us
    pallas_call x1, Pallas kernels, local_terms(): pl.pallas_call(local_kernel, name='local_terms', out_shape=(shape,) * 3,...  4.55 us
    pallas_call x2, Pallas kernels, join(): pl.pallas_call(functools.partial(join_kernel, factor, half), name=f'join{...  4.21 us
    pallas_call x1, Pallas kernels, halves(): pl.pallas_call(halves_kernel, name='halves', out_shape=(jax.ShapeDtypeStr...  4.18 us
    pallas_call x1, Pallas kernels, states(): pl.pallas_call(states_kernel, name='states', out_shape=(shape, shape, jax...  2.81 us
  transfers between devices with their start and end apart: 30, of which 15 were waited for; matrix products, arithmetic and copies ran while one was open for 1% of the time, Pallas kernels for 17%

profile of v5, /device:TPU:1, one launch (start us, length us, event | category | flops | bytes accessed | tf_op | source)
XLA Modules:
  0.0 110.5 jit_solution(5142855960784706211)
XLA Ops:
  0.6 2.8 %states.1 = (f32[144,128]{1,0:T(8,128)}, f32[144,128]{1,0:T(8,128)}, f32[4,192,512]{2,1,0:T(8,128)}) custom-call(bf16[192,512]{1,0:T(8,128)(2,1)} %bitcast.46, bf16[192,512]{1,0:T(8,128)(2,1)} %bitcast.47, bf16[192,512]{1,0:T(8,128)(2,1)} %bitcast.48, bf16[192,512]{1,0:T(8,128)(2,1)} %bitcast.49), custom_call_target="tpu_custom_call" | custom-call | flops 75497472 | bytes 1000000 | tf_op jit(solution)/shard_map/states/pallas_call | solution.py:227
  3.5 3.3 %collective-permute-start = (f32[144,128]{1,0:T(8,128)}, f32[144,128]{1,0:T(8,128)S(1)}, u32[]{:S(2)}, u32[]{:S(2)}) collective-permute-start(f32[144,128]{1,0:T(8,128)} %get-tuple-element.51), channel_id=1, source_target_pairs={{0,1},{1,0},{2,3},{3,2},{4,5},{5,4},{6,7},{7,6},{8,9},{9,8},{10,11... | collective-permute-start | bytes 221192 | tf_op jit(solution)/shard_map/ppermute | solution.py:33
  6.8 1.1 %collective-permute-done = f32[144,128]{1,0:T(8,128)S(1)} collective-permute-done((f32[144,128]{1,0:T(8,128)}, f32[144,128]{1,0:T(8,128)S(1)}, u32[]{:S(2)}, u32[]{:S(2)}) %collective-permute-start) | collective-permute-done | bytes 73760 | tf_op jit(solution)/shard_map/ppermute | solution.py:33
  7.9 0.9 add.132
  9.5 4.2 %halves.1 = (bf16[4,512,384]{2,1,0:T(8,128)(2,1)}, f32[4,512,384]{2,1,0:T(8,128)}) custom-call(s32[4]{0:T(128)} %pad_add_fusion.place, bf16[512,3072]{1,0:T(8,128)(2,1)} %x), custom_call_target="tpu_custom_call" | custom-call | flops 1000000 | bytes 5000000 | tf_op jit(solution)/shard_map/halves/pallas_call | solution.py:241
  14.3 1.6 %collective-permute-start.2 = (f32[144,128]{1,0:T(8,128)S(1)}, f32[144,128]{1,0:T(8,128)S(1)}, u32[]{:S(2)}, u32[]{:S(2)}) collective-permute-start(f32[144,128]{1,0:T(8,128)S(1)} %add.133), channel_id=1, source_target_pairs={{0,6},{1,7},{2,4},{3,5},{4,2},{5,3},{6,0},{7,1},{8,14},{9,15},{10,... | collective-permute-start | bytes 221192 | tf_op jit(solution)/shard_map/ppermute | solution.py:33
  15.9 2.9 %collective-permute-done.2 = f32[144,128]{1,0:T(8,128)S(1)} collective-permute-done((f32[144,128]{1,0:T(8,128)S(1)}, f32[144,128]{1,0:T(8,128)S(1)}, u32[]{:S(2)}, u32[]{:S(2)}) %collective-permute-start.2) | collective-permute-done | bytes 73760 | tf_op jit(solution)/shard_map/ppermute | solution.py:33
  18.8 1.4 %collective-permute-start.3 = (f32[144,128]{1,0:T(8,128)S(1)}, f32[144,128]{1,0:T(8,128)S(1)}, u32[]{:S(2)}, u32[]{:S(2)}) collective-permute-start(f32[144,128]{1,0:T(8,128)S(1)} %add.135), channel_id=1, source_target_pairs={{0,8},{1,9},{2,10},{3,11},{4,12},{5,13},{6,14},{7,15},{8,0},{9,1},... | collective-permute-start | bytes 221192 | tf_op jit(solution)/shard_map/ppermute | solution.py:33
  20.2 1.9 %collective-permute-done.3 = f32[144,128]{1,0:T(8,128)S(1)} collective-permute-done((f32[144,128]{1,0:T(8,128)S(1)}, f32[144,128]{1,0:T(8,128)S(1)}, u32[]{:S(2)}, u32[]{:S(2)}) %collective-permute-start.3) | collective-permute-done | bytes 73760 | tf_op jit(solution)/shard_map/ppermute | solution.py:33
  22.1 2.9 %collective-permute-start.4 = (f32[144,128]{1,0:T(8,128)S(1)}, f32[144,128]{1,0:T(8,128)S(1)}, u32[]{:S(2)}, u32[]{:S(2)}) collective-permute-start(f32[144,128]{1,0:T(8,128)S(1)} %add.137), channel_id=1, source_target_pairs={{0,16},{1,17},{2,18},{3,19},{4,20},{5,21},{6,22},{7,23},{8,24},{9,... | collective-permute-start | bytes 221192 | tf_op jit(solution)/shard_map/ppermute | solution.py:33
  25.1 1.4 %copy-done.2 = f32[4,192,512]{2,1,0:T(8,128)S(1)} copy-done((f32[4,192,512]{2,1,0:T(8,128)S(1)}, f32[4,192,512]{2,1,0:T(8,128)}, u32[]{:S(2)}) %copy-start.2) | copy-done | bytes 1572888
  26.5 4.5 %local_terms.1 = (bf16[2,384,512]{2,1,0:T(8,128)(2,1)S(1)}, bf16[2,384,512]{2,1,0:T(8,128)(2,1)S(1)}, bf16[2,384,512]{2,1,0:T(8,128)(2,1)S(1)}) custom-call(s32[4]{0:T(128)S(1)} %copy-done.1, f32[4,192,512]{2,1,0:T(8,128)S(1)} %copy-done.2, f32[4,192,512]{2,1,0:T(8,128)} %collective-permute-done.5.other), custom_call_target="tpu_custom_call" | custom-call | flops 1006632960 | bytes 5000000 | tf_op jit(solution)/shard_map/local_terms/pallas_call | solution.py:256
  31.1 4.1 %collective-permute-start.6 = (f32[144,128]{1,0:T(8,128)S(1)}, f32[144,128]{1,0:T(8,128)S(1)}, u32[]{:S(2)}, u32[]{:S(2)}) collective-permute-start(f32[144,128]{1,0:T(8,128)S(1)} %add.139), channel_id=1, source_target_pairs={{0,48},{1,49},{2,50},{3,51},{4,52},{5,53},{6,54},{7,55},{8,56},{9,... | collective-permute-start | bytes 221192 | tf_op jit(solution)/shard_map/ppermute | solution.py:33
  35.2 2.6 %terms.3 = (f32[2,2,4,4,24,192]{5,4,3,2,1,0:T(8,128)S(1)}, f32[2,2,4,4,24,192]{5,4,3,2,1,0:T(8,128)S(1)}) custom-call(s32[4]{0:T(128)S(1)} %copy-done.1, bf16[4,512,384]{2,1,0:T(8,128)(2,1)S(1)} %copy-done, f32[4,512,384]{2,1,0:T(8,128)S(1)} %collective-permute-done.7.wide, bf16[2,384,512]{2,1,0:T(8,128)(2,1)S(1)} %get-tuple-element.67.d), custom_call_target="tpu_custom_call" | custom-call | flops 1207959552 | bytes 8000000 | tf_op jit(solution)/shard_map/terms/pallas_call | solution.py:269
  37.9 1.6 %collective-permute-start.8 = (f32[144,128]{1,0:T(8,128)S(1)}, f32[144,128]{1,0:T(8,128)S(1)}, u32[]{:S(2)}, u32[]{:S(2)}) collective-permute-start(f32[144,128]{1,0:T(8,128)S(1)} %add.141), channel_id=1, source_target_pairs={{0,64},{1,65},{2,66},{3,67},{4,68},{5,69},{6,70},{7,71},{8,72},{9,... | collective-permute-start | bytes 221192 | tf_op jit(solution)/shard_map/ppermute | solution.py:33
  39.4 2.6 %terms.4 = (f32[2,2,4,4,24,192]{5,4,3,2,1,0:T(8,128)S(1)}, f32[2,2,4,4,24,192]{5,4,3,2,1,0:T(8,128)S(1)}) custom-call(s32[4]{0:T(128)S(1)} %copy-done.1, bf16[4,512,384]{2,1,0:T(8,128)(2,1)S(1)} %copy-done, f32[4,512,384]{2,1,0:T(8,128)S(1)} %collective-permute-done.7.wide, bf16[2,384,512]{2,1,0:T(8,128)(2,1)S(1)} %get-tuple-element.73.d), custom_call_target="tpu_custom_call" | custom-call | flops 1207959552 | bytes 8000000 | tf_op jit(solution)/shard_map/terms/pallas_call | solution.py:269
  42.1 2.1 %collective-permute-start.9 = (f32[144,128]{1,0:T(8,128)S(1)}, f32[144,128]{1,0:T(8,128)S(1)}, u32[]{:S(2)}, u32[]{:S(2)}) collective-permute-start(f32[144,128]{1,0:T(8,128)S(1)} %add.143), channel_id=1, source_target_pairs={{0,192},{1,193},{2,194},{3,195},{4,196},{5,197},{6,198},{7,199},{8... | collective-permute-start | bytes 221192 | tf_op jit(solution)/shard_map/ppermute | solution.py:33
  44.2 2.6 %terms.5 = (f32[2,2,4,4,24,192]{5,4,3,2,1,0:T(8,128)S(1)}, f32[2,2,4,4,24,192]{5,4,3,2,1,0:T(8,128)S(1)}) custom-call(s32[4]{0:T(128)S(1)} %copy-done.1, bf16[4,512,384]{2,1,0:T(8,128)(2,1)S(1)} %copy-done, f32[4,512,384]{2,1,0:T(8,128)S(1)} %collective-permute-done.7.wide, bf16[2,384,512]{2,1,0:T(8,128)(2,1)S(1)} %get-tuple-element.79.d), custom_call_target="tpu_custom_call" | custom-call | flops 1207959552 | bytes 8000000 | tf_op jit(solution)/shard_map/terms/pallas_call | solution.py:269
  46.9 4.8 %collective-permute-start.10 = (f32[144,128]{1,0:T(8,128)S(1)}, f32[144,128]{1,0:T(8,128)S(1)}, u32[]{:S(2)}, u32[]{:S(2)}) collective-permute-start(f32[144,128]{1,0:T(8,128)S(1)} %select_add_fusion.own), channel_id=1, source_target_pairs={{0,1},{1,0},{2,3},{3,2},{4,5},{5,4},{6,7},{7,6},{8,9},{9,8},{10,11... | collective-permute-start | bytes 221192 | tf_op jit(solution)/shard_map/ppermute | solution.py:33
  51.7 0.9 collective-permute-done.10.other
  52.6 2.1 %join1.1 = (f32[2,4,24,576]{3,2,1,0:T(8,128)S(1)}, f32[2,4,24,576]{3,2,1,0:T(8,128)S(1)}, f32[2,4,24,576]{3,2,1,0:T(8,128)S(1)}, f32[2,4,24,576]{3,2,1,0:T(8,128)S(1)}) custom-call(s32[4]{0:T(128)S(1)} %copy-done.1, f32[144,128]{1,0:T(8,128)S(1)} %select_add_fusion.own, f32[144,128]{1,0:T(8,128)S(1)} %collective-permute-done.10.other, ...), custom_call_target="tpu_custom_call" | custom-call | flops 339738624 | bytes 8000000 | tf_op jit(solution)/shard_map/join1/pallas_call | solution.py:282
  54.7 2.7 %collective-permute-start.18 = (f32[2,4,24,576]{3,2,1,0:T(8,128)S(1)}, f32[2,4,24,576]{3,2,1,0:T(8,128)S(1)}, u32[]{:S(2)}, u32[]{:S(2)}) collective-permute-start(f32[2,4,24,576]{3,2,1,0:T(8,128)S(1)} %get-tuple-element.94), channel_id=1, source_target_pairs={{0,192},{1,193},{2,194},{3,195},{4,196},{5,197},{6,198},{7,199},{8... | collective-permute-start | bytes 1327112 | tf_op jit(solution)/shard_map/ppermute | solution.py:33
  57.4 1.8 %collective-permute-start.11 = (f32[2,4,24,576]{3,2,1,0:T(8,128)S(1)}, f32[2,4,24,576]{3,2,1,0:T(8,128)S(1)}, u32[]{:S(2)}, u32[]{:S(2)}) collective-permute-start(f32[2,4,24,576]{3,2,1,0:T(8,128)S(1)} %get-tuple-element.90), channel_id=1, source_target_pairs={{0,6},{1,7},{2,4},{3,5},{4,2},{5,3},{6,0},{7,1},{8,14},{9,15},{10,... | collective-permute-start | bytes 1327112 | tf_op jit(solution)/shard_map/ppermute | solution.py:33
  59.2 2.1 %join0.1 = (f32[2,4,24,576]{3,2,1,0:T(8,128)S(1)}, f32[2,4,24,576]{3,2,1,0:T(8,128)S(1)}, f32[2,4,24,576]{3,2,1,0:T(8,128)S(1)}, f32[2,4,24,576]{3,2,1,0:T(8,128)S(1)}) custom-call(s32[4]{0:T(128)S(1)} %copy-done.1, f32[144,128]{1,0:T(8,128)S(1)} %select_add_fusion.own, f32[144,128]{1,0:T(8,128)S(1)} %collective-permute-done.10.other, ...), custom_call_target="tpu_custom_call" | custom-call | flops 339738624 | bytes 8000000 | tf_op jit(solution)/shard_map/join0/pallas_call | solution.py:282
  61.4 7.1 %collective-permute-done.18 = f32[2,4,24,576]{3,2,1,0:T(8,128)S(1)} collective-permute-done((f32[2,4,24,576]{3,2,1,0:T(8,128)S(1)}, f32[2,4,24,576]{3,2,1,0:T(8,128)S(1)}, u32[]{:S(2)}, u32[]{:S(2)}) %collective-permute-start.18) | collective-permute-done | bytes 442400 | tf_op jit(solution)/shard_map/ppermute | solution.py:33
  68.6 1.0 collective-permute-done.20
  69.6 1.8 %collective-permute-start.21 = (f32[4,24,576]{2,1,0:T(8,128)S(1)}, f32[4,24,576]{2,1,0:T(8,128)S(1)}, u32[]{:S(2)}, u32[]{:S(2)}) collective-permute-start(f32[4,24,576]{2,1,0:T(8,128)S(1)} %fusion), channel_id=1, source_target_pairs={{0,192},{1,193},{2,194},{3,195},{4,196},{5,197},{6,198},{7,199},{8... | collective-permute-start | bytes 663560 | tf_op jit(solution)/shard_map/ppermute | solution.py:33
  71.5 1.9 %collective-permute-start.14 = (f32[4,24,576]{2,1,0:T(8,128)S(1)}, f32[4,24,576]{2,1,0:T(8,128)S(1)}, u32[]{:S(2)}, u32[]{:S(2)}) collective-permute-start(f32[4,24,576]{2,1,0:T(8,128)S(1)} %fusion.6), channel_id=1, source_target_pairs={{0,6},{1,7},{2,4},{3,5},{4,2},{5,3},{6,0},{7,1},{8,14},{9,15},{10,... | collective-permute-start | bytes 663560 | tf_op jit(solution)/shard_map/ppermute | solution.py:33
  73.4 1.4 %collective-permute-done.19 = f32[4,24,576]{2,1,0:T(8,128)S(1)} collective-permute-done((f32[4,24,576]{2,1,0:T(8,128)S(1)}, f32[4,24,576]{2,1,0:T(8,128)S(1)}, u32[]{:S(2)}, u32[]{:S(2)}) %collective-permute-start.19) | collective-permute-done | bytes 221216 | tf_op jit(solution)/shard_map/ppermute | solution.py:33
  74.9 1.9 %collective-permute-done.21 = f32[4,24,576]{2,1,0:T(8,128)S(1)} collective-permute-done((f32[4,24,576]{2,1,0:T(8,128)S(1)}, f32[4,24,576]{2,1,0:T(8,128)S(1)}, u32[]{:S(2)}, u32[]{:S(2)}) %collective-permute-start.21) | collective-permute-done | bytes 221216 | tf_op jit(solution)/shard_map/ppermute | solution.py:33
  76.9 1.5 %collective-permute-start.22 = (f32[2,24,576]{2,1,0:T(8,128)S(1)}, f32[2,24,576]{2,1,0:T(8,128)S(1)}, u32[]{:S(2)}, u32[]{:S(2)}) collective-permute-start(f32[2,24,576]{2,1,0:T(8,128)S(1)} %pad_maximum_fusion.3), channel_id=1, source_target_pairs={{0,4},{1,5},{2,6},{3,7},{4,0},{5,1},{6,2},{7,3},{8,12},{9,13},{10,... | collective-permute-start | bytes 331784 | tf_op jit(solution)/shard_map/ppermute | solution.py:33
  78.5 1.2 %collective-permute-start.23 = (f32[2,24,576]{2,1,0:T(8,128)S(1)}, f32[2,24,576]{2,1,0:T(8,128)S(1)}, u32[]{:S(2)}, u32[]{:S(2)}) collective-permute-start(f32[2,24,576]{2,1,0:T(8,128)S(1)} %pad_maximum_fusion.4), channel_id=1, source_target_pairs={{0,2},{1,3},{2,0},{3,1},{4,6},{5,7},{6,4},{7,5},{8,10},{9,11},{10,... | collective-permute-start | bytes 331784 | tf_op jit(solution)/shard_map/ppermute | solution.py:33
  79.7 0.9 collective-permute-start.24
  80.8 1.7 %collective-permute-start.15 = (f32[2,24,576]{2,1,0:T(8,128)S(1)}, f32[2,24,576]{2,1,0:T(8,128)S(1)}, u32[]{:S(2)}, u32[]{:S(2)}) collective-permute-start(f32[2,24,576]{2,1,0:T(8,128)S(1)} %pad_maximum_fusion), channel_id=1, source_target_pairs={{0,128},{1,129},{2,130},{3,131},{4,132},{5,133},{6,134},{7,135},{8... | collective-permute-start | bytes 331784 | tf_op jit(solution)/shard_map/ppermute | solution.py:33
  82.6 1.0 collective-permute-start.16
  83.6 0.8 collective-permute-start.17
  84.5 1.6 %collective-permute-done.24 = f32[2,24,576]{2,1,0:T(8,128)S(1)} collective-permute-done((f32[2,24,576]{2,1,0:T(8,128)S(1)}, f32[2,24,576]{2,1,0:T(8,128)S(1)}, u32[]{:S(2)}, u32[]{:S(2)}) %collective-permute-start.24) | collective-permute-done | bytes 110624 | tf_op jit(solution)/shard_map/ppermute | solution.py:33
  86.2 1.2 %collective-permute-done.16 = f32[2,24,576]{2,1,0:T(8,128)S(1)} collective-permute-done((f32[2,24,576]{2,1,0:T(8,128)S(1)}, f32[2,24,576]{2,1,0:T(8,128)S(1)}, u32[]{:S(2)}, u32[]{:S(2)}) %collective-permute-start.16) | collective-permute-done | bytes 110624 | tf_op jit(solution)/shard_map/ppermute | solution.py:33
  87.4 1.6 %collective-permute-done.17 = f32[2,24,576]{2,1,0:T(8,128)S(1)} collective-permute-done((f32[2,24,576]{2,1,0:T(8,128)S(1)}, f32[2,24,576]{2,1,0:T(8,128)S(1)}, u32[]{:S(2)}, u32[]{:S(2)}) %collective-permute-start.17) | collective-permute-done | bytes 110624 | tf_op jit(solution)/shard_map/ppermute | solution.py:33
  89.1 1.7 %collective-permute-start.25 = (f32[12,1152]{1,0:T(8,128)S(1)}, f32[12,1152]{1,0:T(8,128)S(1)}, u32[]{:S(2)}, u32[]{:S(2)}) collective-permute-start(f32[12,1152]{1,0:T(8,128)S(1)} %get-tuple-element.97), channel_id=1, source_target_pairs={{0,24},{1,25},{2,26},{3,27},{4,28},{5,29},{6,30},{7,31},{8,16},{9,... | collective-permute-start | bytes 165896 | tf_op jit(solution)/shard_map/ppermute | solution.py:33
  90.8 1.2 %collective-permute-start.26 = (f32[12,1152]{1,0:T(8,128)S(1)}, f32[12,1152]{1,0:T(8,128)S(1)}, u32[]{:S(2)}, u32[]{:S(2)}) collective-permute-start(f32[12,1152]{1,0:T(8,128)S(1)} %get-tuple-element.99), channel_id=1, source_target_pairs={{0,16},{1,17},{2,18},{3,19},{4,20},{5,21},{6,22},{7,23},{8,24},{9,... | collective-permute-start | bytes 165896 | tf_op jit(solution)/shard_map/ppermute | solution.py:33
  92.0 0.8 collective-permute-start.27
  92.7 1.6 %collective-permute-done.25 = f32[12,1152]{1,0:T(8,128)S(1)} collective-permute-done((f32[12,1152]{1,0:T(8,128)S(1)}, f32[12,1152]{1,0:T(8,128)S(1)}, u32[]{:S(2)}, u32[]{:S(2)}) %collective-permute-start.25) | collective-permute-done | bytes 55328 | tf_op jit(solution)/shard_map/ppermute | solution.py:33
  94.3 1.8 %collective-permute-done.26 = f32[12,1152]{1,0:T(8,128)S(1)} collective-permute-done((f32[12,1152]{1,0:T(8,128)S(1)}, f32[12,1152]{1,0:T(8,128)S(1)}, u32[]{:S(2)}, u32[]{:S(2)}) %collective-permute-start.26) | collective-permute-done | bytes 55328 | tf_op jit(solution)/shard_map/ppermute | solution.py:33
  96.4 2.8 %collective-permute-start.28 = (f32[12,576]{1,0:T(8,128)S(1)}, f32[12,576]{1,0:T(8,128)S(1)}, u32[]{:S(2)}, u32[]{:S(2)}) collective-permute-start(f32[12,576]{1,0:T(8,128)S(1)} %get-tuple-element.116), channel_id=1, source_target_pairs={{0,1},{1,49},{2,3},{3,51},{4,5},{5,53},{6,7},{7,55},{8,9},{9,57},{... | collective-permute-start | bytes 82952 | tf_op jit(solution)/shard_map/ppermute | solution.py:33
  99.1 8.9 %collective-permute-start.29 = (f32[12,576]{1,0:T(8,128)S(1)}, f32[12,576]{1,0:T(8,128)S(1)}, u32[]{:S(2)}, u32[]{:S(2)}) collective-permute-start(f32[12,576]{1,0:T(8,128)S(1)} %get-tuple-element.117), channel_id=1, source_target_pairs={{1,48},{3,50},{5,52},{7,54},{9,56},{11,58},{13,60},{15,62},{17,32}... | collective-permute-start | bytes 82952 | tf_op jit(solution)/shard_map/ppermute | solution.py:33
  108.0 1.7 %collective-permute-done.29 = f32[12,576]{1,0:T(8,128)S(1)} collective-permute-done((f32[12,576]{1,0:T(8,128)S(1)}, f32[12,576]{1,0:T(8,128)S(1)}, u32[]{:S(2)}, u32[]{:S(2)}) %collective-permute-start.29) | collective-permute-done | bytes 27680 | tf_op jit(solution)/shard_map/ppermute | solution.py:33
  109.8 0.7 fusion.31
  (61 shorter events, 2.6 us)
Async XLA Ops:
  3.5 4.5 %collective-permute-start = (f32[144,128]{1,0:T(8,128)}, f32[144,128]{1,0:T(8,128)S(1)}, u32[]{:S(2)}, u32[]{:S(2)}) collective-permute-start(f32[144,128]{1,0:T(8,128)} %get-tuple-element.51), channel_id=1, source_target_pairs={{0,1},{1,0},{2,3},{3,2},{4,5},{5,4},{6,7},{7,6},{8,9},{9,8},{10,11... | collective-permute-start | bytes 221192 | tf_op jit(solution)/shard_map/ppermute | solution.py:33
  8.8 4.9 %collective-permute-start.1 = (f32[144,128]{1,0:T(8,128)S(1)}, f32[144,128]{1,0:T(8,128)S(1)}, u32[]{:S(2)}, u32[]{:S(2)}) collective-permute-start(f32[144,128]{1,0:T(8,128)S(1)} %add.132), channel_id=1, source_target_pairs={{0,2},{1,3},{2,0},{3,1},{4,6},{5,7},{6,4},{7,5},{8,10},{9,11},{10,... | collective-permute-start | bytes 221192 | tf_op jit(solution)/shard_map/ppermute | solution.py:33
  9.5 15.6 %copy-start.1 = (s32[4]{0:T(128)S(1)}, s32[4]{0:T(128)}, u32[]{:S(2)}) copy-start(s32[4]{0:T(128)} %pad_add_fusion.place) | copy-start | bytes 52
  13.7 21.5 %collective-permute-start.7 = (f32[4,512,384]{2,1,0:T(8,128)}, f32[4,512,384]{2,1,0:T(8,128)S(1)}, u32[]{:S(2)}, u32[]{:S(2)}) collective-permute-start(f32[4,512,384]{2,1,0:T(8,128)} %get-tuple-element.65), channel_id=1, source_target_pairs={{0,1},{1,0},{2,3},{3,2},{4,5},{5,4},{6,7},{7,6},{8,9},{9,8},{10,11... | collective-permute-start | bytes 9437192 | tf_op jit(solution)/shard_map/ppermute | solution.py:33
  14.1 10.9 %collective-permute-start.5 = (f32[4,192,512]{2,1,0:T(8,128)}, f32[4,192,512]{2,1,0:T(8,128)}, u32[]{:S(2)}, u32[]{:S(2)}) collective-permute-start(f32[4,192,512]{2,1,0:T(8,128)} %get-tuple-element.57.own), channel_id=1, source_target_pairs={{0,1},{1,0},{2,3},{3,2},{4,5},{5,4},{6,7},{7,6},{8,9},{9,8},{10,11... | collective-permute-start | bytes 4718600 | tf_op jit(solution)/shard_map/ppermute | solution.py:33
  14.3 4.5 %collective-permute-start.2 = (f32[144,128]{1,0:T(8,128)S(1)}, f32[144,128]{1,0:T(8,128)S(1)}, u32[]{:S(2)}, u32[]{:S(2)}) collective-permute-start(f32[144,128]{1,0:T(8,128)S(1)} %add.133), channel_id=1, source_target_pairs={{0,6},{1,7},{2,4},{3,5},{4,2},{5,3},{6,0},{7,1},{8,14},{9,15},{10,... | collective-permute-start | bytes 221192 | tf_op jit(solution)/shard_map/ppermute | solution.py:33
  18.8 3.3 %collective-permute-start.3 = (f32[144,128]{1,0:T(8,128)S(1)}, f32[144,128]{1,0:T(8,128)S(1)}, u32[]{:S(2)}, u32[]{:S(2)}) collective-permute-start(f32[144,128]{1,0:T(8,128)S(1)} %add.135), channel_id=1, source_target_pairs={{0,8},{1,9},{2,10},{3,11},{4,12},{5,13},{6,14},{7,15},{8,0},{9,1},... | collective-permute-start | bytes 221192 | tf_op jit(solution)/shard_map/ppermute | solution.py:33
  22.1 13.1 %copy-start = (bf16[4,512,384]{2,1,0:T(8,128)(2,1)S(1)}, bf16[4,512,384]{2,1,0:T(8,128)(2,1)}, u32[]{:S(2)}) copy-start(bf16[4,512,384]{2,1,0:T(8,128)(2,1)} %get-tuple-element.64.x) | copy-start | bytes 4718596
  22.1 8.9 %collective-permute-start.4 = (f32[144,128]{1,0:T(8,128)S(1)}, f32[144,128]{1,0:T(8,128)S(1)}, u32[]{:S(2)}, u32[]{:S(2)}) collective-permute-start(f32[144,128]{1,0:T(8,128)S(1)} %add.137), channel_id=1, source_target_pairs={{0,16},{1,17},{2,18},{3,19},{4,20},{5,21},{6,22},{7,23},{8,24},{9,... | collective-permute-start | bytes 221192 | tf_op jit(solution)/shard_map/ppermute | solution.py:33
  25.1 1.4 %copy-start.2 = (f32[4,192,512]{2,1,0:T(8,128)S(1)}, f32[4,192,512]{2,1,0:T(8,128)}, u32[]{:S(2)}) copy-start(f32[4,192,512]{2,1,0:T(8,128)} %get-tuple-element.57.own) | copy-start | bytes 4718596
  31.1 6.8 %collective-permute-start.6 = (f32[144,128]{1,0:T(8,128)S(1)}, f32[144,128]{1,0:T(8,128)S(1)}, u32[]{:S(2)}, u32[]{:S(2)}) collective-permute-start(f32[144,128]{1,0:T(8,128)S(1)} %add.139), channel_id=1, source_target_pairs={{0,48},{1,49},{2,50},{3,51},{4,52},{5,53},{6,54},{7,55},{8,56},{9,... | collective-permute-start | bytes 221192 | tf_op jit(solution)/shard_map/ppermute | solution.py:33
  37.9 4.2 %collective-permute-start.8 = (f32[144,128]{1,0:T(8,128)S(1)}, f32[144,128]{1,0:T(8,128)S(1)}, u32[]{:S(2)}, u32[]{:S(2)}) collective-permute-start(f32[144,128]{1,0:T(8,128)S(1)} %add.141), channel_id=1, source_target_pairs={{0,64},{1,65},{2,66},{3,67},{4,68},{5,69},{6,70},{7,71},{8,72},{9,... | collective-permute-start | bytes 221192 | tf_op jit(solution)/shard_map/ppermute | solution.py:33
  42.1 4.7 %collective-permute-start.9 = (f32[144,128]{1,0:T(8,128)S(1)}, f32[144,128]{1,0:T(8,128)S(1)}, u32[]{:S(2)}, u32[]{:S(2)}) collective-permute-start(f32[144,128]{1,0:T(8,128)S(1)} %add.143), channel_id=1, source_target_pairs={{0,192},{1,193},{2,194},{3,195},{4,196},{5,197},{6,198},{7,199},{8... | collective-permute-start | bytes 221192 | tf_op jit(solution)/shard_map/ppermute | solution.py:33
  46.9 5.7 %collective-permute-start.10 = (f32[144,128]{1,0:T(8,128)S(1)}, f32[144,128]{1,0:T(8,128)S(1)}, u32[]{:S(2)}, u32[]{:S(2)}) collective-permute-start(f32[144,128]{1,0:T(8,128)S(1)} %select_add_fusion.own), channel_id=1, source_target_pairs={{0,1},{1,0},{2,3},{3,2},{4,5},{5,4},{6,7},{7,6},{8,9},{9,8},{10,11... | collective-permute-start | bytes 221192 | tf_op jit(solution)/shard_map/ppermute | solution.py:33
  54.7 13.7 %collective-permute-start.18 = (f32[2,4,24,576]{3,2,1,0:T(8,128)S(1)}, f32[2,4,24,576]{3,2,1,0:T(8,128)S(1)}, u32[]{:S(2)}, u32[]{:S(2)}) collective-permute-start(f32[2,4,24,576]{3,2,1,0:T(8,128)S(1)} %get-tuple-element.94), channel_id=1, source_target_pairs={{0,192},{1,193},{2,194},{3,195},{4,196},{5,197},{6,198},{7,199},{8... | collective-permute-start | bytes 1327112 | tf_op jit(solution)/shard_map/ppermute | solution.py:33
  57.4 12.1 %collective-permute-start.20 = (f32[2,4,24,576]{3,2,1,0:T(8,128)S(1)}, f32[2,4,24,576]{3,2,1,0:T(8,128)S(1)}, u32[]{:S(2)}, u32[]{:S(2)}) collective-permute-start(f32[2,4,24,576]{3,2,1,0:T(8,128)S(1)} %get-tuple-element.96), channel_id=1, source_target_pairs={{0,64},{1,65},{2,66},{3,67},{4,68},{5,69},{6,70},{7,71},{8,72},{9,... | collective-permute-start | bytes 1327112 | tf_op jit(solution)/shard_map/ppermute | solution.py:33
  57.4 13.9 %collective-permute-start.11 = (f32[2,4,24,576]{3,2,1,0:T(8,128)S(1)}, f32[2,4,24,576]{3,2,1,0:T(8,128)S(1)}, u32[]{:S(2)}, u32[]{:S(2)}) collective-permute-start(f32[2,4,24,576]{3,2,1,0:T(8,128)S(1)} %get-tuple-element.90), channel_id=1, source_target_pairs={{0,6},{1,7},{2,4},{3,5},{4,2},{5,3},{6,0},{7,1},{8,14},{9,15},{10,... | collective-permute-start | bytes 1327112 | tf_op jit(solution)/shard_map/ppermute | solution.py:33
  59.2 12.2 %collective-permute-start.13 = (f32[2,4,24,576]{3,2,1,0:T(8,128)S(1)}, f32[2,4,24,576]{3,2,1,0:T(8,128)S(1)}, u32[]{:S(2)}, u32[]{:S(2)}) collective-permute-start(f32[2,4,24,576]{3,2,1,0:T(8,128)S(1)} %get-tuple-element.92), channel_id=1, source_target_pairs={{0,2},{1,3},{2,0},{3,1},{4,6},{5,7},{6,4},{7,5},{8,10},{9,11},{10,... | collective-permute-start | bytes 1327112 | tf_op jit(solution)/shard_map/ppermute | solution.py:33
  68.5 6.4 %collective-permute-start.19 = (f32[4,24,576]{2,1,0:T(8,128)S(1)}, f32[4,24,576]{2,1,0:T(8,128)S(1)}, u32[]{:S(2)}, u32[]{:S(2)}) collective-permute-start(f32[4,24,576]{2,1,0:T(8,128)S(1)} %fusion.3), channel_id=1, source_target_pairs={{0,64},{1,65},{2,66},{3,67},{4,68},{5,69},{6,70},{7,71},{8,72},{9,... | collective-permute-start | bytes 663560 | tf_op jit(solution)/shard_map/ppermute | solution.py:33
  69.6 7.2 %collective-permute-start.21 = (f32[4,24,576]{2,1,0:T(8,128)S(1)}, f32[4,24,576]{2,1,0:T(8,128)S(1)}, u32[]{:S(2)}, u32[]{:S(2)}) collective-permute-start(f32[4,24,576]{2,1,0:T(8,128)S(1)} %fusion), channel_id=1, source_target_pairs={{0,192},{1,193},{2,194},{3,195},{4,196},{5,197},{6,198},{7,199},{8... | collective-permute-start | bytes 663560 | tf_op jit(solution)/shard_map/ppermute | solution.py:33
  71.4 9.3 %collective-permute-start.12 = (f32[4,24,576]{2,1,0:T(8,128)S(1)}, f32[4,24,576]{2,1,0:T(8,128)S(1)}, u32[]{:S(2)}, u32[]{:S(2)}) collective-permute-start(f32[4,24,576]{2,1,0:T(8,128)S(1)} %fusion.9), channel_id=1, source_target_pairs={{0,2},{1,3},{2,0},{3,1},{4,6},{5,7},{6,4},{7,5},{8,10},{9,11},{10,... | collective-permute-start | bytes 663560 | tf_op jit(solution)/shard_map/ppermute | solution.py:33
  71.5 9.2 %collective-permute-start.14 = (f32[4,24,576]{2,1,0:T(8,128)S(1)}, f32[4,24,576]{2,1,0:T(8,128)S(1)}, u32[]{:S(2)}, u32[]{:S(2)}) collective-permute-start(f32[4,24,576]{2,1,0:T(8,128)S(1)} %fusion.6), channel_id=1, source_target_pairs={{0,6},{1,7},{2,4},{3,5},{4,2},{5,3},{6,0},{7,1},{8,14},{9,15},{10,... | collective-permute-start | bytes 663560 | tf_op jit(solution)/shard_map/ppermute | solution.py:33
  76.9 6.7 %collective-permute-start.22 = (f32[2,24,576]{2,1,0:T(8,128)S(1)}, f32[2,24,576]{2,1,0:T(8,128)S(1)}, u32[]{:S(2)}, u32[]{:S(2)}) collective-permute-start(f32[2,24,576]{2,1,0:T(8,128)S(1)} %pad_maximum_fusion.3), channel_id=1, source_target_pairs={{0,4},{1,5},{2,6},{3,7},{4,0},{5,1},{6,2},{7,3},{8,12},{9,13},{10,... | collective-permute-start | bytes 331784 | tf_op jit(solution)/shard_map/ppermute | solution.py:33
  78.5 6.0 %collective-permute-start.23 = (f32[2,24,576]{2,1,0:T(8,128)S(1)}, f32[2,24,576]{2,1,0:T(8,128)S(1)}, u32[]{:S(2)}, u32[]{:S(2)}) collective-permute-start(f32[2,24,576]{2,1,0:T(8,128)S(1)} %pad_maximum_fusion.4), channel_id=1, source_target_pairs={{0,2},{1,3},{2,0},{3,1},{4,6},{5,7},{6,4},{7,5},{8,10},{9,11},{10,... | collective-permute-start | bytes 331784 | tf_op jit(solution)/shard_map/ppermute | solution.py:33
  79.7 6.3 %collective-permute-start.24 = (f32[2,24,576]{2,1,0:T(8,128)S(1)}, f32[2,24,576]{2,1,0:T(8,128)S(1)}, u32[]{:S(2)}, u32[]{:S(2)}) collective-permute-start(f32[2,24,576]{2,1,0:T(8,128)S(1)} %pad_maximum_fusion.5), channel_id=1, source_target_pairs={{0,6},{1,7},{2,4},{3,5},{4,2},{5,3},{6,0},{7,1},{8,14},{9,15},{10,... | collective-permute-start | bytes 331784 | tf_op jit(solution)/shard_map/ppermute | solution.py:33
  80.8 5.3 %collective-permute-start.15 = (f32[2,24,576]{2,1,0:T(8,128)S(1)}, f32[2,24,576]{2,1,0:T(8,128)S(1)}, u32[]{:S(2)}, u32[]{:S(2)}) collective-permute-start(f32[2,24,576]{2,1,0:T(8,128)S(1)} %pad_maximum_fusion), channel_id=1, source_target_pairs={{0,128},{1,129},{2,130},{3,131},{4,132},{5,133},{6,134},{7,135},{8... | collective-permute-start | bytes 331784 | tf_op jit(solution)/shard_map/ppermute | solution.py:33
  82.6 4.8 %collective-permute-start.16 = (f32[2,24,576]{2,1,0:T(8,128)S(1)}, f32[2,24,576]{2,1,0:T(8,128)S(1)}, u32[]{:S(2)}, u32[]{:S(2)}) collective-permute-start(f32[2,24,576]{2,1,0:T(8,128)S(1)} %pad_maximum_fusion.1), channel_id=1, source_target_pairs={{0,64},{1,65},{2,66},{3,67},{4,68},{5,69},{6,70},{7,71},{8,72},{9,... | collective-permute-start | bytes 331784 | tf_op jit(solution)/shard_map/ppermute | solution.py:33
  83.6 5.3 %collective-permute-start.17 = (f32[2,24,576]{2,1,0:T(8,128)S(1)}, f32[2,24,576]{2,1,0:T(8,128)S(1)}, u32[]{:S(2)}, u32[]{:S(2)}) collective-permute-start(f32[2,24,576]{2,1,0:T(8,128)S(1)} %pad_maximum_fusion.2), channel_id=1, source_target_pairs={{0,192},{1,193},{2,194},{3,195},{4,196},{5,197},{6,198},{7,199},{8... | collective-permute-start | bytes 331784 | tf_op jit(solution)/shard_map/ppermute | solution.py:33
  89.1 5.2 %collective-permute-start.25 = (f32[12,1152]{1,0:T(8,128)S(1)}, f32[12,1152]{1,0:T(8,128)S(1)}, u32[]{:S(2)}, u32[]{:S(2)}) collective-permute-start(f32[12,1152]{1,0:T(8,128)S(1)} %get-tuple-element.97), channel_id=1, source_target_pairs={{0,24},{1,25},{2,26},{3,27},{4,28},{5,29},{6,30},{7,31},{8,16},{9,... | collective-permute-start | bytes 165896 | tf_op jit(solution)/shard_map/ppermute | solution.py:33
  90.8 5.3 %collective-permute-start.26 = (f32[12,1152]{1,0:T(8,128)S(1)}, f32[12,1152]{1,0:T(8,128)S(1)}, u32[]{:S(2)}, u32[]{:S(2)}) collective-permute-start(f32[12,1152]{1,0:T(8,128)S(1)} %get-tuple-element.99), channel_id=1, source_target_pairs={{0,16},{1,17},{2,18},{3,19},{4,20},{5,21},{6,22},{7,23},{8,24},{9,... | collective-permute-start | bytes 165896 | tf_op jit(solution)/shard_map/ppermute | solution.py:33
  92.0 4.1 %collective-permute-start.27 = (f32[12,1152]{1,0:T(8,128)S(1)}, f32[12,1152]{1,0:T(8,128)S(1)}, u32[]{:S(2)}, u32[]{:S(2)}) collective-permute-start(f32[12,1152]{1,0:T(8,128)S(1)} %get-tuple-element.98), channel_id=1, source_target_pairs={{0,8},{1,9},{2,10},{3,11},{4,12},{5,13},{6,14},{7,15},{8,0},{9,1},... | collective-permute-start | bytes 165896 | tf_op jit(solution)/shard_map/ppermute | solution.py:33
  96.4 11.7 %collective-permute-start.28 = (f32[12,576]{1,0:T(8,128)S(1)}, f32[12,576]{1,0:T(8,128)S(1)}, u32[]{:S(2)}, u32[]{:S(2)}) collective-permute-start(f32[12,576]{1,0:T(8,128)S(1)} %get-tuple-element.116), channel_id=1, source_target_pairs={{0,1},{1,49},{2,3},{3,51},{4,5},{5,53},{6,7},{7,55},{8,9},{9,57},{... | collective-permute-start | bytes 82952 | tf_op jit(solution)/shard_map/ppermute | solution.py:33
  99.1 10.6 %collective-permute-start.29 = (f32[12,576]{1,0:T(8,128)S(1)}, f32[12,576]{1,0:T(8,128)S(1)}, u32[]{:S(2)}, u32[]{:S(2)}) collective-permute-start(f32[12,576]{1,0:T(8,128)S(1)} %get-tuple-element.117), channel_id=1, source_target_pairs={{1,48},{3,50},{5,52},{7,54},{9,56},{11,58},{13,60},{15,62},{17,32}... | collective-permute-start | bytes 82952 | tf_op jit(solution)/shard_map/ppermute | solution.py:33

commit v6 on v5

--- a/solution.py
+++ b/solution.py
@@ -47,6 +47,14 @@
 
 def z_partner(m):
     return lambda y, z, x, c: (y, z ^ m, x, c)
+
+
+def first_partner(m):
+    return lambda y, z, x, c: (y, z, x ^ m, c) if c == 0 else (y ^ m, z, x, c)
+
+
+def second_partner(m):
+    return lambda y, z, x, c: (y ^ m, z, x, c) if c == 0 else (y, z, x ^ m, c)
 
 
 def last_near(y, z, x, c):
@@ -174,7 +182,7 @@
                     outer[part, side, x_to, y] = value[:, WIDTH:]
 
 
-COLUMNS = (((0, 0), (0, 1), (1, 0)), ((1, 1), (2, 0), (2, 1)))
+COLUMNS = tuple((w, side) for w in range(3) for side in range(2))
 ORDERS = ((0, 1, 3, 2), (0, 3, 1, 2))
 
 
@@ -192,20 +200,19 @@
     later = by_head(jnp.where(first, other[...], own[...]))
     steps = ((before, lanes_dot), (later, lanes_dot), (later, dot))
     for part in range(2):
-        for axis in range(2):
-            out = outs[part * 2 + axis]
-            for sa in range(2):
-                a = ORDERS[part][2 * half + sa]
-                at = [(px ^ a, py ^ b) if axis == 0 else (px ^ b, py ^ a) for b in range(4)]
-                pieces = []
-                for w, side in COLUMNS[axis]:
-                    state, multiply = steps[w]
-                    term = jnp.concatenate([outer[w][part, side, i, j] for i, j in at], axis=0)
-                    add = jnp.concatenate([inner[w][part, side, i, j] for i, j in at], axis=0)
-                    high = term.astype(BF16)
-                    low = (term - high.astype(F32)).astype(BF16)
-                    pieces.append(factor * (add + multiply(high, state) + multiply(low, state)))
-                out[sa] = jnp.concatenate(pieces, axis=1).reshape(out.shape[1:])
+        out = outs[part]
+        for sa in range(2):
+            a = ORDERS[part][2 * half + sa]
+            at = [(jnp.where(first, px ^ a, px ^ b), jnp.where(first, py ^ b, py ^ a)) for b in range(4)]
+            pieces = []
+            for w, side in COLUMNS:
+                state, multiply = steps[w]
+                term = jnp.concatenate([outer[w][part, side, i, j] for i, j in at], axis=0)
+                add = jnp.concatenate([inner[w][part, side, i, j] for i, j in at], axis=0)
+                high = term.astype(BF16)
+                low = (term - high.astype(F32)).astype(BF16)
+                pieces.append(factor * (add + multiply(high, state) + multiply(low, state)))
+            out[sa] = jnp.concatenate(pieces, axis=1).reshape(out.shape[1:])
 
 
 VMEM = pl.BlockSpec(memory_space=pltpu.VMEM)
@@ -282,9 +289,9 @@
     return pl.pallas_call(
         functools.partial(join_kernel, factor, half),
         name=f"join{half}",
-        out_shape=(jax.ShapeDtypeStruct((2, 4, 24, 3 * WIDTH), F32),) * 4,
+        out_shape=(jax.ShapeDtypeStruct((2, 4, 24, 6 * WIDTH), F32),) * 2,
         in_specs=[SMEM] + [VMEM] * 8,
-        out_specs=(VMEM,) * 4,
+        out_specs=(VMEM,) * 2,
         cost_estimate=cost(24 * 384 * 192 * 192, 8 * 10**6),
         compiler_params=limit(20),
     )(place, own, other, *inner, *outer)
@@ -317,29 +324,22 @@
 
 def scatter_sum(me, keep, send):
     y, z, x, c = me
-    partners = (x_partner, y_partner)
-    streams = [(part, axis) for part in range(2) for axis in range(2)]
-    one = {}
-    for n, (part, axis) in enumerate(streams):
-        came = permute(send[n], partners[axis]((3, 1)[part]))
-        one[n] = (keep[n][0] + came[0], keep[n][1] + came[1])
-    ends = {}
-    for n, (part, axis) in enumerate(streams):
-        ends[part, axis] = one[n][0] + permute(one[n][1], partners[axis]((1, 3)[part]))
-    chunk = lambda axis, r: jnp.stack([ends[part, axis][r] for part in range(2)])
-    value = [chunk(axis, 0) for axis in range(2)]
+    one = []
+    for part in range(2):
+        came = permute(send[part], first_partner((3, 1)[part]))
+        one.append((keep[part][0] + came[0], keep[part][1] + came[1]))
+    ends = [one[part][0] + permute(one[part][1], first_partner((1, 3)[part])) for part in range(2)]
+    chunk = lambda r: jnp.stack([end[r] for end in ends])
+    value = chunk(0)
     for r in (2, 1, 3):
-        for axis in range(2):
-            value[axis] = value[axis] + permute(chunk(axis, r), partners[1 - axis](r))
-    value = jnp.concatenate(value, axis=2)
+        value = value + permute(chunk(r), second_partner(r))
     chunk = lambda r: value[r >> 1, 12 * (r & 1) : 12 * (r & 1) + 12]
     total = chunk(0)
     for r in (3, 2, 1):
         total = total + permute(chunk(r), z_partner(r))
-    order = COLUMNS[0] + COLUMNS[1]
     column = lambda n: total[:, n * WIDTH : (n + 1) * WIDTH]
     sides = [
-        jnp.concatenate([column(order.index((w, side))) for w in range(3)], axis=1) for side in range(2)
+        jnp.concatenate([column(COLUMNS.index((w, side))) for w in range(3)], axis=1) for side in range(2)
     ]
     block = lambda i: jnp.where(i == 0, *sides)
     same = z >> 2 == c

time: 111 us -> 109 us (0.982)
  starting transfers between devices: 53.5 us -> 45.2 us
  waiting for transfers between devices: 27.7 us -> 34 us
    ppermute x30 -> x23, starting transfers between devices: 53.5 us -> 45.2 us  [permute(): return lax.ppermute(value, SEQ, pairs)]
    ppermute x30 -> x23, waiting for transfers between devices: 27.7 us -> 34 us  [permute(): return lax.ppermute(value, SEQ, pairs)]
  transfers between devices with their start and end apart: 30 -> 23, of which waited for: 15 -> 14; matrix products, arithmetic and copies ran while one was open for 1% -> 1% of each run, Pallas kernels for 17% -> 17%
where the time goes in v6:
time: 109 us
  starting transfers between devices  45.2 us (41%)
  waiting for transfers between devices  34 us (31%)
  Pallas kernels  24 us (22%)
  local copies, waits for them, and re-layouts  2.26 us (2%)
  other arithmetic  2.16 us (2%)
    ppermute x23, starting transfers between devices, permute(): return lax.ppermute(value, SEQ, pairs)  45.2 us
    ppermute x23, waiting for transfers between devices, permute(): return lax.ppermute(value, SEQ, pairs)  34 us
    pallas_call x3, Pallas kernels, terms(): pl.pallas_call(terms_kernel, name='terms', out_shape=(shape, shape), in_s...  7.9 us
    pallas_call x1, Pallas kernels, local_terms(): pl.pallas_call(local_kernel, name='local_terms', out_shape=(shape,) * 3,...  4.55 us
    pallas_call x2, Pallas kernels, join(): pl.pallas_call(functools.partial(join_kernel, factor, half), name=f'join{...  4.54 us
    pallas_call x1, Pallas kernels, halves(): pl.pallas_call(halves_kernel, name='halves', out_shape=(jax.ShapeDtypeStr...  4.2 us
    pallas_call x1, Pallas kernels, states(): pl.pallas_call(states_kernel, name='states', out_shape=(shape, shape, jax...  2.81 us
  transfers between devices with their start and end apart: 23, of which 14 were waited for; matrix products, arithmetic and copies ran while one was open for 1% of the time, Pallas kernels for 17%

profile of v6, /device:TPU:1, one launch (start us, length us, event | category | flops | bytes accessed | tf_op | source)
XLA Modules:
  0.0 108.5 jit_solution(14163696207555389658)
XLA Ops:
  0.6 2.8 %states.1 = (f32[144,128]{1,0:T(8,128)}, f32[144,128]{1,0:T(8,128)}, f32[4,192,512]{2,1,0:T(8,128)}) custom-call(bf16[192,512]{1,0:T(8,128)(2,1)} %bitcast.34, bf16[192,512]{1,0:T(8,128)(2,1)} %bitcast.35, bf16[192,512]{1,0:T(8,128)(2,1)} %bitcast.36, bf16[192,512]{1,0:T(8,128)(2,1)} %bitcast.37), custom_call_target="tpu_custom_call" | custom-call | flops 75497472 | bytes 1000000 | tf_op jit(solution)/shard_map/states/pallas_call | solution.py:234
  3.4 3.3 %collective-permute-start = (f32[144,128]{1,0:T(8,128)}, f32[144,128]{1,0:T(8,128)S(1)}, u32[]{:S(2)}, u32[]{:S(2)}) collective-permute-start(f32[144,128]{1,0:T(8,128)} %get-tuple-element.47), channel_id=1, source_target_pairs={{0,1},{1,0},{2,3},{3,2},{4,5},{5,4},{6,7},{7,6},{8,9},{9,8},{10,11... | collective-permute-start | bytes 221192 | tf_op jit(solution)/shard_map/ppermute | solution.py:33
  6.8 1.1 %collective-permute-done = f32[144,128]{1,0:T(8,128)S(1)} collective-permute-done((f32[144,128]{1,0:T(8,128)}, f32[144,128]{1,0:T(8,128)S(1)}, u32[]{:S(2)}, u32[]{:S(2)}) %collective-permute-start) | collective-permute-done | bytes 73760 | tf_op jit(solution)/shard_map/ppermute | solution.py:33
  7.9 0.9 add.93
  8.8 0.1 collective-permute-start.1
  8.9 0.6 pad_add_fusion.place
  9.5 4.2 %halves.1 = (bf16[4,512,384]{2,1,0:T(8,128)(2,1)}, f32[4,512,384]{2,1,0:T(8,128)}) custom-call(s32[4]{0:T(128)} %pad_add_fusion.place, bf16[512,3072]{1,0:T(8,128)(2,1)} %x), custom_call_target="tpu_custom_call" | custom-call | flops 1000000 | bytes 5000000 | tf_op jit(solution)/shard_map/halves/pallas_call | solution.py:248
  13.7 0.4 collective-permute-start.7
  14.2 0.2 collective-permute-start.5
  14.3 1.6 %collective-permute-start.2 = (f32[144,128]{1,0:T(8,128)S(1)}, f32[144,128]{1,0:T(8,128)S(1)}, u32[]{:S(2)}, u32[]{:S(2)}) collective-permute-start(f32[144,128]{1,0:T(8,128)S(1)} %add.94), channel_id=1, source_target_pairs={{0,6},{1,7},{2,4},{3,5},{4,2},{5,3},{6,0},{7,1},{8,14},{9,15},{10,... | collective-permute-start | bytes 221192 | tf_op jit(solution)/shard_map/ppermute | solution.py:33
  15.9 2.9 %collective-permute-done.2 = f32[144,128]{1,0:T(8,128)S(1)} collective-permute-done((f32[144,128]{1,0:T(8,128)S(1)}, f32[144,128]{1,0:T(8,128)S(1)}, u32[]{:S(2)}, u32[]{:S(2)}) %collective-permute-start.2) | collective-permute-done | bytes 73760 | tf_op jit(solution)/shard_map/ppermute | solution.py:33
  18.9 1.4 %collective-permute-start.3 = (f32[144,128]{1,0:T(8,128)S(1)}, f32[144,128]{1,0:T(8,128)S(1)}, u32[]{:S(2)}, u32[]{:S(2)}) collective-permute-start(f32[144,128]{1,0:T(8,128)S(1)} %add.96), channel_id=1, source_target_pairs={{0,8},{1,9},{2,10},{3,11},{4,12},{5,13},{6,14},{7,15},{8,0},{9,1},... | collective-permute-start | bytes 221192 | tf_op jit(solution)/shard_map/ppermute | solution.py:33
  20.3 1.9 %collective-permute-done.3 = f32[144,128]{1,0:T(8,128)S(1)} collective-permute-done((f32[144,128]{1,0:T(8,128)S(1)}, f32[144,128]{1,0:T(8,128)S(1)}, u32[]{:S(2)}, u32[]{:S(2)}) %collective-permute-start.3) | collective-permute-done | bytes 73760 | tf_op jit(solution)/shard_map/ppermute | solution.py:33
  22.2 2.9 %collective-permute-start.4 = (f32[144,128]{1,0:T(8,128)S(1)}, f32[144,128]{1,0:T(8,128)S(1)}, u32[]{:S(2)}, u32[]{:S(2)}) collective-permute-start(f32[144,128]{1,0:T(8,128)S(1)} %add.98), channel_id=1, source_target_pairs={{0,16},{1,17},{2,18},{3,19},{4,20},{5,21},{6,22},{7,23},{8,24},{9,... | collective-permute-start | bytes 221192 | tf_op jit(solution)/shard_map/ppermute | solution.py:33
  25.1 1.4 %copy-done.2 = f32[4,192,512]{2,1,0:T(8,128)S(1)} copy-done((f32[4,192,512]{2,1,0:T(8,128)S(1)}, f32[4,192,512]{2,1,0:T(8,128)}, u32[]{:S(2)}) %copy-start.2) | copy-done | bytes 1572888
  26.5 4.5 %local_terms.1 = (bf16[2,384,512]{2,1,0:T(8,128)(2,1)S(1)}, bf16[2,384,512]{2,1,0:T(8,128)(2,1)S(1)}, bf16[2,384,512]{2,1,0:T(8,128)(2,1)S(1)}) custom-call(s32[4]{0:T(128)S(1)} %copy-done.1, f32[4,192,512]{2,1,0:T(8,128)S(1)} %copy-done.2, f32[4,192,512]{2,1,0:T(8,128)} %collective-permute-done.5.other), custom_call_target="tpu_custom_call" | custom-call | flops 1006632960 | bytes 5000000 | tf_op jit(solution)/shard_map/local_terms/pallas_call | solution.py:263
  31.1 4.1 %collective-permute-start.6 = (f32[144,128]{1,0:T(8,128)S(1)}, f32[144,128]{1,0:T(8,128)S(1)}, u32[]{:S(2)}, u32[]{:S(2)}) collective-permute-start(f32[144,128]{1,0:T(8,128)S(1)} %add.100), channel_id=1, source_target_pairs={{0,48},{1,49},{2,50},{3,51},{4,52},{5,53},{6,54},{7,55},{8,56},{9,... | collective-permute-start | bytes 221192 | tf_op jit(solution)/shard_map/ppermute | solution.py:33
  35.2 2.6 %terms.3 = (f32[2,2,4,4,24,192]{5,4,3,2,1,0:T(8,128)S(1)}, f32[2,2,4,4,24,192]{5,4,3,2,1,0:T(8,128)S(1)}) custom-call(s32[4]{0:T(128)S(1)} %copy-done.1, bf16[4,512,384]{2,1,0:T(8,128)(2,1)S(1)} %copy-done, f32[4,512,384]{2,1,0:T(8,128)S(1)} %collective-permute-done.7.wide, bf16[2,384,512]{2,1,0:T(8,128)(2,1)S(1)} %get-tuple-element.63.d), custom_call_target="tpu_custom_call" | custom-call | flops 1207959552 | bytes 8000000 | tf_op jit(solution)/shard_map/terms/pallas_call | solution.py:276
  37.9 1.6 %collective-permute-start.8 = (f32[144,128]{1,0:T(8,128)S(1)}, f32[144,128]{1,0:T(8,128)S(1)}, u32[]{:S(2)}, u32[]{:S(2)}) collective-permute-start(f32[144,128]{1,0:T(8,128)S(1)} %add.102), channel_id=1, source_target_pairs={{0,64},{1,65},{2,66},{3,67},{4,68},{5,69},{6,70},{7,71},{8,72},{9,... | collective-permute-start | bytes 221192 | tf_op jit(solution)/shard_map/ppermute | solution.py:33
  39.5 2.6 %terms.4 = (f32[2,2,4,4,24,192]{5,4,3,2,1,0:T(8,128)S(1)}, f32[2,2,4,4,24,192]{5,4,3,2,1,0:T(8,128)S(1)}) custom-call(s32[4]{0:T(128)S(1)} %copy-done.1, bf16[4,512,384]{2,1,0:T(8,128)(2,1)S(1)} %copy-done, f32[4,512,384]{2,1,0:T(8,128)S(1)} %collective-permute-done.7.wide, bf16[2,384,512]{2,1,0:T(8,128)(2,1)S(1)} %get-tuple-element.69.d), custom_call_target="tpu_custom_call" | custom-call | flops 1207959552 | bytes 8000000 | tf_op jit(solution)/shard_map/terms/pallas_call | solution.py:276
  42.1 2.1 %collective-permute-start.9 = (f32[144,128]{1,0:T(8,128)S(1)}, f32[144,128]{1,0:T(8,128)S(1)}, u32[]{:S(2)}, u32[]{:S(2)}) collective-permute-start(f32[144,128]{1,0:T(8,128)S(1)} %add.104), channel_id=1, source_target_pairs={{0,192},{1,193},{2,194},{3,195},{4,196},{5,197},{6,198},{7,199},{8... | collective-permute-start | bytes 221192 | tf_op jit(solution)/shard_map/ppermute | solution.py:33
  44.2 2.6 %terms.5 = (f32[2,2,4,4,24,192]{5,4,3,2,1,0:T(8,128)S(1)}, f32[2,2,4,4,24,192]{5,4,3,2,1,0:T(8,128)S(1)}) custom-call(s32[4]{0:T(128)S(1)} %copy-done.1, bf16[4,512,384]{2,1,0:T(8,128)(2,1)S(1)} %copy-done, f32[4,512,384]{2,1,0:T(8,128)S(1)} %collective-permute-done.7.wide, bf16[2,384,512]{2,1,0:T(8,128)(2,1)S(1)} %get-tuple-element.75.d), custom_call_target="tpu_custom_call" | custom-call | flops 1207959552 | bytes 8000000 | tf_op jit(solution)/shard_map/terms/pallas_call | solution.py:276
  46.9 4.8 %collective-permute-start.10 = (f32[144,128]{1,0:T(8,128)S(1)}, f32[144,128]{1,0:T(8,128)S(1)}, u32[]{:S(2)}, u32[]{:S(2)}) collective-permute-start(f32[144,128]{1,0:T(8,128)S(1)} %select_add_fusion.own), channel_id=1, source_target_pairs={{0,1},{1,0},{2,3},{3,2},{4,5},{5,4},{6,7},{7,6},{8,9},{9,8},{10,11... | collective-permute-start | bytes 221192 | tf_op jit(solution)/shard_map/ppermute | solution.py:33
  51.7 0.9 collective-permute-done.10.other
  52.6 2.3 %join1.1 = (f32[2,4,24,1152]{3,2,1,0:T(8,128)S(1)}, f32[2,4,24,1152]{3,2,1,0:T(8,128)S(1)}) custom-call(s32[4]{0:T(128)S(1)} %copy-done.1, f32[144,128]{1,0:T(8,128)S(1)} %select_add_fusion.own, f32[144,128]{1,0:T(8,128)S(1)} %collective-permute-done.10.other, f32[2,2,4,4,24,192]{5,4,3,2,1,0:T(8,128)S(1)} %get-tuple-element.79.refs_0_, ...), custom_call_target="tpu_custom_call" | custom-call | flops 339738624 | bytes 8000000 | tf_op jit(solution)/shard_map/join1/pallas_call | solution.py:289
  54.9 2.7 %collective-permute-start.11 = (f32[2,4,24,1152]{3,2,1,0:T(8,128)S(1)}, f32[2,4,24,1152]{3,2,1,0:T(8,128)S(1)}, u32[]{:S(2)}, u32[]{:S(2)}) collective-permute-start(f32[2,4,24,1152]{3,2,1,0:T(8,128)S(1)} %get-tuple-element.86), channel_id=1, source_target_pairs={{0,6},{1,193},{2,4},{3,195},{4,2},{5,197},{6,0},{7,199},{8,14},{9,... | collective-permute-start | bytes 2654216 | tf_op jit(solution)/shard_map/ppermute | solution.py:33
  57.6 2.3 %join0.1 = (f32[2,4,24,1152]{3,2,1,0:T(8,128)S(1)}, f32[2,4,24,1152]{3,2,1,0:T(8,128)S(1)}) custom-call(s32[4]{0:T(128)S(1)} %copy-done.1, f32[144,128]{1,0:T(8,128)S(1)} %select_add_fusion.own, f32[144,128]{1,0:T(8,128)S(1)} %collective-permute-done.10.other, f32[2,2,4,4,24,192]{5,4,3,2,1,0:T(8,128)S(1)} %get-tuple-element.79.refs_0_, ...), custom_call_target="tpu_custom_call" | custom-call | flops 339738624 | bytes 8000000 | tf_op jit(solution)/shard_map/join0/pallas_call | solution.py:289
  59.9 8.5 %collective-permute-done.11 = f32[2,4,24,1152]{3,2,1,0:T(8,128)S(1)} collective-permute-done((f32[2,4,24,1152]{3,2,1,0:T(8,128)S(1)}, f32[2,4,24,1152]{3,2,1,0:T(8,128)S(1)}, u32[]{:S(2)}, u32[]{:S(2)}) %collective-permute-start.11) | collective-permute-done | bytes 884768 | tf_op jit(solution)/shard_map/ppermute | solution.py:33
  68.5 0.1 collective-permute-start.12
  68.6 1.3 %collective-permute-done.13 = f32[2,4,24,1152]{3,2,1,0:T(8,128)S(1)} collective-permute-done((f32[2,4,24,1152]{3,2,1,0:T(8,128)S(1)}, f32[2,4,24,1152]{3,2,1,0:T(8,128)S(1)}, u32[]{:S(2)}, u32[]{:S(2)}) %collective-permute-start.13) | collective-permute-done | bytes 884768 | tf_op jit(solution)/shard_map/ppermute | solution.py:33
  69.9 1.5 %collective-permute-start.14 = (f32[4,24,1152]{2,1,0:T(8,128)S(1)}, f32[4,24,1152]{2,1,0:T(8,128)S(1)}, u32[]{:S(2)}, u32[]{:S(2)}) collective-permute-start(f32[4,24,1152]{2,1,0:T(8,128)S(1)} %fusion), channel_id=1, source_target_pairs={{0,6},{1,193},{2,4},{3,195},{4,2},{5,197},{6,0},{7,199},{8,14},{9,... | collective-permute-start | bytes 1327112 | tf_op jit(solution)/shard_map/ppermute | solution.py:33
  71.3 4.7 %collective-permute-done.12 = f32[4,24,1152]{2,1,0:T(8,128)S(1)} collective-permute-done((f32[4,24,1152]{2,1,0:T(8,128)S(1)}, f32[4,24,1152]{2,1,0:T(8,128)S(1)}, u32[]{:S(2)}, u32[]{:S(2)}) %collective-permute-start.12) | collective-permute-done | bytes 442400 | tf_op jit(solution)/shard_map/ppermute | solution.py:33
  76.1 2.5 %collective-permute-done.14 = f32[4,24,1152]{2,1,0:T(8,128)S(1)} collective-permute-done((f32[4,24,1152]{2,1,0:T(8,128)S(1)}, f32[4,24,1152]{2,1,0:T(8,128)S(1)}, u32[]{:S(2)}, u32[]{:S(2)}) %collective-permute-start.14) | collective-permute-done | bytes 442400 | tf_op jit(solution)/shard_map/ppermute | solution.py:33
  78.8 0.7 collective-permute-start.15
  79.5 1.5 %collective-permute-start.16 = (f32[2,24,1152]{2,1,0:T(8,128)S(1)}, f32[2,24,1152]{2,1,0:T(8,128)S(1)}, u32[]{:S(2)}, u32[]{:S(2)}) collective-permute-start(f32[2,24,1152]{2,1,0:T(8,128)S(1)} %pad_maximum_fusion.1), channel_id=1, source_target_pairs={{0,64},{1,3},{2,66},{3,1},{4,68},{5,7},{6,70},{7,5},{8,72},{9,11},... | collective-permute-start | bytes 663560 | tf_op jit(solution)/shard_map/ppermute | solution.py:33
  81.1 1.2 %collective-permute-start.17 = (f32[2,24,1152]{2,1,0:T(8,128)S(1)}, f32[2,24,1152]{2,1,0:T(8,128)S(1)}, u32[]{:S(2)}, u32[]{:S(2)}) collective-permute-start(f32[2,24,1152]{2,1,0:T(8,128)S(1)} %pad_maximum_fusion.2), channel_id=1, source_target_pairs={{0,192},{1,7},{2,194},{3,5},{4,196},{5,3},{6,198},{7,1},{8,200},{9... | collective-permute-start | bytes 663560 | tf_op jit(solution)/shard_map/ppermute | solution.py:33
  82.3 3.1 %collective-permute-done.15 = f32[2,24,1152]{2,1,0:T(8,128)S(1)} collective-permute-done((f32[2,24,1152]{2,1,0:T(8,128)S(1)}, f32[2,24,1152]{2,1,0:T(8,128)S(1)}, u32[]{:S(2)}, u32[]{:S(2)}) %collective-permute-start.15) | collective-permute-done | bytes 221216 | tf_op jit(solution)/shard_map/ppermute | solution.py:33
  85.4 1.5 %collective-permute-done.16 = f32[2,24,1152]{2,1,0:T(8,128)S(1)} collective-permute-done((f32[2,24,1152]{2,1,0:T(8,128)S(1)}, f32[2,24,1152]{2,1,0:T(8,128)S(1)}, u32[]{:S(2)}, u32[]{:S(2)}) %collective-permute-start.16) | collective-permute-done | bytes 221216 | tf_op jit(solution)/shard_map/ppermute | solution.py:33
  86.9 0.6 collective-permute-done.17
  87.6 1.7 %collective-permute-start.18 = (f32[12,1152]{1,0:T(8,128)S(1)}, f32[12,1152]{1,0:T(8,128)S(1)}, u32[]{:S(2)}, u32[]{:S(2)}) collective-permute-start(f32[12,1152]{1,0:T(8,128)S(1)} %get-tuple-element.97), channel_id=1, source_target_pairs={{0,24},{1,25},{2,26},{3,27},{4,28},{5,29},{6,30},{7,31},{8,16},{9,... | collective-permute-start | bytes 165896 | tf_op jit(solution)/shard_map/ppermute | solution.py:33
  89.3 1.2 %collective-permute-start.19 = (f32[12,1152]{1,0:T(8,128)S(1)}, f32[12,1152]{1,0:T(8,128)S(1)}, u32[]{:S(2)}, u32[]{:S(2)}) collective-permute-start(f32[12,1152]{1,0:T(8,128)S(1)} %get-tuple-element.99), channel_id=1, source_target_pairs={{0,16},{1,17},{2,18},{3,19},{4,20},{5,21},{6,22},{7,23},{8,24},{9,... | collective-permute-start | bytes 165896 | tf_op jit(solution)/shard_map/ppermute | solution.py:33
  90.5 0.7 collective-permute-start.20
  91.2 1.6 %collective-permute-done.18 = f32[12,1152]{1,0:T(8,128)S(1)} collective-permute-done((f32[12,1152]{1,0:T(8,128)S(1)}, f32[12,1152]{1,0:T(8,128)S(1)}, u32[]{:S(2)}, u32[]{:S(2)}) %collective-permute-start.18) | collective-permute-done | bytes 55328 | tf_op jit(solution)/shard_map/ppermute | solution.py:33
  92.8 1.8 %collective-permute-done.19 = f32[12,1152]{1,0:T(8,128)S(1)} collective-permute-done((f32[12,1152]{1,0:T(8,128)S(1)}, f32[12,1152]{1,0:T(8,128)S(1)}, u32[]{:S(2)}, u32[]{:S(2)}) %collective-permute-start.19) | collective-permute-done | bytes 55328 | tf_op jit(solution)/shard_map/ppermute | solution.py:33
  94.8 2.8 %collective-permute-start.21 = (f32[12,576]{1,0:T(8,128)S(1)}, f32[12,576]{1,0:T(8,128)S(1)}, u32[]{:S(2)}, u32[]{:S(2)}) collective-permute-start(f32[12,576]{1,0:T(8,128)S(1)} %get-tuple-element.100), channel_id=1, source_target_pairs={{0,1},{1,49},{2,3},{3,51},{4,5},{5,53},{6,7},{7,55},{8,9},{9,57},{... | collective-permute-start | bytes 82952 | tf_op jit(solution)/shard_map/ppermute | solution.py:33
  97.6 8.5 %collective-permute-start.22 = (f32[12,576]{1,0:T(8,128)S(1)}, f32[12,576]{1,0:T(8,128)S(1)}, u32[]{:S(2)}, u32[]{:S(2)}) collective-permute-start(f32[12,576]{1,0:T(8,128)S(1)} %get-tuple-element.101), channel_id=1, source_target_pairs={{1,48},{3,50},{5,52},{7,54},{9,56},{11,58},{13,60},{15,62},{17,32}... | collective-permute-start | bytes 82952 | tf_op jit(solution)/shard_map/ppermute | solution.py:33
  106.1 1.7 %collective-permute-done.22 = f32[12,576]{1,0:T(8,128)S(1)} collective-permute-done((f32[12,576]{1,0:T(8,128)S(1)}, f32[12,576]{1,0:T(8,128)S(1)}, u32[]{:S(2)}, u32[]{:S(2)}) %collective-permute-start.22) | collective-permute-done | bytes 27680 | tf_op jit(solution)/shard_map/ppermute | solution.py:33
  107.9 0.7 fusion.14
  (37 shorter events, 0.8 us)
Async XLA Ops:
  3.4 4.5 %collective-permute-start = (f32[144,128]{1,0:T(8,128)}, f32[144,128]{1,0:T(8,128)S(1)}, u32[]{:S(2)}, u32[]{:S(2)}) collective-permute-start(f32[144,128]{1,0:T(8,128)} %get-tuple-element.47), channel_id=1, source_target_pairs={{0,1},{1,0},{2,3},{3,2},{4,5},{5,4},{6,7},{7,6},{8,9},{9,8},{10,11... | collective-permute-start | bytes 221192 | tf_op jit(solution)/shard_map/ppermute | solution.py:33
  8.8 4.9 %collective-permute-start.1 = (f32[144,128]{1,0:T(8,128)S(1)}, f32[144,128]{1,0:T(8,128)S(1)}, u32[]{:S(2)}, u32[]{:S(2)}) collective-permute-start(f32[144,128]{1,0:T(8,128)S(1)} %add.93), channel_id=1, source_target_pairs={{0,2},{1,3},{2,0},{3,1},{4,6},{5,7},{6,4},{7,5},{8,10},{9,11},{10,... | collective-permute-start | bytes 221192 | tf_op jit(solution)/shard_map/ppermute | solution.py:33
  9.5 15.6 %copy-start.1 = (s32[4]{0:T(128)S(1)}, s32[4]{0:T(128)}, u32[]{:S(2)}) copy-start(s32[4]{0:T(128)} %pad_add_fusion.place) | copy-start | bytes 52
  13.7 21.5 %collective-permute-start.7 = (f32[4,512,384]{2,1,0:T(8,128)}, f32[4,512,384]{2,1,0:T(8,128)S(1)}, u32[]{:S(2)}, u32[]{:S(2)}) collective-permute-start(f32[4,512,384]{2,1,0:T(8,128)} %get-tuple-element.61), channel_id=1, source_target_pairs={{0,1},{1,0},{2,3},{3,2},{4,5},{5,4},{6,7},{7,6},{8,9},{9,8},{10,11... | collective-permute-start | bytes 9437192 | tf_op jit(solution)/shard_map/ppermute | solution.py:33
  14.2 10.9 %collective-permute-start.5 = (f32[4,192,512]{2,1,0:T(8,128)}, f32[4,192,512]{2,1,0:T(8,128)}, u32[]{:S(2)}, u32[]{:S(2)}) collective-permute-start(f32[4,192,512]{2,1,0:T(8,128)} %get-tuple-element.53.own), channel_id=1, source_target_pairs={{0,1},{1,0},{2,3},{3,2},{4,5},{5,4},{6,7},{7,6},{8,9},{9,8},{10,11... | collective-permute-start | bytes 4718600 | tf_op jit(solution)/shard_map/ppermute | solution.py:33
  14.3 4.5 %collective-permute-start.2 = (f32[144,128]{1,0:T(8,128)S(1)}, f32[144,128]{1,0:T(8,128)S(1)}, u32[]{:S(2)}, u32[]{:S(2)}) collective-permute-start(f32[144,128]{1,0:T(8,128)S(1)} %add.94), channel_id=1, source_target_pairs={{0,6},{1,7},{2,4},{3,5},{4,2},{5,3},{6,0},{7,1},{8,14},{9,15},{10,... | collective-permute-start | bytes 221192 | tf_op jit(solution)/shard_map/ppermute | solution.py:33
  18.9 3.3 %collective-permute-start.3 = (f32[144,128]{1,0:T(8,128)S(1)}, f32[144,128]{1,0:T(8,128)S(1)}, u32[]{:S(2)}, u32[]{:S(2)}) collective-permute-start(f32[144,128]{1,0:T(8,128)S(1)} %add.96), channel_id=1, source_target_pairs={{0,8},{1,9},{2,10},{3,11},{4,12},{5,13},{6,14},{7,15},{8,0},{9,1},... | collective-permute-start | bytes 221192 | tf_op jit(solution)/shard_map/ppermute | solution.py:33
  22.2 13.1 %copy-start = (bf16[4,512,384]{2,1,0:T(8,128)(2,1)S(1)}, bf16[4,512,384]{2,1,0:T(8,128)(2,1)}, u32[]{:S(2)}) copy-start(bf16[4,512,384]{2,1,0:T(8,128)(2,1)} %get-tuple-element.60.x) | copy-start | bytes 4718596
  22.2 8.9 %collective-permute-start.4 = (f32[144,128]{1,0:T(8,128)S(1)}, f32[144,128]{1,0:T(8,128)S(1)}, u32[]{:S(2)}, u32[]{:S(2)}) collective-permute-start(f32[144,128]{1,0:T(8,128)S(1)} %add.98), channel_id=1, source_target_pairs={{0,16},{1,17},{2,18},{3,19},{4,20},{5,21},{6,22},{7,23},{8,24},{9,... | collective-permute-start | bytes 221192 | tf_op jit(solution)/shard_map/ppermute | solution.py:33
  25.1 1.4 %copy-start.2 = (f32[4,192,512]{2,1,0:T(8,128)S(1)}, f32[4,192,512]{2,1,0:T(8,128)}, u32[]{:S(2)}) copy-start(f32[4,192,512]{2,1,0:T(8,128)} %get-tuple-element.53.own) | copy-start | bytes 4718596
  31.1 6.8 %collective-permute-start.6 = (f32[144,128]{1,0:T(8,128)S(1)}, f32[144,128]{1,0:T(8,128)S(1)}, u32[]{:S(2)}, u32[]{:S(2)}) collective-permute-start(f32[144,128]{1,0:T(8,128)S(1)} %add.100), channel_id=1, source_target_pairs={{0,48},{1,49},{2,50},{3,51},{4,52},{5,53},{6,54},{7,55},{8,56},{9,... | collective-permute-start | bytes 221192 | tf_op jit(solution)/shard_map/ppermute | solution.py:33
  37.9 4.2 %collective-permute-start.8 = (f32[144,128]{1,0:T(8,128)S(1)}, f32[144,128]{1,0:T(8,128)S(1)}, u32[]{:S(2)}, u32[]{:S(2)}) collective-permute-start(f32[144,128]{1,0:T(8,128)S(1)} %add.102), channel_id=1, source_target_pairs={{0,64},{1,65},{2,66},{3,67},{4,68},{5,69},{6,70},{7,71},{8,72},{9,... | collective-permute-start | bytes 221192 | tf_op jit(solution)/shard_map/ppermute | solution.py:33
  42.1 4.7 %collective-permute-start.9 = (f32[144,128]{1,0:T(8,128)S(1)}, f32[144,128]{1,0:T(8,128)S(1)}, u32[]{:S(2)}, u32[]{:S(2)}) collective-permute-start(f32[144,128]{1,0:T(8,128)S(1)} %add.104), channel_id=1, source_target_pairs={{0,192},{1,193},{2,194},{3,195},{4,196},{5,197},{6,198},{7,199},{8... | collective-permute-start | bytes 221192 | tf_op jit(solution)/shard_map/ppermute | solution.py:33
  46.9 5.7 %collective-permute-start.10 = (f32[144,128]{1,0:T(8,128)S(1)}, f32[144,128]{1,0:T(8,128)S(1)}, u32[]{:S(2)}, u32[]{:S(2)}) collective-permute-start(f32[144,128]{1,0:T(8,128)S(1)} %select_add_fusion.own), channel_id=1, source_target_pairs={{0,1},{1,0},{2,3},{3,2},{4,5},{5,4},{6,7},{7,6},{8,9},{9,8},{10,11... | collective-permute-start | bytes 221192 | tf_op jit(solution)/shard_map/ppermute | solution.py:33
  54.9 13.5 %collective-permute-start.11 = (f32[2,4,24,1152]{3,2,1,0:T(8,128)S(1)}, f32[2,4,24,1152]{3,2,1,0:T(8,128)S(1)}, u32[]{:S(2)}, u32[]{:S(2)}) collective-permute-start(f32[2,4,24,1152]{3,2,1,0:T(8,128)S(1)} %get-tuple-element.86), channel_id=1, source_target_pairs={{0,6},{1,193},{2,4},{3,195},{4,2},{5,197},{6,0},{7,199},{8,14},{9,... | collective-permute-start | bytes 2654216 | tf_op jit(solution)/shard_map/ppermute | solution.py:33
  57.6 12.2 %collective-permute-start.13 = (f32[2,4,24,1152]{3,2,1,0:T(8,128)S(1)}, f32[2,4,24,1152]{3,2,1,0:T(8,128)S(1)}, u32[]{:S(2)}, u32[]{:S(2)}) collective-permute-start(f32[2,4,24,1152]{3,2,1,0:T(8,128)S(1)} %get-tuple-element.88), channel_id=1, source_target_pairs={{0,2},{1,65},{2,0},{3,67},{4,6},{5,69},{6,4},{7,71},{8,10},{9,73},... | collective-permute-start | bytes 2654216 | tf_op jit(solution)/shard_map/ppermute | solution.py:33
  68.5 7.5 %collective-permute-start.12 = (f32[4,24,1152]{2,1,0:T(8,128)S(1)}, f32[4,24,1152]{2,1,0:T(8,128)S(1)}, u32[]{:S(2)}, u32[]{:S(2)}) collective-permute-start(f32[4,24,1152]{2,1,0:T(8,128)S(1)} %fusion.3), channel_id=1, source_target_pairs={{0,2},{1,65},{2,0},{3,67},{4,6},{5,69},{6,4},{7,71},{8,10},{9,73},... | collective-permute-start | bytes 1327112 | tf_op jit(solution)/shard_map/ppermute | solution.py:33
  69.9 8.7 %collective-permute-start.14 = (f32[4,24,1152]{2,1,0:T(8,128)S(1)}, f32[4,24,1152]{2,1,0:T(8,128)S(1)}, u32[]{:S(2)}, u32[]{:S(2)}) collective-permute-start(f32[4,24,1152]{2,1,0:T(8,128)S(1)} %fusion), channel_id=1, source_target_pairs={{0,6},{1,193},{2,4},{3,195},{4,2},{5,197},{6,0},{7,199},{8,14},{9,... | collective-permute-start | bytes 1327112 | tf_op jit(solution)/shard_map/ppermute | solution.py:33
  78.8 6.7 %collective-permute-start.15 = (f32[2,24,1152]{2,1,0:T(8,128)S(1)}, f32[2,24,1152]{2,1,0:T(8,128)S(1)}, u32[]{:S(2)}, u32[]{:S(2)}) collective-permute-start(f32[2,24,1152]{2,1,0:T(8,128)S(1)} %pad_maximum_fusion), channel_id=1, source_target_pairs={{0,128},{1,5},{2,130},{3,7},{4,132},{5,1},{6,134},{7,3},{8,136},{9... | collective-permute-start | bytes 663560 | tf_op jit(solution)/shard_map/ppermute | solution.py:33
  79.5 7.4 %collective-permute-start.16 = (f32[2,24,1152]{2,1,0:T(8,128)S(1)}, f32[2,24,1152]{2,1,0:T(8,128)S(1)}, u32[]{:S(2)}, u32[]{:S(2)}) collective-permute-start(f32[2,24,1152]{2,1,0:T(8,128)S(1)} %pad_maximum_fusion.1), channel_id=1, source_target_pairs={{0,64},{1,3},{2,66},{3,1},{4,68},{5,7},{6,70},{7,5},{8,72},{9,11},... | collective-permute-start | bytes 663560 | tf_op jit(solution)/shard_map/ppermute | solution.py:33
  81.1 6.4 %collective-permute-start.17 = (f32[2,24,1152]{2,1,0:T(8,128)S(1)}, f32[2,24,1152]{2,1,0:T(8,128)S(1)}, u32[]{:S(2)}, u32[]{:S(2)}) collective-permute-start(f32[2,24,1152]{2,1,0:T(8,128)S(1)} %pad_maximum_fusion.2), channel_id=1, source_target_pairs={{0,192},{1,7},{2,194},{3,5},{4,196},{5,3},{6,198},{7,1},{8,200},{9... | collective-permute-start | bytes 663560 | tf_op jit(solution)/shard_map/ppermute | solution.py:33
  87.6 5.2 %collective-permute-start.18 = (f32[12,1152]{1,0:T(8,128)S(1)}, f32[12,1152]{1,0:T(8,128)S(1)}, u32[]{:S(2)}, u32[]{:S(2)}) collective-permute-start(f32[12,1152]{1,0:T(8,128)S(1)} %get-tuple-element.97), channel_id=1, source_target_pairs={{0,24},{1,25},{2,26},{3,27},{4,28},{5,29},{6,30},{7,31},{8,16},{9,... | collective-permute-start | bytes 165896 | tf_op jit(solution)/shard_map/ppermute | solution.py:33
  89.3 5.3 %collective-permute-start.19 = (f32[12,1152]{1,0:T(8,128)S(1)}, f32[12,1152]{1,0:T(8,128)S(1)}, u32[]{:S(2)}, u32[]{:S(2)}) collective-permute-start(f32[12,1152]{1,0:T(8,128)S(1)} %get-tuple-element.99), channel_id=1, source_target_pairs={{0,16},{1,17},{2,18},{3,19},{4,20},{5,21},{6,22},{7,23},{8,24},{9,... | collective-permute-start | bytes 165896 | tf_op jit(solution)/shard_map/ppermute | solution.py:33
  90.5 4.1 %collective-permute-start.20 = (f32[12,1152]{1,0:T(8,128)S(1)}, f32[12,1152]{1,0:T(8,128)S(1)}, u32[]{:S(2)}, u32[]{:S(2)}) collective-permute-start(f32[12,1152]{1,0:T(8,128)S(1)} %get-tuple-element.98), channel_id=1, source_target_pairs={{0,8},{1,9},{2,10},{3,11},{4,12},{5,13},{6,14},{7,15},{8,0},{9,1},... | collective-permute-start | bytes 165896 | tf_op jit(solution)/shard_map/ppermute | solution.py:33
  94.8 11.3 %collective-permute-start.21 = (f32[12,576]{1,0:T(8,128)S(1)}, f32[12,576]{1,0:T(8,128)S(1)}, u32[]{:S(2)}, u32[]{:S(2)}) collective-permute-start(f32[12,576]{1,0:T(8,128)S(1)} %get-tuple-element.100), channel_id=1, source_target_pairs={{0,1},{1,49},{2,3},{3,51},{4,5},{5,53},{6,7},{7,55},{8,9},{9,57},{... | collective-permute-start | bytes 82952 | tf_op jit(solution)/shard_map/ppermute | solution.py:33
  97.6 10.2 %collective-permute-start.22 = (f32[12,576]{1,0:T(8,128)S(1)}, f32[12,576]{1,0:T(8,128)S(1)}, u32[]{:S(2)}, u32[]{:S(2)}) collective-permute-start(f32[12,576]{1,0:T(8,128)S(1)} %get-tuple-element.101), channel_id=1, source_target_pairs={{1,48},{3,50},{5,52},{7,54},{9,56},{11,58},{13,60},{15,62},{17,32}... | collective-permute-start | bytes 82952 | tf_op jit(solution)/shard_map/ppermute | solution.py:33

commit v7 on v6

--- a/solution.py
+++ b/solution.py
@@ -254,7 +254,7 @@
         scratch_shapes=[pltpu.VMEM((2,) + shape, BF16), pltpu.VMEM(shape, F32)]
         + [pltpu.SemaphoreType.DMA((2, NY))] * 2,
         cost_estimate=cost(10**6, 5 * 10**6),
-        compiler_params=limit(62),
+        compiler_params=limit(16),
     )(place, x)
 
 
@@ -305,20 +305,19 @@
     y, z, x, c = me
     before = jnp.zeros_like(total)
     steps = (
-        (x_partner(1), x & 1),
-        (x_partner(3), x >> 1),
-        (z_partner(1), z & 1),
-        (z_partner(2), (z >> 1) & 1),
-        (z_partner(6), z >> 2),
-        (y_partner(1), y & 1),
-        (y_partner(3), y >> 1),
+        (x_partner, x, ((1, 1), (3, 3), (2, 2))),
+        (z_partner, z & 3, ((1, 1), (2, 2), (3, 3))),
+        (z_partner, z >> 2, ((6, 1),)),
+        (y_partner, y, ((1, 1), (3, 3), (2, 2))),
     )
-    for n, (move, bit) in enumerate(steps):
-        came = permute(total, move)
-        if n in works:
-            came, total = works[n](came, total)
-        before = before + jnp.where(bit != c, came, 0.0)
-        total = total + came
+    for n, (partner, place, others) in enumerate(steps):
+        came = [permute(total, partner(move)) for move, _ in others]
+        for work in works[n]:
+            came, total = work(came, total)
+        for a, (_, other) in zip(came, others):
+            earlier = (place ^ other < place) == (c == 0)
+            before = before + jnp.where(earlier, a, 0.0)
+            total = total + a
     return before
 
 
@@ -357,18 +356,19 @@
     place = jnp.stack([c, x, y, block]).astype(jnp.int32)
     mine = [a.T for a in (query_proj, key_proj, value_proj, grad_out)]
     keep, send, wide = states(*mine)
-    theirs = swap_cores(wide)
-    total = keep + swap_cores(send)
+    came, sent = tie(swap_cores(send), wide)
+    theirs = swap_cores(sent)
+    total = keep + came
     made = {}
 
     def halves_work(came, total):
-        total, x = tie(total, inputs)
+        total, x, made["theirs"] = tie(total, inputs, theirs)
         came, (made["mine"], half) = tie(came, halves(place, x))
         made["wide"] = swap_cores(half)
         return came, total
 
     def local_work(came, total):
-        total, there = tie(total, theirs)
+        total, there = tie(total, made["theirs"])
         came, made["local"] = tie(came, local_terms(place, wide, there))
         return came, total
 
@@ -380,7 +380,7 @@
 
         return work
 
-    works = {0: halves_work, 3: local_work, 4: terms_work(0), 5: terms_work(1), 6: terms_work(2)}
+    works = ((halves_work,), (local_work,), (terms_work(0),), (terms_work(1), terms_work(2)))
     before = before_chip(me, total, works)
     across = swap_cores(before)
     inner, outer = zip(*(made[n] for n in range(3)))

time: 109 us -> 105 us (0.963)
  local copies, waits for them, and re-layouts: 2.26 us -> 6.75 us
  waiting for transfers between devices: 34 us -> 29.8 us
  Pallas kernels: 24 us -> 21.8 us
    unnamed x6 -> x12, local copies, waits for them, and re-layouts: 1.42 us -> 5.9 us
    ppermute x23 -> x26, waiting for transfers between devices: 34 us -> 29.8 us  [permute(): return lax.ppermute(value, SEQ, pairs)]
    pallas_call x1, Pallas kernels: 4.2 us -> 2.82 us  [halves(): pl.pallas_call(halves_kernel, name='halves', out_shape=(jax.ShapeDtypeStr...]
    ppermute x23 -> x26, starting transfers between devices: 45.2 us -> 44.4 us  [permute(): return lax.ppermute(value, SEQ, pairs)]
  transfers between devices with their start and end apart: 23 -> 26, of which waited for: 14 -> 12; matrix products, arithmetic and copies ran while one was open for 1% -> 1% of each run, Pallas kernels for 17% -> 16%
where the time goes in v7:
time: 105 us
  starting transfers between devices  44.4 us (42%)
  waiting for transfers between devices  29.8 us (28%)
  Pallas kernels  21.8 us (21%)
  local copies, waits for them, and re-layouts  6.75 us (6%)
  other arithmetic  1.63 us (2%)
    ppermute x26, starting transfers between devices, permute(): return lax.ppermute(value, SEQ, pairs)  44.4 us
    ppermute x26, waiting for transfers between devices, permute(): return lax.ppermute(value, SEQ, pairs)  29.8 us
    pallas_call x3, Pallas kernels, terms(): pl.pallas_call(terms_kernel, name='terms', out_shape=(shape, shape), in_s...  7.91 us
    unnamed x12, local copies, waits for them, and re-layouts  5.9 us
    pallas_call x2, Pallas kernels, join(): pl.pallas_call(functools.partial(join_kernel, factor, half), name=f'join{...  4.55 us
    pallas_call x1, Pallas kernels, local_terms(): pl.pallas_call(local_kernel, name='local_terms', out_shape=(shape,) * 3,...  3.66 us
    pallas_call x1, Pallas kernels, states(): pl.pallas_call(states_kernel, name='states', out_shape=(shape, shape, jax...  2.82 us
    pallas_call x1, Pallas kernels, halves(): pl.pallas_call(halves_kernel, name='halves', out_shape=(jax.ShapeDtypeStr...  2.82 us
  transfers between devices with their start and end apart: 26, of which 12 were waited for; matrix products, arithmetic and copies ran while one was open for 1% of the time, Pallas kernels for 16%

profile of v7, /device:TPU:1, one launch (start us, length us, event | category | flops | bytes accessed | tf_op | source)
XLA Modules:
  0.0 105.2 jit_solution(11271661439182956095)
XLA Ops:
  0.6 2.8 %states.1 = (f32[144,128]{1,0:T(8,128)}, f32[144,128]{1,0:T(8,128)}, f32[4,192,512]{2,1,0:T(8,128)}) custom-call(bf16[192,512]{1,0:T(8,128)(2,1)} %bitcast.34, bf16[192,512]{1,0:T(8,128)(2,1)} %bitcast.35, bf16[192,512]{1,0:T(8,128)(2,1)} %bitcast.36, bf16[192,512]{1,0:T(8,128)(2,1)} %bitcast.37), custom_call_target="tpu_custom_call" | custom-call | flops 75497472 | bytes 1000000 | tf_op jit(solution)/shard_map/states/pallas_call | solution.py:234
  3.5 3.3 %collective-permute-start = (f32[144,128]{1,0:T(8,128)}, f32[144,128]{1,0:T(8,128)S(1)}, u32[]{:S(2)}, u32[]{:S(2)}) collective-permute-start(f32[144,128]{1,0:T(8,128)} %get-tuple-element.56), channel_id=1, source_target_pairs={{0,1},{1,0},{2,3},{3,2},{4,5},{5,4},{6,7},{7,6},{8,9},{9,8},{10,11... | collective-permute-start | bytes 221192 | tf_op jit(solution)/shard_map/ppermute | solution.py:33
  6.8 1.1 %collective-permute-done = f32[144,128]{1,0:T(8,128)S(1)} collective-permute-done((f32[144,128]{1,0:T(8,128)}, f32[144,128]{1,0:T(8,128)S(1)}, u32[]{:S(2)}, u32[]{:S(2)}) %collective-permute-start) | collective-permute-done | bytes 73760 | tf_op jit(solution)/shard_map/ppermute | solution.py:33
  7.9 0.4 collective-permute-start.4
  8.3 0.9 add.105
  9.3 1.3 %collective-permute-start.2 = (f32[144,128]{1,0:T(8,128)S(1)}, f32[144,128]{1,0:T(8,128)S(1)}, u32[]{:S(2)}, u32[]{:S(2)}) collective-permute-start(f32[144,128]{1,0:T(8,128)S(1)} %add.105), channel_id=1, source_target_pairs={{0,6},{1,7},{2,4},{3,5},{4,2},{5,3},{6,0},{7,1},{8,14},{9,15},{10,... | collective-permute-start | bytes 221192 | tf_op jit(solution)/shard_map/ppermute | solution.py:33
  10.5 2.0 %collective-permute-start.3 = (f32[144,128]{1,0:T(8,128)S(1)}, f32[144,128]{1,0:T(8,128)S(1)}, u32[]{:S(2)}, u32[]{:S(2)}) collective-permute-start(f32[144,128]{1,0:T(8,128)S(1)} %add.105), channel_id=1, source_target_pairs={{0,4},{1,5},{2,6},{3,7},{4,0},{5,1},{6,2},{7,3},{8,12},{9,13},{10,... | collective-permute-start | bytes 221192 | tf_op jit(solution)/shard_map/ppermute | solution.py:33
  12.6 1.9 %copy-done.2 = bf16[512,3072]{1,0:T(8,128)(2,1)S(1)} copy-done((bf16[512,3072]{1,0:T(8,128)(2,1)S(1)}, bf16[512,3072]{1,0:T(8,128)(2,1)}, u32[]{:S(2)}) %copy-start.2) | copy-done | bytes 3145752
  14.5 2.8 %halves.1 = (bf16[4,512,384]{2,1,0:T(8,128)(2,1)S(1)}, f32[4,512,384]{2,1,0:T(8,128)}) custom-call(s32[4]{0:T(128)S(1)} %pad_add_fusion.place, bf16[512,3072]{1,0:T(8,128)(2,1)S(1)} %copy-done.2), custom_call_target="tpu_custom_call" | custom-call | flops 1000000 | bytes 5000000 | tf_op jit(solution)/shard_map/halves/pallas_call | solution.py:248
  17.3 1.2 %copy-done = bf16[4,512,384]{2,1,0:T(8,128)(2,1)} copy-done((bf16[4,512,384]{2,1,0:T(8,128)(2,1)}, bf16[4,512,384]{2,1,0:T(8,128)(2,1)S(1)}, u32[]{:S(2)}) %copy-start) | copy-done | bytes 1572888
  18.5 1.1 %collective-permute-start.9 = (f32[4,512,384]{2,1,0:T(8,128)}, f32[4,512,384]{2,1,0:T(8,128)S(1)}, u32[]{:S(2)}, u32[]{:S(2)}) collective-permute-start(f32[4,512,384]{2,1,0:T(8,128)} %get-tuple-element.77), channel_id=1, source_target_pairs={{0,1},{1,0},{2,3},{3,2},{4,5},{5,4},{6,7},{7,6},{8,9},{9,8},{10,11... | collective-permute-start | bytes 9437192 | tf_op jit(solution)/shard_map/ppermute | solution.py:33
  19.8 3.0 %collective-permute-start.6 = (f32[144,128]{1,0:T(8,128)S(1)}, f32[144,128]{1,0:T(8,128)S(1)}, u32[]{:S(2)}, u32[]{:S(2)}) collective-permute-start(f32[144,128]{1,0:T(8,128)S(1)} %add_add_fusion.1), channel_id=1, source_target_pairs={{0,16},{1,17},{2,18},{3,19},{4,20},{5,21},{6,22},{7,23},{8,24},{9,... | collective-permute-start | bytes 221192 | tf_op jit(solution)/shard_map/ppermute | solution.py:33
  22.8 0.5 collective-permute-start.7
  23.3 1.4 %copy-done.3 = f32[4,192,512]{2,1,0:T(8,128)S(1)} copy-done((f32[4,192,512]{2,1,0:T(8,128)S(1)}, f32[4,192,512]{2,1,0:T(8,128)}, u32[]{:S(2)}) %copy-start.3) | copy-done | bytes 1572888
  24.7 1.4 %copy-done.5 = f32[4,192,512]{2,1,0:T(8,128)S(1)} copy-done((f32[4,192,512]{2,1,0:T(8,128)S(1)}, f32[4,192,512]{2,1,0:T(8,128)}, u32[]{:S(2)}) %copy-start.5) | copy-done | bytes 1572888
  26.1 3.7 %local_terms.1 = (bf16[2,384,512]{2,1,0:T(8,128)(2,1)S(1)}, bf16[2,384,512]{2,1,0:T(8,128)(2,1)S(1)}, bf16[2,384,512]{2,1,0:T(8,128)(2,1)S(1)}) custom-call(s32[4]{0:T(128)S(1)} %pad_add_fusion.place, f32[4,192,512]{2,1,0:T(8,128)S(1)} %copy-done.3, f32[4,192,512]{2,1,0:T(8,128)S(1)} %copy-done.5), custom_call_target="tpu_custom_call" | custom-call | flops 1006632960 | bytes 5000000 | tf_op jit(solution)/shard_map/local_terms/pallas_call | solution.py:263
  29.8 4.1 %collective-permute-start.8 = (f32[144,128]{1,0:T(8,128)S(1)}, f32[144,128]{1,0:T(8,128)S(1)}, u32[]{:S(2)}, u32[]{:S(2)}) collective-permute-start(f32[144,128]{1,0:T(8,128)S(1)} %add_add_fusion), channel_id=1, source_target_pairs={{0,48},{1,49},{2,50},{3,51},{4,52},{5,53},{6,54},{7,55},{8,56},{9,... | collective-permute-start | bytes 221192 | tf_op jit(solution)/shard_map/ppermute | solution.py:33
  33.9 2.6 %terms.3 = (f32[2,2,4,4,24,192]{5,4,3,2,1,0:T(8,128)S(1)}, f32[2,2,4,4,24,192]{5,4,3,2,1,0:T(8,128)S(1)}) custom-call(s32[4]{0:T(128)S(1)} %pad_add_fusion.place, bf16[4,512,384]{2,1,0:T(8,128)(2,1)S(1)} %copy-done.1, f32[4,512,384]{2,1,0:T(8,128)S(1)} %collective-permute-done.9.wide, bf16[2,384,512]{2,1,0:T(8,128)(2,1)S(1)} %get-tuple-element.79.d), custom_call_target="tpu_custom_call" | custom-call | flops 1207959552 | bytes 8000000 | tf_op jit(solution)/shard_map/terms/pallas_call | solution.py:276
  36.6 1.4 %collective-permute-start.10 = (f32[144,128]{1,0:T(8,128)S(1)}, f32[144,128]{1,0:T(8,128)S(1)}, u32[]{:S(2)}, u32[]{:S(2)}) collective-permute-start(f32[144,128]{1,0:T(8,128)S(1)} %add.118), channel_id=1, source_target_pairs={{0,64},{1,65},{2,66},{3,67},{4,68},{5,69},{6,70},{7,71},{8,72},{9,... | collective-permute-start | bytes 221192 | tf_op jit(solution)/shard_map/ppermute | solution.py:33
  38.0 1.9 %collective-permute-start.11 = (f32[144,128]{1,0:T(8,128)S(1)}, f32[144,128]{1,0:T(8,128)S(1)}, u32[]{:S(2)}, u32[]{:S(2)}) collective-permute-start(f32[144,128]{1,0:T(8,128)S(1)} %add.118), channel_id=1, source_target_pairs={{0,192},{1,193},{2,194},{3,195},{4,196},{5,197},{6,198},{7,199},{8... | collective-permute-start | bytes 221192 | tf_op jit(solution)/shard_map/ppermute | solution.py:33
  39.9 0.7 collective-permute-start.12
  40.6 2.6 %terms.5 = (f32[2,2,4,4,24,192]{5,4,3,2,1,0:T(8,128)S(1)}, f32[2,2,4,4,24,192]{5,4,3,2,1,0:T(8,128)S(1)}) custom-call(s32[4]{0:T(128)S(1)} %pad_add_fusion.place, bf16[4,512,384]{2,1,0:T(8,128)(2,1)S(1)} %copy-done.1, f32[4,512,384]{2,1,0:T(8,128)S(1)} %collective-permute-done.9.wide, bf16[2,384,512]{2,1,0:T(8,128)(2,1)S(1)} %get-tuple-element.91.d), custom_call_target="tpu_custom_call" | custom-call | flops 1207959552 | bytes 8000000 | tf_op jit(solution)/shard_map/terms/pallas_call | solution.py:276
  43.2 2.6 %terms.4 = (f32[2,2,4,4,24,192]{5,4,3,2,1,0:T(8,128)S(1)}, f32[2,2,4,4,24,192]{5,4,3,2,1,0:T(8,128)S(1)}) custom-call(s32[4]{0:T(128)S(1)} %pad_add_fusion.place, bf16[4,512,384]{2,1,0:T(8,128)(2,1)S(1)} %copy-done.1, f32[4,512,384]{2,1,0:T(8,128)S(1)} %collective-permute-done.9.wide, bf16[2,384,512]{2,1,0:T(8,128)(2,1)S(1)} %get-tuple-element.85.d), custom_call_target="tpu_custom_call" | custom-call | flops 1207959552 | bytes 8000000 | tf_op jit(solution)/shard_map/terms/pallas_call | solution.py:276
  46.0 2.2 %collective-permute-start.13 = (f32[144,128]{1,0:T(8,128)S(1)}, f32[144,128]{1,0:T(8,128)S(1)}, u32[]{:S(2)}, u32[]{:S(2)}) collective-permute-start(f32[144,128]{1,0:T(8,128)S(1)} %select_add_fusion.own), channel_id=1, source_target_pairs={{0,1},{1,0},{2,3},{3,2},{4,5},{5,4},{6,7},{7,6},{8,9},{9,8},{10,11... | collective-permute-start | bytes 221192 | tf_op jit(solution)/shard_map/ppermute | solution.py:33
  48.2 0.9 collective-permute-done.13.other
  49.1 2.3 %join1.1 = (f32[2,4,24,1152]{3,2,1,0:T(8,128)S(1)}, f32[2,4,24,1152]{3,2,1,0:T(8,128)S(1)}) custom-call(s32[4]{0:T(128)S(1)} %pad_add_fusion.place, f32[144,128]{1,0:T(8,128)S(1)} %select_add_fusion.own, f32[144,128]{1,0:T(8,128)S(1)} %collective-permute-done.13.other, f32[2,2,4,4,24,192]{5,4,3,2,1,0:T(8,128)S(1)} %get-tuple-element.97.refs_0_, ...), custom_call_target="tpu_custom_call" | custom-call | flops 339738624 | bytes 8000000 | tf_op jit(solution)/shard_map/join1/pallas_call | solution.py:289
  51.4 2.4 %collective-permute-start.14 = (f32[2,4,24,1152]{3,2,1,0:T(8,128)S(1)}, f32[2,4,24,1152]{3,2,1,0:T(8,128)S(1)}, u32[]{:S(2)}, u32[]{:S(2)}) collective-permute-start(f32[2,4,24,1152]{3,2,1,0:T(8,128)S(1)} %get-tuple-element.104), channel_id=1, source_target_pairs={{0,6},{1,193},{2,4},{3,195},{4,2},{5,197},{6,0},{7,199},{8,14},{9,... | collective-permute-start | bytes 2654216 | tf_op jit(solution)/shard_map/ppermute | solution.py:33
  53.8 2.3 %join0.1 = (f32[2,4,24,1152]{3,2,1,0:T(8,128)S(1)}, f32[2,4,24,1152]{3,2,1,0:T(8,128)S(1)}) custom-call(s32[4]{0:T(128)S(1)} %pad_add_fusion.place, f32[144,128]{1,0:T(8,128)S(1)} %select_add_fusion.own, f32[144,128]{1,0:T(8,128)S(1)} %collective-permute-done.13.other, f32[2,2,4,4,24,192]{5,4,3,2,1,0:T(8,128)S(1)} %get-tuple-element.97.refs_0_, ...), custom_call_target="tpu_custom_call" | custom-call | flops 339738624 | bytes 8000000 | tf_op jit(solution)/shard_map/join0/pallas_call | solution.py:289
  56.1 8.8 %collective-permute-done.14 = f32[2,4,24,1152]{3,2,1,0:T(8,128)S(1)} collective-permute-done((f32[2,4,24,1152]{3,2,1,0:T(8,128)S(1)}, f32[2,4,24,1152]{3,2,1,0:T(8,128)S(1)}, u32[]{:S(2)}, u32[]{:S(2)}) %collective-permute-start.14) | collective-permute-done | bytes 884768 | tf_op jit(solution)/shard_map/ppermute | solution.py:33
  65.0 1.0 collective-permute-done.16
  66.0 1.5 %collective-permute-start.17 = (f32[4,24,1152]{2,1,0:T(8,128)S(1)}, f32[4,24,1152]{2,1,0:T(8,128)S(1)}, u32[]{:S(2)}, u32[]{:S(2)}) collective-permute-start(f32[4,24,1152]{2,1,0:T(8,128)S(1)} %fusion), channel_id=1, source_target_pairs={{0,6},{1,193},{2,4},{3,195},{4,2},{5,197},{6,0},{7,199},{8,14},{9,... | collective-permute-start | bytes 1327112 | tf_op jit(solution)/shard_map/ppermute | solution.py:33
  67.5 4.9 %collective-permute-done.15 = f32[4,24,1152]{2,1,0:T(8,128)S(1)} collective-permute-done((f32[4,24,1152]{2,1,0:T(8,128)S(1)}, f32[4,24,1152]{2,1,0:T(8,128)S(1)}, u32[]{:S(2)}, u32[]{:S(2)}) %collective-permute-start.15) | collective-permute-done | bytes 442400 | tf_op jit(solution)/shard_map/ppermute | solution.py:33
  72.5 2.2 %collective-permute-done.17 = f32[4,24,1152]{2,1,0:T(8,128)S(1)} collective-permute-done((f32[4,24,1152]{2,1,0:T(8,128)S(1)}, f32[4,24,1152]{2,1,0:T(8,128)S(1)}, u32[]{:S(2)}, u32[]{:S(2)}) %collective-permute-start.17) | collective-permute-done | bytes 442400 | tf_op jit(solution)/shard_map/ppermute | solution.py:33
  74.9 2.1 %collective-permute-start.18 = (f32[2,24,1152]{2,1,0:T(8,128)S(1)}, f32[2,24,1152]{2,1,0:T(8,128)S(1)}, u32[]{:S(2)}, u32[]{:S(2)}) collective-permute-start(f32[2,24,1152]{2,1,0:T(8,128)S(1)} %pad_maximum_fusion), channel_id=1, source_target_pairs={{0,128},{1,5},{2,130},{3,7},{4,132},{5,1},{6,134},{7,3},{8,136},{9... | collective-permute-start | bytes 663560 | tf_op jit(solution)/shard_map/ppermute | solution.py:33
  77.0 0.7 collective-permute-start.19
  77.7 0.7 collective-permute-start.20
  78.5 2.8 %collective-permute-done.18 = f32[2,24,1152]{2,1,0:T(8,128)S(1)} collective-permute-done((f32[2,24,1152]{2,1,0:T(8,128)S(1)}, f32[2,24,1152]{2,1,0:T(8,128)S(1)}, u32[]{:S(2)}, u32[]{:S(2)}) %collective-permute-start.18) | collective-permute-done | bytes 221216 | tf_op jit(solution)/shard_map/ppermute | solution.py:33
  81.3 2.3 %collective-permute-done.19 = f32[2,24,1152]{2,1,0:T(8,128)S(1)} collective-permute-done((f32[2,24,1152]{2,1,0:T(8,128)S(1)}, f32[2,24,1152]{2,1,0:T(8,128)S(1)}, u32[]{:S(2)}, u32[]{:S(2)}) %collective-permute-start.19) | collective-permute-done | bytes 221216 | tf_op jit(solution)/shard_map/ppermute | solution.py:33
  83.6 0.5 collective-permute-done.20
  84.2 2.3 %collective-permute-start.21 = (f32[12,1152]{1,0:T(8,128)S(1)}, f32[12,1152]{1,0:T(8,128)S(1)}, u32[]{:S(2)}, u32[]{:S(2)}) collective-permute-start(f32[12,1152]{1,0:T(8,128)S(1)} %get-tuple-element.115), channel_id=1, source_target_pairs={{0,24},{1,25},{2,26},{3,27},{4,28},{5,29},{6,30},{7,31},{8,16},{9,... | collective-permute-start | bytes 165896 | tf_op jit(solution)/shard_map/ppermute | solution.py:33
  86.5 1.0 collective-permute-start.22
  87.5 0.6 collective-permute-start.23
  88.1 1.6 %collective-permute-done.21 = f32[12,1152]{1,0:T(8,128)S(1)} collective-permute-done((f32[12,1152]{1,0:T(8,128)S(1)}, f32[12,1152]{1,0:T(8,128)S(1)}, u32[]{:S(2)}, u32[]{:S(2)}) %collective-permute-start.21) | collective-permute-done | bytes 55328 | tf_op jit(solution)/shard_map/ppermute | solution.py:33
  89.6 2.0 %collective-permute-done.22 = f32[12,1152]{1,0:T(8,128)S(1)} collective-permute-done((f32[12,1152]{1,0:T(8,128)S(1)}, f32[12,1152]{1,0:T(8,128)S(1)}, u32[]{:S(2)}, u32[]{:S(2)}) %collective-permute-start.22) | collective-permute-done | bytes 55328 | tf_op jit(solution)/shard_map/ppermute | solution.py:33
  91.8 2.7 %collective-permute-start.24 = (f32[12,576]{1,0:T(8,128)S(1)}, f32[12,576]{1,0:T(8,128)S(1)}, u32[]{:S(2)}, u32[]{:S(2)}) collective-permute-start(f32[12,576]{1,0:T(8,128)S(1)} %get-tuple-element.118), channel_id=1, source_target_pairs={{0,1},{1,49},{2,3},{3,51},{4,5},{5,53},{6,7},{7,55},{8,9},{9,57},{... | collective-permute-start | bytes 82952 | tf_op jit(solution)/shard_map/ppermute | solution.py:33
  94.4 8.3 %collective-permute-start.25 = (f32[12,576]{1,0:T(8,128)S(1)}, f32[12,576]{1,0:T(8,128)S(1)}, u32[]{:S(2)}, u32[]{:S(2)}) collective-permute-start(f32[12,576]{1,0:T(8,128)S(1)} %get-tuple-element.119), channel_id=1, source_target_pairs={{1,48},{3,50},{5,52},{7,54},{9,56},{11,58},{13,60},{15,62},{17,32}... | collective-permute-start | bytes 82952 | tf_op jit(solution)/shard_map/ppermute | solution.py:33
  102.8 1.7 %collective-permute-done.25 = f32[12,576]{1,0:T(8,128)S(1)} collective-permute-done((f32[12,576]{1,0:T(8,128)S(1)}, f32[12,576]{1,0:T(8,128)S(1)}, u32[]{:S(2)}, u32[]{:S(2)}) %collective-permute-start.25) | collective-permute-done | bytes 27680 | tf_op jit(solution)/shard_map/ppermute | solution.py:33
  104.5 0.7 fusion.14
  (46 shorter events, 1.3 us)
Async XLA Ops:
  3.5 4.5 %collective-permute-start = (f32[144,128]{1,0:T(8,128)}, f32[144,128]{1,0:T(8,128)S(1)}, u32[]{:S(2)}, u32[]{:S(2)}) collective-permute-start(f32[144,128]{1,0:T(8,128)} %get-tuple-element.56), channel_id=1, source_target_pairs={{0,1},{1,0},{2,3},{3,2},{4,5},{5,4},{6,7},{7,6},{8,9},{9,8},{10,11... | collective-permute-start | bytes 221192 | tf_op jit(solution)/shard_map/ppermute | solution.py:33
  7.9 4.7 %collective-permute-start.4 = (f32[4,192,512]{2,1,0:T(8,128)}, f32[4,192,512]{2,1,0:T(8,128)S(1)}, u32[]{:S(2)}, u32[]{:S(2)}) collective-permute-start(f32[4,192,512]{2,1,0:T(8,128)} %get-tuple-element.59.own), channel_id=1, source_target_pairs={{0,1},{1,0},{2,3},{3,2},{4,5},{5,4},{6,7},{7,6},{8,9},{9,8},{10,11... | collective-permute-start | bytes 4718600 | tf_op jit(solution)/shard_map/ppermute | solution.py:33
  9.2 9.4 %collective-permute-start.1 = (f32[144,128]{1,0:T(8,128)S(1)}, f32[144,128]{1,0:T(8,128)S(1)}, u32[]{:S(2)}, u32[]{:S(2)}) collective-permute-start(f32[144,128]{1,0:T(8,128)S(1)} %add.105), channel_id=1, source_target_pairs={{0,2},{1,3},{2,0},{3,1},{4,6},{5,7},{6,4},{7,5},{8,10},{9,11},{10,... | collective-permute-start | bytes 221192 | tf_op jit(solution)/shard_map/ppermute | solution.py:33
  9.3 9.3 %collective-permute-start.2 = (f32[144,128]{1,0:T(8,128)S(1)}, f32[144,128]{1,0:T(8,128)S(1)}, u32[]{:S(2)}, u32[]{:S(2)}) collective-permute-start(f32[144,128]{1,0:T(8,128)S(1)} %add.105), channel_id=1, source_target_pairs={{0,6},{1,7},{2,4},{3,5},{4,2},{5,3},{6,0},{7,1},{8,14},{9,15},{10,... | collective-permute-start | bytes 221192 | tf_op jit(solution)/shard_map/ppermute | solution.py:33
  10.5 8.0 %collective-permute-start.3 = (f32[144,128]{1,0:T(8,128)S(1)}, f32[144,128]{1,0:T(8,128)S(1)}, u32[]{:S(2)}, u32[]{:S(2)}) collective-permute-start(f32[144,128]{1,0:T(8,128)S(1)} %add.105), channel_id=1, source_target_pairs={{0,4},{1,5},{2,6},{3,7},{4,0},{5,1},{6,2},{7,3},{8,12},{9,13},{10,... | collective-permute-start | bytes 221192 | tf_op jit(solution)/shard_map/ppermute | solution.py:33
  12.6 1.9 %copy-start.2 = (bf16[512,3072]{1,0:T(8,128)(2,1)S(1)}, bf16[512,3072]{1,0:T(8,128)(2,1)}, u32[]{:S(2)}) copy-start(bf16[512,3072]{1,0:T(8,128)(2,1)} %x) | copy-start | bytes 9437188
  14.5 2.8 %copy-start.4 = (f32[4,192,512]{2,1,0:T(8,128)}, f32[4,192,512]{2,1,0:T(8,128)S(1)}, u32[]{:S(2)}) copy-start(f32[4,192,512]{2,1,0:T(8,128)S(1)} %collective-permute-done.4.other) | copy-start | bytes 4718596
  17.3 1.2 %copy-start = (bf16[4,512,384]{2,1,0:T(8,128)(2,1)}, bf16[4,512,384]{2,1,0:T(8,128)(2,1)S(1)}, u32[]{:S(2)}) copy-start(bf16[4,512,384]{2,1,0:T(8,128)(2,1)S(1)} %get-tuple-element.76.x) | copy-start | bytes 4718596
  18.5 15.4 %collective-permute-start.9 = (f32[4,512,384]{2,1,0:T(8,128)}, f32[4,512,384]{2,1,0:T(8,128)S(1)}, u32[]{:S(2)}, u32[]{:S(2)}) collective-permute-start(f32[4,512,384]{2,1,0:T(8,128)} %get-tuple-element.77), channel_id=1, source_target_pairs={{0,1},{1,0},{2,3},{3,2},{4,5},{5,4},{6,7},{7,6},{8,9},{9,8},{10,11... | collective-permute-start | bytes 9437192 | tf_op jit(solution)/shard_map/ppermute | solution.py:33
  19.6 14.3 %copy-start.1 = (bf16[4,512,384]{2,1,0:T(8,128)(2,1)S(1)}, bf16[4,512,384]{2,1,0:T(8,128)(2,1)}, u32[]{:S(2)}) copy-start(bf16[4,512,384]{2,1,0:T(8,128)(2,1)} %copy-done) | copy-start | bytes 4718596
  19.6 10.1 %collective-permute-start.5 = (f32[144,128]{1,0:T(8,128)S(1)}, f32[144,128]{1,0:T(8,128)S(1)}, u32[]{:S(2)}, u32[]{:S(2)}) collective-permute-start(f32[144,128]{1,0:T(8,128)S(1)} %add_add_fusion.1), channel_id=1, source_target_pairs={{0,8},{1,9},{2,10},{3,11},{4,12},{5,13},{6,14},{7,15},{8,0},{9,1},... | collective-permute-start | bytes 221192 | tf_op jit(solution)/shard_map/ppermute | solution.py:33
  19.8 10.0 %collective-permute-start.6 = (f32[144,128]{1,0:T(8,128)S(1)}, f32[144,128]{1,0:T(8,128)S(1)}, u32[]{:S(2)}, u32[]{:S(2)}) collective-permute-start(f32[144,128]{1,0:T(8,128)S(1)} %add_add_fusion.1), channel_id=1, source_target_pairs={{0,16},{1,17},{2,18},{3,19},{4,20},{5,21},{6,22},{7,23},{8,24},{9,... | collective-permute-start | bytes 221192 | tf_op jit(solution)/shard_map/ppermute | solution.py:33
  22.8 7.0 %collective-permute-start.7 = (f32[144,128]{1,0:T(8,128)S(1)}, f32[144,128]{1,0:T(8,128)S(1)}, u32[]{:S(2)}, u32[]{:S(2)}) collective-permute-start(f32[144,128]{1,0:T(8,128)S(1)} %add_add_fusion.1), channel_id=1, source_target_pairs={{0,24},{1,25},{2,26},{3,27},{4,28},{5,29},{6,30},{7,31},{8,16},{9,... | collective-permute-start | bytes 221192 | tf_op jit(solution)/shard_map/ppermute | solution.py:33
  23.3 1.4 %copy-start.3 = (f32[4,192,512]{2,1,0:T(8,128)S(1)}, f32[4,192,512]{2,1,0:T(8,128)}, u32[]{:S(2)}) copy-start(f32[4,192,512]{2,1,0:T(8,128)} %get-tuple-element.59.own) | copy-start | bytes 4718596
  24.7 1.4 %copy-start.5 = (f32[4,192,512]{2,1,0:T(8,128)S(1)}, f32[4,192,512]{2,1,0:T(8,128)}, u32[]{:S(2)}) copy-start(f32[4,192,512]{2,1,0:T(8,128)} %copy-done.4) | copy-start | bytes 4718596
  29.8 6.7 %collective-permute-start.8 = (f32[144,128]{1,0:T(8,128)S(1)}, f32[144,128]{1,0:T(8,128)S(1)}, u32[]{:S(2)}, u32[]{:S(2)}) collective-permute-start(f32[144,128]{1,0:T(8,128)S(1)} %add_add_fusion), channel_id=1, source_target_pairs={{0,48},{1,49},{2,50},{3,51},{4,52},{5,53},{6,54},{7,55},{8,56},{9,... | collective-permute-start | bytes 221192 | tf_op jit(solution)/shard_map/ppermute | solution.py:33
  36.6 9.3 %collective-permute-start.10 = (f32[144,128]{1,0:T(8,128)S(1)}, f32[144,128]{1,0:T(8,128)S(1)}, u32[]{:S(2)}, u32[]{:S(2)}) collective-permute-start(f32[144,128]{1,0:T(8,128)S(1)} %add.118), channel_id=1, source_target_pairs={{0,64},{1,65},{2,66},{3,67},{4,68},{5,69},{6,70},{7,71},{8,72},{9,... | collective-permute-start | bytes 221192 | tf_op jit(solution)/shard_map/ppermute | solution.py:33
  38.0 7.9 %collective-permute-start.11 = (f32[144,128]{1,0:T(8,128)S(1)}, f32[144,128]{1,0:T(8,128)S(1)}, u32[]{:S(2)}, u32[]{:S(2)}) collective-permute-start(f32[144,128]{1,0:T(8,128)S(1)} %add.118), channel_id=1, source_target_pairs={{0,192},{1,193},{2,194},{3,195},{4,196},{5,197},{6,198},{7,199},{8... | collective-permute-start | bytes 221192 | tf_op jit(solution)/shard_map/ppermute | solution.py:33
  39.9 6.0 %collective-permute-start.12 = (f32[144,128]{1,0:T(8,128)S(1)}, f32[144,128]{1,0:T(8,128)S(1)}, u32[]{:S(2)}, u32[]{:S(2)}) collective-permute-start(f32[144,128]{1,0:T(8,128)S(1)} %add.118), channel_id=1, source_target_pairs={{0,128},{1,129},{2,130},{3,131},{4,132},{5,133},{6,134},{7,135},{8... | collective-permute-start | bytes 221192 | tf_op jit(solution)/shard_map/ppermute | solution.py:33
  46.0 3.1 %collective-permute-start.13 = (f32[144,128]{1,0:T(8,128)S(1)}, f32[144,128]{1,0:T(8,128)S(1)}, u32[]{:S(2)}, u32[]{:S(2)}) collective-permute-start(f32[144,128]{1,0:T(8,128)S(1)} %select_add_fusion.own), channel_id=1, source_target_pairs={{0,1},{1,0},{2,3},{3,2},{4,5},{5,4},{6,7},{7,6},{8,9},{9,8},{10,11... | collective-permute-start | bytes 221192 | tf_op jit(solution)/shard_map/ppermute | solution.py:33
  51.4 13.5 %collective-permute-start.14 = (f32[2,4,24,1152]{3,2,1,0:T(8,128)S(1)}, f32[2,4,24,1152]{3,2,1,0:T(8,128)S(1)}, u32[]{:S(2)}, u32[]{:S(2)}) collective-permute-start(f32[2,4,24,1152]{3,2,1,0:T(8,128)S(1)} %get-tuple-element.104), channel_id=1, source_target_pairs={{0,6},{1,193},{2,4},{3,195},{4,2},{5,197},{6,0},{7,199},{8,14},{9,... | collective-permute-start | bytes 2654216 | tf_op jit(solution)/shard_map/ppermute | solution.py:33
  53.8 12.2 %collective-permute-start.16 = (f32[2,4,24,1152]{3,2,1,0:T(8,128)S(1)}, f32[2,4,24,1152]{3,2,1,0:T(8,128)S(1)}, u32[]{:S(2)}, u32[]{:S(2)}) collective-permute-start(f32[2,4,24,1152]{3,2,1,0:T(8,128)S(1)} %get-tuple-element.106), channel_id=1, source_target_pairs={{0,2},{1,65},{2,0},{3,67},{4,6},{5,69},{6,4},{7,71},{8,10},{9,73},... | collective-permute-start | bytes 2654216 | tf_op jit(solution)/shard_map/ppermute | solution.py:33
  64.9 7.5 %collective-permute-start.15 = (f32[4,24,1152]{2,1,0:T(8,128)S(1)}, f32[4,24,1152]{2,1,0:T(8,128)S(1)}, u32[]{:S(2)}, u32[]{:S(2)}) collective-permute-start(f32[4,24,1152]{2,1,0:T(8,128)S(1)} %fusion.3), channel_id=1, source_target_pairs={{0,2},{1,65},{2,0},{3,67},{4,6},{5,69},{6,4},{7,71},{8,10},{9,73},... | collective-permute-start | bytes 1327112 | tf_op jit(solution)/shard_map/ppermute | solution.py:33
  66.0 8.7 %collective-permute-start.17 = (f32[4,24,1152]{2,1,0:T(8,128)S(1)}, f32[4,24,1152]{2,1,0:T(8,128)S(1)}, u32[]{:S(2)}, u32[]{:S(2)}) collective-permute-start(f32[4,24,1152]{2,1,0:T(8,128)S(1)} %fusion), channel_id=1, source_target_pairs={{0,6},{1,193},{2,4},{3,195},{4,2},{5,197},{6,0},{7,199},{8,14},{9,... | collective-permute-start | bytes 1327112 | tf_op jit(solution)/shard_map/ppermute | solution.py:33
  74.9 6.4 %collective-permute-start.18 = (f32[2,24,1152]{2,1,0:T(8,128)S(1)}, f32[2,24,1152]{2,1,0:T(8,128)S(1)}, u32[]{:S(2)}, u32[]{:S(2)}) collective-permute-start(f32[2,24,1152]{2,1,0:T(8,128)S(1)} %pad_maximum_fusion), channel_id=1, source_target_pairs={{0,128},{1,5},{2,130},{3,7},{4,132},{5,1},{6,134},{7,3},{8,136},{9... | collective-permute-start | bytes 663560 | tf_op jit(solution)/shard_map/ppermute | solution.py:33
  77.0 6.6 %collective-permute-start.19 = (f32[2,24,1152]{2,1,0:T(8,128)S(1)}, f32[2,24,1152]{2,1,0:T(8,128)S(1)}, u32[]{:S(2)}, u32[]{:S(2)}) collective-permute-start(f32[2,24,1152]{2,1,0:T(8,128)S(1)} %pad_maximum_fusion.1), channel_id=1, source_target_pairs={{0,64},{1,3},{2,66},{3,1},{4,68},{5,7},{6,70},{7,5},{8,72},{9,11},... | collective-permute-start | bytes 663560 | tf_op jit(solution)/shard_map/ppermute | solution.py:33
  77.7 6.4 %collective-permute-start.20 = (f32[2,24,1152]{2,1,0:T(8,128)S(1)}, f32[2,24,1152]{2,1,0:T(8,128)S(1)}, u32[]{:S(2)}, u32[]{:S(2)}) collective-permute-start(f32[2,24,1152]{2,1,0:T(8,128)S(1)} %pad_maximum_fusion.2), channel_id=1, source_target_pairs={{0,192},{1,7},{2,194},{3,5},{4,196},{5,3},{6,198},{7,1},{8,200},{9... | collective-permute-start | bytes 663560 | tf_op jit(solution)/shard_map/ppermute | solution.py:33
  84.2 5.4 %collective-permute-start.21 = (f32[12,1152]{1,0:T(8,128)S(1)}, f32[12,1152]{1,0:T(8,128)S(1)}, u32[]{:S(2)}, u32[]{:S(2)}) collective-permute-start(f32[12,1152]{1,0:T(8,128)S(1)} %get-tuple-element.115), channel_id=1, source_target_pairs={{0,24},{1,25},{2,26},{3,27},{4,28},{5,29},{6,30},{7,31},{8,16},{9,... | collective-permute-start | bytes 165896 | tf_op jit(solution)/shard_map/ppermute | solution.py:33
  86.5 5.1 %collective-permute-start.22 = (f32[12,1152]{1,0:T(8,128)S(1)}, f32[12,1152]{1,0:T(8,128)S(1)}, u32[]{:S(2)}, u32[]{:S(2)}) collective-permute-start(f32[12,1152]{1,0:T(8,128)S(1)} %get-tuple-element.117), channel_id=1, source_target_pairs={{0,16},{1,17},{2,18},{3,19},{4,20},{5,21},{6,22},{7,23},{8,24},{9,... | collective-permute-start | bytes 165896 | tf_op jit(solution)/shard_map/ppermute | solution.py:33
  87.5 4.1 %collective-permute-start.23 = (f32[12,1152]{1,0:T(8,128)S(1)}, f32[12,1152]{1,0:T(8,128)S(1)}, u32[]{:S(2)}, u32[]{:S(2)}) collective-permute-start(f32[12,1152]{1,0:T(8,128)S(1)} %get-tuple-element.116), channel_id=1, source_target_pairs={{0,8},{1,9},{2,10},{3,11},{4,12},{5,13},{6,14},{7,15},{8,0},{9,1},... | collective-permute-start | bytes 165896 | tf_op jit(solution)/shard_map/ppermute | solution.py:33
  91.8 11.0 %collective-permute-start.24 = (f32[12,576]{1,0:T(8,128)S(1)}, f32[12,576]{1,0:T(8,128)S(1)}, u32[]{:S(2)}, u32[]{:S(2)}) collective-permute-start(f32[12,576]{1,0:T(8,128)S(1)} %get-tuple-element.118), channel_id=1, source_target_pairs={{0,1},{1,49},{2,3},{3,51},{4,5},{5,53},{6,7},{7,55},{8,9},{9,57},{... | collective-permute-start | bytes 82952 | tf_op jit(solution)/shard_map/ppermute | solution.py:33
  94.4 10.0 %collective-permute-start.25 = (f32[12,576]{1,0:T(8,128)S(1)}, f32[12,576]{1,0:T(8,128)S(1)}, u32[]{:S(2)}, u32[]{:S(2)}) collective-permute-start(f32[12,576]{1,0:T(8,128)S(1)} %get-tuple-element.119), channel_id=1, source_target_pairs={{1,48},{3,50},{5,52},{7,54},{9,56},{11,58},{13,60},{15,62},{17,32}... | collective-permute-start | bytes 82952 | tf_op jit(solution)/shard_map/ppermute | solution.py:33

commit v8 on v7

--- a/solution.py
+++ b/solution.py
@@ -200,19 +200,24 @@
     later = by_head(jnp.where(first, other[...], own[...]))
     steps = ((before, lanes_dot), (later, lanes_dot), (later, dot))
     for part in range(2):
-        out = outs[part]
-        for sa in range(2):
-            a = ORDERS[part][2 * half + sa]
-            at = [(jnp.where(first, px ^ a, px ^ b), jnp.where(first, py ^ b, py ^ a)) for b in range(4)]
-            pieces = []
-            for w, side in COLUMNS:
-                state, multiply = steps[w]
-                term = jnp.concatenate([outer[w][part, side, i, j] for i, j in at], axis=0)
-                add = jnp.concatenate([inner[w][part, side, i, j] for i, j in at], axis=0)
-                high = term.astype(BF16)
-                low = (term - high.astype(F32)).astype(BF16)
-                pieces.append(factor * (add + multiply(high, state) + multiply(low, state)))
-            out[sa] = jnp.concatenate(pieces, axis=1).reshape(out.shape[1:])
+        blocks = []
+        for side in range(2):
+            for sa in range(2):
+                a = ORDERS[part][2 * half + sa]
+                for b in range(4):
+                    at = (jnp.where(first, px ^ a, px ^ b), jnp.where(first, py ^ b, py ^ a))
+                    blocks.append((side,) + at)
+        pieces = []
+        for w, (state, multiply) in enumerate(steps):
+            term = jnp.concatenate([outer[w][(part,) + at] for at in blocks], axis=0)
+            add = jnp.concatenate([inner[w][(part,) + at] for at in blocks], axis=0)
+            rows = term.shape[0]
+            high = term.astype(BF16)
+            low = (term - high.astype(F32)).astype(BF16)
+            both = multiply(jnp.concatenate([high, low], axis=0), state)
+            total = factor * (add + both[:rows] + both[rows:])
+            pieces += [total[: rows // 2], total[rows // 2 :]]
+        outs[part][...] = jnp.concatenate(pieces, axis=1).reshape(outs[part].shape)
 
 
 VMEM = pl.BlockSpec(memory_space=pltpu.VMEM)

time: 105 us -> 105 us (level)
  Pallas kernels: 21.8 us -> 20.7 us
    pallas_call x2, Pallas kernels: 4.55 us -> 3.44 us  [join(): pl.pallas_call(functools.partial(join_kernel, factor, half), name=f'join{...]
  transfers between devices with their start and end apart: 26 -> 26, of which waited for: 12 -> 12; matrix products, arithmetic and copies ran while one was open for 1% -> 1% of each run, Pallas kernels for 16% -> 15%
where the time goes in v8:
time: 105 us; the launch traced here: 104 us
  starting transfers between devices  44.1 us (42%)
  waiting for transfers between devices  30.4 us (29%)
  Pallas kernels  20.7 us (20%)
  local copies, waits for them, and re-layouts  6.75 us (6%)
  other arithmetic  1.63 us (2%)
    ppermute x26, starting transfers between devices, permute(): return lax.ppermute(value, SEQ, pairs)  44.1 us
    ppermute x26, waiting for transfers between devices, permute(): return lax.ppermute(value, SEQ, pairs)  30.4 us
    pallas_call x3, Pallas kernels, terms(): pl.pallas_call(terms_kernel, name='terms', out_shape=(shape, shape), in_s...  7.91 us
    unnamed x12, local copies, waits for them, and re-layouts  5.9 us
    pallas_call x1, Pallas kernels, local_terms(): pl.pallas_call(local_kernel, name='local_terms', out_shape=(shape,) * 3,...  3.66 us
    pallas_call x2, Pallas kernels, join(): pl.pallas_call(functools.partial(join_kernel, factor, half), name=f'join{...  3.44 us
    pallas_call x1, Pallas kernels, states(): pl.pallas_call(states_kernel, name='states', out_shape=(shape, shape, jax...  2.82 us
    pallas_call x1, Pallas kernels, halves(): pl.pallas_call(halves_kernel, name='halves', out_shape=(jax.ShapeDtypeStr...  2.82 us
  transfers between devices with their start and end apart: 26, of which 12 were waited for; matrix products, arithmetic and copies ran while one was open for 1% of the time, Pallas kernels for 15%

profile of v8, /device:TPU:1, one launch (start us, length us, event | category | flops | bytes accessed | tf_op | source)
XLA Modules:
  0.0 104.5 jit_solution(1482070713475263374)
XLA Ops:
  0.6 2.8 %states.1 = (f32[144,128]{1,0:T(8,128)}, f32[144,128]{1,0:T(8,128)}, f32[4,192,512]{2,1,0:T(8,128)}) custom-call(bf16[192,512]{1,0:T(8,128)(2,1)} %bitcast.34, bf16[192,512]{1,0:T(8,128)(2,1)} %bitcast.35, bf16[192,512]{1,0:T(8,128)(2,1)} %bitcast.36, bf16[192,512]{1,0:T(8,128)(2,1)} %bitcast.37), custom_call_target="tpu_custom_call" | custom-call | flops 75497472 | bytes 1000000 | tf_op jit(solution)/shard_map/states/pallas_call | solution.py:239
  3.5 3.3 %collective-permute-start = (f32[144,128]{1,0:T(8,128)}, f32[144,128]{1,0:T(8,128)S(1)}, u32[]{:S(2)}, u32[]{:S(2)}) collective-permute-start(f32[144,128]{1,0:T(8,128)} %get-tuple-element.56), channel_id=1, source_target_pairs={{0,1},{1,0},{2,3},{3,2},{4,5},{5,4},{6,7},{7,6},{8,9},{9,8},{10,11... | collective-permute-start | bytes 221192 | tf_op jit(solution)/shard_map/ppermute | solution.py:33
  6.8 1.1 %collective-permute-done = f32[144,128]{1,0:T(8,128)S(1)} collective-permute-done((f32[144,128]{1,0:T(8,128)}, f32[144,128]{1,0:T(8,128)S(1)}, u32[]{:S(2)}, u32[]{:S(2)}) %collective-permute-start) | collective-permute-done | bytes 73760 | tf_op jit(solution)/shard_map/ppermute | solution.py:33
  7.9 0.4 collective-permute-start.4
  8.3 0.9 add.105
  9.3 1.3 %collective-permute-start.2 = (f32[144,128]{1,0:T(8,128)S(1)}, f32[144,128]{1,0:T(8,128)S(1)}, u32[]{:S(2)}, u32[]{:S(2)}) collective-permute-start(f32[144,128]{1,0:T(8,128)S(1)} %add.105), channel_id=1, source_target_pairs={{0,6},{1,7},{2,4},{3,5},{4,2},{5,3},{6,0},{7,1},{8,14},{9,15},{10,... | collective-permute-start | bytes 221192 | tf_op jit(solution)/shard_map/ppermute | solution.py:33
  10.5 2.0 %collective-permute-start.3 = (f32[144,128]{1,0:T(8,128)S(1)}, f32[144,128]{1,0:T(8,128)S(1)}, u32[]{:S(2)}, u32[]{:S(2)}) collective-permute-start(f32[144,128]{1,0:T(8,128)S(1)} %add.105), channel_id=1, source_target_pairs={{0,4},{1,5},{2,6},{3,7},{4,0},{5,1},{6,2},{7,3},{8,12},{9,13},{10,... | collective-permute-start | bytes 221192 | tf_op jit(solution)/shard_map/ppermute | solution.py:33
  12.6 1.9 %copy-done.2 = bf16[512,3072]{1,0:T(8,128)(2,1)S(1)} copy-done((bf16[512,3072]{1,0:T(8,128)(2,1)S(1)}, bf16[512,3072]{1,0:T(8,128)(2,1)}, u32[]{:S(2)}) %copy-start.2) | copy-done | bytes 3145752
  14.5 2.8 %halves.1 = (bf16[4,512,384]{2,1,0:T(8,128)(2,1)S(1)}, f32[4,512,384]{2,1,0:T(8,128)}) custom-call(s32[4]{0:T(128)S(1)} %pad_add_fusion.place, bf16[512,3072]{1,0:T(8,128)(2,1)S(1)} %copy-done.2), custom_call_target="tpu_custom_call" | custom-call | flops 1000000 | bytes 5000000 | tf_op jit(solution)/shard_map/halves/pallas_call | solution.py:253
  17.3 1.2 %copy-done = bf16[4,512,384]{2,1,0:T(8,128)(2,1)} copy-done((bf16[4,512,384]{2,1,0:T(8,128)(2,1)}, bf16[4,512,384]{2,1,0:T(8,128)(2,1)S(1)}, u32[]{:S(2)}) %copy-start) | copy-done | bytes 1572888
  18.5 1.1 %collective-permute-start.9 = (f32[4,512,384]{2,1,0:T(8,128)}, f32[4,512,384]{2,1,0:T(8,128)S(1)}, u32[]{:S(2)}, u32[]{:S(2)}) collective-permute-start(f32[4,512,384]{2,1,0:T(8,128)} %get-tuple-element.77), channel_id=1, source_target_pairs={{0,1},{1,0},{2,3},{3,2},{4,5},{5,4},{6,7},{7,6},{8,9},{9,8},{10,11... | collective-permute-start | bytes 9437192 | tf_op jit(solution)/shard_map/ppermute | solution.py:33
  19.8 3.0 %collective-permute-start.6 = (f32[144,128]{1,0:T(8,128)S(1)}, f32[144,128]{1,0:T(8,128)S(1)}, u32[]{:S(2)}, u32[]{:S(2)}) collective-permute-start(f32[144,128]{1,0:T(8,128)S(1)} %add_add_fusion.1), channel_id=1, source_target_pairs={{0,16},{1,17},{2,18},{3,19},{4,20},{5,21},{6,22},{7,23},{8,24},{9,... | collective-permute-start | bytes 221192 | tf_op jit(solution)/shard_map/ppermute | solution.py:33
  22.8 0.5 collective-permute-start.7
  23.3 1.4 %copy-done.3 = f32[4,192,512]{2,1,0:T(8,128)S(1)} copy-done((f32[4,192,512]{2,1,0:T(8,128)S(1)}, f32[4,192,512]{2,1,0:T(8,128)}, u32[]{:S(2)}) %copy-start.3) | copy-done | bytes 1572888
  24.7 1.4 %copy-done.5 = f32[4,192,512]{2,1,0:T(8,128)S(1)} copy-done((f32[4,192,512]{2,1,0:T(8,128)S(1)}, f32[4,192,512]{2,1,0:T(8,128)}, u32[]{:S(2)}) %copy-start.5) | copy-done | bytes 1572888
  26.1 3.7 %local_terms.1 = (bf16[2,384,512]{2,1,0:T(8,128)(2,1)S(1)}, bf16[2,384,512]{2,1,0:T(8,128)(2,1)S(1)}, bf16[2,384,512]{2,1,0:T(8,128)(2,1)S(1)}) custom-call(s32[4]{0:T(128)S(1)} %pad_add_fusion.place, f32[4,192,512]{2,1,0:T(8,128)S(1)} %copy-done.3, f32[4,192,512]{2,1,0:T(8,128)S(1)} %copy-done.5), custom_call_target="tpu_custom_call" | custom-call | flops 1006632960 | bytes 5000000 | tf_op jit(solution)/shard_map/local_terms/pallas_call | solution.py:268
  29.8 4.1 %collective-permute-start.8 = (f32[144,128]{1,0:T(8,128)S(1)}, f32[144,128]{1,0:T(8,128)S(1)}, u32[]{:S(2)}, u32[]{:S(2)}) collective-permute-start(f32[144,128]{1,0:T(8,128)S(1)} %add_add_fusion), channel_id=1, source_target_pairs={{0,48},{1,49},{2,50},{3,51},{4,52},{5,53},{6,54},{7,55},{8,56},{9,... | collective-permute-start | bytes 221192 | tf_op jit(solution)/shard_map/ppermute | solution.py:33
  33.9 2.6 %terms.3 = (f32[2,2,4,4,24,192]{5,4,3,2,1,0:T(8,128)S(1)}, f32[2,2,4,4,24,192]{5,4,3,2,1,0:T(8,128)S(1)}) custom-call(s32[4]{0:T(128)S(1)} %pad_add_fusion.place, bf16[4,512,384]{2,1,0:T(8,128)(2,1)S(1)} %copy-done.1, f32[4,512,384]{2,1,0:T(8,128)S(1)} %collective-permute-done.9.wide, bf16[2,384,512]{2,1,0:T(8,128)(2,1)S(1)} %get-tuple-element.79.d), custom_call_target="tpu_custom_call" | custom-call | flops 1207959552 | bytes 8000000 | tf_op jit(solution)/shard_map/terms/pallas_call | solution.py:281
  36.6 1.4 %collective-permute-start.10 = (f32[144,128]{1,0:T(8,128)S(1)}, f32[144,128]{1,0:T(8,128)S(1)}, u32[]{:S(2)}, u32[]{:S(2)}) collective-permute-start(f32[144,128]{1,0:T(8,128)S(1)} %add.118), channel_id=1, source_target_pairs={{0,64},{1,65},{2,66},{3,67},{4,68},{5,69},{6,70},{7,71},{8,72},{9,... | collective-permute-start | bytes 221192 | tf_op jit(solution)/shard_map/ppermute | solution.py:33
  38.0 1.9 %collective-permute-start.11 = (f32[144,128]{1,0:T(8,128)S(1)}, f32[144,128]{1,0:T(8,128)S(1)}, u32[]{:S(2)}, u32[]{:S(2)}) collective-permute-start(f32[144,128]{1,0:T(8,128)S(1)} %add.118), channel_id=1, source_target_pairs={{0,192},{1,193},{2,194},{3,195},{4,196},{5,197},{6,198},{7,199},{8... | collective-permute-start | bytes 221192 | tf_op jit(solution)/shard_map/ppermute | solution.py:33
  39.9 0.7 collective-permute-start.12
  40.6 2.6 %terms.5 = (f32[2,2,4,4,24,192]{5,4,3,2,1,0:T(8,128)S(1)}, f32[2,2,4,4,24,192]{5,4,3,2,1,0:T(8,128)S(1)}) custom-call(s32[4]{0:T(128)S(1)} %pad_add_fusion.place, bf16[4,512,384]{2,1,0:T(8,128)(2,1)S(1)} %copy-done.1, f32[4,512,384]{2,1,0:T(8,128)S(1)} %collective-permute-done.9.wide, bf16[2,384,512]{2,1,0:T(8,128)(2,1)S(1)} %get-tuple-element.91.d), custom_call_target="tpu_custom_call" | custom-call | flops 1207959552 | bytes 8000000 | tf_op jit(solution)/shard_map/terms/pallas_call | solution.py:281
  43.2 2.6 %terms.4 = (f32[2,2,4,4,24,192]{5,4,3,2,1,0:T(8,128)S(1)}, f32[2,2,4,4,24,192]{5,4,3,2,1,0:T(8,128)S(1)}) custom-call(s32[4]{0:T(128)S(1)} %pad_add_fusion.place, bf16[4,512,384]{2,1,0:T(8,128)(2,1)S(1)} %copy-done.1, f32[4,512,384]{2,1,0:T(8,128)S(1)} %collective-permute-done.9.wide, bf16[2,384,512]{2,1,0:T(8,128)(2,1)S(1)} %get-tuple-element.85.d), custom_call_target="tpu_custom_call" | custom-call | flops 1207959552 | bytes 8000000 | tf_op jit(solution)/shard_map/terms/pallas_call | solution.py:281
  46.0 2.2 %collective-permute-start.13 = (f32[144,128]{1,0:T(8,128)S(1)}, f32[144,128]{1,0:T(8,128)S(1)}, u32[]{:S(2)}, u32[]{:S(2)}) collective-permute-start(f32[144,128]{1,0:T(8,128)S(1)} %select_add_fusion.own), channel_id=1, source_target_pairs={{0,1},{1,0},{2,3},{3,2},{4,5},{5,4},{6,7},{7,6},{8,9},{9,8},{10,11... | collective-permute-start | bytes 221192 | tf_op jit(solution)/shard_map/ppermute | solution.py:33
  48.2 0.9 collective-permute-done.13.other
  49.1 1.7 %join1.1 = (f32[2,4,24,1152]{3,2,1,0:T(8,128)S(1)}, f32[2,4,24,1152]{3,2,1,0:T(8,128)S(1)}) custom-call(s32[4]{0:T(128)S(1)} %pad_add_fusion.place, f32[144,128]{1,0:T(8,128)S(1)} %select_add_fusion.own, f32[144,128]{1,0:T(8,128)S(1)} %collective-permute-done.13.other, f32[2,2,4,4,24,192]{5,4,3,2,1,0:T(8,128)S(1)} %get-tuple-element.97.refs_0_, ...), custom_call_target="tpu_custom_call" | custom-call | flops 339738624 | bytes 8000000 | tf_op jit(solution)/shard_map/join1/pallas_call | solution.py:294
  50.8 2.4 %collective-permute-start.14 = (f32[2,4,24,1152]{3,2,1,0:T(8,128)S(1)}, f32[2,4,24,1152]{3,2,1,0:T(8,128)S(1)}, u32[]{:S(2)}, u32[]{:S(2)}) collective-permute-start(f32[2,4,24,1152]{3,2,1,0:T(8,128)S(1)} %get-tuple-element.104), channel_id=1, source_target_pairs={{0,6},{1,193},{2,4},{3,195},{4,2},{5,197},{6,0},{7,199},{8,14},{9,... | collective-permute-start | bytes 2654216 | tf_op jit(solution)/shard_map/ppermute | solution.py:33
  53.2 1.7 %join0.1 = (f32[2,4,24,1152]{3,2,1,0:T(8,128)S(1)}, f32[2,4,24,1152]{3,2,1,0:T(8,128)S(1)}) custom-call(s32[4]{0:T(128)S(1)} %pad_add_fusion.place, f32[144,128]{1,0:T(8,128)S(1)} %select_add_fusion.own, f32[144,128]{1,0:T(8,128)S(1)} %collective-permute-done.13.other, f32[2,2,4,4,24,192]{5,4,3,2,1,0:T(8,128)S(1)} %get-tuple-element.97.refs_0_, ...), custom_call_target="tpu_custom_call" | custom-call | flops 339738624 | bytes 8000000 | tf_op jit(solution)/shard_map/join0/pallas_call | solution.py:294
  55.0 9.3 %collective-permute-done.14 = f32[2,4,24,1152]{3,2,1,0:T(8,128)S(1)} collective-permute-done((f32[2,4,24,1152]{3,2,1,0:T(8,128)S(1)}, f32[2,4,24,1152]{3,2,1,0:T(8,128)S(1)}, u32[]{:S(2)}, u32[]{:S(2)}) %collective-permute-start.14) | collective-permute-done | bytes 884768 | tf_op jit(solution)/shard_map/ppermute | solution.py:33
  64.5 1.0 collective-permute-done.16
  65.5 1.5 %collective-permute-start.17 = (f32[4,24,1152]{2,1,0:T(8,128)S(1)}, f32[4,24,1152]{2,1,0:T(8,128)S(1)}, u32[]{:S(2)}, u32[]{:S(2)}) collective-permute-start(f32[4,24,1152]{2,1,0:T(8,128)S(1)} %fusion), channel_id=1, source_target_pairs={{0,6},{1,193},{2,4},{3,195},{4,2},{5,197},{6,0},{7,199},{8,14},{9,... | collective-permute-start | bytes 1327112 | tf_op jit(solution)/shard_map/ppermute | solution.py:33
  66.9 4.9 %collective-permute-done.15 = f32[4,24,1152]{2,1,0:T(8,128)S(1)} collective-permute-done((f32[4,24,1152]{2,1,0:T(8,128)S(1)}, f32[4,24,1152]{2,1,0:T(8,128)S(1)}, u32[]{:S(2)}, u32[]{:S(2)}) %collective-permute-start.15) | collective-permute-done | bytes 442400 | tf_op jit(solution)/shard_map/ppermute | solution.py:33
  72.0 2.2 %collective-permute-done.17 = f32[4,24,1152]{2,1,0:T(8,128)S(1)} collective-permute-done((f32[4,24,1152]{2,1,0:T(8,128)S(1)}, f32[4,24,1152]{2,1,0:T(8,128)S(1)}, u32[]{:S(2)}, u32[]{:S(2)}) %collective-permute-start.17) | collective-permute-done | bytes 442400 | tf_op jit(solution)/shard_map/ppermute | solution.py:33
  74.4 2.1 %collective-permute-start.18 = (f32[2,24,1152]{2,1,0:T(8,128)S(1)}, f32[2,24,1152]{2,1,0:T(8,128)S(1)}, u32[]{:S(2)}, u32[]{:S(2)}) collective-permute-start(f32[2,24,1152]{2,1,0:T(8,128)S(1)} %pad_maximum_fusion), channel_id=1, source_target_pairs={{0,128},{1,5},{2,130},{3,7},{4,132},{5,1},{6,134},{7,3},{8,136},{9... | collective-permute-start | bytes 663560 | tf_op jit(solution)/shard_map/ppermute | solution.py:33
  76.5 0.7 collective-permute-start.19
  77.2 0.7 collective-permute-start.20
  77.9 2.8 %collective-permute-done.18 = f32[2,24,1152]{2,1,0:T(8,128)S(1)} collective-permute-done((f32[2,24,1152]{2,1,0:T(8,128)S(1)}, f32[2,24,1152]{2,1,0:T(8,128)S(1)}, u32[]{:S(2)}, u32[]{:S(2)}) %collective-permute-start.18) | collective-permute-done | bytes 221216 | tf_op jit(solution)/shard_map/ppermute | solution.py:33
  80.7 2.3 %collective-permute-done.19 = f32[2,24,1152]{2,1,0:T(8,128)S(1)} collective-permute-done((f32[2,24,1152]{2,1,0:T(8,128)S(1)}, f32[2,24,1152]{2,1,0:T(8,128)S(1)}, u32[]{:S(2)}, u32[]{:S(2)}) %collective-permute-start.19) | collective-permute-done | bytes 221216 | tf_op jit(solution)/shard_map/ppermute | solution.py:33
  83.0 0.5 collective-permute-done.20
  83.7 2.0 %collective-permute-start.21 = (f32[12,1152]{1,0:T(8,128)S(1)}, f32[12,1152]{1,0:T(8,128)S(1)}, u32[]{:S(2)}, u32[]{:S(2)}) collective-permute-start(f32[12,1152]{1,0:T(8,128)S(1)} %get-tuple-element.115), channel_id=1, source_target_pairs={{0,24},{1,25},{2,26},{3,27},{4,28},{5,29},{6,30},{7,31},{8,16},{9,... | collective-permute-start | bytes 165896 | tf_op jit(solution)/shard_map/ppermute | solution.py:33
  85.7 1.0 collective-permute-start.22
  86.7 0.6 collective-permute-start.23
  87.3 1.6 %collective-permute-done.21 = f32[12,1152]{1,0:T(8,128)S(1)} collective-permute-done((f32[12,1152]{1,0:T(8,128)S(1)}, f32[12,1152]{1,0:T(8,128)S(1)}, u32[]{:S(2)}, u32[]{:S(2)}) %collective-permute-start.21) | collective-permute-done | bytes 55328 | tf_op jit(solution)/shard_map/ppermute | solution.py:33
  88.8 2.0 %collective-permute-done.22 = f32[12,1152]{1,0:T(8,128)S(1)} collective-permute-done((f32[12,1152]{1,0:T(8,128)S(1)}, f32[12,1152]{1,0:T(8,128)S(1)}, u32[]{:S(2)}, u32[]{:S(2)}) %collective-permute-start.22) | collective-permute-done | bytes 55328 | tf_op jit(solution)/shard_map/ppermute | solution.py:33
  91.0 2.7 %collective-permute-start.24 = (f32[12,576]{1,0:T(8,128)S(1)}, f32[12,576]{1,0:T(8,128)S(1)}, u32[]{:S(2)}, u32[]{:S(2)}) collective-permute-start(f32[12,576]{1,0:T(8,128)S(1)} %get-tuple-element.118), channel_id=1, source_target_pairs={{0,1},{1,49},{2,3},{3,51},{4,5},{5,53},{6,7},{7,55},{8,9},{9,57},{... | collective-permute-start | bytes 82952 | tf_op jit(solution)/shard_map/ppermute | solution.py:33
  93.7 8.3 %collective-permute-start.25 = (f32[12,576]{1,0:T(8,128)S(1)}, f32[12,576]{1,0:T(8,128)S(1)}, u32[]{:S(2)}, u32[]{:S(2)}) collective-permute-start(f32[12,576]{1,0:T(8,128)S(1)} %get-tuple-element.119), channel_id=1, source_target_pairs={{1,48},{3,50},{5,52},{7,54},{9,56},{11,58},{13,60},{15,62},{17,32}... | collective-permute-start | bytes 82952 | tf_op jit(solution)/shard_map/ppermute | solution.py:33
  102.0 1.7 %collective-permute-done.25 = f32[12,576]{1,0:T(8,128)S(1)} collective-permute-done((f32[12,576]{1,0:T(8,128)S(1)}, f32[12,576]{1,0:T(8,128)S(1)}, u32[]{:S(2)}, u32[]{:S(2)}) %collective-permute-start.25) | collective-permute-done | bytes 27680 | tf_op jit(solution)/shard_map/ppermute | solution.py:33
  103.8 0.7 fusion.14
  (46 shorter events, 1.3 us)
Async XLA Ops:
  3.5 4.5 %collective-permute-start = (f32[144,128]{1,0:T(8,128)}, f32[144,128]{1,0:T(8,128)S(1)}, u32[]{:S(2)}, u32[]{:S(2)}) collective-permute-start(f32[144,128]{1,0:T(8,128)} %get-tuple-element.56), channel_id=1, source_target_pairs={{0,1},{1,0},{2,3},{3,2},{4,5},{5,4},{6,7},{7,6},{8,9},{9,8},{10,11... | collective-permute-start | bytes 221192 | tf_op jit(solution)/shard_map/ppermute | solution.py:33
  7.9 4.7 %collective-permute-start.4 = (f32[4,192,512]{2,1,0:T(8,128)}, f32[4,192,512]{2,1,0:T(8,128)S(1)}, u32[]{:S(2)}, u32[]{:S(2)}) collective-permute-start(f32[4,192,512]{2,1,0:T(8,128)} %get-tuple-element.59.own), channel_id=1, source_target_pairs={{0,1},{1,0},{2,3},{3,2},{4,5},{5,4},{6,7},{7,6},{8,9},{9,8},{10,11... | collective-permute-start | bytes 4718600 | tf_op jit(solution)/shard_map/ppermute | solution.py:33
  9.2 9.4 %collective-permute-start.1 = (f32[144,128]{1,0:T(8,128)S(1)}, f32[144,128]{1,0:T(8,128)S(1)}, u32[]{:S(2)}, u32[]{:S(2)}) collective-permute-start(f32[144,128]{1,0:T(8,128)S(1)} %add.105), channel_id=1, source_target_pairs={{0,2},{1,3},{2,0},{3,1},{4,6},{5,7},{6,4},{7,5},{8,10},{9,11},{10,... | collective-permute-start | bytes 221192 | tf_op jit(solution)/shard_map/ppermute | solution.py:33
  9.3 9.3 %collective-permute-start.2 = (f32[144,128]{1,0:T(8,128)S(1)}, f32[144,128]{1,0:T(8,128)S(1)}, u32[]{:S(2)}, u32[]{:S(2)}) collective-permute-start(f32[144,128]{1,0:T(8,128)S(1)} %add.105), channel_id=1, source_target_pairs={{0,6},{1,7},{2,4},{3,5},{4,2},{5,3},{6,0},{7,1},{8,14},{9,15},{10,... | collective-permute-start | bytes 221192 | tf_op jit(solution)/shard_map/ppermute | solution.py:33
  10.5 8.0 %collective-permute-start.3 = (f32[144,128]{1,0:T(8,128)S(1)}, f32[144,128]{1,0:T(8,128)S(1)}, u32[]{:S(2)}, u32[]{:S(2)}) collective-permute-start(f32[144,128]{1,0:T(8,128)S(1)} %add.105), channel_id=1, source_target_pairs={{0,4},{1,5},{2,6},{3,7},{4,0},{5,1},{6,2},{7,3},{8,12},{9,13},{10,... | collective-permute-start | bytes 221192 | tf_op jit(solution)/shard_map/ppermute | solution.py:33
  12.6 1.9 %copy-start.2 = (bf16[512,3072]{1,0:T(8,128)(2,1)S(1)}, bf16[512,3072]{1,0:T(8,128)(2,1)}, u32[]{:S(2)}) copy-start(bf16[512,3072]{1,0:T(8,128)(2,1)} %x) | copy-start | bytes 9437188
  14.5 2.8 %copy-start.4 = (f32[4,192,512]{2,1,0:T(8,128)}, f32[4,192,512]{2,1,0:T(8,128)S(1)}, u32[]{:S(2)}) copy-start(f32[4,192,512]{2,1,0:T(8,128)S(1)} %collective-permute-done.4.other) | copy-start | bytes 4718596
  17.3 1.2 %copy-start = (bf16[4,512,384]{2,1,0:T(8,128)(2,1)}, bf16[4,512,384]{2,1,0:T(8,128)(2,1)S(1)}, u32[]{:S(2)}) copy-start(bf16[4,512,384]{2,1,0:T(8,128)(2,1)S(1)} %get-tuple-element.76.x) | copy-start | bytes 4718596
  18.5 15.4 %collective-permute-start.9 = (f32[4,512,384]{2,1,0:T(8,128)}, f32[4,512,384]{2,1,0:T(8,128)S(1)}, u32[]{:S(2)}, u32[]{:S(2)}) collective-permute-start(f32[4,512,384]{2,1,0:T(8,128)} %get-tuple-element.77), channel_id=1, source_target_pairs={{0,1},{1,0},{2,3},{3,2},{4,5},{5,4},{6,7},{7,6},{8,9},{9,8},{10,11... | collective-permute-start | bytes 9437192 | tf_op jit(solution)/shard_map/ppermute | solution.py:33
  19.6 14.3 %copy-start.1 = (bf16[4,512,384]{2,1,0:T(8,128)(2,1)S(1)}, bf16[4,512,384]{2,1,0:T(8,128)(2,1)}, u32[]{:S(2)}) copy-start(bf16[4,512,384]{2,1,0:T(8,128)(2,1)} %copy-done) | copy-start | bytes 4718596
  19.6 10.1 %collective-permute-start.5 = (f32[144,128]{1,0:T(8,128)S(1)}, f32[144,128]{1,0:T(8,128)S(1)}, u32[]{:S(2)}, u32[]{:S(2)}) collective-permute-start(f32[144,128]{1,0:T(8,128)S(1)} %add_add_fusion.1), channel_id=1, source_target_pairs={{0,8},{1,9},{2,10},{3,11},{4,12},{5,13},{6,14},{7,15},{8,0},{9,1},... | collective-permute-start | bytes 221192 | tf_op jit(solution)/shard_map/ppermute | solution.py:33
  19.8 10.0 %collective-permute-start.6 = (f32[144,128]{1,0:T(8,128)S(1)}, f32[144,128]{1,0:T(8,128)S(1)}, u32[]{:S(2)}, u32[]{:S(2)}) collective-permute-start(f32[144,128]{1,0:T(8,128)S(1)} %add_add_fusion.1), channel_id=1, source_target_pairs={{0,16},{1,17},{2,18},{3,19},{4,20},{5,21},{6,22},{7,23},{8,24},{9,... | collective-permute-start | bytes 221192 | tf_op jit(solution)/shard_map/ppermute | solution.py:33
  22.8 7.0 %collective-permute-start.7 = (f32[144,128]{1,0:T(8,128)S(1)}, f32[144,128]{1,0:T(8,128)S(1)}, u32[]{:S(2)}, u32[]{:S(2)}) collective-permute-start(f32[144,128]{1,0:T(8,128)S(1)} %add_add_fusion.1), channel_id=1, source_target_pairs={{0,24},{1,25},{2,26},{3,27},{4,28},{5,29},{6,30},{7,31},{8,16},{9,... | collective-permute-start | bytes 221192 | tf_op jit(solution)/shard_map/ppermute | solution.py:33
  23.3 1.4 %copy-start.3 = (f32[4,192,512]{2,1,0:T(8,128)S(1)}, f32[4,192,512]{2,1,0:T(8,128)}, u32[]{:S(2)}) copy-start(f32[4,192,512]{2,1,0:T(8,128)} %get-tuple-element.59.own) | copy-start | bytes 4718596
  24.7 1.4 %copy-start.5 = (f32[4,192,512]{2,1,0:T(8,128)S(1)}, f32[4,192,512]{2,1,0:T(8,128)}, u32[]{:S(2)}) copy-start(f32[4,192,512]{2,1,0:T(8,128)} %copy-done.4) | copy-start | bytes 4718596
  29.8 6.7 %collective-permute-start.8 = (f32[144,128]{1,0:T(8,128)S(1)}, f32[144,128]{1,0:T(8,128)S(1)}, u32[]{:S(2)}, u32[]{:S(2)}) collective-permute-start(f32[144,128]{1,0:T(8,128)S(1)} %add_add_fusion), channel_id=1, source_target_pairs={{0,48},{1,49},{2,50},{3,51},{4,52},{5,53},{6,54},{7,55},{8,56},{9,... | collective-permute-start | bytes 221192 | tf_op jit(solution)/shard_map/ppermute | solution.py:33
  36.6 9.3 %collective-permute-start.10 = (f32[144,128]{1,0:T(8,128)S(1)}, f32[144,128]{1,0:T(8,128)S(1)}, u32[]{:S(2)}, u32[]{:S(2)}) collective-permute-start(f32[144,128]{1,0:T(8,128)S(1)} %add.118), channel_id=1, source_target_pairs={{0,64},{1,65},{2,66},{3,67},{4,68},{5,69},{6,70},{7,71},{8,72},{9,... | collective-permute-start | bytes 221192 | tf_op jit(solution)/shard_map/ppermute | solution.py:33
  38.0 7.9 %collective-permute-start.11 = (f32[144,128]{1,0:T(8,128)S(1)}, f32[144,128]{1,0:T(8,128)S(1)}, u32[]{:S(2)}, u32[]{:S(2)}) collective-permute-start(f32[144,128]{1,0:T(8,128)S(1)} %add.118), channel_id=1, source_target_pairs={{0,192},{1,193},{2,194},{3,195},{4,196},{5,197},{6,198},{7,199},{8... | collective-permute-start | bytes 221192 | tf_op jit(solution)/shard_map/ppermute | solution.py:33
  39.9 6.0 %collective-permute-start.12 = (f32[144,128]{1,0:T(8,128)S(1)}, f32[144,128]{1,0:T(8,128)S(1)}, u32[]{:S(2)}, u32[]{:S(2)}) collective-permute-start(f32[144,128]{1,0:T(8,128)S(1)} %add.118), channel_id=1, source_target_pairs={{0,128},{1,129},{2,130},{3,131},{4,132},{5,133},{6,134},{7,135},{8... | collective-permute-start | bytes 221192 | tf_op jit(solution)/shard_map/ppermute | solution.py:33
  46.0 3.1 %collective-permute-start.13 = (f32[144,128]{1,0:T(8,128)S(1)}, f32[144,128]{1,0:T(8,128)S(1)}, u32[]{:S(2)}, u32[]{:S(2)}) collective-permute-start(f32[144,128]{1,0:T(8,128)S(1)} %select_add_fusion.own), channel_id=1, source_target_pairs={{0,1},{1,0},{2,3},{3,2},{4,5},{5,4},{6,7},{7,6},{8,9},{9,8},{10,11... | collective-permute-start | bytes 221192 | tf_op jit(solution)/shard_map/ppermute | solution.py:33
  50.8 13.5 %collective-permute-start.14 = (f32[2,4,24,1152]{3,2,1,0:T(8,128)S(1)}, f32[2,4,24,1152]{3,2,1,0:T(8,128)S(1)}, u32[]{:S(2)}, u32[]{:S(2)}) collective-permute-start(f32[2,4,24,1152]{3,2,1,0:T(8,128)S(1)} %get-tuple-element.104), channel_id=1, source_target_pairs={{0,6},{1,193},{2,4},{3,195},{4,2},{5,197},{6,0},{7,199},{8,14},{9,... | collective-permute-start | bytes 2654216 | tf_op jit(solution)/shard_map/ppermute | solution.py:33
  53.2 12.2 %collective-permute-start.16 = (f32[2,4,24,1152]{3,2,1,0:T(8,128)S(1)}, f32[2,4,24,1152]{3,2,1,0:T(8,128)S(1)}, u32[]{:S(2)}, u32[]{:S(2)}) collective-permute-start(f32[2,4,24,1152]{3,2,1,0:T(8,128)S(1)} %get-tuple-element.106), channel_id=1, source_target_pairs={{0,2},{1,65},{2,0},{3,67},{4,6},{5,69},{6,4},{7,71},{8,10},{9,73},... | collective-permute-start | bytes 2654216 | tf_op jit(solution)/shard_map/ppermute | solution.py:33
  64.3 7.5 %collective-permute-start.15 = (f32[4,24,1152]{2,1,0:T(8,128)S(1)}, f32[4,24,1152]{2,1,0:T(8,128)S(1)}, u32[]{:S(2)}, u32[]{:S(2)}) collective-permute-start(f32[4,24,1152]{2,1,0:T(8,128)S(1)} %fusion.3), channel_id=1, source_target_pairs={{0,2},{1,65},{2,0},{3,67},{4,6},{5,69},{6,4},{7,71},{8,10},{9,73},... | collective-permute-start | bytes 1327112 | tf_op jit(solution)/shard_map/ppermute | solution.py:33
  65.5 8.7 %collective-permute-start.17 = (f32[4,24,1152]{2,1,0:T(8,128)S(1)}, f32[4,24,1152]{2,1,0:T(8,128)S(1)}, u32[]{:S(2)}, u32[]{:S(2)}) collective-permute-start(f32[4,24,1152]{2,1,0:T(8,128)S(1)} %fusion), channel_id=1, source_target_pairs={{0,6},{1,193},{2,4},{3,195},{4,2},{5,197},{6,0},{7,199},{8,14},{9,... | collective-permute-start | bytes 1327112 | tf_op jit(solution)/shard_map/ppermute | solution.py:33
  74.4 6.4 %collective-permute-start.18 = (f32[2,24,1152]{2,1,0:T(8,128)S(1)}, f32[2,24,1152]{2,1,0:T(8,128)S(1)}, u32[]{:S(2)}, u32[]{:S(2)}) collective-permute-start(f32[2,24,1152]{2,1,0:T(8,128)S(1)} %pad_maximum_fusion), channel_id=1, source_target_pairs={{0,128},{1,5},{2,130},{3,7},{4,132},{5,1},{6,134},{7,3},{8,136},{9... | collective-permute-start | bytes 663560 | tf_op jit(solution)/shard_map/ppermute | solution.py:33
  76.5 6.6 %collective-permute-start.19 = (f32[2,24,1152]{2,1,0:T(8,128)S(1)}, f32[2,24,1152]{2,1,0:T(8,128)S(1)}, u32[]{:S(2)}, u32[]{:S(2)}) collective-permute-start(f32[2,24,1152]{2,1,0:T(8,128)S(1)} %pad_maximum_fusion.1), channel_id=1, source_target_pairs={{0,64},{1,3},{2,66},{3,1},{4,68},{5,7},{6,70},{7,5},{8,72},{9,11},... | collective-permute-start | bytes 663560 | tf_op jit(solution)/shard_map/ppermute | solution.py:33
  77.2 6.4 %collective-permute-start.20 = (f32[2,24,1152]{2,1,0:T(8,128)S(1)}, f32[2,24,1152]{2,1,0:T(8,128)S(1)}, u32[]{:S(2)}, u32[]{:S(2)}) collective-permute-start(f32[2,24,1152]{2,1,0:T(8,128)S(1)} %pad_maximum_fusion.2), channel_id=1, source_target_pairs={{0,192},{1,7},{2,194},{3,5},{4,196},{5,3},{6,198},{7,1},{8,200},{9... | collective-permute-start | bytes 663560 | tf_op jit(solution)/shard_map/ppermute | solution.py:33
  83.7 5.2 %collective-permute-start.21 = (f32[12,1152]{1,0:T(8,128)S(1)}, f32[12,1152]{1,0:T(8,128)S(1)}, u32[]{:S(2)}, u32[]{:S(2)}) collective-permute-start(f32[12,1152]{1,0:T(8,128)S(1)} %get-tuple-element.115), channel_id=1, source_target_pairs={{0,24},{1,25},{2,26},{3,27},{4,28},{5,29},{6,30},{7,31},{8,16},{9,... | collective-permute-start | bytes 165896 | tf_op jit(solution)/shard_map/ppermute | solution.py:33
  85.7 5.1 %collective-permute-start.22 = (f32[12,1152]{1,0:T(8,128)S(1)}, f32[12,1152]{1,0:T(8,128)S(1)}, u32[]{:S(2)}, u32[]{:S(2)}) collective-permute-start(f32[12,1152]{1,0:T(8,128)S(1)} %get-tuple-element.117), channel_id=1, source_target_pairs={{0,16},{1,17},{2,18},{3,19},{4,20},{5,21},{6,22},{7,23},{8,24},{9,... | collective-permute-start | bytes 165896 | tf_op jit(solution)/shard_map/ppermute | solution.py:33
  86.7 4.1 %collective-permute-start.23 = (f32[12,1152]{1,0:T(8,128)S(1)}, f32[12,1152]{1,0:T(8,128)S(1)}, u32[]{:S(2)}, u32[]{:S(2)}) collective-permute-start(f32[12,1152]{1,0:T(8,128)S(1)} %get-tuple-element.116), channel_id=1, source_target_pairs={{0,8},{1,9},{2,10},{3,11},{4,12},{5,13},{6,14},{7,15},{8,0},{9,1},... | collective-permute-start | bytes 165896 | tf_op jit(solution)/shard_map/ppermute | solution.py:33
  91.0 11.0 %collective-permute-start.24 = (f32[12,576]{1,0:T(8,128)S(1)}, f32[12,576]{1,0:T(8,128)S(1)}, u32[]{:S(2)}, u32[]{:S(2)}) collective-permute-start(f32[12,576]{1,0:T(8,128)S(1)} %get-tuple-element.118), channel_id=1, source_target_pairs={{0,1},{1,49},{2,3},{3,51},{4,5},{5,53},{6,7},{7,55},{8,9},{9,57},{... | collective-permute-start | bytes 82952 | tf_op jit(solution)/shard_map/ppermute | solution.py:33
  93.7 10.0 %collective-permute-start.25 = (f32[12,576]{1,0:T(8,128)S(1)}, f32[12,576]{1,0:T(8,128)S(1)}, u32[]{:S(2)}, u32[]{:S(2)}) collective-permute-start(f32[12,576]{1,0:T(8,128)S(1)} %get-tuple-element.119), channel_id=1, source_target_pairs={{1,48},{3,50},{5,52},{7,54},{9,56},{11,58},{13,60},{15,62},{17,32}... | collective-permute-start | bytes 82952 | tf_op jit(solution)/shard_map/ppermute | solution.py:33
